TPU v7x, 256 devices: a whole 4x4x8 slice. The times are simulated.
256 devices in a mesh: grp: 8 (over z_hi, x), frame: 32 (over z_lo, y, core).
Axes of the slice: x: 4, y: 4, z: 8 (z_hi: 2, z_lo: 4; z = z_hi * 4 + z_lo), core: 2. Of those that a mesh axis runs over, the one named last changes fastest.
Arguments:
- hidden_states: bfloat16 [131072, 1280], P(('grp', 'frame')), may hold values from -6 to 6
- norm_gain: float32 [1280], replicated, may hold values from 0.1 to 1.9
- norm_bias: float32 [1280], replicated, may hold values from -3 to 3
- w_query: bfloat16 [1280, 640], replicated, may hold values from -3 to 3, as said below
- w_key: bfloat16 [1280, 640], replicated, may hold values from -3 to 3, as said below
- w_value: bfloat16 [1280, 640], replicated, may hold values from -0.15625 to 0.15625
- w_out: bfloat16 [640, 1280], replicated, may hold values from -0.25 to 0.25
- out_bias: float32 [1280], replicated, may hold values from -3 to 3
Outputs:
- block_out: bfloat16 [131072, 1280], P(('grp', 'frame'))
Inputs may be any that keep to these rules, and one draw needn't show every extreme that they name: `w_query`: scaled by the fan-in. `w_key`: scaled by the fan-in.
All inputs are finite; a program needn't handle non-finite values.
Results may differ from a plain program's by a relative error of at most 0.0078.
Values may be sent and summed in bfloat16 or wider, within the bound.
No kernel may reach another device: no remote copies, remote signals or barrier semaphores. Data moves between devices by JAX's collectives and lax.ppermute only.
A program may use at most 128 MiB of HBM per device.

v0:
```python
import jax
import jax.numpy as jnp
from jax import lax
from jax.sharding import PartitionSpec as P

HEADS = 10
HEAD_DIM = 64


def shifted_2(value, axis, steps):
    count = lax.axis_size(axis)
    initial, last = (max(0, -steps), min(count, count - steps))
    return lax.ppermute(value, axis, [(source, source + steps) for source in range(initial, last)])


def from_root(value, axis, source):
    kept = jnp.where(lax.axis_index(axis) == source, value, 0).astype(value.dtype)
    return lax.psum(kept, axis)


def layer_norm(rows, norm_gain, norm_bias):
    values32 = rows.astype(jnp.float32)
    center = jnp.mean(values32, axis=-1, keepdims=True)
    spread = jnp.mean((values32 - center) ** 2, axis=-1, keepdims=True)
    return ((values32 - center) * lax.rsqrt(spread + 1e-05) * norm_gain + norm_bias).astype(
        jnp.bfloat16
    )


def attend(query, context_keys, context_values):
    tokens = query.shape[0]
    q_heads = query.reshape(tokens, HEADS, HEAD_DIM)
    k_heads = context_keys.reshape(-1, HEADS, HEAD_DIM)
    v_heads = context_values.reshape(-1, HEADS, HEAD_DIM)
    scores = jnp.einsum(
        "qhd,khd->hqk", q_heads, k_heads, preferred_element_type=jnp.float32
    ) * HEAD_DIM ** (-0.5)
    top = jnp.max(scores, axis=-1, keepdims=True)
    raised = jnp.exp(scores - top)
    weights = (raised / jnp.sum(raised, axis=-1, keepdims=True)).astype(jnp.bfloat16)
    mixed = jnp.einsum("hqk,khd->qhd", weights, v_heads, preferred_element_type=jnp.float32)
    return mixed.reshape(tokens, HEADS * HEAD_DIM).astype(jnp.bfloat16)


def body(hidden_states, norm_gain, norm_bias, w_query, w_key, w_value, w_out, out_bias):
    normed = layer_norm(hidden_states, norm_gain, norm_bias)
    keys_own = jnp.dot(normed, w_key, preferred_element_type=jnp.float32).astype(jnp.bfloat16)
    values_own = jnp.dot(normed, w_value, preferred_element_type=jnp.float32).astype(jnp.bfloat16)
    stacked = jnp.stack([keys_own, values_own])
    shifted = shifted_2(stacked, ("grp", "frame"), 1)
    leading = from_root(stacked, ("grp", "frame"), 0)
    query = jnp.dot(normed, w_query, preferred_element_type=jnp.float32).astype(jnp.bfloat16)
    position = lax.axis_index("grp") * lax.axis_size("frame") + lax.axis_index("frame")
    prior = jnp.where(position == 0, stacked, shifted)
    context_keys = jnp.concatenate([leading[0], prior[0]], axis=0)
    context_values = jnp.concatenate([leading[1], prior[1]], axis=0)
    attended = attend(query, context_keys, context_values)
    projected = jnp.dot(attended, w_out, preferred_element_type=jnp.float32)
    total = hidden_states.astype(jnp.float32) + projected + out_bias
    return total.astype(jnp.bfloat16)


def solution(mesh):
    placed = (P(("grp", "frame"), None), P(), P(), P(), P(), P(), P(), P())
    return jax.shard_map(
        body, mesh=mesh, in_specs=placed, out_specs=P(("grp", "frame"), None), check_vma=False
    )
```

profile of v0, /device:TPU:1, one launch (start us, length us, event | category | flops | bytes accessed | tf_op | source)
XLA Modules:
  0.0 325.9 jit_solution(2430438697639655407)
XLA Ops:
  6.5 0.0 copy-start
  6.5 0.0 copy-start.1
  6.5 0.0 copy-start.3
  6.5 0.0 copy-start.4
  6.5 0.0 all-reduce.2.cloned.1.call-start
  6.6 1.7 convert_reduce_fusion
  8.3 0.1 copy-done.1
  8.4 0.5 fusion.10
  8.9 0.0 copy-done.3
  8.9 0.0 copy-done.4
  8.9 0.0 copy-start.2
  8.9 3.8 %fusion.21 = bf16[1,512,640]{2,1,0:T(8,128)(2,1)} fusion(bf16[1280,640]{1,0:T(8,128)(2,1)} %param.13, bf16[512,1280]{1,0:T(8,128)(2,1)S(1)} %copy-done.1, f32[1280]{0:T(1024)S(1)} %copy-done.3, f32[1280]{0:T(1024)S(1)} %copy-done.4, f32[512]{0:T(512)S(1)} %add_rsqrt_fusion, f32[512]{0:T(512)S(1)} %broadcast_multiply_fusion), kind=kOutput, calls=%fused_computation.31 | convolution fusion | flops 843120640 | bytes 3618816 | tf_op jit(solution)/shard_map/dot_general | solution.py:48
  12.6 0.0 copy-done.2
  12.6 2.3 fusion.20
  14.9 3.0 broadcast_select_fusion.1
  17.9 4.8 %collective-permute-start = (bf16[2,512,640]{2,1,0:T(8,128)(2,1)}, bf16[2,512,640]{2,1,0:T(8,128)(2,1)}, u32[]{:S(2)}, u32[]{:S(2)}) collective-permute-start(bf16[2,512,640]{2,1,0:T(8,128)(2,1)} %get-tuple-element.10), channel_id=1, source_target_pairs={{0,1},{1,2},{2,3},{3,4},{4,5},{5,6},{6,7},{7,8},{8,9},{9,10},{10,1... | collective-permute-start | bytes 3932168 | tf_op jit(solution)/shard_map/ppermute | solution.py:13
  22.7 0.0 all-reduce.2.cloned.1.call-update
  22.7 3.6 %convolution_convert_fusion = bf16[512,640]{1,0:T(8,128)(2,1)} fusion(bf16[1280,640]{1,0:T(8,128)(2,1)} %param.11, bf16[512,1280]{1,0:T(8,128)(2,1)S(1)} %copy-done.1, f32[1280]{0:T(1024)S(1)} %copy-done.3, f32[1280]{0:T(1024)S(1)} %copy-done.4, f32[512]{0:T(512)S(1)} %add_rsqrt_fusion, f32[512]{0:T(512)S(1)} %broadcast_multiply_fusion), kind=kOutput, calls=%fused_computation.19 | convolution fusion | flops 843120640 | bytes 3618816 | tf_op jit(solution)/shard_map/dot_general | solution.py:52
  26.4 2.2 copy.16
  28.5 253.6 %all-reduce.2.cloned.1.call-done = bf16[2,512,640]{2,1,0:T(8,128)(2,1)} async-done(((bf16[2,512,640]{2,1,0:T(8,128)(2,1)}), bf16[2,512,640]{2,1,0:T(8,128)(2,1)}) %all-reduce.2.cloned.1.call-update) | async-done | bytes 1310736 | tf_op jit(solution)/shard_map/psum | solution.py:18
  282.1 2.5 fusion.32
  284.6 2.2 copy.14
  286.8 2.2 copy.17
  289.0 0.0 collective-permute-done
  289.0 1.9 broadcast_select_fusion
  290.8 1.2 fusion.33
  292.0 2.2 copy.15
  294.2 2.2 copy.18
  296.3 11.2 %fusion.34 = (f32[10,512]{1,0:T(8,128)S(1)}, f32[10,512,1024]{2,1,0:T(8,128)}) fusion(bf16[512,10,64]{0,2,1:T(8,128)(2,1)} %bitcast.19, bf16[512,10,64]{0,2,1:T(8,128)(2,1)} %bitcast.23, bf16[512,10,64]{0,2,1:T(8,128)(2,1)} %bitcast.21), kind=kOutput, calls=%fused_computation.41 | convolution fusion | flops 689439744 | bytes 22958080 | tf_op jit(solution)/shard_map/sub | solution.py:39
  307.5 0.0 copy-start.5
  307.5 9.2 %fusion.16 = bf16[10,64,512]{2,1,0:T(8,128)(2,1)S(1)} fusion(f32[10,512,1024]{2,1,0:T(8,128)} %get-tuple-element.12, f32[10,512]{1,0:T(8,128)S(1)} %get-tuple-element.11, bf16[512,10,64]{0,2,1:T(8,128)(2,1)} %bitcast.22, bf16[512,10,64]{0,2,1:T(8,128)(2,1)} %bitcast.20), kind=kOutput, calls=%fused_computation.22 | convolution fusion | flops 684523520 | bytes 22958080 | tf_op jit(solution)/shard_map/hqk,khd->qhd/dot_general | solution.py:41
  316.8 0.0 copy-done
  316.8 0.0 copy-done.5
  316.8 2.3 fusion.9
  (2 shorter events, 0.0 us)
Async XLA Ops:
  6.5 310.2 %copy-start = (bf16[640,1280]{1,0:T(8,128)(2,1)S(1)}, bf16[640,1280]{1,0:T(8,128)(2,1)}, u32[]{:S(2)}) copy-start(bf16[640,1280]{1,0:T(8,128)(2,1)} %param.14) | copy-start | bytes 4915204
  6.5 1.8 copy-start.1
  6.5 2.3 copy-start.3
  6.5 2.3 copy-start.4
  6.5 275.6 %all-reduce.2.cloned.1.call-start = ((), (), s32[]{:S(2)}) async-start(), calls=%async_computation | async-start | bytes 2621440 | tf_op jit(solution)/shard_map/psum | solution.py:18
  8.9 3.8 %copy-start.2 = (bf16[1280,640]{1,0:T(8,128)(2,1)S(1)}, bf16[1280,640]{1,0:T(8,128)(2,1)}, u32[]{:S(2)}) copy-start(bf16[1280,640]{1,0:T(8,128)(2,1)} %param.12) | copy-start | bytes 4915204
  17.9 271.0 %collective-permute-start = (bf16[2,512,640]{2,1,0:T(8,128)(2,1)}, bf16[2,512,640]{2,1,0:T(8,128)(2,1)}, u32[]{:S(2)}, u32[]{:S(2)}) collective-permute-start(bf16[2,512,640]{2,1,0:T(8,128)(2,1)} %get-tuple-element.10), channel_id=1, source_target_pairs={{0,1},{1,2},{2,3},{3,4},{4,5},{5,6},{6,7},{7,8},{8,9},{9,10},{10,1... | collective-permute-start | bytes 3932168 | tf_op jit(solution)/shard_map/ppermute | solution.py:13
  307.5 9.2 %copy-start.5 = (f32[1280]{0:T(1024)S(1)}, f32[1280]{0:T(1024)}, u32[]{:S(2)}) copy-start(f32[1280]{0:T(1024)} %param.15) | copy-start | bytes 15364
Sparse Core Ops, SparseCore 0:
  22.8 259.2 all-reduce.1
where the time goes:
time: 327 us; the launch traced here: 326 us
  waiting for transfers between devices  254 us (78%)
  matrix products  32.4 us (10%)
  local copies, waits for them, and re-layouts  14.6 us (4%)
  between operations  13.5 us (4%)
  other arithmetic  7.07 us (2%)
  starting transfers between devices  4.8 us (1%)
    psum x1, waiting for transfers between devices, from_root(): return lax.psum(kept, axis)  254 us
    sub x1, matrix products, attend(): raised = jnp.exp(scores - top)  11.2 us
    dot_general x1, matrix products, attend(): jnp.einsum('hqk,khd->qhd', weights, v_heads, preferred_element_type=jnp.f...  9.21 us
    slice x4, local copies, waits for them, and re-layouts, body(): context_values = jnp.concatenate([leading[1], prior[1]], axis=0)  8 us
  transfers between devices with their start and end apart: 2, of which 1 were waited for; matrix products, arithmetic and copies ran while one was open for 4% of the time, Pallas kernels for 0%

commit v1 on v0

v1 whole, which is shorter than its diff:
```python
import jax
import jax.numpy as jnp
import numpy as np
from jax import lax
from jax.sharding import PartitionSpec as P

HEADS = 10
HEAD_DIM = 64
AXES = ("grp", "frame")


SIZES = {"x": 4, "y": 4, "z": 8}
RING_STEPS = {
    4: (
        (((0, 0), (1, 0)), ((2, 0), (3, 0)), ((0, 1), (3, 1)), ((1, 1), (2, 1))),
        (((0, 0), (3, 0)), ((1, 0), (2, 0)), ((0, 1), (1, 1)), ((2, 1), (3, 1))),
    ),
    8: (
        (((0, 0), (3, 0)), ((0, 1), (5, 1)), ((3, 1), (5, 0))),
        (
            ((0, 0), (6, 0)), ((3, 0), (4, 0)), ((0, 1), (2, 1)), ((5, 1), (4, 1)),
            ((2, 0), (3, 1)), ((5, 0), (6, 1)),
        ),
        (
            ((0, 0), (1, 0)), ((2, 0), (3, 0)), ((4, 0), (5, 0)), ((6, 0), (7, 0)),
            ((0, 1), (7, 1)), ((5, 1), (6, 1)), ((3, 1), (4, 1)), ((1, 1), (2, 1)),
        ),
    ),
}


def device_index(x, y, z, core):
    return ((z // 4) * 4 + x) * 32 + ((z % 4) * 4 + y) * 2 + core


def tree(order):
    holders = {(0, 0, 0, 0), (0, 0, 0, 1)}
    joined = np.full(256, -1, np.int32)
    taken = {"x": 0, "y": 0, "z": 0}
    rounds = []
    for step, axis in enumerate(order):
        pairs = RING_STEPS[SIZES[axis]][taken[axis]]
        taken[axis] += 1
        place = "xyz".index(axis)
        target = [i ^ 1 for i in range(256)]
        lines = {h[:place] + h[place + 1 : 3] for h in holders}
        fresh = set()
        for line in lines:
            for (a, core_a), (b, core_b) in pairs:
                first = line[:place] + (a,) + line[place:] + (core_a,)
                second = line[:place] + (b,) + line[place:] + (core_b,)
                target[device_index(*first)] = device_index(*second)
                target[device_index(*second)] = device_index(*first)
                for source, sink in ((first, second), (second, first)):
                    if core_a == core_b and source in holders and sink not in holders:
                        fresh.add(sink)
                        joined[device_index(*sink)] = step
        holders |= fresh
        rounds.append([(i, target[i]) for i in range(256)])
        assert sorted(target) == list(range(256))
        assert all(i != t for i, t in rounds[-1])
    assert len(holders) == 256
    return rounds, joined


CORE_SWAP = [(i, i ^ 1) for i in range(256)]
NEXT_FRAME = [(i, (i + 1) % 256) for i in range(256)]

ORDERS = ("zzzxxyy", "xxyyzzz", "yyzzzxx")
CHUNKS = (96, 80, 80)


def from_first(rows, position):
    plans = [tree(order) for order in ORDERS]
    table = np.stack([joined for _, joined in plans])
    mine = lax.dynamic_slice_in_dim(jnp.asarray(table), position, 1, axis=1)[:, 0]
    half = rows.shape[0] // 2
    other = lax.ppermute(rows[half:], AXES, CORE_SWAP)
    start = jnp.where(position % 2 == 1, other, rows[:half])
    held = jnp.split(start, np.cumsum(CHUNKS)[:-1], axis=0)
    for step in range(len(ORDERS[0])):
        for which, (rounds, _) in enumerate(plans):
            come = lax.ppermute(held[which], AXES, rounds[step])
            held[which] = jnp.where(mine[which] == step, come, held[which])
    return held + [lax.ppermute(piece, AXES, CORE_SWAP) for piece in held]


def layer_norm(rows, norm_gain, norm_bias):
    values32 = rows.astype(jnp.float32)
    center = jnp.mean(values32, axis=-1, keepdims=True)
    spread = jnp.mean((values32 - center) ** 2, axis=-1, keepdims=True)
    return ((values32 - center) * lax.rsqrt(spread + 1e-05) * norm_gain + norm_bias).astype(
        jnp.bfloat16
    )


def project(rows, weight):
    return jnp.dot(rows, weight, preferred_element_type=jnp.float32).astype(jnp.bfloat16)


def attend(query, context_keys, context_values):
    tokens = query.shape[0]
    q_heads = query.reshape(tokens, HEADS, HEAD_DIM)
    k_heads = context_keys.reshape(-1, HEADS, HEAD_DIM)
    v_heads = context_values.reshape(-1, HEADS, HEAD_DIM)
    scores = jnp.einsum(
        "qhd,khd->hqk", q_heads, k_heads, preferred_element_type=jnp.float32
    ) * HEAD_DIM ** (-0.5)
    top = jnp.max(scores, axis=-1, keepdims=True)
    raised = jnp.exp(scores - top)
    weights = (raised / jnp.sum(raised, axis=-1, keepdims=True)).astype(jnp.bfloat16)
    mixed = jnp.einsum("hqk,khd->qhd", weights, v_heads, preferred_element_type=jnp.float32)
    return mixed.reshape(tokens, HEADS * HEAD_DIM).astype(jnp.bfloat16)


def body(hidden_states, norm_gain, norm_bias, w_query, w_key, w_value, w_out, out_bias):
    position = lax.axis_index("grp") * lax.axis_size("frame") + lax.axis_index("frame")
    shifted = lax.ppermute(hidden_states, AXES, NEXT_FRAME)
    leading = from_first(hidden_states, position)
    query = project(layer_norm(hidden_states, norm_gain, norm_bias), w_query)
    prior = jnp.where(position == 0, hidden_states, shifted)
    context = jnp.concatenate(leading + [prior], axis=0)
    normed = layer_norm(context, norm_gain, norm_bias)
    attended = attend(query, project(normed, w_key), project(normed, w_value))
    projected = jnp.dot(attended, w_out, preferred_element_type=jnp.float32)
    total = hidden_states.astype(jnp.float32) + projected + out_bias
    return total.astype(jnp.bfloat16)


def solution(mesh):
    placed = (P(AXES, None), P(), P(), P(), P(), P(), P(), P())
    return jax.shard_map(
        body, mesh=mesh, in_specs=placed, out_specs=P(AXES, None), check_vma=False
    )
```

time: 327 us -> 121 us (0.37)
  waiting for transfers between devices: 254 us -> 33.8 us
  starting transfers between devices: 4.8 us -> 25.5 us
  local copies, waits for them, and re-layouts: 14.6 us -> 7.43 us
    psum x1 -> x0, waiting for transfers between devices: 254 us -> none  [from_root(): return lax.psum(kept, axis)]
    ppermute x1 -> x26, waiting for transfers between devices: 0.01 us -> 33.8 us  [the longest x21 32.5 us: from_first(): come = lax.ppermute(held[which], AXES, rounds[step])]
    ppermute x1 -> x26, starting transfers between devices: 4.76 us -> 25.5 us  [the longest x21 14.5 us: from_first(): come = lax.ppermute(held[which], AXES, rounds[step])]
    slice x6 -> x2, local copies, waits for them, and re-layouts: 12.4 us -> 2.58 us  [the longest x1 2 us: from_first(): other = lax.ppermute(rows[half:], AXES, CORE_SWAP)]
  transfers between devices with their start and end apart: 2 -> 26, of which waited for: 1 -> 15; matrix products, arithmetic and copies ran while one was open for 4% -> 12% of each run, Pallas kernels for 0% -> 0%
where the time goes in v1:
time: 121 us
  waiting for transfers between devices  33.8 us (28%)
  matrix products  31.6 us (26%)
  starting transfers between devices  25.5 us (21%)
  between operations  13.9 us (11%)
  other arithmetic  8.71 us (7%)
  local copies, waits for them, and re-layouts  7.43 us (6%)
    ppermute x21, waiting for transfers between devices, from_first(): come = lax.ppermute(held[which], AXES, rounds[step])  32.5 us
    ppermute x21, starting transfers between devices, from_first(): come = lax.ppermute(held[which], AXES, rounds[step])  14.5 us
    sub x1, matrix products, attend(): raised = jnp.exp(scores - top)  11.2 us
    dot_general x1, matrix products, attend(): jnp.einsum('hqk,khd->qhd', weights, v_heads, preferred_element_type=jnp.f...  9.29 us
    dot_general x3, matrix products, project(): jnp.dot(rows, weight, preferred_element_type=jnp.float32)  8.88 us
    ppermute x3, starting transfers between devices, from_first(): return held + [lax.ppermute(piece, AXES, CORE_SWAP) for piece in held]  7.67 us
    ppermute x1, starting transfers between devices, body(): shifted = lax.ppermute(hidden_states, AXES, NEXT_FRAME)  2.69 us
    select_n x17, other arithmetic, from_first(): held[which] = jnp.where(mine[which] == step, come, held[which])  2.44 us
  transfers between devices with their start and end apart: 26, of which 15 were waited for; matrix products, arithmetic and copies ran while one was open for 12% of the time, Pallas kernels for 0%

profile of v1, /device:TPU:1, one launch (start us, length us, event | category | flops | bytes accessed | tf_op | source)
XLA Modules:
  0.0 120.9 jit_solution(4982898492585559954)
XLA Ops:
  0.0 2.7 %collective-permute-start.25 = (bf16[512,1280]{1,0:T(8,128)(2,1)}, bf16[512,1280]{1,0:T(8,128)(2,1)}, u32[]{:S(2)}, u32[]{:S(2)}) collective-permute-start(bf16[512,1280]{1,0:T(8,128)(2,1)} %param.9), channel_id=1, source_target_pairs={{0,1},{1,2},{2,3},{3,4},{4,5},{5,6},{6,7},{7,8},{8,9},{9,10},{10,1... | collective-permute-start | bytes 3932168 | tf_op jit(solution)/shard_map/ppermute | solution.py:118
  2.7 2.0 %slice.14 = bf16[256,1280]{1,0:T(8,128)(2,1)} slice(bf16[512,1280]{1,0:T(8,128)(2,1)} %param.9), slice={[256:512], [0:1280]} | slice | bytes 1310720 | tf_op jit(solution)/shard_map/slice | solution.py:78
  4.7 0.7 collective-permute-start
  5.4 0.8 constant_dynamic-slice_fusion
  6.1 0.6 fusion.32
  20.2 0.0 copy-start.7
  20.2 1.6 %convert_reduce_fusion.1 = f32[512]{0:T(512)S(1)} fusion(bf16[512,1280]{1,0:T(8,128)(2,1)} %param.9), kind=kLoop, calls=%fused_computation.17 | loop fusion | flops 1310208 | bytes 1312768 | tf_op jit(solution)/shard_map/reduce_sum | solution.py:90
  21.8 0.5 fusion.16
  22.3 1.2 slice_select_fusion
  23.5 0.8 copy-done.2
  24.3 2.1 %collective-permute-start.15 = (bf16[80,1280]{1,0:T(8,128)(2,1)S(1)}, bf16[80,1280]{1,0:T(8,128)(2,1)}, u32[]{:S(2)}, u32[]{:S(2)}) collective-permute-start(bf16[80,1280]{1,0:T(8,128)(2,1)S(1)} %get-tuple-element.13), channel_id=1, source_target_pairs={{0,2},{1,7},{2,0},{3,5},{4,6},{5,3},{6,4},{7,1},{8,9},{9,8},{10,11... | collective-permute-start | bytes 614408 | tf_op jit(solution)/shard_map/ppermute | solution.py:83
  26.5 2.3 %convolution_convert_fusion.2 = bf16[512,640]{1,0:T(8,128)(2,1)} fusion(bf16[1280,640]{1,0:T(8,128)(2,1)S(1)} %copy-done.3, bf16[512,1280]{1,0:T(8,128)(2,1)S(1)} %copy-done.1, f32[1280]{0:T(1024)S(1)} %copy-done.6, f32[1280]{0:T(1024)S(1)} %copy-done.7, f32[512]{0:T(512)S(1)} %add_rsqrt_fusion.1, f32[512]{0:T(512)S(1)} %broadcast_multiply_fusion.1), kind=kOutput, calls=%fused_computation.29 | convolution fusion | flops 843120640 | bytes 3618816 | tf_op jit(solution)/shard_map/dot_general | solution.py:98
  28.8 2.2 %copy.11 = bf16[512,640]{0,1:T(8,128)(2,1)} copy(bf16[512,640]{1,0:T(8,128)(2,1)} %convolution_convert_fusion.2) | data formatting | bytes 1310720 | tf_op jit(solution)/shard_map/convert_element_type | solution.py:98
  31.0 1.0 split.12
  31.9 4.3 %collective-permute-start.1 = (bf16[96,1280]{1,0:T(8,128)(2,1)S(1)}, bf16[96,1280]{1,0:T(8,128)(2,1)S(1)}, u32[]{:S(2)}, u32[]{:S(2)}) collective-permute-start(bf16[96,1280]{1,0:T(8,128)(2,1)S(1)} %split.12), channel_id=1, source_target_pairs={{0,24},{1,137},{2,3},{3,2},{4,5},{5,4},{6,7},{7,6},{8,9},{9,8},{10... | collective-permute-start | bytes 737288 | tf_op jit(solution)/shard_map/ppermute | solution.py:83
  36.2 1.1 broadcast_select_fusion.7
  37.3 0.1 collective-permute-start.16
  37.4 0.1 collective-permute-start.9
  37.5 2.5 %collective-permute-done.1 = bf16[96,1280]{1,0:T(8,128)(2,1)S(1)} collective-permute-done((bf16[96,1280]{1,0:T(8,128)(2,1)S(1)}, bf16[96,1280]{1,0:T(8,128)(2,1)S(1)}, u32[]{:S(2)}, u32[]{:S(2)}) %collective-permute-start.1) | collective-permute-done | bytes 245792 | tf_op jit(solution)/shard_map/ppermute | solution.py:83
  40.1 1.0 broadcast_select_fusion
  41.0 0.1 collective-permute-start.2
  41.1 1.2 collective-permute-done.16
  42.3 3.2 %collective-permute-start.17 = (bf16[80,1280]{1,0:T(8,128)(2,1)S(1)}, bf16[80,1280]{1,0:T(8,128)(2,1)S(1)}, u32[]{:S(2)}, u32[]{:S(2)}) collective-permute-start(bf16[80,1280]{1,0:T(8,128)(2,1)S(1)} %broadcast_select_fusion.8), channel_id=1, source_target_pairs={{0,24},{1,137},{2,26},{3,139},{4,28},{5,141},{6,30},{7,143},{8,9},... | collective-permute-start | bytes 614408 | tf_op jit(solution)/shard_map/ppermute | solution.py:83
  45.5 0.1 collective-permute-start.10
  45.6 1.7 %collective-permute-done.2 = bf16[96,1280]{1,0:T(8,128)(2,1)S(1)} collective-permute-done((bf16[96,1280]{1,0:T(8,128)(2,1)S(1)}, bf16[96,1280]{1,0:T(8,128)(2,1)S(1)}, u32[]{:S(2)}, u32[]{:S(2)}) %collective-permute-start.2) | collective-permute-done | bytes 245792 | tf_op jit(solution)/shard_map/ppermute | solution.py:83
  47.4 0.1 collective-permute-start.3
  47.5 3.7 %collective-permute-done.17 = bf16[80,1280]{1,0:T(8,128)(2,1)S(1)} collective-permute-done((bf16[80,1280]{1,0:T(8,128)(2,1)S(1)}, bf16[80,1280]{1,0:T(8,128)(2,1)S(1)}, u32[]{:S(2)}, u32[]{:S(2)}) %collective-permute-start.17) | collective-permute-done | bytes 204832 | tf_op jit(solution)/shard_map/ppermute | solution.py:83
  51.2 0.1 collective-permute-start.18
  51.3 0.1 collective-permute-done.10
  51.5 0.1 collective-permute-start.11
  51.6 2.3 %collective-permute-done.3 = bf16[96,1280]{1,0:T(8,128)(2,1)S(1)} collective-permute-done((bf16[96,1280]{1,0:T(8,128)(2,1)S(1)}, bf16[96,1280]{1,0:T(8,128)(2,1)S(1)}, u32[]{:S(2)}, u32[]{:S(2)}) %collective-permute-start.3) | collective-permute-done | bytes 245792 | tf_op jit(solution)/shard_map/ppermute | solution.py:83
  53.9 0.1 collective-permute-start.4
  54.0 3.2 %collective-permute-done.18 = bf16[80,1280]{1,0:T(8,128)(2,1)S(1)} collective-permute-done((bf16[80,1280]{1,0:T(8,128)(2,1)S(1)}, bf16[80,1280]{1,0:T(8,128)(2,1)S(1)}, u32[]{:S(2)}, u32[]{:S(2)}) %collective-permute-start.18) | collective-permute-done | bytes 204832 | tf_op jit(solution)/shard_map/ppermute | solution.py:83
  57.1 0.1 collective-permute-start.19
  57.3 3.2 %collective-permute-start.12 = (bf16[80,1280]{1,0:T(8,128)(2,1)S(1)}, bf16[80,1280]{1,0:T(8,128)(2,1)S(1)}, u32[]{:S(2)}, u32[]{:S(2)}) collective-permute-start(bf16[80,1280]{1,0:T(8,128)(2,1)S(1)} %broadcast_select_fusion.17), channel_id=1, source_target_pairs={{0,24},{1,137},{2,26},{3,139},{4,28},{5,141},{6,30},{7,143},{8,9},... | collective-permute-start | bytes 614408 | tf_op jit(solution)/shard_map/ppermute | solution.py:83
  60.5 0.3 collective-permute-start.5
  60.8 2.2 %collective-permute-done.19 = bf16[80,1280]{1,0:T(8,128)(2,1)S(1)} collective-permute-done((bf16[80,1280]{1,0:T(8,128)(2,1)S(1)}, bf16[80,1280]{1,0:T(8,128)(2,1)S(1)}, u32[]{:S(2)}, u32[]{:S(2)}) %collective-permute-start.19) | collective-permute-done | bytes 204832 | tf_op jit(solution)/shard_map/ppermute | solution.py:83
  63.1 0.1 collective-permute-start.20
  63.2 2.5 %collective-permute-done.12 = bf16[80,1280]{1,0:T(8,128)(2,1)S(1)} collective-permute-done((bf16[80,1280]{1,0:T(8,128)(2,1)S(1)}, bf16[80,1280]{1,0:T(8,128)(2,1)S(1)}, u32[]{:S(2)}, u32[]{:S(2)}) %collective-permute-start.12) | collective-permute-done | bytes 204832 | tf_op jit(solution)/shard_map/ppermute | solution.py:83
  65.7 0.1 collective-permute-start.13
  65.8 0.3 collective-permute-done.5
  66.2 0.1 collective-permute-start.6
  66.3 4.5 %collective-permute-done.20 = bf16[80,1280]{1,0:T(8,128)(2,1)S(1)} collective-permute-done((bf16[80,1280]{1,0:T(8,128)(2,1)S(1)}, bf16[80,1280]{1,0:T(8,128)(2,1)S(1)}, u32[]{:S(2)}, u32[]{:S(2)}) %collective-permute-start.20) | collective-permute-done | bytes 204832 | tf_op jit(solution)/shard_map/ppermute | solution.py:83
  70.8 0.1 collective-permute-start.21
  70.9 1.9 %collective-permute-done.6 = bf16[96,1280]{1,0:T(8,128)(2,1)S(1)} collective-permute-done((bf16[96,1280]{1,0:T(8,128)(2,1)S(1)}, bf16[96,1280]{1,0:T(8,128)(2,1)S(1)}, u32[]{:S(2)}, u32[]{:S(2)}) %collective-permute-start.6) | collective-permute-done | bytes 245792 | tf_op jit(solution)/shard_map/ppermute | solution.py:83
  72.8 0.1 collective-permute-start.7
  73.0 0.1 collective-permute-start.14
  73.1 6.3 %collective-permute-done.7 = bf16[96,1280]{1,0:T(8,128)(2,1)S(1)} collective-permute-done((bf16[96,1280]{1,0:T(8,128)(2,1)S(1)}, bf16[96,1280]{1,0:T(8,128)(2,1)S(1)}, u32[]{:S(2)}, u32[]{:S(2)}) %collective-permute-start.7) | collective-permute-done | bytes 245792 | tf_op jit(solution)/shard_map/ppermute | solution.py:83
  79.4 0.1 constant_dynamic-update-slice_fusion.5
  79.5 7.1 %collective-permute-start.22 = (bf16[96,1280]{1,0:T(8,128)(2,1)S(1)}, bf16[96,1280]{1,0:T(8,128)(2,1)S(1)}, u32[]{:S(2)}, u32[]{:S(2)}) collective-permute-start(bf16[96,1280]{1,0:T(8,128)(2,1)S(1)} %get-tuple-element.10), channel_id=1, source_target_pairs={{0,1},{1,0},{2,3},{3,2},{4,5},{5,4},{6,7},{7,6},{8,9},{9,8},{10,11... | collective-permute-start | bytes 737288 | tf_op jit(solution)/shard_map/ppermute | solution.py:85
  86.5 0.1 constant_dynamic-update-slice_fusion.4
  86.6 0.1 constant_dynamic-update-slice_fusion.3
  86.7 0.1 collective-permute-start.24
  86.8 0.5 collective-permute-start.23
  87.3 0.4 collective-permute-done.22
  87.7 0.8 collective-permute-done.23
  88.6 1.6 %select_dynamic-update-slice_fusion = bf16[1024,1280]{1,0:T(8,128)(2,1)S(1)} fusion(bf16[1024,1280]{1,0:T(8,128)(2,1)S(1)} %constant_dynamic-update-slice_fusion, bf16[512,1280]{1,0:T(8,128)(2,1)S(1)} %copy-done.1, bf16[512,1280]{1,0:T(8,128)(2,1)} %collective-permute-done.25, pred[]{:T(512)S(6)} %eq.177), kind=kLoop, calls=%fused_computation.35 | loop fusion | flops 655360 | bytes 3932161 | tf_op jit(solution)/shard_map/concatenate | solution.py:122
  90.2 0.4 convert_reduce_fusion
  90.7 0.8 fusion.8
  91.5 3.3 %convolution_convert_fusion = bf16[1024,640]{0,1:T(8,128)(2,1)} fusion(bf16[1280,640]{1,0:T(8,128)(2,1)S(1)} %copy-done, bf16[1024,1280]{1,0:T(8,128)(2,1)S(1)} %select_dynamic-update-slice_fusion, f32[1280]{0:T(1024)S(1)} %copy-done.6, f32[1280]{0:T(1024)S(1)} %copy-done.7, f32[1024]{0:T(1024)S(1)} %add_rsqrt_fusion, f32[1024]{0:T(1024)S(1)} %broadcast_multiply_fusion), kind=kOutput, calls=%fused_computation.27 | convolution fusion | flops 1686241280 | bytes 5588992 | tf_op jit(solution)/shard_map/dot_general | solution.py:98
  94.8 3.3 %convolution_convert_fusion.1 = bf16[1024,640]{0,1:T(8,128)(2,1)} fusion(bf16[1280,640]{1,0:T(8,128)(2,1)S(1)} %copy-done.4, bf16[1024,1280]{1,0:T(8,128)(2,1)S(1)} %select_dynamic-update-slice_fusion, f32[1280]{0:T(1024)S(1)} %copy-done.6, f32[1280]{0:T(1024)S(1)} %copy-done.7, f32[1024]{0:T(1024)S(1)} %add_rsqrt_fusion, f32[1024]{0:T(1024)S(1)} %broadcast_multiply_fusion), kind=kOutput, calls=%fused_computation.28 | convolution fusion | flops 1686241280 | bytes 5588992 | tf_op jit(solution)/shard_map/dot_general | solution.py:98
  98.1 11.2 %fusion.33 = (f32[10,512]{1,0:T(8,128)S(1)}, f32[10,512,1024]{2,1,0:T(8,128)}) fusion(bf16[512,10,64]{0,2,1:T(8,128)(2,1)} %bitcast.37, bf16[1024,10,64]{0,2,1:T(8,128)(2,1)} %bitcast.39), kind=kOutput, calls=%fused_computation.72 | convolution fusion | flops 686818304 | bytes 22958080 | tf_op jit(solution)/shard_map/sub | solution.py:110
  109.3 9.3 %fusion.22 = bf16[10,64,512]{2,1,0:T(8,128)(2,1)S(1)} fusion(bf16[1024,10,64]{0,2,1:T(8,128)(2,1)} %bitcast.38, f32[10,512,1024]{2,1,0:T(8,128)} %get-tuple-element.19, f32[10,512]{1,0:T(8,128)S(1)} %get-tuple-element.18), kind=kOutput, calls=%fused_computation.30 | convolution fusion | flops 681902080 | bytes 22958080 | tf_op jit(solution)/shard_map/hqk,khd->qhd/dot_general | solution.py:112
  118.6 2.3 %fusion.15 = bf16[512,1280]{1,0:T(8,128)(2,1)} fusion(bf16[512,640]{0,1:T(8,128)(2,1)S(1)} %bitcast.40, bf16[640,1280]{1,0:T(8,128)(2,1)S(1)} %copy-done.5, bf16[512,1280]{1,0:T(8,128)(2,1)S(1)} %copy-done.1, f32[1280]{0:T(1024)S(1)} %copy-done.8), kind=kOutput, calls=%fused_computation.21 | convolution fusion | flops 841482240 | bytes 4920320 | tf_op jit(solution)/shard_map/dot_general | solution.py:125
  (51 shorter events, 0.6 us)
Async XLA Ops:
  0.0 91.5 %copy-start = (bf16[1280,640]{1,0:T(8,128)(2,1)S(1)}, bf16[1280,640]{1,0:T(8,128)(2,1)}, u32[]{:S(2)}) copy-start(bf16[1280,640]{1,0:T(8,128)(2,1)} %param.13) | copy-start | bytes 4915204
  0.0 21.8 %copy-start.1 = (bf16[512,1280]{1,0:T(8,128)(2,1)S(1)}, bf16[512,1280]{1,0:T(8,128)(2,1)}, u32[]{:S(2)}) copy-start(bf16[512,1280]{1,0:T(8,128)(2,1)} %param.9) | copy-start | bytes 3932164
  0.0 88.6 %collective-permute-start.25 = (bf16[512,1280]{1,0:T(8,128)(2,1)}, bf16[512,1280]{1,0:T(8,128)(2,1)}, u32[]{:S(2)}, u32[]{:S(2)}) collective-permute-start(bf16[512,1280]{1,0:T(8,128)(2,1)} %param.9), channel_id=1, source_target_pairs={{0,1},{1,2},{2,3},{3,4},{4,5},{5,6},{6,7},{7,8},{8,9},{9,10},{10,1... | collective-permute-start | bytes 3932168 | tf_op jit(solution)/shard_map/ppermute | solution.py:118
  4.7 17.6 %collective-permute-start = (bf16[256,1280]{1,0:T(8,128)(2,1)}, bf16[256,1280]{1,0:T(8,128)(2,1)}, u32[]{:S(2)}, u32[]{:S(2)}) collective-permute-start(bf16[256,1280]{1,0:T(8,128)(2,1)} %slice.14), channel_id=1, source_target_pairs={{0,1},{1,0},{2,3},{3,2},{4,5},{5,4},{6,7},{7,6},{8,9},{9,8},{10,11... | collective-permute-start | bytes 1966088 | tf_op jit(solution)/shard_map/ppermute | solution.py:78
  20.1 6.3 %copy-start.6 = (f32[1280]{0:T(1024)S(1)}, f32[1280]{0:T(1024)}, u32[]{:S(2)}) copy-start(f32[1280]{0:T(1024)} %param.11) | copy-start | bytes 15364
  20.2 6.3 %copy-start.7 = (f32[1280]{0:T(1024)S(1)}, f32[1280]{0:T(1024)}, u32[]{:S(2)}) copy-start(f32[1280]{0:T(1024)} %param.10) | copy-start | bytes 15364
  21.8 4.7 %copy-start.3 = (bf16[1280,640]{1,0:T(8,128)(2,1)S(1)}, bf16[1280,640]{1,0:T(8,128)(2,1)}, u32[]{:S(2)}) copy-start(bf16[1280,640]{1,0:T(8,128)(2,1)} %param.12) | copy-start | bytes 4915204
  23.5 0.8 copy-start.2
  24.3 11.9 %collective-permute-start.15 = (bf16[80,1280]{1,0:T(8,128)(2,1)S(1)}, bf16[80,1280]{1,0:T(8,128)(2,1)}, u32[]{:S(2)}, u32[]{:S(2)}) collective-permute-start(bf16[80,1280]{1,0:T(8,128)(2,1)S(1)} %get-tuple-element.13), channel_id=1, source_target_pairs={{0,2},{1,7},{2,0},{3,5},{4,6},{5,3},{6,4},{7,1},{8,9},{9,8},{10,11... | collective-permute-start | bytes 614408 | tf_op jit(solution)/shard_map/ppermute | solution.py:83
  26.5 9.8 %collective-permute-start.8 = (bf16[80,1280]{1,0:T(8,128)(2,1)S(1)}, bf16[80,1280]{1,0:T(8,128)(2,1)}, u32[]{:S(2)}, u32[]{:S(2)}) collective-permute-start(bf16[80,1280]{1,0:T(8,128)(2,1)S(1)} %get-tuple-element.14), channel_id=1, source_target_pairs={{0,32},{1,97},{2,3},{3,2},{4,5},{5,4},{6,7},{7,6},{8,9},{9,8},{10,... | collective-permute-start | bytes 614408 | tf_op jit(solution)/shard_map/ppermute | solution.py:83
  31.9 8.1 %collective-permute-start.1 = (bf16[96,1280]{1,0:T(8,128)(2,1)S(1)}, bf16[96,1280]{1,0:T(8,128)(2,1)S(1)}, u32[]{:S(2)}, u32[]{:S(2)}) collective-permute-start(bf16[96,1280]{1,0:T(8,128)(2,1)S(1)} %split.12), channel_id=1, source_target_pairs={{0,24},{1,137},{2,3},{3,2},{4,5},{5,4},{6,7},{7,6},{8,9},{9,8},{10... | collective-permute-start | bytes 737288 | tf_op jit(solution)/shard_map/ppermute | solution.py:83
  37.3 5.0 %collective-permute-start.16 = (bf16[80,1280]{1,0:T(8,128)(2,1)S(1)}, bf16[80,1280]{1,0:T(8,128)(2,1)S(1)}, u32[]{:S(2)}, u32[]{:S(2)}) collective-permute-start(bf16[80,1280]{1,0:T(8,128)(2,1)S(1)} %get-tuple-element.11), channel_id=1, source_target_pairs={{0,6},{1,3},{2,4},{3,1},{4,2},{5,7},{6,0},{7,5},{8,9},{9,8},{10,11... | collective-permute-start | bytes 614408 | tf_op jit(solution)/shard_map/ppermute | solution.py:83
  37.4 8.1 %collective-permute-start.9 = (bf16[80,1280]{1,0:T(8,128)(2,1)S(1)}, bf16[80,1280]{1,0:T(8,128)(2,1)S(1)}, u32[]{:S(2)}, u32[]{:S(2)}) collective-permute-start(bf16[80,1280]{1,0:T(8,128)(2,1)S(1)} %get-tuple-element.12), channel_id=1, source_target_pairs={{0,96},{1,33},{2,3},{3,2},{4,5},{5,4},{6,7},{7,6},{8,9},{9,8},{10,... | collective-permute-start | bytes 614408 | tf_op jit(solution)/shard_map/ppermute | solution.py:83
  41.0 6.3 %collective-permute-start.2 = (bf16[96,1280]{1,0:T(8,128)(2,1)S(1)}, bf16[96,1280]{1,0:T(8,128)(2,1)S(1)}, u32[]{:S(2)}, u32[]{:S(2)}) collective-permute-start(bf16[96,1280]{1,0:T(8,128)(2,1)S(1)} %broadcast_select_fusion), channel_id=1, source_target_pairs={{0,144},{1,17},{2,3},{3,2},{4,5},{5,4},{6,7},{7,6},{8,9},{9,8},{10... | collective-permute-start | bytes 737288 | tf_op jit(solution)/shard_map/ppermute | solution.py:83
  42.3 8.9 %collective-permute-start.17 = (bf16[80,1280]{1,0:T(8,128)(2,1)S(1)}, bf16[80,1280]{1,0:T(8,128)(2,1)S(1)}, u32[]{:S(2)}, u32[]{:S(2)}) collective-permute-start(bf16[80,1280]{1,0:T(8,128)(2,1)S(1)} %broadcast_select_fusion.8), channel_id=1, source_target_pairs={{0,24},{1,137},{2,26},{3,139},{4,28},{5,141},{6,30},{7,143},{8,9},... | collective-permute-start | bytes 614408 | tf_op jit(solution)/shard_map/ppermute | solution.py:83
  45.5 5.9 %collective-permute-start.10 = (bf16[80,1280]{1,0:T(8,128)(2,1)S(1)}, bf16[80,1280]{1,0:T(8,128)(2,1)S(1)}, u32[]{:S(2)}, u32[]{:S(2)}) collective-permute-start(bf16[80,1280]{1,0:T(8,128)(2,1)S(1)} %broadcast_select_fusion.15), channel_id=1, source_target_pairs={{0,2},{1,7},{2,0},{3,5},{4,6},{5,3},{6,4},{7,1},{8,9},{9,8},{10,11... | collective-permute-start | bytes 614408 | tf_op jit(solution)/shard_map/ppermute | solution.py:83
  47.4 6.4 %collective-permute-start.3 = (bf16[96,1280]{1,0:T(8,128)(2,1)S(1)}, bf16[96,1280]{1,0:T(8,128)(2,1)S(1)}, u32[]{:S(2)}, u32[]{:S(2)}) collective-permute-start(bf16[96,1280]{1,0:T(8,128)(2,1)S(1)} %broadcast_select_fusion.1), channel_id=1, source_target_pairs={{0,8},{1,153},{2,3},{3,2},{4,5},{5,4},{6,7},{7,6},{8,0},{9,17},{10... | collective-permute-start | bytes 737288 | tf_op jit(solution)/shard_map/ppermute | solution.py:83
  51.2 5.9 %collective-permute-start.18 = (bf16[80,1280]{1,0:T(8,128)(2,1)S(1)}, bf16[80,1280]{1,0:T(8,128)(2,1)S(1)}, u32[]{:S(2)}, u32[]{:S(2)}) collective-permute-start(bf16[80,1280]{1,0:T(8,128)(2,1)S(1)} %broadcast_select_fusion.9), channel_id=1, source_target_pairs={{0,144},{1,17},{2,146},{3,19},{4,148},{5,21},{6,150},{7,23},{8,9},... | collective-permute-start | bytes 614408 | tf_op jit(solution)/shard_map/ppermute | solution.py:83
  51.5 5.8 %collective-permute-start.11 = (bf16[80,1280]{1,0:T(8,128)(2,1)S(1)}, bf16[80,1280]{1,0:T(8,128)(2,1)S(1)}, u32[]{:S(2)}, u32[]{:S(2)}) collective-permute-start(bf16[80,1280]{1,0:T(8,128)(2,1)S(1)} %broadcast_select_fusion.16), channel_id=1, source_target_pairs={{0,6},{1,3},{2,4},{3,1},{4,2},{5,7},{6,0},{7,5},{8,9},{9,8},{10,11... | collective-permute-start | bytes 614408 | tf_op jit(solution)/shard_map/ppermute | solution.py:83
  53.9 6.6 %collective-permute-start.4 = (bf16[96,1280]{1,0:T(8,128)(2,1)S(1)}, bf16[96,1280]{1,0:T(8,128)(2,1)S(1)}, u32[]{:S(2)}, u32[]{:S(2)}) collective-permute-start(bf16[96,1280]{1,0:T(8,128)(2,1)S(1)} %broadcast_select_fusion.2), channel_id=1, source_target_pairs={{0,32},{1,97},{2,3},{3,2},{4,5},{5,4},{6,7},{7,6},{8,40},{9,105},{... | collective-permute-start | bytes 737288 | tf_op jit(solution)/shard_map/ppermute | solution.py:83
  57.1 5.9 %collective-permute-start.19 = (bf16[80,1280]{1,0:T(8,128)(2,1)S(1)}, bf16[80,1280]{1,0:T(8,128)(2,1)S(1)}, u32[]{:S(2)}, u32[]{:S(2)}) collective-permute-start(bf16[80,1280]{1,0:T(8,128)(2,1)S(1)} %broadcast_select_fusion.10), channel_id=1, source_target_pairs={{0,8},{1,153},{2,10},{3,155},{4,12},{5,157},{6,14},{7,159},{8,0},{... | collective-permute-start | bytes 614408 | tf_op jit(solution)/shard_map/ppermute | solution.py:83
  57.3 8.4 %collective-permute-start.12 = (bf16[80,1280]{1,0:T(8,128)(2,1)S(1)}, bf16[80,1280]{1,0:T(8,128)(2,1)S(1)}, u32[]{:S(2)}, u32[]{:S(2)}) collective-permute-start(bf16[80,1280]{1,0:T(8,128)(2,1)S(1)} %broadcast_select_fusion.17), channel_id=1, source_target_pairs={{0,24},{1,137},{2,26},{3,139},{4,28},{5,141},{6,30},{7,143},{8,9},... | collective-permute-start | bytes 614408 | tf_op jit(solution)/shard_map/ppermute | solution.py:83
  60.5 5.6 %collective-permute-start.5 = (bf16[96,1280]{1,0:T(8,128)(2,1)S(1)}, bf16[96,1280]{1,0:T(8,128)(2,1)S(1)}, u32[]{:S(2)}, u32[]{:S(2)}) collective-permute-start(bf16[96,1280]{1,0:T(8,128)(2,1)S(1)} %broadcast_select_fusion.3), channel_id=1, source_target_pairs={{0,96},{1,33},{2,3},{3,2},{4,5},{5,4},{6,7},{7,6},{8,104},{9,41},{... | collective-permute-start | bytes 737288 | tf_op jit(solution)/shard_map/ppermute | solution.py:83
  63.1 7.7 %collective-permute-start.20 = (bf16[80,1280]{1,0:T(8,128)(2,1)S(1)}, bf16[80,1280]{1,0:T(8,128)(2,1)S(1)}, u32[]{:S(2)}, u32[]{:S(2)}) collective-permute-start(bf16[80,1280]{1,0:T(8,128)(2,1)S(1)} %broadcast_select_fusion.11), channel_id=1, source_target_pairs={{0,32},{1,97},{2,34},{3,99},{4,36},{5,101},{6,38},{7,103},{8,40},{... | collective-permute-start | bytes 614408 | tf_op jit(solution)/shard_map/ppermute | solution.py:83
  65.7 7.2 %collective-permute-start.13 = (bf16[80,1280]{1,0:T(8,128)(2,1)S(1)}, bf16[80,1280]{1,0:T(8,128)(2,1)S(1)}, u32[]{:S(2)}, u32[]{:S(2)}) collective-permute-start(bf16[80,1280]{1,0:T(8,128)(2,1)S(1)} %broadcast_select_fusion.18), channel_id=1, source_target_pairs={{0,144},{1,17},{2,146},{3,19},{4,148},{5,21},{6,150},{7,23},{8,9},... | collective-permute-start | bytes 614408 | tf_op jit(solution)/shard_map/ppermute | solution.py:83
  66.2 6.6 %collective-permute-start.6 = (bf16[96,1280]{1,0:T(8,128)(2,1)S(1)}, bf16[96,1280]{1,0:T(8,128)(2,1)S(1)}, u32[]{:S(2)}, u32[]{:S(2)}) collective-permute-start(bf16[96,1280]{1,0:T(8,128)(2,1)S(1)} %broadcast_select_fusion.4), channel_id=1, source_target_pairs={{0,2},{1,7},{2,0},{3,5},{4,6},{5,3},{6,4},{7,1},{8,10},{9,15},{10,... | collective-permute-start | bytes 737288 | tf_op jit(solution)/shard_map/ppermute | solution.py:83
  70.8 15.8 %collective-permute-start.21 = (bf16[80,1280]{1,0:T(8,128)(2,1)S(1)}, bf16[80,1280]{1,0:T(8,128)(2,1)S(1)}, u32[]{:S(2)}, u32[]{:S(2)}) collective-permute-start(bf16[80,1280]{1,0:T(8,128)(2,1)S(1)} %broadcast_select_fusion.12), channel_id=1, source_target_pairs={{0,96},{1,33},{2,98},{3,35},{4,100},{5,37},{6,102},{7,39},{8,104},... | collective-permute-start | bytes 614408 | tf_op jit(solution)/shard_map/ppermute | solution.py:83
  72.8 6.6 %collective-permute-start.7 = (bf16[96,1280]{1,0:T(8,128)(2,1)S(1)}, bf16[96,1280]{1,0:T(8,128)(2,1)S(1)}, u32[]{:S(2)}, u32[]{:S(2)}) collective-permute-start(bf16[96,1280]{1,0:T(8,128)(2,1)S(1)} %broadcast_select_fusion.5), channel_id=1, source_target_pairs={{0,6},{1,3},{2,4},{3,1},{4,2},{5,7},{6,0},{7,5},{8,14},{9,11},{10,... | collective-permute-start | bytes 737288 | tf_op jit(solution)/shard_map/ppermute | solution.py:83
  73.0 13.6 %collective-permute-start.14 = (bf16[80,1280]{1,0:T(8,128)(2,1)S(1)}, bf16[80,1280]{1,0:T(8,128)(2,1)S(1)}, u32[]{:S(2)}, u32[]{:S(2)}) collective-permute-start(bf16[80,1280]{1,0:T(8,128)(2,1)S(1)} %broadcast_select_fusion.19), channel_id=1, source_target_pairs={{0,8},{1,153},{2,10},{3,155},{4,12},{5,157},{6,14},{7,159},{8,0},{... | collective-permute-start | bytes 614408 | tf_op jit(solution)/shard_map/ppermute | solution.py:83
  79.5 8.2 %collective-permute-start.22 = (bf16[96,1280]{1,0:T(8,128)(2,1)S(1)}, bf16[96,1280]{1,0:T(8,128)(2,1)S(1)}, u32[]{:S(2)}, u32[]{:S(2)}) collective-permute-start(bf16[96,1280]{1,0:T(8,128)(2,1)S(1)} %get-tuple-element.10), channel_id=1, source_target_pairs={{0,1},{1,0},{2,3},{3,2},{4,5},{5,4},{6,7},{7,6},{8,9},{9,8},{10,11... | collective-permute-start | bytes 737288 | tf_op jit(solution)/shard_map/ppermute | solution.py:85
  86.7 1.9 %collective-permute-start.24 = (bf16[80,1280]{1,0:T(8,128)(2,1)S(1)}, bf16[80,1280]{1,0:T(8,128)(2,1)S(1)}, u32[]{:S(2)}, u32[]{:S(2)}) collective-permute-start(bf16[80,1280]{1,0:T(8,128)(2,1)S(1)} %get-tuple-element.6), channel_id=1, source_target_pairs={{0,1},{1,0},{2,3},{3,2},{4,5},{5,4},{6,7},{7,6},{8,9},{9,8},{10,11... | collective-permute-start | bytes 614408 | tf_op jit(solution)/shard_map/ppermute | solution.py:85
  86.8 1.8 %collective-permute-start.23 = (bf16[80,1280]{1,0:T(8,128)(2,1)S(1)}, bf16[80,1280]{1,0:T(8,128)(2,1)S(1)}, u32[]{:S(2)}, u32[]{:S(2)}) collective-permute-start(bf16[80,1280]{1,0:T(8,128)(2,1)S(1)} %get-tuple-element.8), channel_id=1, source_target_pairs={{0,1},{1,0},{2,3},{3,2},{4,5},{5,4},{6,7},{7,6},{8,9},{9,8},{10,11... | collective-permute-start | bytes 614408 | tf_op jit(solution)/shard_map/ppermute | solution.py:85
  91.5 3.3 %copy-start.4 = (bf16[1280,640]{1,0:T(8,128)(2,1)S(1)}, bf16[1280,640]{1,0:T(8,128)(2,1)}, u32[]{:S(2)}) copy-start(bf16[1280,640]{1,0:T(8,128)(2,1)} %param.14) | copy-start | bytes 4915204
  109.3 9.3 %copy-start.5 = (bf16[640,1280]{1,0:T(8,128)(2,1)S(1)}, bf16[640,1280]{1,0:T(8,128)(2,1)}, u32[]{:S(2)}) copy-start(bf16[640,1280]{1,0:T(8,128)(2,1)} %param.15) | copy-start | bytes 4915204
  109.3 9.3 %copy-start.8 = (f32[1280]{0:T(1024)S(1)}, f32[1280]{0:T(1024)}, u32[]{:S(2)}) copy-start(f32[1280]{0:T(1024)} %param.16) | copy-start | bytes 15364

commit v2 on v0

v2 whole, which is shorter than its diff:
```python
import jax
import jax.numpy as jnp
from jax import lax
from jax.sharding import PartitionSpec as P

HEADS = 10
HEAD_DIM = 64
AXES = ("grp", "frame")


SIZES = {"x": 4, "y": 4, "z": 8}

EVEN4 = (((0, 0), (1, 0)), ((2, 0), (3, 0)), ((0, 1), (3, 1)), ((1, 1), (2, 1)))
ODD4 = (((0, 0), (3, 0)), ((1, 0), (2, 0)), ((0, 1), (1, 1)), ((2, 1), (3, 1)))
EVEN8 = (
    ((0, 0), (1, 0)), ((2, 0), (3, 0)), ((4, 0), (5, 0)), ((6, 0), (7, 0)),
    ((0, 1), (7, 1)), ((5, 1), (6, 1)), ((3, 1), (4, 1)), ((1, 1), (2, 1)),
)
ODD8 = (
    ((0, 0), (7, 0)), ((5, 0), (6, 0)), ((3, 0), (4, 0)), ((1, 0), (2, 0)),
    ((0, 1), (1, 1)), ((2, 1), (3, 1)), ((4, 1), (5, 1)), ((6, 1), (7, 1)),
)
HALF8 = (((0, 0), (4, 0)), ((0, 1), (4, 1)))
FIRST8 = (((0, 0), (3, 0)), ((0, 1), (5, 1)), ((3, 1), (5, 0)))
SECOND8 = (
    ((0, 0), (6, 0)), ((3, 0), (4, 0)), ((0, 1), (2, 1)), ((5, 1), (4, 1)),
    ((2, 0), (3, 1)), ((5, 0), (6, 1)),
)


def device_index(x, y, z, core):
    return ((z // 4) * 4 + x) * 32 + ((z % 4) * 4 + y) * 2 + core


def permutation(axis, pairs, lines):
    place = "xyz".index(axis)
    target = [i ^ 1 for i in range(256)]
    for line in lines:
        for (a, core_a), (b, core_b) in pairs:
            first = device_index(*line[:place], a, *line[place:], core_a)
            second = device_index(*line[:place], b, *line[place:], core_b)
            target[first], target[second] = second, first
    assert sorted(target) == list(range(256))
    assert all(target[i] != i for i in range(256))
    return [(i, target[i]) for i in range(256)]


def all_lines(axis):
    sizes = [SIZES[other] for other in "xyz" if other != axis]
    return [(a, b) for a in range(sizes[0]) for b in range(sizes[1])]


def tree(steps):
    held = {"x": {0}, "y": {0}, "z": {0}}
    rounds = []
    for axis, pairs in steps:
        others = [other for other in "xyz" if other != axis]
        lines = set()
        for a in held[others[0]]:
            for b in held[others[1]]:
                lines.add((a, b))
                lines.add((-a % SIZES[others[0]], -b % SIZES[others[1]]))
        if len({end for pair in pairs for end in pair}) == 2 * SIZES[axis]:
            lines = all_lines(axis)
        before = {name: sum(1 << v for v in nodes) for name, nodes in held.items()}
        rounds.append((permutation(axis, pairs, lines), before))
        fresh = set()
        for (a, core_a), (b, core_b) in pairs:
            if core_a == core_b == 0:
                fresh |= {b} if a in held[axis] else set()
                fresh |= {a} if b in held[axis] else set()
        held[axis] = held[axis] | fresh
    assert all(len(held[name]) == SIZES[name] for name in "xyz")
    return rounds


CORE_SWAP = [(i, i ^ 1) for i in range(256)]
NEXT_FRAME = [(i, (i + 1) % 256) for i in range(256)]
X, Y = [("x", EVEN4), ("x", ODD4)], [("y", EVEN4), ("y", ODD4)]
Z = [("z", FIRST8), ("z", SECOND8), ("z", EVEN8)]
PLANS = (
    (96, X + Y + Z, 0),
    (96, Y + Z + X, 0),
    (64, [("z", HALF8), ("z", EVEN8), ("z", ODD8)] + X + Y, 1),
)


def from_first(rows):
    grp, frame = lax.axis_index("grp"), lax.axis_index("frame")
    core = frame % 2
    place = {"x": grp % 4, "y": frame // 2 % 4, "z": grp // 4 * 4 + frame // 8}
    place = {n: jnp.where(core == 1, (SIZES[n] - v) % SIZES[n], v) for n, v in place.items()}

    def holds(before):
        inside = [(before[n] >> place[n]) & 1 for n in "xyz"]
        return inside[0] * inside[1] * inside[2] == 1

    half = rows.shape[0] // 2
    other = lax.ppermute(rows, AXES, CORE_SWAP)
    pieces, start = [], 0
    for size, _, _ in PLANS:
        pieces.append(
            jnp.where(
                core == 1, other[half + start : half + start + size], rows[start : start + size]
            )
        )
        start += size
    trees = [tree(steps) for _, steps, _ in PLANS]
    for step in range(len(trees[0])):
        for which, (_, _, skip) in enumerate(PLANS):
            if step == len(trees[which]):
                continue
            pairs, before = trees[which][step]
            piece = pieces[which]
            if skip <= step < skip + 2:
                middle = piece.shape[0] // 2
                piece, sent = piece[:middle], piece[middle:]
            else:
                sent = piece
            come = lax.ppermute(sent, AXES, pairs)
            pieces[which] = jnp.where(holds(before), piece, come)
    for back in (1, 0):
        for which, (_, steps, skip) in enumerate(PLANS):
            axis, pairs = steps[skip + back]
            come = lax.ppermute(
                pieces[which], AXES, permutation(axis, pairs, all_lines(axis))
            )
            pieces[which] = jnp.concatenate([pieces[which], come], axis=0)
    return pieces + [lax.ppermute(piece, AXES, CORE_SWAP) for piece in pieces]


def layer_norm(rows, norm_gain, norm_bias):
    values32 = rows.astype(jnp.float32)
    center = jnp.mean(values32, axis=-1, keepdims=True)
    spread = jnp.mean((values32 - center) ** 2, axis=-1, keepdims=True)
    return ((values32 - center) * lax.rsqrt(spread + 1e-05) * norm_gain + norm_bias).astype(
        jnp.bfloat16
    )


def project(rows, weight):
    return jnp.dot(rows, weight, preferred_element_type=jnp.float32).astype(jnp.bfloat16)


def attend(query, context_keys, context_values):
    tokens = query.shape[0]
    q_heads = query.reshape(tokens, HEADS, HEAD_DIM)
    k_heads = context_keys.reshape(-1, HEADS, HEAD_DIM)
    v_heads = context_values.reshape(-1, HEADS, HEAD_DIM)
    scores = jnp.einsum(
        "qhd,khd->hqk", q_heads, k_heads, preferred_element_type=jnp.float32
    ) * HEAD_DIM ** (-0.5)
    top = jnp.max(scores, axis=-1, keepdims=True)
    raised = jnp.exp(scores - top)
    weights = (raised / jnp.sum(raised, axis=-1, keepdims=True)).astype(jnp.bfloat16)
    mixed = jnp.einsum("hqk,khd->qhd", weights, v_heads, preferred_element_type=jnp.float32)
    return mixed.reshape(tokens, HEADS * HEAD_DIM).astype(jnp.bfloat16)


def body(hidden_states, norm_gain, norm_bias, w_query, w_key, w_value, w_out, out_bias):
    position = lax.axis_index("grp") * lax.axis_size("frame") + lax.axis_index("frame")
    shifted = lax.ppermute(hidden_states, AXES, NEXT_FRAME)
    leading = from_first(hidden_states)
    query = project(layer_norm(hidden_states, norm_gain, norm_bias), w_query)
    prior = jnp.where(position == 0, hidden_states, shifted)
    context = jnp.concatenate(leading + [prior], axis=0)
    normed = layer_norm(context, norm_gain, norm_bias)
    attended = attend(query, project(normed, w_key), project(normed, w_value))
    projected = jnp.dot(attended, w_out, preferred_element_type=jnp.float32)
    total = hidden_states.astype(jnp.float32) + projected + out_bias
    return total.astype(jnp.bfloat16)


def solution(mesh):
    placed = (P(AXES, None), P(), P(), P(), P(), P(), P(), P())
    return jax.shard_map(
        body, mesh=mesh, in_specs=placed, out_specs=P(AXES, None), check_vma=False
    )
```

time: 327 us -> 128 us (0.39)
  waiting for transfers between devices: 254 us -> 31.6 us
  starting transfers between devices: 4.8 us -> 52.4 us
  between operations: 13.5 us -> 0.51 us
  local copies, waits for them, and re-layouts: 14.6 us -> 2.35 us
    psum x1 -> x0, waiting for transfers between devices: 254 us -> none  [from_root(): return lax.psum(kept, axis)]
    ppermute x1 -> x32, starting transfers between devices: 4.76 us -> 52.4 us  [the longest x21 25.4 us: from_first(): come = lax.ppermute(sent, AXES, pairs)]
    ppermute x1 -> x32, waiting for transfers between devices: 0.01 us -> 31.6 us  [the longest x21 17.9 us: from_first(): come = lax.ppermute(sent, AXES, pairs)]
    slice x6, local copies, waits for them, and re-layouts: 12.4 us -> 0.04 us  [from_first(): piece, sent = (piece[:middle], piece[middle:])]
  transfers between devices with their start and end apart: 2 -> 32, of which waited for: 1 -> 13; matrix products, arithmetic and copies ran while one was open for 4% -> 8% of each run, Pallas kernels for 0% -> 0%
where the time goes in v2:
time: 128 us; the launch traced here: 127 us
  starting transfers between devices  52.4 us (41%)
  matrix products  31.6 us (25%)
  waiting for transfers between devices  31.6 us (25%)
  other arithmetic  8.76 us (7%)
  local copies, waits for them, and re-layouts  2.35 us (2%)
    ppermute x21, starting transfers between devices, from_first(): come = lax.ppermute(sent, AXES, pairs)  25.4 us
    ppermute x3, starting transfers between devices, from_first(): return pieces + [lax.ppermute(piece, AXES, CORE_SWAP) for piece in pieces]  18.5 us
    ppermute x21, waiting for transfers between devices, from_first(): come = lax.ppermute(sent, AXES, pairs)  17.9 us
    ppermute x6, waiting for transfers between devices, from_first(): lax.ppermute(pieces[which], AXES, permutation(axis, pairs, all_lines(axis)))  12.8 us
    sub x1, matrix products, attend(): raised = jnp.exp(scores - top)  11.2 us
    dot_general x1, matrix products, attend(): jnp.einsum('hqk,khd->qhd', weights, v_heads, preferred_element_type=jnp.f...  9.29 us
    dot_general x3, matrix products, project(): jnp.dot(rows, weight, preferred_element_type=jnp.float32)  8.85 us
    ppermute x6, starting transfers between devices, from_first(): lax.ppermute(pieces[which], AXES, permutation(axis, pairs, all_lines(axis)))  5.23 us
  transfers between devices with their start and end apart: 32, of which 13 were waited for; matrix products, arithmetic and copies ran while one was open for 8% of the time, Pallas kernels for 0%

profile of v2, /device:TPU:1, one launch (start us, length us, event | category | flops | bytes accessed | tf_op | source)
XLA Modules:
  0.0 127.3 jit_solution(7116889498935837742)
XLA Ops:
  0.0 3.3 %collective-permute-start = (bf16[512,1280]{1,0:T(8,128)(2,1)}, bf16[512,1280]{1,0:T(8,128)(2,1)}, u32[]{:S(2)}, u32[]{:S(2)}) collective-permute-start(bf16[512,1280]{1,0:T(8,128)(2,1)} %param.8), channel_id=1, source_target_pairs={{0,1},{1,0},{2,3},{3,2},{4,5},{5,4},{6,7},{7,6},{8,9},{9,8},{10,11... | collective-permute-start | bytes 3932168 | tf_op jit(solution)/shard_map/ppermute | solution.py:99
  3.3 1.7 %convert_reduce_fusion.1 = f32[512]{0:T(512)S(1)} fusion(bf16[512,1280]{1,0:T(8,128)(2,1)} %param.8), kind=kLoop, calls=%fused_computation.17 | loop fusion | flops 1310208 | bytes 1312768 | tf_op jit(solution)/shard_map/reduce_sum | solution.py:134
  5.0 1.8 %fusion.16 = f32[512]{0:T(512)S(1)} fusion(bf16[512,1280]{1,0:T(8,128)(2,1)} %param.8, f32[512]{0:T(512)S(1)} %broadcast_multiply_fusion.1), kind=kLoop, calls=%fused_computation.22 | loop fusion | flops 2620928 | bytes 1314816 | tf_op jit(solution)/shard_map/reduce_sum | solution.py:135
  6.9 2.2 %convolution_convert_fusion.2 = bf16[512,640]{1,0:T(8,128)(2,1)} fusion(bf16[1280,640]{1,0:T(8,128)(2,1)S(1)} %copy-done.2, bf16[512,1280]{1,0:T(8,128)(2,1)S(1)} %copy-done.1, f32[1280]{0:T(1024)S(1)} %copy-done.5, f32[1280]{0:T(1024)S(1)} %copy-done.6, f32[512]{0:T(512)S(1)} %add_rsqrt_fusion.1, f32[512]{0:T(512)S(1)} %broadcast_multiply_fusion.1), kind=kOutput, calls=%fused_computation.29 | convolution fusion | flops 843120640 | bytes 3618816 | tf_op jit(solution)/shard_map/dot_general | solution.py:142
  9.1 2.2 %copy.10 = bf16[512,640]{0,1:T(8,128)(2,1)} copy(bf16[512,640]{1,0:T(8,128)(2,1)} %convolution_convert_fusion.2) | data formatting | bytes 1310720 | tf_op jit(solution)/shard_map/convert_element_type | solution.py:142
  11.3 0.0 collective-permute-done
  11.3 1.1 slice_select_fusion
  12.5 2.1 %collective-permute-start.1 = (bf16[48,1280]{1,0:T(8,128)(2,1)S(1)}, bf16[48,1280]{1,0:T(8,128)(2,1)S(1)}, u32[]{:S(2)}, u32[]{:S(2)}) collective-permute-start(bf16[48,1280]{1,0:T(8,128)(2,1)S(1)} %slice.74), channel_id=1, source_target_pairs={{0,32},{1,97},{2,34},{3,99},{4,36},{5,101},{6,38},{7,103},{8,40},{... | collective-permute-start | bytes 368648 | tf_op jit(solution)/shard_map/ppermute | solution.py:120
  14.6 2.7 %collective-permute-start.10 = (bf16[48,1280]{1,0:T(8,128)(2,1)S(1)}, bf16[48,1280]{1,0:T(8,128)(2,1)S(1)}, u32[]{:S(2)}, u32[]{:S(2)}) collective-permute-start(bf16[48,1280]{1,0:T(8,128)(2,1)S(1)} %slice.79), channel_id=1, source_target_pairs={{0,2},{1,7},{2,0},{3,5},{4,6},{5,3},{6,4},{7,1},{8,10},{9,15},{10,... | collective-permute-start | bytes 368648 | tf_op jit(solution)/shard_map/ppermute | solution.py:120
  17.3 0.9 slice_select_fusion.2
  18.3 6.1 %collective-permute-start.19 = (bf16[64,1280]{1,0:T(8,128)(2,1)S(1)}, bf16[64,1280]{1,0:T(8,128)(2,1)S(1)}, u32[]{:S(2)}, u32[]{:S(2)}) collective-permute-start(bf16[64,1280]{1,0:T(8,128)(2,1)S(1)} %slice_select_fusion.2), channel_id=1, source_target_pairs={{0,128},{1,129},{2,3},{3,2},{4,5},{5,4},{6,7},{7,6},{8,9},{9,8},{1... | collective-permute-start | bytes 491528 | tf_op jit(solution)/shard_map/ppermute | solution.py:120
  24.4 0.0 collective-permute-done.1
  24.4 0.1 collective-permute-start.2
  24.5 3.9 %collective-permute-done.10 = bf16[48,1280]{1,0:T(8,128)(2,1)S(1)} collective-permute-done((bf16[48,1280]{1,0:T(8,128)(2,1)S(1)}, bf16[48,1280]{1,0:T(8,128)(2,1)S(1)}, u32[]{:S(2)}, u32[]{:S(2)}) %collective-permute-start.10) | collective-permute-done | bytes 122912 | tf_op jit(solution)/shard_map/ppermute | solution.py:120
  28.4 0.1 collective-permute-start.11
  28.5 0.1 collective-permute-start.20
  28.7 3.2 %collective-permute-start.3 = (bf16[24,1280]{1,0:T(8,128)(2,1)S(1)}, bf16[24,1280]{1,0:T(8,128)(2,1)S(1)}, u32[]{:S(2)}, u32[]{:S(2)}) collective-permute-start(bf16[24,1280]{1,0:T(8,128)(2,1)S(1)} %slice_select_fusion.7), channel_id=1, source_target_pairs={{0,2},{1,7},{2,0},{3,5},{4,6},{5,3},{6,4},{7,1},{8,10},{9,15},{10,... | collective-permute-start | bytes 184328 | tf_op jit(solution)/shard_map/ppermute | solution.py:120
  31.9 0.0 collective-permute-done.11
  31.9 0.1 collective-permute-start.12
  32.0 1.5 %collective-permute-done.3 = bf16[24,1280]{1,0:T(8,128)(2,1)S(1)} collective-permute-done((bf16[24,1280]{1,0:T(8,128)(2,1)S(1)}, bf16[24,1280]{1,0:T(8,128)(2,1)S(1)}, u32[]{:S(2)}, u32[]{:S(2)}) %collective-permute-start.3) | collective-permute-done | bytes 61472 | tf_op jit(solution)/shard_map/ppermute | solution.py:120
  33.6 0.1 collective-permute-start.4
  33.7 0.1 collective-permute-start.21
  33.8 4.3 %collective-permute-done.12 = bf16[24,1280]{1,0:T(8,128)(2,1)S(1)} collective-permute-done((bf16[24,1280]{1,0:T(8,128)(2,1)S(1)}, bf16[24,1280]{1,0:T(8,128)(2,1)S(1)}, u32[]{:S(2)}, u32[]{:S(2)}) %collective-permute-start.12) | collective-permute-done | bytes 61472 | tf_op jit(solution)/shard_map/ppermute | solution.py:120
  38.1 1.7 %collective-permute-start.13 = (bf16[24,1280]{1,0:T(8,128)(2,1)S(1)}, bf16[24,1280]{1,0:T(8,128)(2,1)S(1)}, u32[]{:S(2)}, u32[]{:S(2)}) collective-permute-start(bf16[24,1280]{1,0:T(8,128)(2,1)S(1)} %broadcast_select_fusion.1), channel_id=1, source_target_pairs={{0,144},{1,17},{2,146},{3,19},{4,148},{5,21},{6,150},{7,23},{8,9},... | collective-permute-start | bytes 184328 | tf_op jit(solution)/shard_map/ppermute | solution.py:120
  39.9 0.1 collective-permute-start.22
  40.0 0.0 collective-permute-done.4
  40.0 1.5 %collective-permute-start.5 = (bf16[24,1280]{1,0:T(8,128)(2,1)S(1)}, bf16[24,1280]{1,0:T(8,128)(2,1)S(1)}, u32[]{:S(2)}, u32[]{:S(2)}) collective-permute-start(bf16[24,1280]{1,0:T(8,128)(2,1)S(1)} %broadcast_select_fusion.7), channel_id=1, source_target_pairs={{0,24},{1,137},{2,26},{3,139},{4,28},{5,141},{6,30},{7,143},{8,9},... | collective-permute-start | bytes 184328 | tf_op jit(solution)/shard_map/ppermute | solution.py:120
  41.5 2.6 %collective-permute-done.22 = bf16[16,1280]{1,0:T(8,128)(2,1)S(1)} collective-permute-done((bf16[16,1280]{1,0:T(8,128)(2,1)S(1)}, bf16[16,1280]{1,0:T(8,128)(2,1)S(1)}, u32[]{:S(2)}, u32[]{:S(2)}) %collective-permute-start.22) | collective-permute-done | bytes 40992 | tf_op jit(solution)/shard_map/ppermute | solution.py:120
  44.1 0.1 collective-permute-start.23
  44.3 0.3 collective-permute-start.14
  44.5 2.8 %collective-permute-done.23 = bf16[16,1280]{1,0:T(8,128)(2,1)S(1)} collective-permute-done((bf16[16,1280]{1,0:T(8,128)(2,1)S(1)}, bf16[16,1280]{1,0:T(8,128)(2,1)S(1)}, u32[]{:S(2)}, u32[]{:S(2)}) %collective-permute-start.23) | collective-permute-done | bytes 40992 | tf_op jit(solution)/shard_map/ppermute | solution.py:120
  47.4 0.1 collective-permute-start.24
  47.5 0.0 collective-permute-done.5
  47.5 1.0 collective-permute-start.6
  48.5 0.3 collective-permute-done.14
  48.8 0.7 collective-permute-start.15
  49.5 2.1 %collective-permute-done.6 = bf16[24,1280]{1,0:T(8,128)(2,1)S(1)} collective-permute-done((bf16[24,1280]{1,0:T(8,128)(2,1)S(1)}, bf16[24,1280]{1,0:T(8,128)(2,1)S(1)}, u32[]{:S(2)}, u32[]{:S(2)}) %collective-permute-start.6) | collective-permute-done | bytes 61472 | tf_op jit(solution)/shard_map/ppermute | solution.py:120
  51.6 2.2 %collective-permute-start.7 = (bf16[24,1280]{1,0:T(8,128)(2,1)S(1)}, bf16[24,1280]{1,0:T(8,128)(2,1)S(1)}, u32[]{:S(2)}, u32[]{:S(2)}) collective-permute-start(bf16[24,1280]{1,0:T(8,128)(2,1)S(1)} %broadcast_select_fusion.9), channel_id=1, source_target_pairs={{0,8},{1,153},{2,10},{3,155},{4,12},{5,157},{6,14},{7,159},{8,0},{... | collective-permute-start | bytes 184328 | tf_op jit(solution)/shard_map/ppermute | solution.py:120
  53.8 1.8 %collective-permute-start.25 = (bf16[16,1280]{1,0:T(8,128)(2,1)S(1)}, bf16[16,1280]{1,0:T(8,128)(2,1)S(1)}, u32[]{:S(2)}, u32[]{:S(2)}) collective-permute-start(bf16[16,1280]{1,0:T(8,128)(2,1)S(1)} %broadcast_select_fusion.13), channel_id=1, source_target_pairs={{0,6},{1,3},{2,4},{3,1},{4,2},{5,7},{6,0},{7,5},{8,14},{9,11},{10,... | collective-permute-start | bytes 122888 | tf_op jit(solution)/shard_map/ppermute | solution.py:120
  55.6 0.3 collective-permute-done.7
  56.0 0.5 collective-permute-start.8
  56.5 1.1 collective-permute-start.16
  57.6 1.5 %collective-permute-done.8 = bf16[24,1280]{1,0:T(8,128)(2,1)S(1)} collective-permute-done((bf16[24,1280]{1,0:T(8,128)(2,1)S(1)}, bf16[24,1280]{1,0:T(8,128)(2,1)S(1)}, u32[]{:S(2)}, u32[]{:S(2)}) %collective-permute-start.8) | collective-permute-done | bytes 61472 | tf_op jit(solution)/shard_map/ppermute | solution.py:125
  59.2 2.0 %collective-permute-start.9 = (bf16[48,1280]{1,0:T(8,128)(2,1)S(1)}, bf16[48,1280]{1,0:T(8,128)(2,1)S(1)}, u32[]{:S(2)}, u32[]{:S(2)}) collective-permute-start(bf16[48,1280]{1,0:T(8,128)(2,1)S(1)} %pad_maximum_fusion.3), channel_id=1, source_target_pairs={{0,32},{1,97},{2,34},{3,99},{4,36},{5,101},{6,38},{7,103},{8,40},{... | collective-permute-start | bytes 368648 | tf_op jit(solution)/shard_map/ppermute | solution.py:125
  61.1 3.1 %collective-permute-done.9 = bf16[48,1280]{1,0:T(8,128)(2,1)S(1)} collective-permute-done((bf16[48,1280]{1,0:T(8,128)(2,1)S(1)}, bf16[48,1280]{1,0:T(8,128)(2,1)S(1)}, u32[]{:S(2)}, u32[]{:S(2)}) %collective-permute-start.9) | collective-permute-done | bytes 122912 | tf_op jit(solution)/shard_map/ppermute | solution.py:125
  64.2 1.3 collective-permute-start.17
  65.5 11.0 %collective-permute-start.28 = (bf16[96,1280]{1,0:T(8,128)(2,1)S(1)}, bf16[96,1280]{1,0:T(8,128)(2,1)S(1)}, u32[]{:S(2)}, u32[]{:S(2)}) collective-permute-start(bf16[96,1280]{1,0:T(8,128)(2,1)S(1)} %pad_maximum_fusion), channel_id=1, source_target_pairs={{0,1},{1,0},{2,3},{3,2},{4,5},{5,4},{6,7},{7,6},{8,9},{9,8},{10,11... | collective-permute-start | bytes 737288 | tf_op jit(solution)/shard_map/ppermute | solution.py:129
  76.5 0.1 collective-permute-start.18
  76.6 4.9 %collective-permute-done.18 = bf16[48,1280]{1,0:T(8,128)(2,1)S(1)} collective-permute-done((bf16[48,1280]{1,0:T(8,128)(2,1)S(1)}, bf16[48,1280]{1,0:T(8,128)(2,1)S(1)}, u32[]{:S(2)}, u32[]{:S(2)}) %collective-permute-start.18) | collective-permute-done | bytes 122912 | tf_op jit(solution)/shard_map/ppermute | solution.py:125
  81.6 0.1 collective-permute-start.26
  81.7 4.0 %collective-permute-start.29 = (bf16[96,1280]{1,0:T(8,128)(2,1)S(1)}, bf16[96,1280]{1,0:T(8,128)(2,1)S(1)}, u32[]{:S(2)}, u32[]{:S(2)}) collective-permute-start(bf16[96,1280]{1,0:T(8,128)(2,1)S(1)} %pad_maximum_fusion.1), channel_id=1, source_target_pairs={{0,1},{1,0},{2,3},{3,2},{4,5},{5,4},{6,7},{7,6},{8,9},{9,8},{10,11... | collective-permute-start | bytes 737288 | tf_op jit(solution)/shard_map/ppermute | solution.py:129
  85.8 1.3 %collective-permute-start.27 = (bf16[32,1280]{1,0:T(8,128)(2,1)S(1)}, bf16[32,1280]{1,0:T(8,128)(2,1)S(1)}, u32[]{:S(2)}, u32[]{:S(2)}) collective-permute-start(bf16[32,1280]{1,0:T(8,128)(2,1)S(1)} %pad_maximum_fusion.5), channel_id=1, source_target_pairs={{0,8},{1,153},{2,10},{3,155},{4,12},{5,157},{6,14},{7,159},{8,0},{... | collective-permute-start | bytes 245768 | tf_op jit(solution)/shard_map/ppermute | solution.py:125
  87.0 3.3 %collective-permute-done.27 = bf16[32,1280]{1,0:T(8,128)(2,1)S(1)} collective-permute-done((bf16[32,1280]{1,0:T(8,128)(2,1)S(1)}, bf16[32,1280]{1,0:T(8,128)(2,1)S(1)}, u32[]{:S(2)}, u32[]{:S(2)}) %collective-permute-start.27) | collective-permute-done | bytes 81952 | tf_op jit(solution)/shard_map/ppermute | solution.py:125
  90.4 3.5 %collective-permute-start.30 = (bf16[64,1280]{1,0:T(8,128)(2,1)S(1)}, bf16[64,1280]{1,0:T(8,128)(2,1)S(1)}, u32[]{:S(2)}, u32[]{:S(2)}) collective-permute-start(bf16[64,1280]{1,0:T(8,128)(2,1)S(1)} %pad_maximum_fusion.2), channel_id=1, source_target_pairs={{0,1},{1,0},{2,3},{3,2},{4,5},{5,4},{6,7},{7,6},{8,9},{9,8},{10,11... | collective-permute-start | bytes 491528 | tf_op jit(solution)/shard_map/ppermute | solution.py:129
  93.9 1.0 collective-permute-done.30
  94.9 1.6 %select_dynamic-update-slice_fusion = bf16[1024,1280]{1,0:T(8,128)(2,1)S(1)} fusion(bf16[1024,1280]{1,0:T(8,128)(2,1)S(1)} %constant_dynamic-update-slice_fusion, bf16[512,1280]{1,0:T(8,128)(2,1)S(1)} %copy-done.1, bf16[512,1280]{1,0:T(8,128)(2,1)} %collective-permute-done.31, pred[]{:T(512)S(6)} %eq.97), kind=kLoop, calls=%fused_computation.35 | loop fusion | flops 655360 | bytes 3932161 | tf_op jit(solution)/shard_map/concatenate | solution.py:166
  96.5 0.4 convert_reduce_fusion
  97.0 0.8 fusion.8
  97.8 0.0 copy-start.3
  97.8 3.3 %convolution_convert_fusion = bf16[1024,640]{0,1:T(8,128)(2,1)} fusion(bf16[1280,640]{1,0:T(8,128)(2,1)S(1)} %copy-done, bf16[1024,1280]{1,0:T(8,128)(2,1)S(1)} %select_dynamic-update-slice_fusion, f32[1280]{0:T(1024)S(1)} %copy-done.5, f32[1280]{0:T(1024)S(1)} %copy-done.6, f32[1024]{0:T(1024)S(1)} %add_rsqrt_fusion, f32[1024]{0:T(1024)S(1)} %broadcast_multiply_fusion), kind=kOutput, calls=%fused_computation.27 | convolution fusion | flops 1686241280 | bytes 5588992 | tf_op jit(solution)/shard_map/dot_general | solution.py:142
  101.1 3.3 %convolution_convert_fusion.1 = bf16[1024,640]{0,1:T(8,128)(2,1)} fusion(bf16[1280,640]{1,0:T(8,128)(2,1)S(1)} %copy-done.3, bf16[1024,1280]{1,0:T(8,128)(2,1)S(1)} %select_dynamic-update-slice_fusion, f32[1280]{0:T(1024)S(1)} %copy-done.5, f32[1280]{0:T(1024)S(1)} %copy-done.6, f32[1024]{0:T(1024)S(1)} %add_rsqrt_fusion, f32[1024]{0:T(1024)S(1)} %broadcast_multiply_fusion), kind=kOutput, calls=%fused_computation.28 | convolution fusion | flops 1686241280 | bytes 5588992 | tf_op jit(solution)/shard_map/dot_general | solution.py:142
  104.4 11.2 %fusion.31 = (f32[10,512]{1,0:T(8,128)S(1)}, f32[10,512,1024]{2,1,0:T(8,128)}) fusion(bf16[512,10,64]{0,2,1:T(8,128)(2,1)} %bitcast.16, bf16[1024,10,64]{0,2,1:T(8,128)(2,1)} %bitcast.18), kind=kOutput, calls=%fused_computation.83 | convolution fusion | flops 686818304 | bytes 22958080 | tf_op jit(solution)/shard_map/sub | solution.py:154
  115.6 9.3 %fusion.22 = bf16[10,64,512]{2,1,0:T(8,128)(2,1)S(1)} fusion(bf16[1024,10,64]{0,2,1:T(8,128)(2,1)} %bitcast.17, f32[10,512,1024]{2,1,0:T(8,128)} %get-tuple-element.14, f32[10,512]{1,0:T(8,128)S(1)} %get-tuple-element.13), kind=kOutput, calls=%fused_computation.30 | convolution fusion | flops 681902080 | bytes 22958080 | tf_op jit(solution)/shard_map/hqk,khd->qhd/dot_general | solution.py:156
  125.0 2.3 %fusion.15 = bf16[512,1280]{1,0:T(8,128)(2,1)} fusion(bf16[512,640]{0,1:T(8,128)(2,1)S(1)} %bitcast.19, bf16[640,1280]{1,0:T(8,128)(2,1)S(1)} %copy-done.4, bf16[512,1280]{1,0:T(8,128)(2,1)S(1)} %copy-done.1, f32[1280]{0:T(1024)S(1)} %copy-done.7), kind=kOutput, calls=%fused_computation.21 | convolution fusion | flops 841482240 | bytes 4920320 | tf_op jit(solution)/shard_map/dot_general | solution.py:169
  (76 shorter events, 0.6 us)
Async XLA Ops:
  0.0 97.8 %copy-start = (bf16[1280,640]{1,0:T(8,128)(2,1)S(1)}, bf16[1280,640]{1,0:T(8,128)(2,1)}, u32[]{:S(2)}) copy-start(bf16[1280,640]{1,0:T(8,128)(2,1)} %param.12) | copy-start | bytes 4915204
  0.0 6.8 %copy-start.1 = (bf16[512,1280]{1,0:T(8,128)(2,1)S(1)}, bf16[512,1280]{1,0:T(8,128)(2,1)}, u32[]{:S(2)}) copy-start(bf16[512,1280]{1,0:T(8,128)(2,1)} %param.8) | copy-start | bytes 3932164
  0.0 6.9 %copy-start.5 = (f32[1280]{0:T(1024)S(1)}, f32[1280]{0:T(1024)}, u32[]{:S(2)}) copy-start(f32[1280]{0:T(1024)} %param.10) | copy-start | bytes 15364
  0.0 6.9 %copy-start.6 = (f32[1280]{0:T(1024)S(1)}, f32[1280]{0:T(1024)}, u32[]{:S(2)}) copy-start(f32[1280]{0:T(1024)} %param.9) | copy-start | bytes 15364
  0.0 11.3 %collective-permute-start = (bf16[512,1280]{1,0:T(8,128)(2,1)}, bf16[512,1280]{1,0:T(8,128)(2,1)}, u32[]{:S(2)}, u32[]{:S(2)}) collective-permute-start(bf16[512,1280]{1,0:T(8,128)(2,1)} %param.8), channel_id=1, source_target_pairs={{0,1},{1,0},{2,3},{3,2},{4,5},{5,4},{6,7},{7,6},{8,9},{9,8},{10,11... | collective-permute-start | bytes 3932168 | tf_op jit(solution)/shard_map/ppermute | solution.py:99
  3.3 91.6 %collective-permute-start.31 = (bf16[512,1280]{1,0:T(8,128)(2,1)}, bf16[512,1280]{1,0:T(8,128)(2,1)}, u32[]{:S(2)}, u32[]{:S(2)}) collective-permute-start(bf16[512,1280]{1,0:T(8,128)(2,1)} %param.8), channel_id=1, source_target_pairs={{0,1},{1,2},{2,3},{3,4},{4,5},{5,6},{6,7},{7,8},{8,9},{9,10},{10,1... | collective-permute-start | bytes 3932168 | tf_op jit(solution)/shard_map/ppermute | solution.py:162
  3.3 3.5 %copy-start.2 = (bf16[1280,640]{1,0:T(8,128)(2,1)S(1)}, bf16[1280,640]{1,0:T(8,128)(2,1)}, u32[]{:S(2)}) copy-start(bf16[1280,640]{1,0:T(8,128)(2,1)} %param.11) | copy-start | bytes 4915204
  12.5 11.9 %collective-permute-start.1 = (bf16[48,1280]{1,0:T(8,128)(2,1)S(1)}, bf16[48,1280]{1,0:T(8,128)(2,1)S(1)}, u32[]{:S(2)}, u32[]{:S(2)}) collective-permute-start(bf16[48,1280]{1,0:T(8,128)(2,1)S(1)} %slice.74), channel_id=1, source_target_pairs={{0,32},{1,97},{2,34},{3,99},{4,36},{5,101},{6,38},{7,103},{8,40},{... | collective-permute-start | bytes 368648 | tf_op jit(solution)/shard_map/ppermute | solution.py:120
  14.6 13.8 %collective-permute-start.10 = (bf16[48,1280]{1,0:T(8,128)(2,1)S(1)}, bf16[48,1280]{1,0:T(8,128)(2,1)S(1)}, u32[]{:S(2)}, u32[]{:S(2)}) collective-permute-start(bf16[48,1280]{1,0:T(8,128)(2,1)S(1)} %slice.79), channel_id=1, source_target_pairs={{0,2},{1,7},{2,0},{3,5},{4,6},{5,3},{6,4},{7,1},{8,10},{9,15},{10,... | collective-permute-start | bytes 368648 | tf_op jit(solution)/shard_map/ppermute | solution.py:120
  18.3 10.2 %collective-permute-start.19 = (bf16[64,1280]{1,0:T(8,128)(2,1)S(1)}, bf16[64,1280]{1,0:T(8,128)(2,1)S(1)}, u32[]{:S(2)}, u32[]{:S(2)}) collective-permute-start(bf16[64,1280]{1,0:T(8,128)(2,1)S(1)} %slice_select_fusion.2), channel_id=1, source_target_pairs={{0,128},{1,129},{2,3},{3,2},{4,5},{5,4},{6,7},{7,6},{8,9},{9,8},{1... | collective-permute-start | bytes 491528 | tf_op jit(solution)/shard_map/ppermute | solution.py:120
  24.4 4.3 %collective-permute-start.2 = (bf16[24,1280]{1,0:T(8,128)(2,1)S(1)}, bf16[24,1280]{1,0:T(8,128)(2,1)S(1)}, u32[]{:S(2)}, u32[]{:S(2)}) collective-permute-start(bf16[24,1280]{1,0:T(8,128)(2,1)S(1)} %slice.76), channel_id=1, source_target_pairs={{0,96},{1,33},{2,98},{3,35},{4,100},{5,37},{6,102},{7,39},{8,104},... | collective-permute-start | bytes 184328 | tf_op jit(solution)/shard_map/ppermute | solution.py:120
  28.4 3.5 %collective-permute-start.11 = (bf16[24,1280]{1,0:T(8,128)(2,1)S(1)}, bf16[24,1280]{1,0:T(8,128)(2,1)S(1)}, u32[]{:S(2)}, u32[]{:S(2)}) collective-permute-start(bf16[24,1280]{1,0:T(8,128)(2,1)S(1)} %slice.81), channel_id=1, source_target_pairs={{0,6},{1,3},{2,4},{3,1},{4,2},{5,7},{6,0},{7,5},{8,14},{9,11},{10,... | collective-permute-start | bytes 184328 | tf_op jit(solution)/shard_map/ppermute | solution.py:120
  28.5 5.1 %collective-permute-start.20 = (bf16[32,1280]{1,0:T(8,128)(2,1)S(1)}, bf16[32,1280]{1,0:T(8,128)(2,1)S(1)}, u32[]{:S(2)}, u32[]{:S(2)}) collective-permute-start(bf16[32,1280]{1,0:T(8,128)(2,1)S(1)} %slice.84), channel_id=1, source_target_pairs={{0,8},{1,153},{2,10},{3,155},{4,12},{5,157},{6,14},{7,159},{8,0},{... | collective-permute-start | bytes 245768 | tf_op jit(solution)/shard_map/ppermute | solution.py:120
  28.7 4.9 %collective-permute-start.3 = (bf16[24,1280]{1,0:T(8,128)(2,1)S(1)}, bf16[24,1280]{1,0:T(8,128)(2,1)S(1)}, u32[]{:S(2)}, u32[]{:S(2)}) collective-permute-start(bf16[24,1280]{1,0:T(8,128)(2,1)S(1)} %slice_select_fusion.7), channel_id=1, source_target_pairs={{0,2},{1,7},{2,0},{3,5},{4,6},{5,3},{6,4},{7,1},{8,10},{9,15},{10,... | collective-permute-start | bytes 184328 | tf_op jit(solution)/shard_map/ppermute | solution.py:120
  31.9 6.2 %collective-permute-start.12 = (bf16[24,1280]{1,0:T(8,128)(2,1)S(1)}, bf16[24,1280]{1,0:T(8,128)(2,1)S(1)}, u32[]{:S(2)}, u32[]{:S(2)}) collective-permute-start(bf16[24,1280]{1,0:T(8,128)(2,1)S(1)} %slice_select_fusion.6), channel_id=1, source_target_pairs={{0,24},{1,137},{2,26},{3,139},{4,28},{5,141},{6,30},{7,143},{8,9},... | collective-permute-start | bytes 184328 | tf_op jit(solution)/shard_map/ppermute | solution.py:120
  33.6 6.4 %collective-permute-start.4 = (bf16[24,1280]{1,0:T(8,128)(2,1)S(1)}, bf16[24,1280]{1,0:T(8,128)(2,1)S(1)}, u32[]{:S(2)}, u32[]{:S(2)}) collective-permute-start(bf16[24,1280]{1,0:T(8,128)(2,1)S(1)} %broadcast_select_fusion.6), channel_id=1, source_target_pairs={{0,6},{1,3},{2,4},{3,1},{4,2},{5,7},{6,0},{7,5},{8,14},{9,11},{10,... | collective-permute-start | bytes 184328 | tf_op jit(solution)/shard_map/ppermute | solution.py:120
  33.7 6.2 %collective-permute-start.21 = (bf16[16,1280]{1,0:T(8,128)(2,1)S(1)}, bf16[16,1280]{1,0:T(8,128)(2,1)S(1)}, u32[]{:S(2)}, u32[]{:S(2)}) collective-permute-start(bf16[16,1280]{1,0:T(8,128)(2,1)S(1)} %slice.86), channel_id=1, source_target_pairs={{0,152},{1,9},{2,154},{3,11},{4,156},{5,13},{6,158},{7,15},{8,16},... | collective-permute-start | bytes 122888 | tf_op jit(solution)/shard_map/ppermute | solution.py:120
  38.1 6.1 %collective-permute-start.13 = (bf16[24,1280]{1,0:T(8,128)(2,1)S(1)}, bf16[24,1280]{1,0:T(8,128)(2,1)S(1)}, u32[]{:S(2)}, u32[]{:S(2)}) collective-permute-start(bf16[24,1280]{1,0:T(8,128)(2,1)S(1)} %broadcast_select_fusion.1), channel_id=1, source_target_pairs={{0,144},{1,17},{2,146},{3,19},{4,148},{5,21},{6,150},{7,23},{8,9},... | collective-permute-start | bytes 184328 | tf_op jit(solution)/shard_map/ppermute | solution.py:120
  39.9 4.2 %collective-permute-start.22 = (bf16[16,1280]{1,0:T(8,128)(2,1)S(1)}, bf16[16,1280]{1,0:T(8,128)(2,1)S(1)}, u32[]{:S(2)}, u32[]{:S(2)}) collective-permute-start(bf16[16,1280]{1,0:T(8,128)(2,1)S(1)} %slice_select_fusion.8), channel_id=1, source_target_pairs={{0,32},{1,97},{2,34},{3,99},{4,36},{5,101},{6,38},{7,103},{8,40},{... | collective-permute-start | bytes 122888 | tf_op jit(solution)/shard_map/ppermute | solution.py:120
  40.0 7.5 %collective-permute-start.5 = (bf16[24,1280]{1,0:T(8,128)(2,1)S(1)}, bf16[24,1280]{1,0:T(8,128)(2,1)S(1)}, u32[]{:S(2)}, u32[]{:S(2)}) collective-permute-start(bf16[24,1280]{1,0:T(8,128)(2,1)S(1)} %broadcast_select_fusion.7), channel_id=1, source_target_pairs={{0,24},{1,137},{2,26},{3,139},{4,28},{5,141},{6,30},{7,143},{8,9},... | collective-permute-start | bytes 184328 | tf_op jit(solution)/shard_map/ppermute | solution.py:120
  44.1 3.2 %collective-permute-start.23 = (bf16[16,1280]{1,0:T(8,128)(2,1)S(1)}, bf16[16,1280]{1,0:T(8,128)(2,1)S(1)}, u32[]{:S(2)}, u32[]{:S(2)}) collective-permute-start(bf16[16,1280]{1,0:T(8,128)(2,1)S(1)} %broadcast_select_fusion.11), channel_id=1, source_target_pairs={{0,96},{1,33},{2,98},{3,35},{4,100},{5,37},{6,102},{7,39},{8,104},... | collective-permute-start | bytes 122888 | tf_op jit(solution)/shard_map/ppermute | solution.py:120
  44.3 4.6 %collective-permute-start.14 = (bf16[24,1280]{1,0:T(8,128)(2,1)S(1)}, bf16[24,1280]{1,0:T(8,128)(2,1)S(1)}, u32[]{:S(2)}, u32[]{:S(2)}) collective-permute-start(bf16[24,1280]{1,0:T(8,128)(2,1)S(1)} %broadcast_select_fusion.2), channel_id=1, source_target_pairs={{0,8},{1,153},{2,10},{3,155},{4,12},{5,157},{6,14},{7,159},{8,0},{... | collective-permute-start | bytes 184328 | tf_op jit(solution)/shard_map/ppermute | solution.py:120
  47.4 6.4 %collective-permute-start.24 = (bf16[16,1280]{1,0:T(8,128)(2,1)S(1)}, bf16[16,1280]{1,0:T(8,128)(2,1)S(1)}, u32[]{:S(2)}, u32[]{:S(2)}) collective-permute-start(bf16[16,1280]{1,0:T(8,128)(2,1)S(1)} %broadcast_select_fusion.12), channel_id=1, source_target_pairs={{0,2},{1,7},{2,0},{3,5},{4,6},{5,3},{6,4},{7,1},{8,10},{9,15},{10,... | collective-permute-start | bytes 122888 | tf_op jit(solution)/shard_map/ppermute | solution.py:120
  47.5 4.1 %collective-permute-start.6 = (bf16[24,1280]{1,0:T(8,128)(2,1)S(1)}, bf16[24,1280]{1,0:T(8,128)(2,1)S(1)}, u32[]{:S(2)}, u32[]{:S(2)}) collective-permute-start(bf16[24,1280]{1,0:T(8,128)(2,1)S(1)} %broadcast_select_fusion.8), channel_id=1, source_target_pairs={{0,144},{1,17},{2,146},{3,19},{4,148},{5,21},{6,150},{7,23},{8,9},... | collective-permute-start | bytes 184328 | tf_op jit(solution)/shard_map/ppermute | solution.py:120
  48.8 7.7 %collective-permute-start.15 = (bf16[24,1280]{1,0:T(8,128)(2,1)S(1)}, bf16[24,1280]{1,0:T(8,128)(2,1)S(1)}, u32[]{:S(2)}, u32[]{:S(2)}) collective-permute-start(bf16[24,1280]{1,0:T(8,128)(2,1)S(1)} %broadcast_select_fusion.3), channel_id=1, source_target_pairs={{0,32},{1,97},{2,34},{3,99},{4,36},{5,101},{6,38},{7,103},{8,40},{... | collective-permute-start | bytes 184328 | tf_op jit(solution)/shard_map/ppermute | solution.py:120
  51.6 4.4 %collective-permute-start.7 = (bf16[24,1280]{1,0:T(8,128)(2,1)S(1)}, bf16[24,1280]{1,0:T(8,128)(2,1)S(1)}, u32[]{:S(2)}, u32[]{:S(2)}) collective-permute-start(bf16[24,1280]{1,0:T(8,128)(2,1)S(1)} %broadcast_select_fusion.9), channel_id=1, source_target_pairs={{0,8},{1,153},{2,10},{3,155},{4,12},{5,157},{6,14},{7,159},{8,0},{... | collective-permute-start | bytes 184328 | tf_op jit(solution)/shard_map/ppermute | solution.py:120
  53.8 27.7 %collective-permute-start.25 = (bf16[16,1280]{1,0:T(8,128)(2,1)S(1)}, bf16[16,1280]{1,0:T(8,128)(2,1)S(1)}, u32[]{:S(2)}, u32[]{:S(2)}) collective-permute-start(bf16[16,1280]{1,0:T(8,128)(2,1)S(1)} %broadcast_select_fusion.13), channel_id=1, source_target_pairs={{0,6},{1,3},{2,4},{3,1},{4,2},{5,7},{6,0},{7,5},{8,14},{9,11},{10,... | collective-permute-start | bytes 122888 | tf_op jit(solution)/shard_map/ppermute | solution.py:120
  56.0 3.2 %collective-permute-start.8 = (bf16[24,1280]{1,0:T(8,128)(2,1)S(1)}, bf16[24,1280]{1,0:T(8,128)(2,1)S(1)}, u32[]{:S(2)}, u32[]{:S(2)}) collective-permute-start(bf16[24,1280]{1,0:T(8,128)(2,1)S(1)} %get-tuple-element.10), channel_id=1, source_target_pairs={{0,96},{1,33},{2,98},{3,35},{4,100},{5,37},{6,102},{7,39},{8,104},... | collective-permute-start | bytes 184328 | tf_op jit(solution)/shard_map/ppermute | solution.py:125
  56.5 7.7 %collective-permute-start.16 = (bf16[24,1280]{1,0:T(8,128)(2,1)S(1)}, bf16[24,1280]{1,0:T(8,128)(2,1)S(1)}, u32[]{:S(2)}, u32[]{:S(2)}) collective-permute-start(bf16[24,1280]{1,0:T(8,128)(2,1)S(1)} %broadcast_select_fusion.4), channel_id=1, source_target_pairs={{0,96},{1,33},{2,98},{3,35},{4,100},{5,37},{6,102},{7,39},{8,104},... | collective-permute-start | bytes 184328 | tf_op jit(solution)/shard_map/ppermute | solution.py:120
  59.2 5.0 %collective-permute-start.9 = (bf16[48,1280]{1,0:T(8,128)(2,1)S(1)}, bf16[48,1280]{1,0:T(8,128)(2,1)S(1)}, u32[]{:S(2)}, u32[]{:S(2)}) collective-permute-start(bf16[48,1280]{1,0:T(8,128)(2,1)S(1)} %pad_maximum_fusion.3), channel_id=1, source_target_pairs={{0,32},{1,97},{2,34},{3,99},{4,36},{5,101},{6,38},{7,103},{8,40},{... | collective-permute-start | bytes 368648 | tf_op jit(solution)/shard_map/ppermute | solution.py:125
  64.2 12.3 %collective-permute-start.17 = (bf16[24,1280]{1,0:T(8,128)(2,1)S(1)}, bf16[24,1280]{1,0:T(8,128)(2,1)S(1)}, u32[]{:S(2)}, u32[]{:S(2)}) collective-permute-start(bf16[24,1280]{1,0:T(8,128)(2,1)S(1)} %get-tuple-element.8), channel_id=1, source_target_pairs={{0,6},{1,3},{2,4},{3,1},{4,2},{5,7},{6,0},{7,5},{8,14},{9,11},{10,... | collective-permute-start | bytes 184328 | tf_op jit(solution)/shard_map/ppermute | solution.py:125
  65.5 28.3 %collective-permute-start.28 = (bf16[96,1280]{1,0:T(8,128)(2,1)S(1)}, bf16[96,1280]{1,0:T(8,128)(2,1)S(1)}, u32[]{:S(2)}, u32[]{:S(2)}) collective-permute-start(bf16[96,1280]{1,0:T(8,128)(2,1)S(1)} %pad_maximum_fusion), channel_id=1, source_target_pairs={{0,1},{1,0},{2,3},{3,2},{4,5},{5,4},{6,7},{7,6},{8,9},{9,8},{10,11... | collective-permute-start | bytes 737288 | tf_op jit(solution)/shard_map/ppermute | solution.py:129
  76.5 5.0 %collective-permute-start.18 = (bf16[48,1280]{1,0:T(8,128)(2,1)S(1)}, bf16[48,1280]{1,0:T(8,128)(2,1)S(1)}, u32[]{:S(2)}, u32[]{:S(2)}) collective-permute-start(bf16[48,1280]{1,0:T(8,128)(2,1)S(1)} %pad_maximum_fusion.4), channel_id=1, source_target_pairs={{0,2},{1,7},{2,0},{3,5},{4,6},{5,3},{6,4},{7,1},{8,10},{9,15},{10,... | collective-permute-start | bytes 368648 | tf_op jit(solution)/shard_map/ppermute | solution.py:125
  81.6 4.2 %collective-permute-start.26 = (bf16[16,1280]{1,0:T(8,128)(2,1)S(1)}, bf16[16,1280]{1,0:T(8,128)(2,1)S(1)}, u32[]{:S(2)}, u32[]{:S(2)}) collective-permute-start(bf16[16,1280]{1,0:T(8,128)(2,1)S(1)} %get-tuple-element.6), channel_id=1, source_target_pairs={{0,152},{1,9},{2,154},{3,11},{4,156},{5,13},{6,158},{7,15},{8,16},... | collective-permute-start | bytes 122888 | tf_op jit(solution)/shard_map/ppermute | solution.py:125
  81.7 12.2 %collective-permute-start.29 = (bf16[96,1280]{1,0:T(8,128)(2,1)S(1)}, bf16[96,1280]{1,0:T(8,128)(2,1)S(1)}, u32[]{:S(2)}, u32[]{:S(2)}) collective-permute-start(bf16[96,1280]{1,0:T(8,128)(2,1)S(1)} %pad_maximum_fusion.1), channel_id=1, source_target_pairs={{0,1},{1,0},{2,3},{3,2},{4,5},{5,4},{6,7},{7,6},{8,9},{9,8},{10,11... | collective-permute-start | bytes 737288 | tf_op jit(solution)/shard_map/ppermute | solution.py:129
  85.8 4.6 %collective-permute-start.27 = (bf16[32,1280]{1,0:T(8,128)(2,1)S(1)}, bf16[32,1280]{1,0:T(8,128)(2,1)S(1)}, u32[]{:S(2)}, u32[]{:S(2)}) collective-permute-start(bf16[32,1280]{1,0:T(8,128)(2,1)S(1)} %pad_maximum_fusion.5), channel_id=1, source_target_pairs={{0,8},{1,153},{2,10},{3,155},{4,12},{5,157},{6,14},{7,159},{8,0},{... | collective-permute-start | bytes 245768 | tf_op jit(solution)/shard_map/ppermute | solution.py:125
  90.4 4.5 %collective-permute-start.30 = (bf16[64,1280]{1,0:T(8,128)(2,1)S(1)}, bf16[64,1280]{1,0:T(8,128)(2,1)S(1)}, u32[]{:S(2)}, u32[]{:S(2)}) collective-permute-start(bf16[64,1280]{1,0:T(8,128)(2,1)S(1)} %pad_maximum_fusion.2), channel_id=1, source_target_pairs={{0,1},{1,0},{2,3},{3,2},{4,5},{5,4},{6,7},{7,6},{8,9},{9,8},{10,11... | collective-permute-start | bytes 491528 | tf_op jit(solution)/shard_map/ppermute | solution.py:129
  97.8 3.3 %copy-start.3 = (bf16[1280,640]{1,0:T(8,128)(2,1)S(1)}, bf16[1280,640]{1,0:T(8,128)(2,1)}, u32[]{:S(2)}) copy-start(bf16[1280,640]{1,0:T(8,128)(2,1)} %param.13) | copy-start | bytes 4915204
  115.6 9.3 %copy-start.4 = (bf16[640,1280]{1,0:T(8,128)(2,1)S(1)}, bf16[640,1280]{1,0:T(8,128)(2,1)}, u32[]{:S(2)}) copy-start(bf16[640,1280]{1,0:T(8,128)(2,1)} %param.14) | copy-start | bytes 4915204
  115.6 9.3 %copy-start.7 = (f32[1280]{0:T(1024)S(1)}, f32[1280]{0:T(1024)}, u32[]{:S(2)}) copy-start(f32[1280]{0:T(1024)} %param.15) | copy-start | bytes 15364

commit v3 on v0

v3 whole, which is shorter than its diff:
```python
import jax
import jax.numpy as jnp
from jax import lax
from jax.experimental import pallas as pl
from jax.experimental.pallas import tpu as pltpu
from jax.sharding import PartitionSpec as P

HEADS = 10
HEAD_DIM = 64
PAIR = 2 * HEAD_DIM
BLOCK = 256
VMEM_BYTES = 40 << 20
AXES = ("grp", "frame")
EARLY = 5


SIZES = {"x": 4, "y": 4, "z": 8}

STEPS = {
    4: (((0, 1),), ((0, 3), (1, 2))),
    8: (((0, 3),), ((0, 6), (3, 4)), ((0, 1), (3, 2), (4, 5), (6, 7))),
}
ORDER = "xxzzzyy"
SPLITS = 2


def device_index(place, core):
    if core == 1:
        place = {n: -v % SIZES[n] for n, v in place.items()}
    x, y, z = place["x"], place["y"], place["z"]
    return ((z // 4) * 4 + x) * 32 + ((z % 4) * 4 + y) * 2 + core


def tree():
    held = {name: [0] for name in "xyz"}
    taken = {name: 0 for name in "xyz"}
    rounds = []
    for axis in ORDER:
        step = STEPS[SIZES[axis]][taken[axis]]
        taken[axis] += 1
        pairs = []
        for core in range(2):
            for x in held["x"]:
                for y in held["y"]:
                    for z in held["z"]:
                        place = {"x": x, "y": y, "z": z}
                        for source, sink in step:
                            if place[axis] == source:
                                pairs.append(
                                    (
                                        device_index(place, core),
                                        device_index({**place, axis: sink}, core),
                                    )
                                )
        before = {name: sum(1 << v for v in nodes) for name, nodes in held.items()}
        rounds.append((sorted(pairs), before))
        held[axis] = held[axis] + [sink for _, sink in step]
    assert all(len(held[name]) == SIZES[name] for name in "xyz")
    return rounds


def exchange(step):
    pairs = []
    for core in range(2):
        for y in range(4):
            for z in range(8):
                for a, b in (((0, 1), (2, 3)), ((0, 3), (1, 2)))[step]:
                    ends = [device_index({"x": v, "y": y, "z": z}, core) for v in (a, b)]
                    pairs += [(ends[0], ends[1]), (ends[1], ends[0])]
    return sorted(pairs)


CORE_SWAP = [(i, i ^ 1) for i in range(256)]
NEXT_FRAME = [(i, (i + 1) % 256) for i in range(256)]


def holding():
    grp, frame = lax.axis_index("grp"), lax.axis_index("frame")
    core = frame % 2
    place = {"x": grp % 4, "y": frame // 2 % 4, "z": grp // 4 * 4 + frame // 8}
    place = {n: jnp.where(core == 1, (SIZES[n] - v) % SIZES[n], v) for n, v in place.items()}

    def holds(before):
        inside = [(before[n] >> place[n]) & 1 for n in "xyz"]
        return inside[0] * inside[1] * inside[2] == 1

    return core == 1, holds


def scatter(rows):
    second, holds = holding()
    quarter = rows.shape[0] // 4
    quarters = [rows[quarter * i : quarter * (i + 1)] for i in range(4)]
    sinks = [device_index({"x": 1, "y": 0, "z": 0}, core) for core in range(2)]
    near = lax.ppermute(quarters[1], AXES, [(0, sinks[0])])
    far = lax.ppermute(quarters[3], AXES, [(0, sinks[1])])
    other = lax.ppermute(quarters[2], AXES, CORE_SWAP)
    return jnp.where(
        holds({n: 1 for n in "xyz"}),
        jnp.where(second, other, quarters[0]),
        jnp.where(second, far, near),
    )


def spread(piece, steps):
    _, holds = holding()
    rounds = tree()
    for step in steps:
        pairs, before = rounds[step]
        sent = piece
        if step < SPLITS:
            middle = piece.shape[0] // 2
            piece, sent = piece[:middle], piece[middle:]
        come = lax.ppermute(sent, AXES, pairs)
        piece = jnp.where(holds(before), piece, come)
    return piece


def gather(piece):
    for step in reversed(range(SPLITS)):
        come = lax.ppermute(piece, AXES, exchange(step))
        piece = jnp.concatenate([piece, come], axis=0)
    return piece


def normed(rows, gain, bias):
    values = rows.astype(jnp.float32)
    center = jnp.mean(values, axis=-1, keepdims=True)
    values = values - center
    spread = jnp.mean(values * values, axis=-1, keepdims=True)
    return (values * lax.rsqrt(spread + 1e-05) * gain + bias).astype(jnp.bfloat16)


def project(rows, weight):
    return jnp.dot(rows, weight, preferred_element_type=jnp.float32)


def query_kernel(rows_ref, gain_ref, bias_ref, weight_ref, out_ref):
    rows = normed(rows_ref[...], gain_ref[...], bias_ref[...])
    query = project(rows, weight_ref[...]).astype(jnp.bfloat16)
    out_ref[...] = query * jnp.bfloat16(HEAD_DIM ** (-0.5))


def pair_lanes(shape):
    return lax.broadcasted_iota(jnp.int32, shape, 1) < HEAD_DIM


def context(rows, gain, bias, key_ref, value_ref):
    rows = normed(rows, gain, bias)
    keys = project(rows, key_ref[...]).astype(jnp.bfloat16)
    values = project(rows, value_ref[...]).astype(jnp.bfloat16)
    lane = lax.broadcasted_iota(jnp.int32, (rows.shape[0], PAIR), 1)
    first = lane < HEAD_DIM
    none = jnp.zeros((rows.shape[0], PAIR), jnp.bfloat16)
    heads = []
    for pair in range(HEADS // 2):
        columns = slice(pair * PAIR, (pair + 1) * PAIR)
        key, value = keys[:, columns], values[:, columns]
        one_right = jnp.where(lane == HEAD_DIM, 1.0, 0.0).astype(jnp.bfloat16)
        one_left = jnp.where(lane == 0, 1.0, 0.0).astype(jnp.bfloat16)
        heads.append((jnp.where(first, key, none), jnp.where(first, value, one_right)))
        heads.append((jnp.where(first, none, key), jnp.where(first, one_left, value)))
    return heads


def attend(query, key, value):
    scores = lax.dot_general(
        query, key, (((1,), (1,)), ((), ())), preferred_element_type=jnp.float32
    )
    top = jnp.max(scores, axis=-1, keepdims=True)
    raised = jnp.exp(scores - top).astype(jnp.bfloat16)
    return jnp.dot(raised, value, preferred_element_type=jnp.float32), top


def part_kernel(
    first_ref, rows_ref, own_ref, query_ref, gain_ref, bias_ref, key_ref, value_ref, sum_ref, top_ref
):
    rows = jnp.where(first_ref[0] == 1, own_ref[...], rows_ref[...])
    heads = context(rows, gain_ref[...], bias_ref[...], key_ref, value_ref)
    for start in range(0, query_ref.shape[0], BLOCK):
        block = pl.ds(start, BLOCK)
        tops = []
        for head, (key, value) in enumerate(heads):
            pair = head // 2
            mixed, top = attend(query_ref[block, pair * PAIR : (pair + 1) * PAIR], key, value)
            sum_ref[block, head * PAIR : (head + 1) * PAIR] = mixed
            tops.append(top)
        top_ref[block, :] = jnp.concatenate(
            tops + [jnp.zeros((BLOCK, PAIR - HEADS), jnp.float32)], axis=1
        )


def last_kernel(
    rows_ref, query_ref, gain_ref, bias_ref, key_ref, value_ref,
    sum_a_ref, top_a_ref, sum_b_ref, top_b_ref, hidden_ref, out_weight_ref, out_bias_ref, out_ref,
):
    heads = context(rows_ref[...], gain_ref[...], bias_ref[...], key_ref, value_ref)
    for start in range(0, query_ref.shape[0], BLOCK):
        block = pl.ds(start, BLOCK)
        left = pair_lanes((BLOCK, PAIR))
        mixed = []
        for pair in range(HEADS // 2):
            query = query_ref[block, pair * PAIR : (pair + 1) * PAIR]
            parts = []
            for head in (2 * pair, 2 * pair + 1):
                columns = slice(head * PAIR, (head + 1) * PAIR)
                total, top = attend(query, *heads[head])
                top_a, top_b = top_a_ref[block, head : head + 1], top_b_ref[block, head : head + 1]
                most = jnp.maximum(top, jnp.maximum(top_a, top_b))
                total = (
                    total * jnp.exp(top - most)
                    + sum_a_ref[block, columns] * jnp.exp(top_a - most)
                    + sum_b_ref[block, columns] * jnp.exp(top_b - most)
                )
                ones = HEAD_DIM if head % 2 == 0 else 0
                parts.append(total / total[:, ones : ones + 1])
            mixed.append(jnp.where(left, parts[0], parts[1]).astype(jnp.bfloat16))
        attended = jnp.concatenate(mixed, axis=1)
        projected = project(attended, out_weight_ref[...])
        total = hidden_ref[block, :].astype(jnp.float32) + projected + out_bias_ref[...]
        out_ref[block, :] = total.astype(jnp.bfloat16)


def call(kernel, outs, *operands, scalars=0, flops=0, exps=0):
    whole = pl.BlockSpec(memory_space=pltpu.VMEM)
    specs = [pl.BlockSpec(memory_space=pltpu.SMEM)] * scalars
    return pl.pallas_call(
        kernel,
        out_shape=outs,
        in_specs=specs + [whole] * (len(operands) - scalars),
        out_specs=jax.tree.map(lambda _: whole, outs),
        compiler_params=pltpu.CompilerParams(vmem_limit_bytes=VMEM_BYTES),
        cost_estimate=pl.CostEstimate(flops=flops, bytes_accessed=8 << 20, transcendentals=exps),
    )(*operands)


def body(hidden_states, norm_gain, norm_bias, w_query, w_key, w_value, w_out, out_bias):
    position = lax.axis_index("grp") * lax.axis_size("frame") + lax.axis_index("frame")
    at_start = jnp.where(position == 0, 1, 0).astype(jnp.int32).reshape(1)
    gain, bias = norm_gain.reshape(1, -1), norm_bias.reshape(1, -1)
    tokens, width = hidden_states.shape
    inner = w_query.shape[1]
    shifted = lax.ppermute(hidden_states, AXES, NEXT_FRAME)
    piece = scatter(hidden_states)
    query = call(
        query_kernel, jax.ShapeDtypeStruct((tokens, inner), jnp.bfloat16),
        hidden_states, gain, bias, w_query, flops=2 * tokens * width * inner,
    )
    piece = spread(piece, range(1, EARLY))
    piece, shifted, query = lax.optimization_barrier((piece, shifted, query))
    partial = (
        jax.ShapeDtypeStruct((tokens, HEADS * PAIR), jnp.float32),
        jax.ShapeDtypeStruct((tokens, PAIR), jnp.float32),
    )

    def part(rows, own, flag):
        return call(
            part_kernel, partial, flag, rows, own, query, gain, bias, w_key, w_value,
            scalars=1, flops=4 * rows.shape[0] * inner * (width + 8 * tokens),
            exps=rows.shape[0] * tokens * HEADS,
        )

    prior = part(shifted, hidden_states, at_start)
    piece = spread(piece, range(EARLY, len(ORDER)))
    half = gather(piece)
    other = lax.ppermute(half, AXES, CORE_SWAP)
    near = part(half, half, jnp.zeros((1,), jnp.int32))
    return call(
        last_kernel, jax.ShapeDtypeStruct((tokens, width), jnp.bfloat16),
        other, query, gain, bias, w_key, w_value, *prior, *near,
        hidden_states, w_out, out_bias.reshape(1, -1),
        flops=4 * other.shape[0] * inner * (width + 8 * tokens),
    )


def solution(mesh):
    placed = (P(AXES, None), P(), P(), P(), P(), P(), P(), P())
    return jax.shard_map(
        body, mesh=mesh, in_specs=placed, out_specs=P(AXES, None), check_vma=False
    )
```

time: 327 us -> 99.1 us (0.30)
  waiting for transfers between devices: 254 us -> 21.6 us
  matrix products: 32.4 us -> 0 us
  starting transfers between devices: 4.8 us -> 35.9 us
  Pallas kernels: 0 us -> 28.1 us
  between operations: 13.5 us -> 0.45 us
  local copies, waits for them, and re-layouts: 14.6 us -> 6.37 us
    psum x1 -> x0, waiting for transfers between devices: 254 us -> none  [from_root(): return lax.psum(kept, axis)]
    ppermute x1 -> x13, starting transfers between devices: 4.76 us -> 35.9 us  [the longest x1 11.4 us: body(): other = lax.ppermute(half, AXES, CORE_SWAP)]
    pallas_call x0 -> x4, Pallas kernels: none -> 28.1 us  [call(): pl.pallas_call(kernel, out_shape=outs, in_specs=specs + [whole] * (len(op...]
    ppermute x1 -> x13, waiting for transfers between devices: 0.01 us -> 21.6 us  [the longest x6 11.8 us: spread(): come = lax.ppermute(sent, AXES, pairs)]
    dot_general x5 -> x0, matrix products: 21.2 us -> none  [the longest x1 9.21 us: attend(): jnp.einsum('hqk,khd->qhd', weights, v_heads, preferred_element_type=jnp.f...]
    sub x1 -> x0, matrix products: 11.2 us -> none  [attend(): raised = jnp.exp(scores - top)]
    slice x6 -> x2, local copies, waits for them, and re-layouts: 12.4 us -> 1.35 us  [the longest x1 1.34 us: scatter(): quarters = [rows[quarter * i:quarter * (i + 1)] for i in range(4)]]
    unnamed x12 -> x28, local copies, waits for them, and re-layouts: 0.08 us -> 5.01 us
  transfers between devices with their start and end apart: 2 -> 13, of which waited for: 1 -> 8; matrix products, arithmetic and copies ran while one was open for 4% -> 1% of each run, Pallas kernels for 0% -> 14%
where the time goes in v3:
time: 99.1 us; the launch traced here: 97.1 us
  starting transfers between devices  35.9 us (36%)
  Pallas kernels  28.1 us (28%)
  waiting for transfers between devices  21.6 us (22%)
  local copies, waits for them, and re-layouts  6.37 us (6%)
  other arithmetic  4.74 us (5%)
    pallas_call x4, Pallas kernels, call(): pl.pallas_call(kernel, out_shape=outs, in_specs=specs + [whole] * (len(op...  28.1 us
    ppermute x6, waiting for transfers between devices, spread(): come = lax.ppermute(sent, AXES, pairs)  11.8 us
    ppermute x1, starting transfers between devices, body(): other = lax.ppermute(half, AXES, CORE_SWAP)  11.4 us
    ppermute x6, starting transfers between devices, spread(): come = lax.ppermute(sent, AXES, pairs)  10.5 us
    ppermute x2, starting transfers between devices, gather(): come = lax.ppermute(piece, AXES, exchange(step))  9.24 us
    ppermute x2, waiting for transfers between devices, gather(): come = lax.ppermute(piece, AXES, exchange(step))  7.48 us
    unnamed x28, local copies, waits for them, and re-layouts  5.01 us
    ppermute x1, starting transfers between devices, scatter(): other = lax.ppermute(quarters[2], AXES, CORE_SWAP)  3.33 us
  transfers between devices with their start and end apart: 13, of which 8 were waited for; matrix products, arithmetic and copies ran while one was open for 1% of the time, Pallas kernels for 14%

profile of v3, /device:TPU:1, one launch (start us, length us, event | category | flops | bytes accessed | tf_op | source)
XLA Modules:
  0.0 97.1 jit_solution(14312253604769839213)
XLA Ops:
  0.0 0.0 copy-start
  0.0 1.3 %fusion = (bf16[128,1280]{1,0:T(8,128)(2,1)S(1)}, bf16[128,1280]{1,0:T(8,128)(2,1)S(1)}, bf16[128,1280]{1,0:T(8,128)(2,1)S(1)}) fusion(bf16[512,1280]{1,0:T(8,128)(2,1)} %hidden_ref.1), kind=kLoop, calls=%fused_computation.9 | loop fusion | bytes 1966080 | tf_op jit(solution)/shard_map/slice | solution.py:93
  1.3 3.3 %collective-permute-start = (bf16[128,1280]{1,0:T(8,128)(2,1)S(1)}, bf16[128,1280]{1,0:T(8,128)(2,1)S(1)}, u32[]{:S(2)}, u32[]{:S(2)}) collective-permute-start(bf16[128,1280]{1,0:T(8,128)(2,1)S(1)} %get-tuple-element.19), channel_id=1, source_target_pairs={{0,1},{1,0},{2,3},{3,2},{4,5},{5,4},{6,7},{7,6},{8,9},{9,8},{10,11... | collective-permute-start | bytes 983048 | tf_op jit(solution)/shard_map/ppermute | solution.py:97
  4.7 0.7 collective-permute-start.2
  5.3 0.7 collective-permute-start.1
  6.2 0.0 collective-permute-done
  6.2 0.0 collective-permute-done.2
  6.2 0.0 collective-permute-done.1
  6.2 0.0 copy-done
  6.2 0.1 select_select_fusion
  6.3 0.0 copy-start.11
  6.3 0.0 copy-start.12
  6.3 1.4 %collective-permute-start.3 = (bf16[64,1280]{1,0:T(8,128)(2,1)S(1)}, bf16[64,1280]{1,0:T(8,128)(2,1)S(1)}, u32[]{:S(2)}, u32[]{:S(2)}) collective-permute-start(bf16[64,1280]{1,0:T(8,128)(2,1)S(1)} %slice.25), channel_id=1, source_target_pairs={{0,96},{1,33},{32,64},{97,65}} | collective-permute-start | bytes 491528 | tf_op jit(solution)/shard_map/ppermute | solution.py:114
  7.7 4.0 %collective-permute-done.3 = bf16[64,1280]{1,0:T(8,128)(2,1)S(1)} collective-permute-done((bf16[64,1280]{1,0:T(8,128)(2,1)S(1)}, bf16[64,1280]{1,0:T(8,128)(2,1)S(1)}, u32[]{:S(2)}, u32[]{:S(2)}) %collective-permute-start.3) | collective-permute-done | bytes 163872 | tf_op jit(solution)/shard_map/ppermute | solution.py:114
  11.8 1.9 %collective-permute-start.4 = (bf16[64,1280]{1,0:T(8,128)(2,1)S(1)}, bf16[64,1280]{1,0:T(8,128)(2,1)S(1)}, u32[]{:S(2)}, u32[]{:S(2)}) collective-permute-start(bf16[64,1280]{1,0:T(8,128)(2,1)S(1)} %slice_select_fusion), channel_id=1, source_target_pairs={{0,24},{1,137},{32,56},{33,169},{64,88},{65,201},{96,120},{97,233}} | collective-permute-start | bytes 491528 | tf_op jit(solution)/shard_map/ppermute | solution.py:114
  13.7 0.1 collective-permute-start.7
  13.8 2.1 %collective-permute-done.4 = bf16[64,1280]{1,0:T(8,128)(2,1)S(1)} collective-permute-done((bf16[64,1280]{1,0:T(8,128)(2,1)S(1)}, bf16[64,1280]{1,0:T(8,128)(2,1)S(1)}, u32[]{:S(2)}, u32[]{:S(2)}) %collective-permute-start.4) | collective-permute-done | bytes 163872 | tf_op jit(solution)/shard_map/ppermute | solution.py:114
  16.0 1.3 %collective-permute-start.5 = (bf16[64,1280]{1,0:T(8,128)(2,1)S(1)}, bf16[64,1280]{1,0:T(8,128)(2,1)S(1)}, u32[]{:S(2)}, u32[]{:S(2)}) collective-permute-start(bf16[64,1280]{1,0:T(8,128)(2,1)S(1)} %broadcast_select_fusion), channel_id=1, source_target_pairs={{0,144},{1,17},{24,128},{32,176},{33,49},{56,160},{64,208},{65,81}... | collective-permute-start | bytes 491528 | tf_op jit(solution)/shard_map/ppermute | solution.py:114
  17.3 2.5 %collective-permute-done.5 = bf16[64,1280]{1,0:T(8,128)(2,1)S(1)} collective-permute-done((bf16[64,1280]{1,0:T(8,128)(2,1)S(1)}, bf16[64,1280]{1,0:T(8,128)(2,1)S(1)}, u32[]{:S(2)}, u32[]{:S(2)}) %collective-permute-start.5) | collective-permute-done | bytes 163872 | tf_op jit(solution)/shard_map/ppermute | solution.py:114
  19.8 0.0 copy-start.10
  19.8 2.0 %collective-permute-start.6 = (bf16[64,1280]{1,0:T(8,128)(2,1)S(1)}, bf16[64,1280]{1,0:T(8,128)(2,1)}, u32[]{:S(2)}, u32[]{:S(2)}) collective-permute-start(bf16[64,1280]{1,0:T(8,128)(2,1)S(1)} %broadcast_select_fusion.1), channel_id=1, source_target_pairs={{0,8},{1,153},{17,9},{24,16},{32,40},{33,185},{49,41},{56,48},{64,... | collective-permute-start | bytes 491528 | tf_op jit(solution)/shard_map/ppermute | solution.py:114
  21.7 0.0 copy-done.11
  21.8 0.0 copy-done.12
  21.8 0.0 copy-start.1
  21.8 1.4 %copy-done.1 = bf16[1280,640]{1,0:T(8,128)(2,1)S(1)} copy-done((bf16[1280,640]{1,0:T(8,128)(2,1)S(1)}, bf16[1280,640]{1,0:T(8,128)(2,1)}, u32[]{:S(2)}) %copy-start.1) | copy-done | bytes 1638424
  23.2 1.8 %shard_map.82.query_ref = bf16[512,640]{1,0:T(8,128)(2,1)S(1)} custom-call(bf16[512,1280]{1,0:T(8,128)(2,1)S(1)} %copy-done, f32[1,1280]{1,0:T(1,128)S(1)} %reshape.12.gain_ref, f32[1,1280]{1,0:T(1,128)S(1)} %reshape.13.bias_ref, bf16[1280,640]{1,0:T(8,128)(2,1)S(1)} %copy-done.1), custom_call_target="tpu_custom_call" | custom-call | flops 838860800 | bytes 8388608 | tf_op jit(solution)/shard_map/pallas_call | solution.py:227
  25.0 0.0 copy-done.10
  25.0 0.0 copy-start.13
  25.0 0.0 collective-permute-done.6
  25.0 0.9 broadcast_select_fusion.2
  26.0 0.0 copy-start.9
  26.0 2.3 %collective-permute-done.7.rows_ref = bf16[512,1280]{1,0:T(8,128)(2,1)S(1)} collective-permute-done((bf16[512,1280]{1,0:T(8,128)(2,1)S(1)}, bf16[512,1280]{1,0:T(8,128)(2,1)S(1)}, u32[]{:S(2)}, u32[]{:S(2)}) %collective-permute-start.7) | collective-permute-done | bytes 1310752 | tf_op jit(solution)/shard_map/ppermute | solution.py:243
  28.3 1.9 %collective-permute-start.8 = (bf16[64,1280]{1,0:T(8,128)(2,1)S(1)}, bf16[64,1280]{1,0:T(8,128)(2,1)}, u32[]{:S(2)}, u32[]{:S(2)}) collective-permute-start(bf16[64,1280]{1,0:T(8,128)(2,1)S(1)} %broadcast_select_fusion.2), channel_id=1, source_target_pairs={{0,2},{1,7},{8,10},{9,15},{16,18},{17,23},{24,26},{25,31},{32,34},... | collective-permute-start | bytes 491528 | tf_op jit(solution)/shard_map/ppermute | solution.py:114
  30.3 0.0 copy-done.9
  30.3 1.6 %collective-permute-done.8 = bf16[64,1280]{1,0:T(8,128)(2,1)} collective-permute-done((bf16[64,1280]{1,0:T(8,128)(2,1)S(1)}, bf16[64,1280]{1,0:T(8,128)(2,1)}, u32[]{:S(2)}, u32[]{:S(2)}) %collective-permute-start.8) | collective-permute-done | bytes 163872 | tf_op jit(solution)/shard_map/ppermute | solution.py:114
  31.9 0.9 broadcast_select_fusion.3
  32.8 0.0 copy-start.8
  32.8 2.0 %collective-permute-start.9 = (bf16[64,1280]{1,0:T(8,128)(2,1)S(1)}, bf16[64,1280]{1,0:T(8,128)(2,1)}, u32[]{:S(2)}, u32[]{:S(2)}) collective-permute-start(bf16[64,1280]{1,0:T(8,128)(2,1)S(1)} %broadcast_select_fusion.3), channel_id=1, source_target_pairs={{0,6},{1,3},{2,4},{7,5},{8,14},{9,11},{10,12},{15,13},{16,22},{17,... | collective-permute-start | bytes 491528 | tf_op jit(solution)/shard_map/ppermute | solution.py:114
  34.8 0.0 copy-done.8
  34.8 1.6 %collective-permute-done.9 = bf16[64,1280]{1,0:T(8,128)(2,1)} collective-permute-done((bf16[64,1280]{1,0:T(8,128)(2,1)S(1)}, bf16[64,1280]{1,0:T(8,128)(2,1)}, u32[]{:S(2)}, u32[]{:S(2)}) %collective-permute-start.9) | collective-permute-done | bytes 163872 | tf_op jit(solution)/shard_map/ppermute | solution.py:114
  36.4 0.9 broadcast_select_fusion.4
  37.3 1.6 %collective-permute-start.10 = (bf16[64,1280]{1,0:T(8,128)(2,1)S(1)}, bf16[64,1280]{1,0:T(8,128)(2,1)S(1)}, u32[]{:S(2)}, u32[]{:S(2)}) collective-permute-start(bf16[64,1280]{1,0:T(8,128)(2,1)S(1)} %broadcast_select_fusion.4), channel_id=1, source_target_pairs={{0,96},{1,33},{2,98},{3,35},{4,100},{5,37},{6,102},{7,39},{8,104},... | collective-permute-start | bytes 491528 | tf_op jit(solution)/shard_map/ppermute | solution.py:121
  39.0 2.7 %collective-permute-done.10 = bf16[64,1280]{1,0:T(8,128)(2,1)S(1)} collective-permute-done((bf16[64,1280]{1,0:T(8,128)(2,1)S(1)}, bf16[64,1280]{1,0:T(8,128)(2,1)S(1)}, u32[]{:S(2)}, u32[]{:S(2)}) %collective-permute-start.10) | collective-permute-done | bytes 163872 | tf_op jit(solution)/shard_map/ppermute | solution.py:121
  41.7 0.0 copy-start.7
  41.7 0.7 copy-done.7
  42.3 0.7 pad_maximum_fusion.1
  43.1 7.6 %collective-permute-start.11 = (bf16[128,1280]{1,0:T(8,128)(2,1)}, bf16[128,1280]{1,0:T(8,128)(2,1)}, u32[]{:S(2)}, u32[]{:S(2)}) collective-permute-start(bf16[128,1280]{1,0:T(8,128)(2,1)} %pad_maximum_fusion.1), channel_id=1, source_target_pairs={{0,32},{1,97},{2,34},{3,99},{4,36},{5,101},{6,38},{7,103},{8,40},{... | collective-permute-start | bytes 983048 | tf_op jit(solution)/shard_map/ppermute | solution.py:121
  50.7 0.0 copy-done.13
  50.7 4.8 %collective-permute-done.11 = bf16[128,1280]{1,0:T(8,128)(2,1)} collective-permute-done((bf16[128,1280]{1,0:T(8,128)(2,1)}, bf16[128,1280]{1,0:T(8,128)(2,1)}, u32[]{:S(2)}, u32[]{:S(2)}) %collective-permute-start.11) | collective-permute-done | bytes 327712 | tf_op jit(solution)/shard_map/ppermute | solution.py:121
  55.5 1.1 %pad_maximum_fusion.rows_ref.own_ref = bf16[256,1280]{1,0:T(8,128)(2,1)S(1)} fusion(bf16[128,1280]{1,0:T(8,128)(2,1)} %collective-permute-done.11, bf16[64,1280]{1,0:T(8,128)(2,1)} %copy-done.7, bf16[64,1280]{1,0:T(8,128)(2,1)S(1)} %broadcast_select_fusion.4), kind=kLoop, calls=%fused_computation | loop fusion | flops 1966080 | bytes 1310720 | tf_op jit(solution)/shard_map/concatenate | solution.py:122
  56.5 11.4 %collective-permute-start.12 = (bf16[256,1280]{1,0:T(8,128)(2,1)S(1)}, bf16[256,1280]{1,0:T(8,128)(2,1)S(1)}, u32[]{:S(2)}, u32[]{:S(2)}) collective-permute-start(bf16[256,1280]{1,0:T(8,128)(2,1)S(1)} %pad_maximum_fusion.rows_ref.own_ref), channel_id=1, source_target_pairs={{0,1},{1,0},{2,3},{3,2},{4,5},{5,4},{6,7},{7,6},{8,9},{9,8},{10,11... | collective-permute-start | bytes 1966088 | tf_op jit(solution)/shard_map/ppermute | solution.py:266
  67.9 0.0 copy-start.2
  67.9 1.4 %copy-done.2 = bf16[1280,640]{1,0:T(8,128)(2,1)S(1)} copy-done((bf16[1280,640]{1,0:T(8,128)(2,1)S(1)}, bf16[1280,640]{1,0:T(8,128)(2,1)}, u32[]{:S(2)}) %copy-start.2) | copy-done | bytes 1638424
  69.4 1.4 %copy-done.4 = bf16[1280,640]{1,0:T(8,128)(2,1)S(1)} copy-done((bf16[1280,640]{1,0:T(8,128)(2,1)S(1)}, bf16[1280,640]{1,0:T(8,128)(2,1)}, u32[]{:S(2)}) %copy-start.4) | copy-done | bytes 1638424
  70.8 0.0 copy-start.3
  70.8 0.0 copy-start.5
  70.8 8.9 %shard_map.83 = (f32[512,1280]{1,0:T(8,128)S(1)}, f32[512,128]{1,0:T(8,128)S(1)}) custom-call(s32[1]{0:T(128)} %bitcast.first_ref, bf16[512,1280]{1,0:T(8,128)(2,1)S(1)} %collective-permute-done.7.rows_ref, bf16[512,1280]{1,0:T(8,128)(2,1)S(1)} %copy-done, bf16[512,640]{1,0:T(8,128)(2,1)S(1)} %shard_map.82.query_ref, f32[1,1280]{1,0:T(1,128)S(1)} %reshape.12.gain_ref, ...), custom_call_target="tpu_custom_call" | custom-call | flops 7046430720 | bytes 8388608 | tf_op jit(solution)/shard_map/pallas_call | solution.py:227
  79.7 0.0 copy-done.3
  79.7 0.0 copy-done.5
  79.7 0.0 copy-start.6
  79.8 3.1 %shard_map.84 = (f32[512,1280]{1,0:T(8,128)S(1)}, f32[512,128]{1,0:T(8,128)S(1)}) custom-call(s32[1]{0:T(128)} %constant.131.clone.1.first_ref, bf16[256,1280]{1,0:T(8,128)(2,1)S(1)} %pad_maximum_fusion.rows_ref.own_ref, bf16[256,1280]{1,0:T(8,128)(2,1)S(1)} %pad_maximum_fusion.rows_ref.own_ref, bf16[512,640]{1,0:T(8,128)(2,1)S(1)} %shard_map.82.query_ref, ...), custom_call_target="tpu_custom_call" | custom-call | flops 3523215360 | bytes 8388608 | tf_op jit(solution)/shard_map/pallas_call | solution.py:227
  82.9 0.0 collective-permute-done.12.rows_ref
  82.9 0.0 copy-done.6
  82.9 14.2 %shard_map.85 = bf16[512,1280]{1,0:T(8,128)(2,1)} custom-call(bf16[256,1280]{1,0:T(8,128)(2,1)S(1)} %collective-permute-done.12.rows_ref, bf16[512,640]{1,0:T(8,128)(2,1)S(1)} %shard_map.82.query_ref, f32[1,1280]{1,0:T(1,128)S(1)} %reshape.12.gain_ref, f32[1,1280]{1,0:T(1,128)S(1)} %reshape.13.bias_ref, bf16[1280,640]{1,0:T(8,128)(2,1)S(1)} %copy-done.3, ...), custom_call_target="tpu_custom_call" | custom-call | flops 3523215360 | bytes 8388608 | tf_op jit(solution)/shard_map/pallas_call | solution.py:227
  (8 shorter events, 0.1 us)
Async XLA Ops:
  0.0 6.2 %copy-start = (bf16[512,1280]{1,0:T(8,128)(2,1)S(1)}, bf16[512,1280]{1,0:T(8,128)(2,1)}, u32[]{:S(2)}) copy-start(bf16[512,1280]{1,0:T(8,128)(2,1)} %hidden_ref.1) | copy-start | bytes 3932164
  1.3 4.8 %collective-permute-start = (bf16[128,1280]{1,0:T(8,128)(2,1)S(1)}, bf16[128,1280]{1,0:T(8,128)(2,1)S(1)}, u32[]{:S(2)}, u32[]{:S(2)}) collective-permute-start(bf16[128,1280]{1,0:T(8,128)(2,1)S(1)} %get-tuple-element.19), channel_id=1, source_target_pairs={{0,1},{1,0},{2,3},{3,2},{4,5},{5,4},{6,7},{7,6},{8,9},{9,8},{10,11... | collective-permute-start | bytes 983048 | tf_op jit(solution)/shard_map/ppermute | solution.py:97
  4.7 1.5 %collective-permute-start.2 = (bf16[128,1280]{1,0:T(8,128)(2,1)S(1)}, bf16[128,1280]{1,0:T(8,128)(2,1)S(1)}, u32[]{:S(2)}, u32[]{:S(2)}) collective-permute-start(bf16[128,1280]{1,0:T(8,128)(2,1)S(1)} %get-tuple-element.20), channel_id=1, source_target_pairs={{0,32}} | collective-permute-start | bytes 983048 | tf_op jit(solution)/shard_map/ppermute | solution.py:95
  5.3 0.8 collective-permute-start.1
  6.3 15.5 %copy-start.11 = (f32[1280]{0:T(1024)S(1)}, f32[1280]{0:T(1024)}, u32[]{:S(2)}) copy-start(f32[1280]{0:T(1024)} %param.9) | copy-start | bytes 15364
  6.3 15.5 %copy-start.12 = (f32[1280]{0:T(1024)S(1)}, f32[1280]{0:T(1024)}, u32[]{:S(2)}) copy-start(f32[1280]{0:T(1024)} %param.10) | copy-start | bytes 15364
  6.3 5.4 %collective-permute-start.3 = (bf16[64,1280]{1,0:T(8,128)(2,1)S(1)}, bf16[64,1280]{1,0:T(8,128)(2,1)S(1)}, u32[]{:S(2)}, u32[]{:S(2)}) collective-permute-start(bf16[64,1280]{1,0:T(8,128)(2,1)S(1)} %slice.25), channel_id=1, source_target_pairs={{0,96},{1,33},{32,64},{97,65}} | collective-permute-start | bytes 491528 | tf_op jit(solution)/shard_map/ppermute | solution.py:114
  11.8 4.2 %collective-permute-start.4 = (bf16[64,1280]{1,0:T(8,128)(2,1)S(1)}, bf16[64,1280]{1,0:T(8,128)(2,1)S(1)}, u32[]{:S(2)}, u32[]{:S(2)}) collective-permute-start(bf16[64,1280]{1,0:T(8,128)(2,1)S(1)} %slice_select_fusion), channel_id=1, source_target_pairs={{0,24},{1,137},{32,56},{33,169},{64,88},{65,201},{96,120},{97,233}} | collective-permute-start | bytes 491528 | tf_op jit(solution)/shard_map/ppermute | solution.py:114
  13.7 14.6 %collective-permute-start.7 = (bf16[512,1280]{1,0:T(8,128)(2,1)S(1)}, bf16[512,1280]{1,0:T(8,128)(2,1)S(1)}, u32[]{:S(2)}, u32[]{:S(2)}) collective-permute-start(bf16[512,1280]{1,0:T(8,128)(2,1)S(1)} %copy-done), channel_id=1, source_target_pairs={{0,1},{1,2},{2,3},{3,4},{4,5},{5,6},{6,7},{7,8},{8,9},{9,10},{10,1... | collective-permute-start | bytes 3932168 | tf_op jit(solution)/shard_map/ppermute | solution.py:243
  16.0 3.8 %collective-permute-start.5 = (bf16[64,1280]{1,0:T(8,128)(2,1)S(1)}, bf16[64,1280]{1,0:T(8,128)(2,1)S(1)}, u32[]{:S(2)}, u32[]{:S(2)}) collective-permute-start(bf16[64,1280]{1,0:T(8,128)(2,1)S(1)} %broadcast_select_fusion), channel_id=1, source_target_pairs={{0,144},{1,17},{24,128},{32,176},{33,49},{56,160},{64,208},{65,81}... | collective-permute-start | bytes 491528 | tf_op jit(solution)/shard_map/ppermute | solution.py:114
  19.8 5.2 %copy-start.10 = (bf16[64,1280]{1,0:T(8,128)(2,1)}, bf16[64,1280]{1,0:T(8,128)(2,1)S(1)}, u32[]{:S(2)}) copy-start(bf16[64,1280]{1,0:T(8,128)(2,1)S(1)} %broadcast_select_fusion.1) | copy-start | bytes 491524
  19.8 5.3 %collective-permute-start.6 = (bf16[64,1280]{1,0:T(8,128)(2,1)S(1)}, bf16[64,1280]{1,0:T(8,128)(2,1)}, u32[]{:S(2)}, u32[]{:S(2)}) collective-permute-start(bf16[64,1280]{1,0:T(8,128)(2,1)S(1)} %broadcast_select_fusion.1), channel_id=1, source_target_pairs={{0,8},{1,153},{17,9},{24,16},{32,40},{33,185},{49,41},{56,48},{64,... | collective-permute-start | bytes 491528 | tf_op jit(solution)/shard_map/ppermute | solution.py:114
  21.8 1.4 %copy-start.1 = (bf16[1280,640]{1,0:T(8,128)(2,1)S(1)}, bf16[1280,640]{1,0:T(8,128)(2,1)}, u32[]{:S(2)}) copy-start(bf16[1280,640]{1,0:T(8,128)(2,1)} %weight_ref.1) | copy-start | bytes 4915204
  25.0 25.7 %copy-start.13 = (f32[1280]{0:T(1024)S(1)}, f32[1280]{0:T(1024)}, u32[]{:S(2)}) copy-start(f32[1280]{0:T(1024)} %param.15) | copy-start | bytes 15364
  26.0 4.3 %copy-start.9 = (bf16[64,1280]{1,0:T(8,128)(2,1)}, bf16[64,1280]{1,0:T(8,128)(2,1)S(1)}, u32[]{:S(2)}) copy-start(bf16[64,1280]{1,0:T(8,128)(2,1)S(1)} %broadcast_select_fusion.2) | copy-start | bytes 491524
  28.3 3.5 %collective-permute-start.8 = (bf16[64,1280]{1,0:T(8,128)(2,1)S(1)}, bf16[64,1280]{1,0:T(8,128)(2,1)}, u32[]{:S(2)}, u32[]{:S(2)}) collective-permute-start(bf16[64,1280]{1,0:T(8,128)(2,1)S(1)} %broadcast_select_fusion.2), channel_id=1, source_target_pairs={{0,2},{1,7},{8,10},{9,15},{16,18},{17,23},{24,26},{25,31},{32,34},... | collective-permute-start | bytes 491528 | tf_op jit(solution)/shard_map/ppermute | solution.py:114
  32.8 2.0 %copy-start.8 = (bf16[64,1280]{1,0:T(8,128)(2,1)}, bf16[64,1280]{1,0:T(8,128)(2,1)S(1)}, u32[]{:S(2)}) copy-start(bf16[64,1280]{1,0:T(8,128)(2,1)S(1)} %broadcast_select_fusion.3) | copy-start | bytes 491524
  32.8 3.5 %collective-permute-start.9 = (bf16[64,1280]{1,0:T(8,128)(2,1)S(1)}, bf16[64,1280]{1,0:T(8,128)(2,1)}, u32[]{:S(2)}, u32[]{:S(2)}) collective-permute-start(bf16[64,1280]{1,0:T(8,128)(2,1)S(1)} %broadcast_select_fusion.3), channel_id=1, source_target_pairs={{0,6},{1,3},{2,4},{7,5},{8,14},{9,11},{10,12},{15,13},{16,22},{17,... | collective-permute-start | bytes 491528 | tf_op jit(solution)/shard_map/ppermute | solution.py:114
  37.3 4.4 %collective-permute-start.10 = (bf16[64,1280]{1,0:T(8,128)(2,1)S(1)}, bf16[64,1280]{1,0:T(8,128)(2,1)S(1)}, u32[]{:S(2)}, u32[]{:S(2)}) collective-permute-start(bf16[64,1280]{1,0:T(8,128)(2,1)S(1)} %broadcast_select_fusion.4), channel_id=1, source_target_pairs={{0,96},{1,33},{2,98},{3,35},{4,100},{5,37},{6,102},{7,39},{8,104},... | collective-permute-start | bytes 491528 | tf_op jit(solution)/shard_map/ppermute | solution.py:121
  41.7 0.7 copy-start.7
  43.1 12.4 %collective-permute-start.11 = (bf16[128,1280]{1,0:T(8,128)(2,1)}, bf16[128,1280]{1,0:T(8,128)(2,1)}, u32[]{:S(2)}, u32[]{:S(2)}) collective-permute-start(bf16[128,1280]{1,0:T(8,128)(2,1)} %pad_maximum_fusion.1), channel_id=1, source_target_pairs={{0,32},{1,97},{2,34},{3,99},{4,36},{5,101},{6,38},{7,103},{8,40},{... | collective-permute-start | bytes 983048 | tf_op jit(solution)/shard_map/ppermute | solution.py:121
  56.5 26.4 %collective-permute-start.12 = (bf16[256,1280]{1,0:T(8,128)(2,1)S(1)}, bf16[256,1280]{1,0:T(8,128)(2,1)S(1)}, u32[]{:S(2)}, u32[]{:S(2)}) collective-permute-start(bf16[256,1280]{1,0:T(8,128)(2,1)S(1)} %pad_maximum_fusion.rows_ref.own_ref), channel_id=1, source_target_pairs={{0,1},{1,0},{2,3},{3,2},{4,5},{5,4},{6,7},{7,6},{8,9},{9,8},{10,11... | collective-permute-start | bytes 1966088 | tf_op jit(solution)/shard_map/ppermute | solution.py:266
  67.9 1.4 %copy-start.2 = (bf16[1280,640]{1,0:T(8,128)(2,1)S(1)}, bf16[1280,640]{1,0:T(8,128)(2,1)}, u32[]{:S(2)}) copy-start(bf16[1280,640]{1,0:T(8,128)(2,1)} %key_ref.5) | copy-start | bytes 4915204
  69.4 1.4 %copy-start.4 = (bf16[1280,640]{1,0:T(8,128)(2,1)S(1)}, bf16[1280,640]{1,0:T(8,128)(2,1)}, u32[]{:S(2)}) copy-start(bf16[1280,640]{1,0:T(8,128)(2,1)} %value_ref.5) | copy-start | bytes 4915204
  70.8 8.9 %copy-start.3 = (bf16[1280,640]{1,0:T(8,128)(2,1)S(1)}, bf16[1280,640]{1,0:T(8,128)(2,1)}, u32[]{:S(2)}) copy-start(bf16[1280,640]{1,0:T(8,128)(2,1)} %key_ref.5) | copy-start | bytes 4915204
  70.8 8.9 %copy-start.5 = (bf16[1280,640]{1,0:T(8,128)(2,1)S(1)}, bf16[1280,640]{1,0:T(8,128)(2,1)}, u32[]{:S(2)}) copy-start(bf16[1280,640]{1,0:T(8,128)(2,1)} %value_ref.5) | copy-start | bytes 4915204
  79.7 3.2 %copy-start.6 = (bf16[640,1280]{1,0:T(8,128)(2,1)S(1)}, bf16[640,1280]{1,0:T(8,128)(2,1)}, u32[]{:S(2)}) copy-start(bf16[640,1280]{1,0:T(8,128)(2,1)} %out_weight_ref.1) | copy-start | bytes 4915204

commit v4 on v3

v4 whole, which is shorter than its diff:
```python
import functools

import jax
import jax.numpy as jnp
from jax import lax
from jax.experimental import pallas as pl
from jax.experimental.pallas import tpu as pltpu
from jax.sharding import PartitionSpec as P

HEADS = 10
HEAD_DIM = 64
PAIR = 2 * HEAD_DIM
HALF = HEADS // 2
OUT_TILE = 256
VMEM_BYTES = 40 << 20
AXES = ("grp", "frame")


SIZES = {"x": 4, "y": 4, "z": 8}

STEPS = {
    4: (((0, 1),), ((0, 3), (1, 2))),
    8: (((0, 3),), ((0, 6), (3, 4)), ((0, 1), (3, 2), (4, 5), (6, 7))),
}
ORDER = "xxzzzyy"
SPLITS = 2


def device_index(place, core):
    if core == 1:
        place = {n: -v % SIZES[n] for n, v in place.items()}
    x, y, z = place["x"], place["y"], place["z"]
    return ((z // 4) * 4 + x) * 32 + ((z % 4) * 4 + y) * 2 + core


def tree():
    held = {name: [0] for name in "xyz"}
    taken = {name: 0 for name in "xyz"}
    rounds = []
    for axis in ORDER:
        step = STEPS[SIZES[axis]][taken[axis]]
        taken[axis] += 1
        pairs = []
        for core in range(2):
            for x in held["x"]:
                for y in held["y"]:
                    for z in held["z"]:
                        place = {"x": x, "y": y, "z": z}
                        for source, sink in step:
                            if place[axis] == source:
                                pairs.append(
                                    (
                                        device_index(place, core),
                                        device_index({**place, axis: sink}, core),
                                    )
                                )
        before = {name: sum(1 << v for v in nodes) for name, nodes in held.items()}
        rounds.append((sorted(pairs), before))
        held[axis] = held[axis] + [sink for _, sink in step]
    assert all(len(held[name]) == SIZES[name] for name in "xyz")
    return rounds


def exchange(step):
    pairs = []
    for core in range(2):
        for y in range(4):
            for z in range(8):
                for a, b in (((0, 1), (2, 3)), ((0, 3), (1, 2)))[step]:
                    ends = [device_index({"x": v, "y": y, "z": z}, core) for v in (a, b)]
                    pairs += [(ends[0], ends[1]), (ends[1], ends[0])]
    return sorted(pairs)


CORE_SWAP = [(i, i ^ 1) for i in range(256)]
NEXT_FRAME = [(i, (i + 1) % 256) for i in range(256)]


def holding():
    grp, frame = lax.axis_index("grp"), lax.axis_index("frame")
    core = frame % 2
    place = {"x": grp % 4, "y": frame // 2 % 4, "z": grp // 4 * 4 + frame // 8}
    place = {n: jnp.where(core == 1, (SIZES[n] - v) % SIZES[n], v) for n, v in place.items()}

    def holds(before):
        inside = [(before[n] >> place[n]) & 1 for n in "xyz"]
        return inside[0] * inside[1] * inside[2] == 1

    return core == 1, holds


def scatter(rows):
    second, holds = holding()
    quarter = rows.shape[0] // 4
    quarters = [rows[quarter * i : quarter * (i + 1)] for i in range(4)]
    sinks = [device_index({"x": 1, "y": 0, "z": 0}, core) for core in range(2)]
    near = lax.ppermute(quarters[1], AXES, [(0, sinks[0])])
    far = lax.ppermute(quarters[3], AXES, [(0, sinks[1])])
    other = lax.ppermute(quarters[2], AXES, CORE_SWAP)
    return jnp.where(
        holds({n: 1 for n in "xyz"}),
        jnp.where(second, other, quarters[0]),
        jnp.where(second, far, near),
    )


def spread(piece, steps):
    _, holds = holding()
    rounds = tree()
    for step in steps:
        pairs, before = rounds[step]
        sent = piece
        if step < SPLITS:
            middle = piece.shape[0] // 2
            piece, sent = piece[:middle], piece[middle:]
        come = lax.ppermute(sent, AXES, pairs)
        piece = jnp.where(holds(before), piece, come)
    return piece


def normed(rows, gain, bias):
    values = rows.astype(jnp.float32)
    center = jnp.mean(values, axis=-1, keepdims=True)
    values = values - center
    spread = jnp.mean(values * values, axis=-1, keepdims=True)
    return (values * lax.rsqrt(spread + 1e-05) * gain + bias).astype(jnp.bfloat16)


def project(rows, weight):
    return jnp.dot(rows, weight, preferred_element_type=jnp.float32)


def lanes_of(rows):
    return lax.broadcasted_iota(jnp.int32, (rows, PAIR), 1)


def columns(index):
    return slice(index * PAIR, (index + 1) * PAIR)


def own_lanes(head, array, fill):
    left = lanes_of(array.shape[0]) < HEAD_DIM
    other = jnp.full(array.shape, fill, jnp.bfloat16)
    return jnp.where(left, array, other) if head % 2 == 0 else jnp.where(left, other, array)


def attend(head, query, key, value, carried=None):
    scores = lax.dot_general(
        query, own_lanes(head, key, 0.0), (((1,), (1,)), ((), ())),
        preferred_element_type=jnp.float32,
    )
    tiles = [scores[:, i : i + PAIR] for i in range(0, scores.shape[1], PAIR)]
    top = functools.reduce(jnp.maximum, tiles)
    top = jnp.broadcast_to(jnp.max(top, axis=-1, keepdims=True), top.shape)
    if carried is not None:
        top = jnp.maximum(top, carried[1])
    raised = [jnp.exp(tile - top).astype(jnp.bfloat16) for tile in tiles]
    total = project(jnp.concatenate(raised, axis=1), own_lanes(head, value, 1.0))
    if carried is not None:
        total = total + carried[0] * jnp.exp(carried[1] - top)
    return total, top


def query_kernel(rows_ref, gain_ref, bias_ref, weight_ref, out_ref):
    rows = normed(rows_ref[...], gain_ref[...], bias_ref[...])
    query = project(rows, weight_ref[...]).astype(jnp.bfloat16)
    out_ref[...] = query * jnp.bfloat16(HEAD_DIM ** (-0.5))


def context_kernel(
    first_ref, rows_ref, own_ref, gain_ref, bias_ref, key_ref, value_ref, keys_ref, values_ref
):
    rows = jnp.where(first_ref[0] == 1, own_ref[...], rows_ref[...])
    rows = normed(rows, gain_ref[...], bias_ref[...])
    keys_ref[...] = project(rows, key_ref[...]).astype(jnp.bfloat16)
    values_ref[...] = project(rows, value_ref[...]).astype(jnp.bfloat16)


def heads_kernel(query_ref, keys_ref, values_ref, sum_ref, top_ref, *, heads):
    for place, head in enumerate(heads):
        pair = columns(head // 2)
        sum_ref[:, columns(place)], top_ref[:, columns(place)] = attend(
            head, query_ref[:, pair], keys_ref[:, pair], values_ref[:, pair]
        )


def state(refs, head):
    place = columns(head % HALF)
    sum_ref, top_ref = refs[:2] if head < HALF else refs[2:]
    return sum_ref.at[:, place], top_ref.at[:, place]


def own_context(rows_refs, gain_ref, bias_ref, key_ref, value_ref):
    rows = [ref[...] for ref in rows_refs]
    rows = rows[0] if len(rows) == 1 else jnp.concatenate(rows, axis=0)
    rows = normed(rows, gain_ref[...], bias_ref[...])
    keys = project(rows, key_ref[...]).astype(jnp.bfloat16)
    values = project(rows, value_ref[...]).astype(jnp.bfloat16)
    return keys, values


def more_kernel(query_ref, gain_ref, bias_ref, key_ref, value_ref, *refs):
    rows, carried, out = refs[:-8], refs[-8:-4], refs[-4:]
    keys, values = own_context(rows, gain_ref, bias_ref, key_ref, value_ref)
    for head in range(HEADS):
        pair = columns(head // 2)
        before = [ref[...] for ref in state(carried, head)]
        sum_ref, top_ref = state(out, head)
        sum_ref[...], top_ref[...] = attend(
            head, query_ref[:, pair], keys[:, pair], values[:, pair], before
        )


def last_kernel(query_ref, gain_ref, bias_ref, key_ref, value_ref, *refs):
    rows, carried = refs[:-9], refs[-9:-5]
    hidden_ref, out_weight_ref, out_bias_ref, out_ref, mixed_ref = refs[-5:]
    keys, values = own_context(rows, gain_ref, bias_ref, key_ref, value_ref)
    left = lanes_of(query_ref.shape[0]) < HEAD_DIM
    for pair in range(HEADS // 2):
        place = columns(pair)
        even, odd = (
            attend(
                head, query_ref[:, place], keys[:, place], values[:, place],
                [ref[...] for ref in state(carried, head)],
            )[0]
            for head in (2 * pair, 2 * pair + 1)
        )
        weight = pltpu.roll(jnp.where(left, odd, even), HEAD_DIM, 1)
        mixed_ref[:, place] = (jnp.where(left, even, odd) / weight).astype(jnp.bfloat16)
    for start in range(0, out_ref.shape[1], OUT_TILE):
        tile = slice(start, start + OUT_TILE)
        total = project(mixed_ref[...], out_weight_ref[:, tile])
        total = hidden_ref[:, tile].astype(jnp.float32) + total + out_bias_ref[:, tile]
        out_ref[:, tile] = total.astype(jnp.bfloat16)


def call(kernel, outs, *operands, scalars=0, flops=0, exps=0, aliases=None, scratch=()):
    whole = pl.BlockSpec(memory_space=pltpu.VMEM)
    specs = [pl.BlockSpec(memory_space=pltpu.SMEM)] * scalars
    return pl.pallas_call(
        kernel,
        out_shape=outs,
        in_specs=specs + [whole] * (len(operands) - scalars),
        out_specs=jax.tree.map(lambda _: whole, outs),
        scratch_shapes=scratch,
        input_output_aliases=aliases or {},
        compiler_params=pltpu.CompilerParams(vmem_limit_bytes=VMEM_BYTES),
        cost_estimate=pl.CostEstimate(flops=flops, bytes_accessed=1 << 20, transcendentals=exps),
    )(*operands)


def halves(tokens):
    return (jax.ShapeDtypeStruct((tokens, HALF * PAIR), jnp.float32),) * 2


def body(hidden_states, norm_gain, norm_bias, w_query, w_key, w_value, w_out, out_bias):
    position = lax.axis_index("grp") * lax.axis_size("frame") + lax.axis_index("frame")
    at_start = jnp.where(position == 0, 1, 0).astype(jnp.int32).reshape(1)
    norm = (norm_gain.reshape(1, -1), norm_bias.reshape(1, -1))
    tokens, width = hidden_states.shape
    inner = w_query.shape[1]
    narrow = jax.ShapeDtypeStruct((tokens, inner), jnp.bfloat16)
    tie = lax.optimization_barrier

    shifted = lax.ppermute(hidden_states, AXES, NEXT_FRAME)
    piece = scatter(hidden_states)
    query = call(
        query_kernel, narrow, hidden_states, *norm, w_query, flops=2 * tokens * width * inner
    )
    piece, query = tie((piece, query))
    piece = spread(piece, range(1, 4))

    piece, shifted = tie((piece, shifted))
    keys, values = call(
        context_kernel, (narrow, narrow), at_start, shifted, hidden_states, *norm, w_key, w_value,
        scalars=1, flops=4 * tokens * width * inner,
    )
    piece = spread(piece, [4])
    held = ()
    for half in range(2):
        piece, keys, values = tie((piece, keys, values))
        held += call(
            functools.partial(heads_kernel, heads=range(half * HALF, (half + 1) * HALF)),
            halves(tokens), query, keys, values,
            flops=8 * HALF * tokens * tokens * PAIR, exps=HALF * tokens * tokens,
        )
        piece = spread(piece, [5 + half])
        piece, held = tie((piece, held))

    def more(rows, held):
        return call(
            more_kernel, halves(tokens) * 2, query, *norm, w_key, w_value, *rows, *held,
            aliases={5 + len(rows) + i: i for i in range(4)}, flops=4 * tokens * width * inner,
        )

    come = lax.ppermute(piece, AXES, exchange(1))
    early = jnp.concatenate([piece, come], axis=0)
    early_other = lax.ppermute(early, AXES, CORE_SWAP)
    late = lax.ppermute(early, AXES, exchange(0))
    held = more([early, early_other], held)
    late, held = tie((late, held))
    late_other = lax.ppermute(late, AXES, CORE_SWAP)
    held = more([late], held)
    return call(
        last_kernel, jax.ShapeDtypeStruct((tokens, width), jnp.bfloat16),
        query, *norm, w_key, w_value, late_other, *held, hidden_states, w_out,
        out_bias.reshape(1, -1),
        flops=4 * tokens * width * inner, scratch=[pltpu.VMEM((tokens, inner), jnp.bfloat16)],
    )


def solution(mesh):
    placed = (P(AXES, None), P(), P(), P(), P(), P(), P(), P())
    return jax.shard_map(
        body, mesh=mesh, in_specs=placed, out_specs=P(AXES, None), check_vma=False
    )
```

time: 99.1 us -> 91.5 us (0.923); the launches traced: 97.1 us -> 90.8 us
  waiting for transfers between devices: 21.6 us -> 10.9 us
  local copies, waits for them, and re-layouts: 6.37 us -> 14.1 us
  Pallas kernels: 28.1 us -> 25.1 us
    ppermute x3 -> x4, starting transfers between devices: 20.7 us -> 10.3 us  [the longest x1 8.73 us: body(): early_other = lax.ppermute(early, AXES, CORE_SWAP)]
    ppermute x6, starting transfers between devices: 10.5 us -> 20.2 us  [spread(): come = lax.ppermute(sent, AXES, pairs)]
    unnamed x28 -> x45, local copies, waits for them, and re-layouts: 5.01 us -> 11.9 us
    ppermute x6, waiting for transfers between devices: 11.8 us -> 5.08 us  [spread(): come = lax.ppermute(sent, AXES, pairs)]
    pallas_call x4 -> x7, Pallas kernels: 28.1 us -> 25.1 us  [call(): pl.pallas_call(kernel, out_shape=outs, in_specs=specs + [whole] * (len(op...]
    ppermute x1, waiting for transfers between devices: 2.33 us -> 0.01 us  [body(): shifted = lax.ppermute(hidden_states, AXES, NEXT_FRAME)]
    concatenate x2 -> x0, other arithmetic: 1.8 us -> none  [gather(): piece = jnp.concatenate([piece, come], axis=0)]
    ppermute x3 -> x4, waiting for transfers between devices: 7.48 us -> 5.8 us  [the longest x1 2.94 us: body(): come = lax.ppermute(piece, AXES, exchange(1))]
  transfers between devices with their start and end apart: 13 -> 14, of which waited for: 8 -> 6; matrix products, arithmetic and copies ran while one was open for 1% -> 3% of each run, Pallas kernels for 14% -> 21%
where the time goes in v4:
time: 91.5 us; the launch traced here: 90.8 us
  starting transfers between devices  35 us (38%)
  Pallas kernels  25.1 us (27%)
  local copies, waits for them, and re-layouts  14.1 us (15%)
  waiting for transfers between devices  10.9 us (12%)
  other arithmetic  5.37 us (6%)
    pallas_call x7, Pallas kernels, call(): pl.pallas_call(kernel, out_shape=outs, in_specs=specs + [whole] * (len(op...  25.1 us
    ppermute x6, starting transfers between devices, spread(): come = lax.ppermute(sent, AXES, pairs)  20.2 us
    unnamed x45, local copies, waits for them, and re-layouts  11.9 us
    ppermute x1, starting transfers between devices, body(): early_other = lax.ppermute(early, AXES, CORE_SWAP)  8.73 us
    ppermute x6, waiting for transfers between devices, spread(): come = lax.ppermute(sent, AXES, pairs)  5.08 us
    select_n x6, other arithmetic, spread(): piece = jnp.where(holds(before), piece, come)  4.21 us
    ppermute x1, starting transfers between devices, scatter(): other = lax.ppermute(quarters[2], AXES, CORE_SWAP)  3.23 us
    ppermute x1, waiting for transfers between devices, body(): come = lax.ppermute(piece, AXES, exchange(1))  2.94 us
  transfers between devices with their start and end apart: 14, of which 6 were waited for; matrix products, arithmetic and copies ran while one was open for 3% of the time, Pallas kernels for 21%

profile of v4, /device:TPU:1, one launch (start us, length us, event | category | flops | bytes accessed | tf_op | source)
XLA Modules:
  0.0 90.8 jit_solution(12744460321490717933)
XLA Ops:
  0.0 2.1 %fusion = (bf16[128,1280]{1,0:T(8,128)(2,1)}, bf16[128,1280]{1,0:T(8,128)(2,1)S(1)}, bf16[128,1280]{1,0:T(8,128)(2,1)S(1)}) fusion(bf16[512,1280]{1,0:T(8,128)(2,1)} %refs_5_.1), kind=kLoop, calls=%fused_computation.9 | loop fusion | bytes 1966080 | tf_op jit(solution)/shard_map/slice | solution.py:95
  2.1 3.2 %collective-permute-start = (bf16[128,1280]{1,0:T(8,128)(2,1)}, bf16[128,1280]{1,0:T(8,128)(2,1)S(1)}, u32[]{:S(2)}, u32[]{:S(2)}) collective-permute-start(bf16[128,1280]{1,0:T(8,128)(2,1)} %get-tuple-element.79), channel_id=1, source_target_pairs={{0,1},{1,0},{2,3},{3,2},{4,5},{5,4},{6,7},{7,6},{8,9},{9,8},{10,11... | collective-permute-start | bytes 983048 | tf_op jit(solution)/shard_map/ppermute | solution.py:99
  5.3 0.7 collective-permute-start.1
  6.0 0.7 collective-permute-start.2
  6.8 0.0 copy-done.19
  6.9 0.0 copy-done.20
  6.9 0.0 copy-done.11
  6.9 3.1 %shard_map.82.query_ref = bf16[512,640]{1,0:T(8,128)(2,1)S(1)} custom-call(bf16[512,1280]{1,0:T(8,128)(2,1)} %refs_5_.1, f32[1,1280]{1,0:T(1,128)S(1)} %reshape.12.gain_ref, f32[1,1280]{1,0:T(1,128)S(1)} %reshape.13.bias_ref, bf16[1280,640]{1,0:T(8,128)(2,1)S(1)} %copy-done.11), custom_call_target="tpu_custom_call" | custom-call | flops 838860800 | bytes 1048576 | tf_op jit(solution)/shard_map/pallas_call | solution.py:240
  10.0 0.8 copy-done.6
  10.8 0.0 collective-permute-done
  10.9 0.0 collective-permute-done.1
  10.9 0.0 collective-permute-done.2
  10.9 0.0 copy-start.1
  10.9 1.2 %select_select_fusion = bf16[128,1280]{1,0:T(8,128)(2,1)S(1)} fusion(bf16[128,1280]{1,0:T(8,128)(2,1)S(1)} %collective-permute-done.1, bf16[128,1280]{1,0:T(8,128)(2,1)S(1)} %collective-permute-done.2, bf16[128,1280]{1,0:T(8,128)(2,1)S(1)} %collective-permute-done, bf16[512,1280]{1,0:T(8,128)(2,1)} %refs_5_.1, pred[]{:T(512)S(6)} %eq.73, pred[]{:T(512)S(6)} %eq.74), kind=kLoop, calls=%fused_computation | loop fusion | flops 491520 | bytes 1638402 | tf_op jit(solution)/shard_map/jit(_where)/select_n | solution.py:100
  12.0 0.0 copy-start.18
  12.0 0.7 copy-done.18
  12.8 2.2 %collective-permute-start.3 = (bf16[64,1280]{1,0:T(8,128)(2,1)S(1)}, bf16[64,1280]{1,0:T(8,128)(2,1)}, u32[]{:S(2)}, u32[]{:S(2)}) collective-permute-start(bf16[64,1280]{1,0:T(8,128)(2,1)S(1)} %slice.23), channel_id=1, source_target_pairs={{0,96},{1,33},{32,64},{97,65}} | collective-permute-start | bytes 491528 | tf_op jit(solution)/shard_map/ppermute | solution.py:116
  15.0 0.0 collective-permute-start.6
  15.0 1.6 %collective-permute-done.3 = bf16[64,1280]{1,0:T(8,128)(2,1)} collective-permute-done((bf16[64,1280]{1,0:T(8,128)(2,1)S(1)}, bf16[64,1280]{1,0:T(8,128)(2,1)}, u32[]{:S(2)}, u32[]{:S(2)}) %collective-permute-start.3) | collective-permute-done | bytes 163872 | tf_op jit(solution)/shard_map/ppermute | solution.py:116
  16.6 0.9 %slice_select_fusion = bf16[64,1280]{1,0:T(8,128)(2,1)S(1)} fusion(bf16[64,1280]{1,0:T(8,128)(2,1)} %collective-permute-done.3, bf16[128,1280]{1,0:T(8,128)(2,1)} %copy-done.18, pred[]{:T(512)S(6)} %eq.80), kind=kLoop, calls=%fused_computation.1 | loop fusion | flops 81920 | bytes 491521 | tf_op jit(solution)/shard_map/jit(_where)/select_n | solution.py:117
  17.5 6.3 %collective-permute-start.4 = (bf16[64,1280]{1,0:T(8,128)(2,1)S(1)}, bf16[64,1280]{1,0:T(8,128)(2,1)}, u32[]{:S(2)}, u32[]{:S(2)}) collective-permute-start(bf16[64,1280]{1,0:T(8,128)(2,1)S(1)} %slice_select_fusion), channel_id=1, source_target_pairs={{0,24},{1,137},{32,56},{33,169},{64,88},{65,201},{96,120},{97,233}} | collective-permute-start | bytes 491528 | tf_op jit(solution)/shard_map/ppermute | solution.py:116
  23.8 1.6 %collective-permute-done.4 = bf16[64,1280]{1,0:T(8,128)(2,1)} collective-permute-done((bf16[64,1280]{1,0:T(8,128)(2,1)S(1)}, bf16[64,1280]{1,0:T(8,128)(2,1)}, u32[]{:S(2)}, u32[]{:S(2)}) %collective-permute-start.4) | collective-permute-done | bytes 163872 | tf_op jit(solution)/shard_map/ppermute | solution.py:116
  25.3 0.7 broadcast_select_fusion
  26.0 1.9 %collective-permute-start.5 = (bf16[64,1280]{1,0:T(8,128)(2,1)}, bf16[64,1280]{1,0:T(8,128)(2,1)}, u32[]{:S(2)}, u32[]{:S(2)}) collective-permute-start(bf16[64,1280]{1,0:T(8,128)(2,1)} %broadcast_select_fusion), channel_id=1, source_target_pairs={{0,144},{1,17},{24,128},{32,176},{33,49},{56,160},{64,208},{65,81}... | collective-permute-start | bytes 491528 | tf_op jit(solution)/shard_map/ppermute | solution.py:116
  28.0 1.9 %collective-permute-done.5 = bf16[64,1280]{1,0:T(8,128)(2,1)} collective-permute-done((bf16[64,1280]{1,0:T(8,128)(2,1)}, bf16[64,1280]{1,0:T(8,128)(2,1)}, u32[]{:S(2)}, u32[]{:S(2)}) %collective-permute-start.5) | collective-permute-done | bytes 163872 | tf_op jit(solution)/shard_map/ppermute | solution.py:116
  29.9 0.9 %broadcast_select_fusion.1 = bf16[64,1280]{1,0:T(8,128)(2,1)S(1)} fusion(bf16[64,1280]{1,0:T(8,128)(2,1)} %broadcast_select_fusion, bf16[64,1280]{1,0:T(8,128)(2,1)} %collective-permute-done.5, pred[]{:T(512)S(6)} %eq.78), kind=kLoop, calls=%fused_computation.3 | loop fusion | flops 81920 | bytes 491521 | tf_op jit(solution)/shard_map/jit(_where)/select_n | solution.py:117
  30.8 0.0 collective-permute-done.6.rows_ref
  30.8 5.9 %collective-permute-start.7 = (bf16[64,1280]{1,0:T(8,128)(2,1)S(1)}, bf16[64,1280]{1,0:T(8,128)(2,1)}, u32[]{:S(2)}, u32[]{:S(2)}) collective-permute-start(bf16[64,1280]{1,0:T(8,128)(2,1)S(1)} %broadcast_select_fusion.1), channel_id=1, source_target_pairs={{0,8},{1,153},{17,9},{24,16},{32,40},{33,185},{49,41},{56,48},{64,... | collective-permute-start | bytes 491528 | tf_op jit(solution)/shard_map/ppermute | solution.py:116
  36.7 4.5 %shard_map.83 = (bf16[512,640]{1,0:T(8,128)(2,1)S(1)}, bf16[512,640]{1,0:T(8,128)(2,1)S(1)}) custom-call(s32[1]{0:T(128)} %bitcast.first_ref, bf16[512,1280]{1,0:T(8,128)(2,1)} %collective-permute-done.6.rows_ref, bf16[512,1280]{1,0:T(8,128)(2,1)} %refs_5_.1, f32[1,1280]{1,0:T(1,128)S(1)} %reshape.12.gain_ref, f32[1,1280]{1,0:T(1,128)S(1)} %reshape.13.bias_ref, ...), custom_call_target="tpu_custom_call" | custom-call | flops 1677721600 | bytes 1048576 | tf_op jit(solution)/shard_map/pallas_call | solution.py:240
  41.3 0.0 copy-start.12
  41.3 0.8 copy-done.12
  42.1 0.8 copy-done.15
  42.9 0.0 collective-permute-done.7
  42.9 0.7 broadcast_select_fusion.2
  43.6 1.9 %collective-permute-start.8 = (bf16[64,1280]{1,0:T(8,128)(2,1)}, bf16[64,1280]{1,0:T(8,128)(2,1)}, u32[]{:S(2)}, u32[]{:S(2)}) collective-permute-start(bf16[64,1280]{1,0:T(8,128)(2,1)} %broadcast_select_fusion.2), channel_id=1, source_target_pairs={{0,2},{1,7},{8,10},{9,15},{16,18},{17,23},{24,26},{25,31},{32,34},... | collective-permute-start | bytes 491528 | tf_op jit(solution)/shard_map/ppermute | solution.py:116
  45.6 1.1 %copy-done.7 = bf16[512,640]{1,0:T(8,128)(2,1)S(1)} copy-done((bf16[512,640]{1,0:T(8,128)(2,1)S(1)}, bf16[512,640]{1,0:T(8,128)(2,1)}, u32[]{:S(2)}) %copy-start.7) | copy-done | bytes 655384
  46.7 1.1 %copy-done.13 = bf16[512,640]{1,0:T(8,128)(2,1)S(1)} copy-done((bf16[512,640]{1,0:T(8,128)(2,1)S(1)}, bf16[512,640]{1,0:T(8,128)(2,1)}, u32[]{:S(2)}) %copy-start.13) | copy-done | bytes 655384
  47.8 1.1 %copy-done.16 = bf16[512,640]{1,0:T(8,128)(2,1)S(1)} copy-done((bf16[512,640]{1,0:T(8,128)(2,1)S(1)}, bf16[512,640]{1,0:T(8,128)(2,1)}, u32[]{:S(2)}) %copy-start.16) | copy-done | bytes 655384
  48.8 1.9 %shard_map.84 = (f32[512,640]{1,0:T(8,128)S(1)}, f32[512,640]{1,0:T(8,128)S(1)}) custom-call(bf16[512,640]{1,0:T(8,128)(2,1)S(1)} %copy-done.7, bf16[512,640]{1,0:T(8,128)(2,1)S(1)} %copy-done.13, bf16[512,640]{1,0:T(8,128)(2,1)S(1)} %copy-done.16), custom_call_target="tpu_custom_call" | custom-call | flops 1342177280 | bytes 1048576 | tf_op jit(solution)/shard_map/pallas_call | solution.py:240
  50.8 0.0 copy-start.2
  50.8 1.1 %copy-done.2 = f32[512,640]{1,0:T(8,128)} copy-done((f32[512,640]{1,0:T(8,128)}, f32[512,640]{1,0:T(8,128)S(1)}, u32[]{:S(2)}) %copy-start.2) | copy-done | bytes 1310744
  51.8 1.1 %copy-done.4 = f32[512,640]{1,0:T(8,128)} copy-done((f32[512,640]{1,0:T(8,128)}, f32[512,640]{1,0:T(8,128)S(1)}, u32[]{:S(2)}) %copy-start.4) | copy-done | bytes 1310744
  52.9 0.0 collective-permute-done.8
  52.9 0.9 %broadcast_select_fusion.3 = bf16[64,1280]{1,0:T(8,128)(2,1)S(1)} fusion(bf16[64,1280]{1,0:T(8,128)(2,1)} %broadcast_select_fusion.2, bf16[64,1280]{1,0:T(8,128)(2,1)} %collective-permute-done.8, pred[]{:T(512)S(6)} %eq.76), kind=kLoop, calls=%fused_computation.5 | loop fusion | flops 81920 | bytes 491521 | tf_op jit(solution)/shard_map/jit(_where)/select_n | solution.py:117
  53.9 2.0 %collective-permute-start.9 = (bf16[64,1280]{1,0:T(8,128)(2,1)S(1)}, bf16[64,1280]{1,0:T(8,128)(2,1)}, u32[]{:S(2)}, u32[]{:S(2)}) collective-permute-start(bf16[64,1280]{1,0:T(8,128)(2,1)S(1)} %broadcast_select_fusion.3), channel_id=1, source_target_pairs={{0,6},{1,3},{2,4},{7,5},{8,14},{9,11},{10,12},{15,13},{16,22},{17,... | collective-permute-start | bytes 491528 | tf_op jit(solution)/shard_map/ppermute | solution.py:116
  55.8 1.1 %copy-done.8 = bf16[512,640]{1,0:T(8,128)(2,1)S(1)} copy-done((bf16[512,640]{1,0:T(8,128)(2,1)S(1)}, bf16[512,640]{1,0:T(8,128)(2,1)}, u32[]{:S(2)}) %copy-start.8) | copy-done | bytes 655384
  56.9 1.1 %copy-done.14 = bf16[512,640]{1,0:T(8,128)(2,1)S(1)} copy-done((bf16[512,640]{1,0:T(8,128)(2,1)S(1)}, bf16[512,640]{1,0:T(8,128)(2,1)}, u32[]{:S(2)}) %copy-start.14) | copy-done | bytes 655384
  58.0 1.1 %copy-done.17 = bf16[512,640]{1,0:T(8,128)(2,1)S(1)} copy-done((bf16[512,640]{1,0:T(8,128)(2,1)S(1)}, bf16[512,640]{1,0:T(8,128)(2,1)}, u32[]{:S(2)}) %copy-start.17) | copy-done | bytes 655384
  59.1 1.9 %shard_map.85 = (f32[512,640]{1,0:T(8,128)S(1)}, f32[512,640]{1,0:T(8,128)S(1)}) custom-call(bf16[512,640]{1,0:T(8,128)(2,1)S(1)} %copy-done.8, bf16[512,640]{1,0:T(8,128)(2,1)S(1)} %copy-done.14, bf16[512,640]{1,0:T(8,128)(2,1)S(1)} %copy-done.17), custom_call_target="tpu_custom_call" | custom-call | flops 1342177280 | bytes 1048576 | tf_op jit(solution)/shard_map/pallas_call | solution.py:240
  61.0 0.0 copy-start.9
  61.0 0.0 collective-permute-done.9
  61.1 1.3 %collective-permute-start.10 = (bf16[64,1280]{1,0:T(8,128)(2,1)S(1)}, bf16[64,1280]{1,0:T(8,128)(2,1)S(1)}, u32[]{:S(2)}, u32[]{:S(2)}) collective-permute-start(bf16[64,1280]{1,0:T(8,128)(2,1)S(1)} %broadcast_select_fusion.4), channel_id=1, source_target_pairs={{0,96},{1,33},{2,98},{3,35},{4,100},{5,37},{6,102},{7,39},{8,104},... | collective-permute-start | bytes 491528 | tf_op jit(solution)/shard_map/ppermute | solution.py:296
  62.4 2.9 %collective-permute-done.10 = bf16[64,1280]{1,0:T(8,128)(2,1)S(1)} collective-permute-done((bf16[64,1280]{1,0:T(8,128)(2,1)S(1)}, bf16[64,1280]{1,0:T(8,128)(2,1)S(1)}, u32[]{:S(2)}, u32[]{:S(2)}) %collective-permute-start.10) | collective-permute-done | bytes 163872 | tf_op jit(solution)/shard_map/ppermute | solution.py:296
  65.3 0.0 copy-start.21
  65.4 8.7 %collective-permute-start.12 = (bf16[128,1280]{1,0:T(8,128)(2,1)S(1)}, bf16[128,1280]{1,0:T(8,128)(2,1)S(1)}, u32[]{:S(2)}, u32[]{:S(2)}) collective-permute-start(bf16[128,1280]{1,0:T(8,128)(2,1)S(1)} %constant_dynamic-update-slice_fusion.refs_0_), channel_id=1, source_target_pairs={{0,1},{1,0},{2,3},{3,2},{4,5},{5,4},{6,7},{7,6},{8,9},{9,8},{10,11... | collective-permute-start | bytes 983048 | tf_op jit(solution)/shard_map/ppermute | solution.py:298
  74.1 0.0 collective-permute-start.11
  74.1 1.3 %collective-permute-done.12.refs_1_ = bf16[128,1280]{1,0:T(8,128)(2,1)S(1)} collective-permute-done((bf16[128,1280]{1,0:T(8,128)(2,1)S(1)}, bf16[128,1280]{1,0:T(8,128)(2,1)S(1)}, u32[]{:S(2)}, u32[]{:S(2)}) %collective-permute-start.12) | collective-permute-done | bytes 327712 | tf_op jit(solution)/shard_map/ppermute | solution.py:298
  75.3 0.0 copy-done.9
  75.3 4.3 %shard_map.86 = (f32[512,640]{1,0:T(8,128)S(1)}, f32[512,640]{1,0:T(8,128)S(1)}, f32[512,640]{1,0:T(8,128)S(1)}, f32[512,640]{1,0:T(8,128)S(1)}) custom-call(bf16[512,640]{1,0:T(8,128)(2,1)S(1)} %copy-done.9, f32[1,1280]{1,0:T(1,128)S(1)} %reshape.12.gain_ref, ...), custom_call_target="tpu_custom_call", output_to_operand_aliasing={{0}: (7, {}), {1}: (8, {}), {2}: (9, {}), {3}: (10, {})} | custom-call | flops 1677721600 | bytes 1048576 | tf_op jit(solution)/shard_map/pallas_call | solution.py:240
  79.6 1.6 %collective-permute-done.11.refs_0_ = bf16[128,1280]{1,0:T(8,128)(2,1)S(1)} collective-permute-done((bf16[128,1280]{1,0:T(8,128)(2,1)S(1)}, bf16[128,1280]{1,0:T(8,128)(2,1)S(1)}, u32[]{:S(2)}, u32[]{:S(2)}) %collective-permute-start.11) | collective-permute-done | bytes 327712 | tf_op jit(solution)/shard_map/ppermute | solution.py:299
  81.2 0.2 collective-permute-start.13
  81.5 3.1 %shard_map.87 = (f32[512,640]{1,0:T(8,128)S(1)}, f32[512,640]{1,0:T(8,128)S(1)}, f32[512,640]{1,0:T(8,128)S(1)}, f32[512,640]{1,0:T(8,128)S(1)}) custom-call(bf16[512,640]{1,0:T(8,128)(2,1)S(1)} %copy-done.9, f32[1,1280]{1,0:T(1,128)S(1)} %reshape.12.gain_ref, ...), custom_call_target="tpu_custom_call", output_to_operand_aliasing={{0}: (6, {}), {1}: (7, {}), {2}: (8, {}), {3}: (9, {})} | custom-call | flops 1677721600 | bytes 1048576 | tf_op jit(solution)/shard_map/pallas_call | solution.py:240
  84.6 0.0 collective-permute-done.13.refs_0_
  84.6 6.2 %shard_map.88 = bf16[512,1280]{1,0:T(8,128)(2,1)} custom-call(bf16[512,640]{1,0:T(8,128)(2,1)S(1)} %copy-done.9, f32[1,1280]{1,0:T(1,128)S(1)} %reshape.12.gain_ref, f32[1,1280]{1,0:T(1,128)S(1)} %reshape.13.bias_ref, bf16[1280,640]{1,0:T(8,128)(2,1)S(1)} %copy-done, bf16[1280,640]{1,0:T(8,128)(2,1)S(1)} %copy-done.1, ...), custom_call_target="tpu_custom_call" | custom-call | flops 1677721600 | bytes 1048576 | tf_op jit(solution)/shard_map/pallas_call | solution.py:240
  (29 shorter events, 0.1 us)
Async XLA Ops:
  0.0 6.8 %copy-start.19 = (f32[1280]{0:T(1024)S(1)}, f32[1280]{0:T(1024)}, u32[]{:S(2)}) copy-start(f32[1280]{0:T(1024)} %param.9) | copy-start | bytes 15364
  0.0 6.8 %copy-start.20 = (f32[1280]{0:T(1024)S(1)}, f32[1280]{0:T(1024)}, u32[]{:S(2)}) copy-start(f32[1280]{0:T(1024)} %param.10) | copy-start | bytes 15364
  0.0 6.9 %copy-start.11 = (bf16[1280,640]{1,0:T(8,128)(2,1)S(1)}, bf16[1280,640]{1,0:T(8,128)(2,1)}, u32[]{:S(2)}) copy-start(bf16[1280,640]{1,0:T(8,128)(2,1)} %weight_ref.1) | copy-start | bytes 4915204
  2.1 8.8 %collective-permute-start = (bf16[128,1280]{1,0:T(8,128)(2,1)}, bf16[128,1280]{1,0:T(8,128)(2,1)S(1)}, u32[]{:S(2)}, u32[]{:S(2)}) collective-permute-start(bf16[128,1280]{1,0:T(8,128)(2,1)} %get-tuple-element.79), channel_id=1, source_target_pairs={{0,1},{1,0},{2,3},{3,2},{4,5},{5,4},{6,7},{7,6},{8,9},{9,8},{10,11... | collective-permute-start | bytes 983048 | tf_op jit(solution)/shard_map/ppermute | solution.py:99
  5.3 5.5 %collective-permute-start.1 = (bf16[128,1280]{1,0:T(8,128)(2,1)S(1)}, bf16[128,1280]{1,0:T(8,128)(2,1)S(1)}, u32[]{:S(2)}, u32[]{:S(2)}) collective-permute-start(bf16[128,1280]{1,0:T(8,128)(2,1)S(1)} %get-tuple-element.81), channel_id=1, source_target_pairs={{0,97}} | collective-permute-start | bytes 983048 | tf_op jit(solution)/shard_map/ppermute | solution.py:98
  6.0 4.9 %collective-permute-start.2 = (bf16[128,1280]{1,0:T(8,128)(2,1)S(1)}, bf16[128,1280]{1,0:T(8,128)(2,1)S(1)}, u32[]{:S(2)}, u32[]{:S(2)}) collective-permute-start(bf16[128,1280]{1,0:T(8,128)(2,1)S(1)} %get-tuple-element.80), channel_id=1, source_target_pairs={{0,32}} | collective-permute-start | bytes 983048 | tf_op jit(solution)/shard_map/ppermute | solution.py:97
  10.0 0.8 copy-start.6
  10.9 25.8 %copy-start.1 = (bf16[1280,640]{1,0:T(8,128)(2,1)S(1)}, bf16[1280,640]{1,0:T(8,128)(2,1)}, u32[]{:S(2)}) copy-start(bf16[1280,640]{1,0:T(8,128)(2,1)} %value_ref.7) | copy-start | bytes 4915204
  12.0 0.7 copy-start.18
  12.8 23.9 %copy-start = (bf16[1280,640]{1,0:T(8,128)(2,1)S(1)}, bf16[1280,640]{1,0:T(8,128)(2,1)}, u32[]{:S(2)}) copy-start(bf16[1280,640]{1,0:T(8,128)(2,1)} %key_ref.7) | copy-start | bytes 4915204
  12.8 3.8 %collective-permute-start.3 = (bf16[64,1280]{1,0:T(8,128)(2,1)S(1)}, bf16[64,1280]{1,0:T(8,128)(2,1)}, u32[]{:S(2)}, u32[]{:S(2)}) collective-permute-start(bf16[64,1280]{1,0:T(8,128)(2,1)S(1)} %slice.23), channel_id=1, source_target_pairs={{0,96},{1,33},{32,64},{97,65}} | collective-permute-start | bytes 491528 | tf_op jit(solution)/shard_map/ppermute | solution.py:116
  15.0 15.9 %collective-permute-start.6 = (bf16[512,1280]{1,0:T(8,128)(2,1)}, bf16[512,1280]{1,0:T(8,128)(2,1)}, u32[]{:S(2)}, u32[]{:S(2)}) collective-permute-start(bf16[512,1280]{1,0:T(8,128)(2,1)} %refs_5_.1), channel_id=1, source_target_pairs={{0,1},{1,2},{2,3},{3,4},{4,5},{5,6},{6,7},{7,8},{8,9},{9,10},{10,1... | collective-permute-start | bytes 3932168 | tf_op jit(solution)/shard_map/ppermute | solution.py:265
  17.5 7.8 %collective-permute-start.4 = (bf16[64,1280]{1,0:T(8,128)(2,1)S(1)}, bf16[64,1280]{1,0:T(8,128)(2,1)}, u32[]{:S(2)}, u32[]{:S(2)}) collective-permute-start(bf16[64,1280]{1,0:T(8,128)(2,1)S(1)} %slice_select_fusion), channel_id=1, source_target_pairs={{0,24},{1,137},{32,56},{33,169},{64,88},{65,201},{96,120},{97,233}} | collective-permute-start | bytes 491528 | tf_op jit(solution)/shard_map/ppermute | solution.py:116
  26.0 3.8 %collective-permute-start.5 = (bf16[64,1280]{1,0:T(8,128)(2,1)}, bf16[64,1280]{1,0:T(8,128)(2,1)}, u32[]{:S(2)}, u32[]{:S(2)}) collective-permute-start(bf16[64,1280]{1,0:T(8,128)(2,1)} %broadcast_select_fusion), channel_id=1, source_target_pairs={{0,144},{1,17},{24,128},{32,176},{33,49},{56,160},{64,208},{65,81}... | collective-permute-start | bytes 491528 | tf_op jit(solution)/shard_map/ppermute | solution.py:116
  30.8 12.1 %collective-permute-start.7 = (bf16[64,1280]{1,0:T(8,128)(2,1)S(1)}, bf16[64,1280]{1,0:T(8,128)(2,1)}, u32[]{:S(2)}, u32[]{:S(2)}) collective-permute-start(bf16[64,1280]{1,0:T(8,128)(2,1)S(1)} %broadcast_select_fusion.1), channel_id=1, source_target_pairs={{0,8},{1,153},{17,9},{24,16},{32,40},{33,185},{49,41},{56,48},{64,... | collective-permute-start | bytes 491528 | tf_op jit(solution)/shard_map/ppermute | solution.py:116
  41.3 0.8 copy-start.12
  42.1 0.8 copy-start.15
  43.6 9.3 %collective-permute-start.8 = (bf16[64,1280]{1,0:T(8,128)(2,1)}, bf16[64,1280]{1,0:T(8,128)(2,1)}, u32[]{:S(2)}, u32[]{:S(2)}) collective-permute-start(bf16[64,1280]{1,0:T(8,128)(2,1)} %broadcast_select_fusion.2), channel_id=1, source_target_pairs={{0,2},{1,7},{8,10},{9,15},{16,18},{17,23},{24,26},{25,31},{32,34},... | collective-permute-start | bytes 491528 | tf_op jit(solution)/shard_map/ppermute | solution.py:116
  45.6 1.1 %copy-start.7 = (bf16[512,640]{1,0:T(8,128)(2,1)S(1)}, bf16[512,640]{1,0:T(8,128)(2,1)}, u32[]{:S(2)}) copy-start(bf16[512,640]{1,0:T(8,128)(2,1)} %copy-done.6) | copy-start | bytes 1966084
  46.7 1.1 %copy-start.13 = (bf16[512,640]{1,0:T(8,128)(2,1)S(1)}, bf16[512,640]{1,0:T(8,128)(2,1)}, u32[]{:S(2)}) copy-start(bf16[512,640]{1,0:T(8,128)(2,1)} %copy-done.12) | copy-start | bytes 1966084
  47.7 1.1 %copy-start.16 = (bf16[512,640]{1,0:T(8,128)(2,1)S(1)}, bf16[512,640]{1,0:T(8,128)(2,1)}, u32[]{:S(2)}) copy-start(bf16[512,640]{1,0:T(8,128)(2,1)} %copy-done.15) | copy-start | bytes 1966084
  50.8 1.1 %copy-start.2 = (f32[512,640]{1,0:T(8,128)}, f32[512,640]{1,0:T(8,128)S(1)}, u32[]{:S(2)}) copy-start(f32[512,640]{1,0:T(8,128)S(1)} %get-tuple-element.62.refs_2_) | copy-start | bytes 3932164
  51.8 1.1 %copy-start.4 = (f32[512,640]{1,0:T(8,128)}, f32[512,640]{1,0:T(8,128)S(1)}, u32[]{:S(2)}) copy-start(f32[512,640]{1,0:T(8,128)S(1)} %get-tuple-element.63.refs_3_) | copy-start | bytes 3932164
  53.9 7.2 %collective-permute-start.9 = (bf16[64,1280]{1,0:T(8,128)(2,1)S(1)}, bf16[64,1280]{1,0:T(8,128)(2,1)}, u32[]{:S(2)}, u32[]{:S(2)}) collective-permute-start(bf16[64,1280]{1,0:T(8,128)(2,1)S(1)} %broadcast_select_fusion.3), channel_id=1, source_target_pairs={{0,6},{1,3},{2,4},{7,5},{8,14},{9,11},{10,12},{15,13},{16,22},{17,... | collective-permute-start | bytes 491528 | tf_op jit(solution)/shard_map/ppermute | solution.py:116
  55.8 1.1 %copy-start.8 = (bf16[512,640]{1,0:T(8,128)(2,1)S(1)}, bf16[512,640]{1,0:T(8,128)(2,1)}, u32[]{:S(2)}) copy-start(bf16[512,640]{1,0:T(8,128)(2,1)} %copy-done.6) | copy-start | bytes 1966084
  56.9 1.1 %copy-start.14 = (bf16[512,640]{1,0:T(8,128)(2,1)S(1)}, bf16[512,640]{1,0:T(8,128)(2,1)}, u32[]{:S(2)}) copy-start(bf16[512,640]{1,0:T(8,128)(2,1)} %copy-done.12) | copy-start | bytes 1966084
  58.0 1.1 %copy-start.17 = (bf16[512,640]{1,0:T(8,128)(2,1)S(1)}, bf16[512,640]{1,0:T(8,128)(2,1)}, u32[]{:S(2)}) copy-start(bf16[512,640]{1,0:T(8,128)(2,1)} %copy-done.15) | copy-start | bytes 1966084
  59.1 16.3 %copy-start.3 = (f32[512,640]{1,0:T(8,128)S(1)}, f32[512,640]{1,0:T(8,128)}, u32[]{:S(2)}) copy-start(f32[512,640]{1,0:T(8,128)} %copy-done.2) | copy-start | bytes 3932164
  59.1 16.3 %copy-start.5 = (f32[512,640]{1,0:T(8,128)S(1)}, f32[512,640]{1,0:T(8,128)}, u32[]{:S(2)}) copy-start(f32[512,640]{1,0:T(8,128)} %copy-done.4) | copy-start | bytes 3932164
  61.0 14.3 %copy-start.9 = (bf16[512,640]{1,0:T(8,128)(2,1)S(1)}, bf16[512,640]{1,0:T(8,128)(2,1)}, u32[]{:S(2)}) copy-start(bf16[512,640]{1,0:T(8,128)(2,1)} %copy-done.6) | copy-start | bytes 1966084
  61.1 4.3 %collective-permute-start.10 = (bf16[64,1280]{1,0:T(8,128)(2,1)S(1)}, bf16[64,1280]{1,0:T(8,128)(2,1)S(1)}, u32[]{:S(2)}, u32[]{:S(2)}) collective-permute-start(bf16[64,1280]{1,0:T(8,128)(2,1)S(1)} %broadcast_select_fusion.4), channel_id=1, source_target_pairs={{0,96},{1,33},{2,98},{3,35},{4,100},{5,37},{6,102},{7,39},{8,104},... | collective-permute-start | bytes 491528 | tf_op jit(solution)/shard_map/ppermute | solution.py:296
  65.3 16.1 %copy-start.21 = (f32[1280]{0:T(1024)S(1)}, f32[1280]{0:T(1024)}, u32[]{:S(2)}) copy-start(f32[1280]{0:T(1024)} %param.15) | copy-start | bytes 15364
  65.4 10.0 %collective-permute-start.12 = (bf16[128,1280]{1,0:T(8,128)(2,1)S(1)}, bf16[128,1280]{1,0:T(8,128)(2,1)S(1)}, u32[]{:S(2)}, u32[]{:S(2)}) collective-permute-start(bf16[128,1280]{1,0:T(8,128)(2,1)S(1)} %constant_dynamic-update-slice_fusion.refs_0_), channel_id=1, source_target_pairs={{0,1},{1,0},{2,3},{3,2},{4,5},{5,4},{6,7},{7,6},{8,9},{9,8},{10,11... | collective-permute-start | bytes 983048 | tf_op jit(solution)/shard_map/ppermute | solution.py:298
  74.1 7.1 %collective-permute-start.11 = (bf16[128,1280]{1,0:T(8,128)(2,1)S(1)}, bf16[128,1280]{1,0:T(8,128)(2,1)S(1)}, u32[]{:S(2)}, u32[]{:S(2)}) collective-permute-start(bf16[128,1280]{1,0:T(8,128)(2,1)S(1)} %constant_dynamic-update-slice_fusion.refs_0_), channel_id=1, source_target_pairs={{0,32},{1,97},{2,34},{3,99},{4,36},{5,101},{6,38},{7,103},{8,40},{... | collective-permute-start | bytes 983048 | tf_op jit(solution)/shard_map/ppermute | solution.py:299
  81.2 3.3 %collective-permute-start.13 = (bf16[128,1280]{1,0:T(8,128)(2,1)S(1)}, bf16[128,1280]{1,0:T(8,128)(2,1)S(1)}, u32[]{:S(2)}, u32[]{:S(2)}) collective-permute-start(bf16[128,1280]{1,0:T(8,128)(2,1)S(1)} %collective-permute-done.11.refs_0_), channel_id=1, source_target_pairs={{0,1},{1,0},{2,3},{3,2},{4,5},{5,4},{6,7},{7,6},{8,9},{9,8},{10,11... | collective-permute-start | bytes 983048 | tf_op jit(solution)/shard_map/ppermute | solution.py:302
  81.4 3.1 %copy-start.10 = (bf16[640,1280]{1,0:T(8,128)(2,1)S(1)}, bf16[640,1280]{1,0:T(8,128)(2,1)}, u32[]{:S(2)}) copy-start(bf16[640,1280]{1,0:T(8,128)(2,1)} %refs_6_.1) | copy-start | bytes 4915204

commit v5 on v4

v5 whole, which is shorter than its diff:
```python
import functools

import jax
import jax.numpy as jnp
from jax import lax
from jax.experimental import pallas as pl
from jax.experimental.pallas import tpu as pltpu
from jax.sharding import PartitionSpec as P

HEADS = 10
HEAD_DIM = 64
PAIR = 2 * HEAD_DIM
GROUPS = ((0,), (1, 2), (3, 4))
OUT_TILE = 256
VMEM_BYTES = 16 << 20
AXES = ("grp", "frame")


SIZES = {"x": 4, "y": 4, "z": 8}

STEPS = {
    4: (((0, 1),), ((0, 3), (1, 2))),
    8: (((0, 3),), ((0, 6), (3, 4)), ((0, 1), (3, 2), (4, 5), (6, 7))),
}
ORDER = "zzzyy"


def device_index(place, core):
    if core == 1:
        place = {n: -v % SIZES[n] for n, v in place.items()}
    x, y, z = place["x"], place["y"], place["z"]
    return ((z // 4) * 4 + x) * 32 + ((z % 4) * 4 + y) * 2 + core


def tree():
    held = {"x": list(range(4)), "y": [0], "z": [0]}
    taken = {name: 0 for name in "xyz"}
    rounds = []
    for axis in ORDER:
        step = STEPS[SIZES[axis]][taken[axis]]
        taken[axis] += 1
        pairs = []
        for core in range(2):
            for x in held["x"]:
                for y in held["y"]:
                    for z in held["z"]:
                        place = {"x": x, "y": y, "z": z}
                        for source, sink in step:
                            if place[axis] == source:
                                pairs.append(
                                    (
                                        device_index(place, core),
                                        device_index({**place, axis: sink}, core),
                                    )
                                )
        before = {name: sum(1 << v for v in nodes) for name, nodes in held.items()}
        rounds.append((sorted(pairs), before))
        held[axis] = held[axis] + [sink for _, sink in step]
    assert all(len(held[name]) == SIZES[name] for name in "xyz")
    return rounds


def exchange(step):
    pairs = []
    for core in range(2):
        for y in range(4):
            for z in range(8):
                for a, b in (((0, 1), (2, 3)), ((0, 3), (1, 2)))[step]:
                    ends = [device_index({"x": v, "y": y, "z": z}, core) for v in (a, b)]
                    pairs += [(ends[0], ends[1]), (ends[1], ends[0])]
    return sorted(pairs)


CORE_SWAP = [(i, i ^ 1) for i in range(256)]
NEXT_FRAME = [(i, (i + 1) % 256) for i in range(256)]


def holding():
    grp, frame = lax.axis_index("grp"), lax.axis_index("frame")
    second = frame % 2 == 1
    place = {"x": grp % 4, "y": frame // 2 % 4, "z": grp // 4 * 4 + frame // 8}
    return second, {n: jnp.where(second, (SIZES[n] - v) % SIZES[n], v) for n, v in place.items()}


def flags(width):
    second, place = holding()
    answers = [
        jnp.where(second, 1, 0),
        jnp.where(lax.axis_index("grp") + lax.axis_index("frame") == 0, 1, 0),
        place["x"] % 2,
        place["x"] // 2,
    ]
    for _, before in tree():
        inside = [(before[n] >> place[n]) & 1 for n in "xyz"]
        answers.append(inside[0] * inside[1] * inside[2])
    bits = sum(answer << i for i, answer in enumerate(answers)).astype(jnp.int32)
    return jnp.full((8, width), bits)


def along_x(x):
    return [[device_index({"x": v, "y": 0, "z": 0}, core) for v in (0, x)] for core in range(2)]


def choose(bits_ref, index, yes, no):
    flag = (bits_ref[:1, :] >> index) & 1 == 1
    return jnp.where(flag, yes.astype(jnp.float32), no.astype(jnp.float32))


def split_kernel(bits_ref, rows_ref, other_ref, *refs):
    parts, token_ref = refs[:4], refs[4]
    size = parts[0].shape[0]
    for i, part in enumerate(parts):
        place = pl.ds(i * size, size)
        there = pl.ds((4 + i) * size, size)
        part[...] = choose(bits_ref, 0, other_ref[there, :], rows_ref[place, :]).astype(jnp.bfloat16)
    token_ref[...] = bits_ref[...]


def pick_kernel(bits_ref, zero_ref, one_ref, two_ref, three_ref, out_ref, token_ref):
    low = choose(bits_ref, 2, one_ref[...], zero_ref[...])
    high = choose(bits_ref, 2, three_ref[...], two_ref[...])
    out_ref[...] = choose(bits_ref, 3, high, low).astype(jnp.bfloat16)
    token_ref[...] = bits_ref[...]


def merge_kernel(bits_ref, piece_ref, come_ref, out_ref, token_ref, *, step):
    piece = choose(bits_ref, 4 + step, piece_ref[...], come_ref[...])
    out_ref[...] = piece.astype(jnp.bfloat16)
    token_ref[...] = bits_ref[...]


def pass_kernel(bits_ref, piece_ref, out_ref, token_ref):
    out_ref[...] = piece_ref[...]
    token_ref[...] = bits_ref[...]


def join_kernel(bits_ref, piece_ref, come_ref, out_ref, token_ref):
    out_ref[: piece_ref.shape[0], :] = piece_ref[...]
    out_ref[piece_ref.shape[0] :, :] = come_ref[...]
    token_ref[...] = bits_ref[...]


def normed(rows, gain, bias):
    values = rows.astype(jnp.float32)
    center = jnp.mean(values, axis=-1, keepdims=True)
    values = values - center
    spread = jnp.mean(values * values, axis=-1, keepdims=True)
    return (values * lax.rsqrt(spread + 1e-05) * gain + bias).astype(jnp.bfloat16)


def project(rows, weight):
    return jnp.dot(rows, weight, preferred_element_type=jnp.float32)


def lanes_of(rows):
    return lax.broadcasted_iota(jnp.int32, (rows, PAIR), 1)


def columns(index):
    return slice(index * PAIR, (index + 1) * PAIR)


def own_lanes(head, array, fill):
    left = lanes_of(array.shape[0]) < HEAD_DIM
    other = jnp.full(array.shape, fill, jnp.bfloat16)
    return jnp.where(left, array, other) if head % 2 == 0 else jnp.where(left, other, array)


def attend(head, query, key, value, carried=None):
    scores = lax.dot_general(
        query, own_lanes(head, key, 0.0), (((1,), (1,)), ((), ())),
        preferred_element_type=jnp.float32,
    )
    tiles = [scores[:, i : i + PAIR] for i in range(0, scores.shape[1], PAIR)]
    top = functools.reduce(jnp.maximum, tiles)
    top = jnp.broadcast_to(jnp.max(top, axis=-1, keepdims=True), top.shape)
    if carried is not None:
        top = jnp.maximum(top, carried[1])
    raised = [jnp.exp(tile - top).astype(jnp.bfloat16) for tile in tiles]
    total = project(jnp.concatenate(raised, axis=1), own_lanes(head, value, 1.0))
    if carried is not None:
        total = total + carried[0] * jnp.exp(carried[1] - top)
    return total, top


def query_kernel(bits_ref, rows_ref, gain_ref, bias_ref, weight_ref, out_ref, token_ref):
    rows = normed(rows_ref[...], gain_ref[...], bias_ref[...])
    query = project(rows, weight_ref[...]).astype(jnp.bfloat16)
    out_ref[...] = query * jnp.bfloat16(HEAD_DIM ** (-0.5))
    token_ref[...] = bits_ref[...]


def prior_kernel(*refs, pairs):
    if pairs == GROUPS[0]:
        bits_ref, rows_ref, own_ref, gain_ref, bias_ref = refs[:5]
        rows = choose(bits_ref, 1, own_ref[...], rows_ref[...])
        rows = normed(rows, gain_ref[...], bias_ref[...])
        refs[-2][...] = rows
        query_ref, key_ref, value_ref, sum_ref, top_ref = refs[5:10]
    else:
        bits_ref, rows_ref, query_ref, key_ref, value_ref, sum_ref, top_ref = refs[:7]
        rows = rows_ref[...]
    lanes = slice(pairs[0] * PAIR, (pairs[-1] + 1) * PAIR)
    keys = project(rows, key_ref[:, lanes]).astype(jnp.bfloat16)
    values = project(rows, value_ref[:, lanes]).astype(jnp.bfloat16)
    for place, head in enumerate(range(2 * pairs[0], 2 * pairs[-1] + 2)):
        pair = columns(place // 2)
        sum_ref[:, columns(place)], top_ref[:, columns(place)] = attend(
            head, query_ref[:, columns(head // 2)], keys[:, pair], values[:, pair]
        )
    refs[-1][...] = bits_ref[...]


def state(refs, head):
    for group, pairs in enumerate(GROUPS):
        if head // 2 in pairs:
            place = columns(head - 2 * pairs[0])
            return refs[2 * group].at[:, place], refs[2 * group + 1].at[:, place]


def own_context(rows_refs, gain_ref, bias_ref, key_ref, value_ref):
    rows = [ref[...] for ref in rows_refs]
    rows = rows[0] if len(rows) == 1 else jnp.concatenate(rows, axis=0)
    rows = normed(rows, gain_ref[...], bias_ref[...])
    keys = project(rows, key_ref[...]).astype(jnp.bfloat16)
    values = project(rows, value_ref[...]).astype(jnp.bfloat16)
    return keys, values


def more_kernel(bits_ref, query_ref, gain_ref, bias_ref, key_ref, value_ref, *refs):
    *refs, token_ref = refs
    size = 2 * len(GROUPS)
    rows, carried, out = refs[: -2 * size], refs[-2 * size : -size], refs[-size:]
    token_ref[...] = bits_ref[...]
    keys, values = own_context(rows, gain_ref, bias_ref, key_ref, value_ref)
    for head in range(HEADS):
        pair = columns(head // 2)
        before = [ref[...] for ref in state(carried, head)]
        sum_ref, top_ref = state(out, head)
        sum_ref[...], top_ref[...] = attend(
            head, query_ref[:, pair], keys[:, pair], values[:, pair], before
        )


def last_kernel(query_ref, gain_ref, bias_ref, key_ref, value_ref, *refs):
    rows, carried = refs[: -5 - 2 * len(GROUPS)], refs[-5 - 2 * len(GROUPS) : -5]
    hidden_ref, out_weight_ref, out_bias_ref, out_ref, mixed_ref = refs[-5:]
    keys, values = own_context(rows, gain_ref, bias_ref, key_ref, value_ref)
    left = lanes_of(query_ref.shape[0]) < HEAD_DIM
    for pair in range(HEADS // 2):
        place = columns(pair)
        even, odd = (
            attend(
                head, query_ref[:, place], keys[:, place], values[:, place],
                [ref[...] for ref in state(carried, head)],
            )[0]
            for head in (2 * pair, 2 * pair + 1)
        )
        weight = pltpu.roll(jnp.where(left, odd, even), HEAD_DIM, 1)
        mixed_ref[:, place] = (jnp.where(left, even, odd) / weight).astype(jnp.bfloat16)
    for start in range(0, out_ref.shape[1], OUT_TILE):
        tile = slice(start, start + OUT_TILE)
        total = project(mixed_ref[...], out_weight_ref[:, tile])
        total = hidden_ref[:, tile].astype(jnp.float32) + total + out_bias_ref[:, tile]
        out_ref[:, tile] = total.astype(jnp.bfloat16)


def call(kernel, outs, *operands, flops=0, exps=0, aliases=None, scratch=(), token=True):
    whole = pl.BlockSpec(memory_space=pltpu.VMEM)
    outs = tuple(outs)
    if token:
        outs += (jax.ShapeDtypeStruct(operands[0].shape, operands[0].dtype),)
    return pl.pallas_call(
        kernel,
        out_shape=outs,
        in_specs=[whole] * len(operands),
        out_specs=(whole,) * len(outs),
        scratch_shapes=scratch,
        input_output_aliases=aliases or {},
        compiler_params=pltpu.CompilerParams(vmem_limit_bytes=VMEM_BYTES),
        cost_estimate=pl.CostEstimate(flops=flops, bytes_accessed=1 << 18, transcendentals=exps),
    )(*operands)


def body(hidden_states, norm_gain, norm_bias, w_query, w_key, w_value, w_out, out_bias):
    norm = (norm_gain.reshape(1, -1), norm_bias.reshape(1, -1))
    tokens, width = hidden_states.shape
    inner = w_query.shape[1]
    quarter = tokens // 8
    bits = flags(width)
    rounds = tree()

    def rows_of(count):
        return jax.ShapeDtypeStruct((count, width), jnp.bfloat16)

    shifted = lax.ppermute(hidden_states, AXES, NEXT_FRAME)
    other = lax.ppermute(hidden_states, AXES, CORE_SWAP)
    *parts, bits = call(split_kernel, [rows_of(quarter)] * 4, bits, hidden_states, other)
    for x in (1, 3, 2):
        parts[x] = lax.ppermute(parts[x], AXES, along_x(x))
    query, bits = call(
        query_kernel, [jax.ShapeDtypeStruct((tokens, inner), jnp.bfloat16)],
        bits, hidden_states, *norm, w_query, flops=2 * tokens * width * inner,
    )
    piece, bits = call(pick_kernel, [rows_of(quarter)], bits, *parts)

    held = []
    for step, (pairs, _) in enumerate(rounds):
        come = lax.ppermute(piece, AXES, pairs)
        group = step - len(rounds) + len(GROUPS)
        if group >= 0:
            size = 2 * len(GROUPS[group])
            outs = [jax.ShapeDtypeStruct((tokens, size * PAIR), jnp.float32)] * 2
            rows = [shifted, hidden_states, *norm]
            if group > 0:
                rows = [prior]
            sum_, top, *made, bits = call(
                functools.partial(prior_kernel, pairs=GROUPS[group]),
                outs + [rows_of(tokens)] * (group == 0),
                bits, *rows, query, w_key, w_value,
                flops=4 * size * tokens * tokens * PAIR, exps=size * tokens * tokens,
            )
            held += [sum_, top]
            prior = made[0] if made else prior
        piece, bits = call(
            functools.partial(merge_kernel, step=step), [rows_of(quarter)], bits, piece, come
        )

    def more(bits, rows, held):
        *held, bits = call(
            more_kernel, [jax.ShapeDtypeStruct(h.shape, h.dtype) for h in held],
            bits, query, *norm, w_key, w_value, *rows, *held,
            aliases={6 + len(rows) + i: i for i in range(len(held))}, flops=4 * tokens * width * inner,
        )
        return held, bits

    come = lax.ppermute(piece, AXES, exchange(1))
    early, bits = call(join_kernel, [rows_of(2 * quarter)], bits, piece, come)
    early_other = lax.ppermute(early, AXES, CORE_SWAP)
    late = lax.ppermute(early, AXES, exchange(0))
    held, bits = more(bits, [early, early_other], held)
    late, bits = call(pass_kernel, [rows_of(2 * quarter)], bits, late)
    late_other = lax.ppermute(late, AXES, CORE_SWAP)
    held, bits = more(bits, [late], held)
    (out,) = call(
        last_kernel, [rows_of(tokens)],
        query, *norm, w_key, w_value, late_other, *held, hidden_states, w_out,
        out_bias.reshape(1, -1),
        flops=4 * tokens * width * inner, scratch=[pltpu.VMEM((tokens, inner), jnp.bfloat16)],
        token=False,
    )
    return out


def solution(mesh):
    placed = (P(AXES, None), P(), P(), P(), P(), P(), P(), P())
    return jax.shard_map(
        body, mesh=mesh, in_specs=placed, out_specs=P(AXES, None), check_vma=False
    )
```

time: 91.5 us -> 65.3 us (0.71)
  the two profiles are of different devices: /device:TPU:1 before, /device:TPU:177 now
where the time goes in v5:
time: 65.3 us; the launch traced here: 65 us
  Pallas kernels  22.5 us (34%)
  waiting for transfers between devices  19.8 us (30%)
  starting transfers between devices  19.7 us (30%)
  local copies, waits for them, and re-layouts  2.79 us (4%)
    pallas_call x16, Pallas kernels, call(): pl.pallas_call(kernel, out_shape=outs, in_specs=[whole] * len(operands),...  22.5 us
    ppermute x5, waiting for transfers between devices, body(): come = lax.ppermute(piece, AXES, pairs)  10.6 us
    ppermute x1, starting transfers between devices, body(): early_other = lax.ppermute(early, AXES, CORE_SWAP)  7.93 us
    ppermute x5, starting transfers between devices, body(): come = lax.ppermute(piece, AXES, pairs)  3.98 us
    ppermute x1, waiting for transfers between devices, body(): shifted = lax.ppermute(hidden_states, AXES, NEXT_FRAME)  3.6 us
    ppermute x1, waiting for transfers between devices, body(): come = lax.ppermute(piece, AXES, exchange(1))  3.26 us
    unnamed x18, local copies, waits for them, and re-layouts  2.77 us
    ppermute x1, starting transfers between devices, body(): late = lax.ppermute(early, AXES, exchange(0))  2.47 us
  transfers between devices with their start and end apart: 14, of which 5 were waited for; matrix products, arithmetic and copies ran while one was open for 0% of the time, Pallas kernels for 27%

profile of v5, /device:TPU:177, one launch (start us, length us, event | category | flops | bytes accessed | tf_op | source)
XLA Modules:
  0.0 65.0 jit_solution(15427255444223276331)
XLA Ops:
  0.0 0.7 %collective-permute-start = (bf16[512,1280]{1,0:T(8,128)(2,1)}, bf16[512,1280]{1,0:T(8,128)(2,1)S(1)}, u32[]{:S(2)}, u32[]{:S(2)}) collective-permute-start(bf16[512,1280]{1,0:T(8,128)(2,1)} %refs_7_.3), channel_id=1, source_target_pairs={{0,1},{1,0},{2,3},{3,2},{4,5},{5,4},{6,7},{7,6},{8,9},{9,8},{10,11... | collective-permute-start | bytes 3932168 | tf_op jit(solution)/shard_map/ppermute | solution.py:297
  0.7 0.9 %collective-permute-start.6 = (bf16[512,1280]{1,0:T(8,128)(2,1)}, bf16[512,1280]{1,0:T(8,128)(2,1)S(1)}, u32[]{:S(2)}, u32[]{:S(2)}) collective-permute-start(bf16[512,1280]{1,0:T(8,128)(2,1)} %refs_7_.3), channel_id=1, source_target_pairs={{0,1},{1,2},{2,3},{3,4},{4,5},{5,6},{6,7},{7,8},{8,9},{9,10},{10,1... | collective-permute-start | bytes 3932168 | tf_op jit(solution)/shard_map/ppermute | solution.py:296
  1.6 2.0 %collective-permute-done.other_ref = bf16[512,1280]{1,0:T(8,128)(2,1)S(1)} collective-permute-done((bf16[512,1280]{1,0:T(8,128)(2,1)}, bf16[512,1280]{1,0:T(8,128)(2,1)S(1)}, u32[]{:S(2)}, u32[]{:S(2)}) %collective-permute-start) | collective-permute-done | bytes 1310752 | tf_op jit(solution)/shard_map/ppermute | solution.py:297
  3.6 0.0 copy-start.2
  3.6 1.3 %copy-done.2 = bf16[512,1280]{1,0:T(8,128)(2,1)S(1)} copy-done((bf16[512,1280]{1,0:T(8,128)(2,1)S(1)}, bf16[512,1280]{1,0:T(8,128)(2,1)}, u32[]{:S(2)}) %copy-start.2) | copy-done | bytes 1310744
  4.9 0.0 copy-start.6
  4.9 0.0 copy-start.7
  4.9 0.0 copy-start.3
  4.9 0.2 shard_map.82
  5.0 0.8 %collective-permute-start.1 = (bf16[64,1280]{1,0:T(8,128)(2,1)S(1)}, bf16[64,1280]{1,0:T(8,128)(2,1)S(1)}, u32[]{:S(2)}, u32[]{:S(2)}) collective-permute-start(bf16[64,1280]{1,0:T(8,128)(2,1)S(1)} %get-tuple-element.55), channel_id=1, source_target_pairs={{0,32},{1,97}} | collective-permute-start | bytes 491528 | tf_op jit(solution)/shard_map/ppermute | solution.py:300
  5.8 0.7 %collective-permute-start.2 = (bf16[64,1280]{1,0:T(8,128)(2,1)S(1)}, bf16[64,1280]{1,0:T(8,128)(2,1)S(1)}, u32[]{:S(2)}, u32[]{:S(2)}) collective-permute-start(bf16[64,1280]{1,0:T(8,128)(2,1)S(1)} %get-tuple-element.56), channel_id=1, source_target_pairs={{0,64},{1,65}} | collective-permute-start | bytes 491528 | tf_op jit(solution)/shard_map/ppermute | solution.py:300
  6.5 0.7 %collective-permute-start.3 = (bf16[64,1280]{1,0:T(8,128)(2,1)S(1)}, bf16[64,1280]{1,0:T(8,128)(2,1)S(1)}, u32[]{:S(2)}, u32[]{:S(2)}) collective-permute-start(bf16[64,1280]{1,0:T(8,128)(2,1)S(1)} %get-tuple-element.57), channel_id=1, source_target_pairs={{0,96},{1,33}} | collective-permute-start | bytes 491528 | tf_op jit(solution)/shard_map/ppermute | solution.py:300
  7.2 0.0 copy-done.6
  7.2 0.0 copy-done.7
  7.3 0.0 copy-done.3
  7.3 0.0 copy-start.5
  7.3 1.4 %copy-done.5 = bf16[1280,640]{1,0:T(8,128)(2,1)S(1)} copy-done((bf16[1280,640]{1,0:T(8,128)(2,1)S(1)}, bf16[1280,640]{1,0:T(8,128)(2,1)}, u32[]{:S(2)}) %copy-start.5) | copy-done | bytes 1638424
  8.7 0.0 copy-start
  8.7 0.0 copy-start.1
  8.7 1.8 %shard_map.83 = (bf16[512,640]{1,0:T(8,128)(2,1)S(1)}, s32[8,1280]{1,0:T(8,128)S(1)}) custom-call(s32[8,1280]{1,0:T(8,128)S(1)} %get-tuple-element.51.bits_ref, bf16[512,1280]{1,0:T(8,128)(2,1)S(1)} %copy-done.3, f32[1,1280]{1,0:T(1,128)S(1)} %reshape.9.gain_ref.refs_3_, f32[1,1280]{1,0:T(1,128)S(1)} %reshape.10.bias_ref.refs_4_, bf16[1280,640]{1,0:T(8,128)(2,1)S(1)} %copy-done.5), custom_call_target="tpu_custom_call" | custom-call | flops 838860800 | bytes 262144 | tf_op jit(solution)/shard_map/pallas_call | solution.py:273
  10.5 0.0 collective-permute-done.1.one_ref
  10.5 0.0 collective-permute-done.2.two_ref
  10.5 0.0 collective-permute-done.3.three_ref
  10.6 0.1 shard_map.84
  10.7 0.7 %collective-permute-start.4 = (bf16[64,1280]{1,0:T(8,128)(2,1)S(1)}, bf16[64,1280]{1,0:T(8,128)(2,1)S(1)}, u32[]{:S(2)}, u32[]{:S(2)}) collective-permute-start(bf16[64,1280]{1,0:T(8,128)(2,1)S(1)} %get-tuple-element.59.piece_ref), channel_id=1, source_target_pairs={{0,24},{1,137},{32,56},{33,169},{64,88},{65,201},{96,120},{97,233}} | collective-permute-start | bytes 491528 | tf_op jit(solution)/shard_map/ppermute | solution.py:309
  11.3 0.0 collective-permute-done.4.come_ref
  11.4 0.7 %collective-permute-start.5 = (bf16[64,1280]{1,0:T(8,128)(2,1)S(1)}, bf16[64,1280]{1,0:T(8,128)(2,1)S(1)}, u32[]{:S(2)}, u32[]{:S(2)}) collective-permute-start(bf16[64,1280]{1,0:T(8,128)(2,1)S(1)} %get-tuple-element.61.piece_ref), channel_id=1, source_target_pairs={{0,144},{1,17},{24,128},{32,176},{33,49},{56,160},{64,208},{65,81}... | collective-permute-start | bytes 491528 | tf_op jit(solution)/shard_map/ppermute | solution.py:309
  12.1 0.0 collective-permute-done.5.come_ref
  12.2 0.7 %collective-permute-start.7 = (bf16[64,1280]{1,0:T(8,128)(2,1)S(1)}, bf16[64,1280]{1,0:T(8,128)(2,1)S(1)}, u32[]{:S(2)}, u32[]{:S(2)}) collective-permute-start(bf16[64,1280]{1,0:T(8,128)(2,1)S(1)} %get-tuple-element.64.piece_ref), channel_id=1, source_target_pairs={{0,8},{1,153},{17,9},{24,16},{32,40},{33,185},{49,41},{56,48},{64,... | collective-permute-start | bytes 491528 | tf_op jit(solution)/shard_map/ppermute | solution.py:309
  12.8 3.6 %collective-permute-done.6.refs_1_ = bf16[512,1280]{1,0:T(8,128)(2,1)S(1)} collective-permute-done((bf16[512,1280]{1,0:T(8,128)(2,1)}, bf16[512,1280]{1,0:T(8,128)(2,1)S(1)}, u32[]{:S(2)}, u32[]{:S(2)}) %collective-permute-start.6) | collective-permute-done | bytes 1310752 | tf_op jit(solution)/shard_map/ppermute | solution.py:296
  16.4 0.0 copy-done
  16.4 0.0 copy-done.1
  16.4 2.5 %shard_map.87 = (f32[512,256]{1,0:T(8,128)S(1)}, f32[512,256]{1,0:T(8,128)S(1)}, bf16[512,1280]{1,0:T(8,128)(2,1)S(1)}, s32[8,1280]{1,0:T(8,128)S(1)}) custom-call(s32[8,1280]{1,0:T(8,128)S(1)} %get-tuple-element.62.refs_0_, bf16[512,1280]{1,0:T(8,128)(2,1)S(1)} %collective-permute-done.6.refs_1_, bf16[512,1280]{1,0:T(8,128)(2,1)S(1)} %copy-done.3, ...), custom_call_target="tpu_custom_call" | custom-call | flops 268435456 | bytes 262144 | tf_op jit(solution)/shard_map/pallas_call | solution.py:273
  19.0 0.0 collective-permute-done.7.come_ref
  19.0 0.7 %collective-permute-start.8 = (bf16[64,1280]{1,0:T(8,128)(2,1)S(1)}, bf16[64,1280]{1,0:T(8,128)(2,1)S(1)}, u32[]{:S(2)}, u32[]{:S(2)}) collective-permute-start(bf16[64,1280]{1,0:T(8,128)(2,1)S(1)} %get-tuple-element.68.piece_ref), channel_id=1, source_target_pairs={{0,2},{1,7},{8,10},{9,15},{16,18},{17,23},{24,26},{25,31},{32,34},... | collective-permute-start | bytes 491528 | tf_op jit(solution)/shard_map/ppermute | solution.py:309
  19.7 2.3 %shard_map.89 = (f32[512,512]{1,0:T(8,128)S(1)}, f32[512,512]{1,0:T(8,128)S(1)}, s32[8,1280]{1,0:T(8,128)S(1)}) custom-call(s32[8,1280]{1,0:T(8,128)S(1)} %get-tuple-element.65.refs_0_, bf16[512,1280]{1,0:T(8,128)(2,1)S(1)} %get-tuple-element.66.refs_1_, bf16[512,640]{1,0:T(8,128)(2,1)S(1)} %get-tuple-element.52.refs_5_.refs_2_.query_ref, ...), custom_call_target="tpu_custom_call" | custom-call | flops 536870912 | bytes 262144 | tf_op jit(solution)/shard_map/pallas_call | solution.py:273
  22.0 0.0 collective-permute-done.8.come_ref
  22.1 1.3 %collective-permute-start.9 = (bf16[64,1280]{1,0:T(8,128)(2,1)S(1)}, bf16[64,1280]{1,0:T(8,128)(2,1)S(1)}, u32[]{:S(2)}, u32[]{:S(2)}) collective-permute-start(bf16[64,1280]{1,0:T(8,128)(2,1)S(1)} %get-tuple-element.71.piece_ref), channel_id=1, source_target_pairs={{0,6},{1,3},{2,4},{7,5},{8,14},{9,11},{10,12},{15,13},{16,22},{17,... | collective-permute-start | bytes 491528 | tf_op jit(solution)/shard_map/ppermute | solution.py:309
  23.4 2.3 %shard_map.91 = (f32[512,512]{1,0:T(8,128)S(1)}, f32[512,512]{1,0:T(8,128)S(1)}, s32[8,1280]{1,0:T(8,128)S(1)}) custom-call(s32[8,1280]{1,0:T(8,128)S(1)} %get-tuple-element.69.refs_0_, bf16[512,1280]{1,0:T(8,128)(2,1)S(1)} %get-tuple-element.66.refs_1_, bf16[512,640]{1,0:T(8,128)(2,1)S(1)} %get-tuple-element.52.refs_5_.refs_2_.query_ref, ...), custom_call_target="tpu_custom_call" | custom-call | flops 536870912 | bytes 262144 | tf_op jit(solution)/shard_map/pallas_call | solution.py:273
  25.7 10.5 %collective-permute-done.9.come_ref = bf16[64,1280]{1,0:T(8,128)(2,1)S(1)} collective-permute-done((bf16[64,1280]{1,0:T(8,128)(2,1)S(1)}, bf16[64,1280]{1,0:T(8,128)(2,1)S(1)}, u32[]{:S(2)}, u32[]{:S(2)}) %collective-permute-start.9) | collective-permute-done | bytes 163872 | tf_op jit(solution)/shard_map/ppermute | solution.py:309
  36.3 1.3 %collective-permute-start.10 = (bf16[64,1280]{1,0:T(8,128)(2,1)S(1)}, bf16[64,1280]{1,0:T(8,128)(2,1)S(1)}, u32[]{:S(2)}, u32[]{:S(2)}) collective-permute-start(bf16[64,1280]{1,0:T(8,128)(2,1)S(1)} %get-tuple-element.73.piece_ref), channel_id=1, source_target_pairs={{0,96},{1,33},{2,98},{3,35},{4,100},{5,37},{6,102},{7,39},{8,104},... | collective-permute-start | bytes 491528 | tf_op jit(solution)/shard_map/ppermute | solution.py:337
  37.6 3.3 %collective-permute-done.10.come_ref = bf16[64,1280]{1,0:T(8,128)(2,1)S(1)} collective-permute-done((bf16[64,1280]{1,0:T(8,128)(2,1)S(1)}, bf16[64,1280]{1,0:T(8,128)(2,1)S(1)}, u32[]{:S(2)}, u32[]{:S(2)}) %collective-permute-start.10) | collective-permute-done | bytes 163872 | tf_op jit(solution)/shard_map/ppermute | solution.py:337
  40.9 7.9 %collective-permute-start.11 = (bf16[128,1280]{1,0:T(8,128)(2,1)S(1)}, bf16[128,1280]{1,0:T(8,128)(2,1)S(1)}, u32[]{:S(2)}, u32[]{:S(2)}) collective-permute-start(bf16[128,1280]{1,0:T(8,128)(2,1)S(1)} %get-tuple-element.75.refs_0_), channel_id=1, source_target_pairs={{0,1},{1,0},{2,3},{3,2},{4,5},{5,4},{6,7},{7,6},{8,9},{9,8},{10,11... | collective-permute-start | bytes 983048 | tf_op jit(solution)/shard_map/ppermute | solution.py:339
  48.8 2.5 %collective-permute-start.12 = (bf16[128,1280]{1,0:T(8,128)(2,1)S(1)}, bf16[128,1280]{1,0:T(8,128)(2,1)S(1)}, u32[]{:S(2)}, u32[]{:S(2)}) collective-permute-start(bf16[128,1280]{1,0:T(8,128)(2,1)S(1)} %get-tuple-element.75.refs_0_), channel_id=1, source_target_pairs={{0,32},{1,97},{2,34},{3,99},{4,36},{5,101},{6,38},{7,103},{8,40},{... | collective-permute-start | bytes 983048 | tf_op jit(solution)/shard_map/ppermute | solution.py:340
  51.3 0.0 collective-permute-done.11.refs_1_
  51.3 0.0 copy-start.8
  51.3 4.3 %shard_map.94 = (f32[512,256]{1,0:T(8,128)S(1)}, f32[512,256]{1,0:T(8,128)S(1)}, f32[512,512]{1,0:T(8,128)S(1)}, f32[512,512]{1,0:T(8,128)S(1)}, f32[512,512]{1,...) custom-call(s32[8,1280]{1,0:T(8,128)S(1)} %get-tuple-element.74.bits, ...), custom_call_target="tpu_custom_call", output_to_operand_aliasing={{0}: (8, {}), {1}: (9, {}), {2}: (10, {}), {3}: (11, {}), {... | custom-call | flops 1677721600 | bytes 262144 | tf_op jit(solution)/shard_map/pallas_call | solution.py:273
  55.6 0.4 collective-permute-done.12.piece_ref
  56.0 0.3 collective-permute-start.13
  56.3 0.0 copy-done.8
  56.3 0.0 copy-start.4
  56.3 3.7 %shard_map.96 = (f32[512,256]{1,0:T(8,128)S(1)}, f32[512,256]{1,0:T(8,128)S(1)}, f32[512,512]{1,0:T(8,128)S(1)}, f32[512,512]{1,0:T(8,128)S(1)}, f32[512,512]{1,...) custom-call(s32[8,1280]{1,0:T(8,128)S(1)} %get-tuple-element.84.bits, ...), custom_call_target="tpu_custom_call", output_to_operand_aliasing={{0}: (7, {}), {1}: (8, {}), {2}: (9, {}), {3}: (10, {}), {4... | custom-call | flops 1677721600 | bytes 262144 | tf_op jit(solution)/shard_map/pallas_call | solution.py:273
  60.0 0.0 collective-permute-done.13.refs_0_
  60.0 0.0 copy-done.4
  60.0 5.0 %shard_map.97 = bf16[512,1280]{1,0:T(8,128)(2,1)} custom-call(bf16[512,640]{1,0:T(8,128)(2,1)S(1)} %get-tuple-element.52.refs_5_.refs_2_.query_ref, f32[1,1280]{1,0:T(1,128)S(1)} %reshape.9.gain_ref.refs_3_, f32[1,1280]{1,0:T(1,128)S(1)} %reshape.10.bias_ref.refs_4_, bf16[1280,640]{1,0:T(8,128)(2,1)S(1)} %copy-done, bf16[1280,640]{1,0:T(8,128)(2,1)S(1)} %copy-done.1, ...), custom_call_target="tpu_custom_call" | custom-call | flops 1677721600 | bytes 262144 | tf_op jit(solution)/shard_map/pallas_call | solution.py:273
  (11 shorter events, 0.3 us)
Async XLA Ops:
  0.0 3.5 %collective-permute-start = (bf16[512,1280]{1,0:T(8,128)(2,1)}, bf16[512,1280]{1,0:T(8,128)(2,1)S(1)}, u32[]{:S(2)}, u32[]{:S(2)}) collective-permute-start(bf16[512,1280]{1,0:T(8,128)(2,1)} %refs_7_.3), channel_id=1, source_target_pairs={{0,1},{1,0},{2,3},{3,2},{4,5},{5,4},{6,7},{7,6},{8,9},{9,8},{10,11... | collective-permute-start | bytes 3932168 | tf_op jit(solution)/shard_map/ppermute | solution.py:297
  0.7 15.8 %collective-permute-start.6 = (bf16[512,1280]{1,0:T(8,128)(2,1)}, bf16[512,1280]{1,0:T(8,128)(2,1)S(1)}, u32[]{:S(2)}, u32[]{:S(2)}) collective-permute-start(bf16[512,1280]{1,0:T(8,128)(2,1)} %refs_7_.3), channel_id=1, source_target_pairs={{0,1},{1,2},{2,3},{3,4},{4,5},{5,6},{6,7},{7,8},{8,9},{9,10},{10,1... | collective-permute-start | bytes 3932168 | tf_op jit(solution)/shard_map/ppermute | solution.py:296
  3.6 1.3 %copy-start.2 = (bf16[512,1280]{1,0:T(8,128)(2,1)S(1)}, bf16[512,1280]{1,0:T(8,128)(2,1)}, u32[]{:S(2)}) copy-start(bf16[512,1280]{1,0:T(8,128)(2,1)} %refs_7_.3) | copy-start | bytes 3932164
  4.9 2.3 %copy-start.6 = (f32[1280]{0:T(1024)S(1)}, f32[1280]{0:T(1024)}, u32[]{:S(2)}) copy-start(f32[1280]{0:T(1024)} %param.10) | copy-start | bytes 15364
  4.9 2.4 %copy-start.7 = (f32[1280]{0:T(1024)S(1)}, f32[1280]{0:T(1024)}, u32[]{:S(2)}) copy-start(f32[1280]{0:T(1024)} %param.9) | copy-start | bytes 15364
  4.9 2.4 %copy-start.3 = (bf16[512,1280]{1,0:T(8,128)(2,1)S(1)}, bf16[512,1280]{1,0:T(8,128)(2,1)}, u32[]{:S(2)}) copy-start(bf16[512,1280]{1,0:T(8,128)(2,1)} %refs_7_.3) | copy-start | bytes 3932164
  5.0 5.5 %collective-permute-start.1 = (bf16[64,1280]{1,0:T(8,128)(2,1)S(1)}, bf16[64,1280]{1,0:T(8,128)(2,1)S(1)}, u32[]{:S(2)}, u32[]{:S(2)}) collective-permute-start(bf16[64,1280]{1,0:T(8,128)(2,1)S(1)} %get-tuple-element.55), channel_id=1, source_target_pairs={{0,32},{1,97}} | collective-permute-start | bytes 491528 | tf_op jit(solution)/shard_map/ppermute | solution.py:300
  5.8 4.7 %collective-permute-start.2 = (bf16[64,1280]{1,0:T(8,128)(2,1)S(1)}, bf16[64,1280]{1,0:T(8,128)(2,1)S(1)}, u32[]{:S(2)}, u32[]{:S(2)}) collective-permute-start(bf16[64,1280]{1,0:T(8,128)(2,1)S(1)} %get-tuple-element.56), channel_id=1, source_target_pairs={{0,64},{1,65}} | collective-permute-start | bytes 491528 | tf_op jit(solution)/shard_map/ppermute | solution.py:300
  6.5 4.0 %collective-permute-start.3 = (bf16[64,1280]{1,0:T(8,128)(2,1)S(1)}, bf16[64,1280]{1,0:T(8,128)(2,1)S(1)}, u32[]{:S(2)}, u32[]{:S(2)}) collective-permute-start(bf16[64,1280]{1,0:T(8,128)(2,1)S(1)} %get-tuple-element.57), channel_id=1, source_target_pairs={{0,96},{1,33}} | collective-permute-start | bytes 491528 | tf_op jit(solution)/shard_map/ppermute | solution.py:300
  7.3 1.4 %copy-start.5 = (bf16[1280,640]{1,0:T(8,128)(2,1)S(1)}, bf16[1280,640]{1,0:T(8,128)(2,1)}, u32[]{:S(2)}) copy-start(bf16[1280,640]{1,0:T(8,128)(2,1)} %weight_ref.1) | copy-start | bytes 4915204
  8.7 7.7 %copy-start = (bf16[1280,640]{1,0:T(8,128)(2,1)S(1)}, bf16[1280,640]{1,0:T(8,128)(2,1)}, u32[]{:S(2)}) copy-start(bf16[1280,640]{1,0:T(8,128)(2,1)} %key_ref.5) | copy-start | bytes 4915204
  8.7 7.7 %copy-start.1 = (bf16[1280,640]{1,0:T(8,128)(2,1)S(1)}, bf16[1280,640]{1,0:T(8,128)(2,1)}, u32[]{:S(2)}) copy-start(bf16[1280,640]{1,0:T(8,128)(2,1)} %value_ref.5) | copy-start | bytes 4915204
  10.7 0.7 %collective-permute-start.4 = (bf16[64,1280]{1,0:T(8,128)(2,1)S(1)}, bf16[64,1280]{1,0:T(8,128)(2,1)S(1)}, u32[]{:S(2)}, u32[]{:S(2)}) collective-permute-start(bf16[64,1280]{1,0:T(8,128)(2,1)S(1)} %get-tuple-element.59.piece_ref), channel_id=1, source_target_pairs={{0,24},{1,137},{32,56},{33,169},{64,88},{65,201},{96,120},{97,233}} | collective-permute-start | bytes 491528 | tf_op jit(solution)/shard_map/ppermute | solution.py:309
  11.4 0.7 %collective-permute-start.5 = (bf16[64,1280]{1,0:T(8,128)(2,1)S(1)}, bf16[64,1280]{1,0:T(8,128)(2,1)S(1)}, u32[]{:S(2)}, u32[]{:S(2)}) collective-permute-start(bf16[64,1280]{1,0:T(8,128)(2,1)S(1)} %get-tuple-element.61.piece_ref), channel_id=1, source_target_pairs={{0,144},{1,17},{24,128},{32,176},{33,49},{56,160},{64,208},{65,81}... | collective-permute-start | bytes 491528 | tf_op jit(solution)/shard_map/ppermute | solution.py:309
  12.2 6.8 %collective-permute-start.7 = (bf16[64,1280]{1,0:T(8,128)(2,1)S(1)}, bf16[64,1280]{1,0:T(8,128)(2,1)S(1)}, u32[]{:S(2)}, u32[]{:S(2)}) collective-permute-start(bf16[64,1280]{1,0:T(8,128)(2,1)S(1)} %get-tuple-element.64.piece_ref), channel_id=1, source_target_pairs={{0,8},{1,153},{17,9},{24,16},{32,40},{33,185},{49,41},{56,48},{64,... | collective-permute-start | bytes 491528 | tf_op jit(solution)/shard_map/ppermute | solution.py:309
  19.0 3.0 %collective-permute-start.8 = (bf16[64,1280]{1,0:T(8,128)(2,1)S(1)}, bf16[64,1280]{1,0:T(8,128)(2,1)S(1)}, u32[]{:S(2)}, u32[]{:S(2)}) collective-permute-start(bf16[64,1280]{1,0:T(8,128)(2,1)S(1)} %get-tuple-element.68.piece_ref), channel_id=1, source_target_pairs={{0,2},{1,7},{8,10},{9,15},{16,18},{17,23},{24,26},{25,31},{32,34},... | collective-permute-start | bytes 491528 | tf_op jit(solution)/shard_map/ppermute | solution.py:309
  22.1 14.2 %collective-permute-start.9 = (bf16[64,1280]{1,0:T(8,128)(2,1)S(1)}, bf16[64,1280]{1,0:T(8,128)(2,1)S(1)}, u32[]{:S(2)}, u32[]{:S(2)}) collective-permute-start(bf16[64,1280]{1,0:T(8,128)(2,1)S(1)} %get-tuple-element.71.piece_ref), channel_id=1, source_target_pairs={{0,6},{1,3},{2,4},{7,5},{8,14},{9,11},{10,12},{15,13},{16,22},{17,... | collective-permute-start | bytes 491528 | tf_op jit(solution)/shard_map/ppermute | solution.py:309
  36.3 4.6 %collective-permute-start.10 = (bf16[64,1280]{1,0:T(8,128)(2,1)S(1)}, bf16[64,1280]{1,0:T(8,128)(2,1)S(1)}, u32[]{:S(2)}, u32[]{:S(2)}) collective-permute-start(bf16[64,1280]{1,0:T(8,128)(2,1)S(1)} %get-tuple-element.73.piece_ref), channel_id=1, source_target_pairs={{0,96},{1,33},{2,98},{3,35},{4,100},{5,37},{6,102},{7,39},{8,104},... | collective-permute-start | bytes 491528 | tf_op jit(solution)/shard_map/ppermute | solution.py:337
  40.9 10.4 %collective-permute-start.11 = (bf16[128,1280]{1,0:T(8,128)(2,1)S(1)}, bf16[128,1280]{1,0:T(8,128)(2,1)S(1)}, u32[]{:S(2)}, u32[]{:S(2)}) collective-permute-start(bf16[128,1280]{1,0:T(8,128)(2,1)S(1)} %get-tuple-element.75.refs_0_), channel_id=1, source_target_pairs={{0,1},{1,0},{2,3},{3,2},{4,5},{5,4},{6,7},{7,6},{8,9},{9,8},{10,11... | collective-permute-start | bytes 983048 | tf_op jit(solution)/shard_map/ppermute | solution.py:339
  48.8 7.1 %collective-permute-start.12 = (bf16[128,1280]{1,0:T(8,128)(2,1)S(1)}, bf16[128,1280]{1,0:T(8,128)(2,1)S(1)}, u32[]{:S(2)}, u32[]{:S(2)}) collective-permute-start(bf16[128,1280]{1,0:T(8,128)(2,1)S(1)} %get-tuple-element.75.refs_0_), channel_id=1, source_target_pairs={{0,32},{1,97},{2,34},{3,99},{4,36},{5,101},{6,38},{7,103},{8,40},{... | collective-permute-start | bytes 983048 | tf_op jit(solution)/shard_map/ppermute | solution.py:340
  51.3 5.0 %copy-start.8 = (f32[1280]{0:T(1024)S(1)}, f32[1280]{0:T(1024)}, u32[]{:S(2)}) copy-start(f32[1280]{0:T(1024)} %param.15) | copy-start | bytes 15364
  56.0 4.0 %collective-permute-start.13 = (bf16[128,1280]{1,0:T(8,128)(2,1)S(1)}, bf16[128,1280]{1,0:T(8,128)(2,1)S(1)}, u32[]{:S(2)}, u32[]{:S(2)}) collective-permute-start(bf16[128,1280]{1,0:T(8,128)(2,1)S(1)} %get-tuple-element.83.refs_0_), channel_id=1, source_target_pairs={{0,1},{1,0},{2,3},{3,2},{4,5},{5,4},{6,7},{7,6},{8,9},{9,8},{10,11... | collective-permute-start | bytes 983048 | tf_op jit(solution)/shard_map/ppermute | solution.py:343
  56.3 3.7 %copy-start.4 = (bf16[640,1280]{1,0:T(8,128)(2,1)S(1)}, bf16[640,1280]{1,0:T(8,128)(2,1)}, u32[]{:S(2)}) copy-start(bf16[640,1280]{1,0:T(8,128)(2,1)} %refs_8_.1) | copy-start | bytes 4915204

commit v6 on v5

v6 whole, which is shorter than its diff:
```python
import functools

import jax
import jax.numpy as jnp
from jax import lax
from jax.experimental import pallas as pl
from jax.experimental.pallas import tpu as pltpu
from jax.sharding import PartitionSpec as P

HEADS = 10
HEAD_DIM = 64
PAIR = 2 * HEAD_DIM
GROUPS = ((0,), (1, 2), (3, 4))
OUT_TILE = 256
VMEM_BYTES = 16 << 20
AXES = ("grp", "frame")


SIZES = {"x": 4, "y": 4, "z": 8}

FIRST, SECOND = ((0, 1),), ((0, 3), (1, 2))
ROUNDS = (
    ({"x": FIRST}, {"y": FIRST}, {"x": FIRST, "y": FIRST}),
    ({"x": SECOND}, {"z": ((0, 3),)}, {"x": SECOND, "z": ((0, 3),)}),
    ({"y": SECOND}, {"z": ((0, 6), (3, 4))}, {"y": SECOND, "z": ((0, 6), (3, 4))}),
    ({"z": ((0, 1), (3, 2), (4, 5), (6, 7))},),
)


def device_index(place, core):
    if core == 1:
        place = {n: -v % SIZES[n] for n, v in place.items()}
    x, y, z = place["x"], place["y"], place["z"]
    return ((z // 4) * 4 + x) * 32 + ((z % 4) * 4 + y) * 2 + core


def chips():
    return [{"x": x, "y": y, "z": z} for x in range(4) for y in range(4) for z in range(8)]


def plan():
    held = {name: [0] for name in "xyz"}
    rounds = []
    for sends in ROUNDS:
        made = []
        for send in sends:
            pairs = []
            for chip in chips():
                moves = {n: dict(send[n]) for n in send}
                if all(chip[n] in held[n] for n in "xyz") and all(chip[n] in moves[n] for n in send):
                    sink = {**chip, **{n: moves[n][chip[n]] for n in send}}
                    pairs += [(device_index(chip, c), device_index(sink, c)) for c in range(2)]
            sinks = {n: [to for _, to in send[n]] if n in send else held[n] for n in "xyz"}
            made.append((sorted(pairs), {n: sum(1 << v for v in sinks[n]) for n in "xyz"}))
        for send in sends:
            held = {
                n: sorted(set(held[n]) | {to for _, to in send.get(n, ())}) for n in "xyz"
            }
        rounds.append(made)
    assert all(len(held[n]) == SIZES[n] for n in "xyz")
    return rounds


def exchange(axis):
    pairs = []
    for chip in chips():
        other = {**chip, axis: chip[axis] ^ 1}
        pairs += [(device_index(chip, core), device_index(other, core)) for core in range(2)]
    return sorted(pairs)


CORE_SWAP = [(i, i ^ 1) for i in range(256)]
NEXT_FRAME = [(i, (i + 1) % 256) for i in range(256)]


def flags(rounds, width):
    grp, frame = lax.axis_index("grp"), lax.axis_index("frame")
    second = frame % 2
    place = {"x": grp % 4, "y": frame // 2 % 4, "z": grp // 4 * 4 + frame // 8}
    place = {n: jnp.where(second == 1, (SIZES[n] - v) % SIZES[n], v) for n, v in place.items()}
    bits = second + jnp.where(grp + frame == 0, 2, 0)
    for step, sends in enumerate(rounds):
        for which, (_, sinks) in enumerate(sends):
            inside = [(sinks[n] >> place[n]) & 1 for n in "xyz"]
            bits += (inside[0] * inside[1] * inside[2] * (which + 1)) << (2 + 2 * step)
    return jnp.full((8, width), bits.astype(jnp.int32))


def choose(bits_ref, index, yes, no):
    flag = (bits_ref[:1, :] >> index) & 1 == 1
    return jnp.where(flag, yes.astype(jnp.float32), no.astype(jnp.float32))


def low_kernel(bits_ref, rows_ref, low_ref, token_ref):
    low_ref[...] = rows_ref[: low_ref.shape[0], :]
    token_ref[...] = bits_ref[...]


def split_kernel(bits_ref, rows_ref, other_ref, *refs):
    *parts, token_ref = refs
    size = parts[0].shape[0]
    for i, part in enumerate(parts):
        place, there = pl.ds(i * size, size), pl.ds((4 + i) * size, size)
        part[...] = choose(bits_ref, 0, other_ref[there, :], rows_ref[place, :]).astype(jnp.bfloat16)
    token_ref[...] = bits_ref[...]


def pick_kernel(bits_ref, *refs, step, count):
    parts, outs, token_ref = refs[:count], refs[count:-1], refs[-1]
    piece = choose(bits_ref, 2 + 2 * step, parts[1][...], parts[0][...])
    if count == 4:
        high = choose(bits_ref, 2 + 2 * step, parts[3][...], parts[2][...])
        piece = choose(bits_ref, 3 + 2 * step, high, piece)
    piece = piece.astype(jnp.bfloat16)
    size = outs[0].shape[0]
    for i, out in enumerate(outs):
        out[...] = piece[i * size : (i + 1) * size, :]
    token_ref[...] = bits_ref[...]


def join_kernel(bits_ref, *refs, count, each):
    parts, outs, token_ref = refs[:count], refs[count:-1], refs[-1]
    start = 0
    for i, part in enumerate(parts):
        rows = part.shape[0]
        outs[0][start : start + rows, :] = part[...]
        start += rows
        if each:
            outs[1 + i // 2][i % 2 * rows : (i % 2 + 1) * rows, :] = part[...]
    token_ref[...] = bits_ref[...]


def normed(rows, gain, bias):
    values = rows.astype(jnp.float32)
    center = jnp.mean(values, axis=-1, keepdims=True)
    values = values - center
    spread = jnp.mean(values * values, axis=-1, keepdims=True)
    return (values * lax.rsqrt(spread + 1e-05) * gain + bias).astype(jnp.bfloat16)


def project(rows, weight):
    return jnp.dot(rows, weight, preferred_element_type=jnp.float32)


def lanes_of(rows):
    return lax.broadcasted_iota(jnp.int32, (rows, PAIR), 1)


def columns(index):
    return slice(index * PAIR, (index + 1) * PAIR)


def own_lanes(head, array, fill):
    left = lanes_of(array.shape[0]) < HEAD_DIM
    other = jnp.full(array.shape, fill, jnp.bfloat16)
    return jnp.where(left, array, other) if head % 2 == 0 else jnp.where(left, other, array)


def attend(head, query, key, value, carried=None):
    scores = lax.dot_general(
        query, own_lanes(head, key, 0.0), (((1,), (1,)), ((), ())),
        preferred_element_type=jnp.float32,
    )
    tiles = [scores[:, i : i + PAIR] for i in range(0, scores.shape[1], PAIR)]
    top = functools.reduce(jnp.maximum, tiles)
    top = jnp.broadcast_to(jnp.max(top, axis=-1, keepdims=True), top.shape)
    if carried is not None:
        top = jnp.maximum(top, carried[1])
    raised = [jnp.exp(tile - top).astype(jnp.bfloat16) for tile in tiles]
    total = project(jnp.concatenate(raised, axis=1), own_lanes(head, value, 1.0))
    if carried is not None:
        total = total + carried[0] * jnp.exp(carried[1] - top)
    return total, top


def query_kernel(bits_ref, rows_ref, gain_ref, bias_ref, weight_ref, out_ref, token_ref):
    rows = normed(rows_ref[...], gain_ref[...], bias_ref[...])
    query = project(rows, weight_ref[...]).astype(jnp.bfloat16)
    out_ref[...] = query * jnp.bfloat16(HEAD_DIM ** (-0.5))
    token_ref[...] = bits_ref[...]


def prior_kernel(*refs, pairs):
    if pairs == GROUPS[0]:
        bits_ref, rows_ref, own_ref, gain_ref, bias_ref = refs[:5]
        rows = choose(bits_ref, 1, own_ref[...], rows_ref[...])
        rows = normed(rows, gain_ref[...], bias_ref[...])
        refs[-2][...] = rows
        query_ref, key_ref, value_ref, sum_ref, top_ref = refs[5:10]
    else:
        bits_ref, rows_ref, query_ref, key_ref, value_ref, sum_ref, top_ref = refs[:7]
        rows = rows_ref[...]
    lanes = slice(pairs[0] * PAIR, (pairs[-1] + 1) * PAIR)
    keys = project(rows, key_ref[:, lanes]).astype(jnp.bfloat16)
    values = project(rows, value_ref[:, lanes]).astype(jnp.bfloat16)
    for place, head in enumerate(range(2 * pairs[0], 2 * pairs[-1] + 2)):
        pair = columns(place // 2)
        sum_ref[:, columns(place)], top_ref[:, columns(place)] = attend(
            head, query_ref[:, columns(head // 2)], keys[:, pair], values[:, pair]
        )
    refs[-1][...] = bits_ref[...]


def state(refs, head):
    for group, pairs in enumerate(GROUPS):
        if head // 2 in pairs:
            place = columns(head - 2 * pairs[0])
            return refs[2 * group].at[:, place], refs[2 * group + 1].at[:, place]


def context(rows_refs, gain_ref, bias_ref, key_ref, value_ref):
    rows = [ref[...] for ref in rows_refs]
    rows = rows[0] if len(rows) == 1 else jnp.concatenate(rows, axis=0)
    rows = normed(rows, gain_ref[...], bias_ref[...])
    keys = project(rows, key_ref[...]).astype(jnp.bfloat16)
    values = project(rows, value_ref[...]).astype(jnp.bfloat16)
    return keys, values


def context_kernel(
    bits_ref, rows_ref, gain_ref, bias_ref, key_ref, value_ref, keys_ref, values_ref, token_ref
):
    keys_ref[...], values_ref[...] = context([rows_ref], gain_ref, bias_ref, key_ref, value_ref)
    token_ref[...] = bits_ref[...]


def more_kernel(bits_ref, query_ref, gain_ref, bias_ref, key_ref, value_ref, *refs):
    *refs, token_ref = refs
    size = 2 * len(GROUPS)
    rows, carried, out = refs[: -2 * size], refs[-2 * size : -size], refs[-size:]
    keys, values = context(rows, gain_ref, bias_ref, key_ref, value_ref)
    for head in range(HEADS):
        pair = columns(head // 2)
        before = [ref[...] for ref in state(carried, head)]
        sum_ref, top_ref = state(out, head)
        sum_ref[...], top_ref[...] = attend(
            head, query_ref[:, pair], keys[:, pair], values[:, pair], before
        )
    token_ref[...] = bits_ref[...]


def last_kernel(
    bits_ref, query_ref, gain_ref, bias_ref, key_ref, value_ref, rows_ref, keys_ref, values_ref,
    hidden_ref, out_weight_ref, out_bias_ref, *refs,
):
    *carried, out_ref, mixed_ref = refs
    keys, values = context([rows_ref], gain_ref, bias_ref, key_ref, value_ref)
    keys = jnp.concatenate([keys_ref[...], keys], axis=0)
    values = jnp.concatenate([values_ref[...], values], axis=0)
    left = lanes_of(query_ref.shape[0]) < HEAD_DIM
    for pair in range(HEADS // 2):
        place = columns(pair)
        even, odd = (
            attend(
                head, query_ref[:, place], keys[:, place], values[:, place],
                [ref[...] for ref in state(carried, head)],
            )[0]
            for head in (2 * pair, 2 * pair + 1)
        )
        weight = pltpu.roll(jnp.where(left, odd, even), HEAD_DIM, 1)
        mixed_ref[:, place] = (jnp.where(left, even, odd) / weight).astype(jnp.bfloat16)
    for start in range(0, out_ref.shape[1], OUT_TILE):
        tile = slice(start, start + OUT_TILE)
        total = project(mixed_ref[...], out_weight_ref[:, tile])
        total = hidden_ref[:, tile].astype(jnp.float32) + total + out_bias_ref[:, tile]
        out_ref[:, tile] = total.astype(jnp.bfloat16)


def call(kernel, outs, *operands, flops=0, exps=0, aliases=None, scratch=(), token=True):
    whole = pl.BlockSpec(memory_space=pltpu.VMEM)
    outs = tuple(outs)
    if token:
        outs += (jax.ShapeDtypeStruct(operands[0].shape, operands[0].dtype),)
    return pl.pallas_call(
        kernel,
        out_shape=outs,
        in_specs=[whole] * len(operands),
        out_specs=(whole,) * len(outs),
        scratch_shapes=scratch,
        input_output_aliases=aliases or {},
        compiler_params=pltpu.CompilerParams(vmem_limit_bytes=VMEM_BYTES),
        cost_estimate=pl.CostEstimate(flops=flops, bytes_accessed=1 << 18, transcendentals=exps),
    )(*operands)


def body(hidden_states, norm_gain, norm_bias, w_query, w_key, w_value, w_out, out_bias):
    norm = (norm_gain.reshape(1, -1), norm_bias.reshape(1, -1))
    tokens, width = hidden_states.shape
    inner = w_query.shape[1]
    rounds = plan()
    bits = flags(rounds, width)

    def array(rows, columns=width, dtype=jnp.bfloat16):
        return jax.ShapeDtypeStruct((rows, columns), dtype)

    def move(value, pairs):
        return lax.ppermute(value, AXES, pairs)

    def prior(bits, group, rows):
        size = 2 * len(GROUPS[group])
        return call(
            functools.partial(prior_kernel, pairs=GROUPS[group]),
            [array(tokens, size * PAIR, jnp.float32)] * 2 + [array(tokens)] * (group == 0),
            bits, *rows, query, w_key, w_value,
            flops=4 * size * tokens * tokens * PAIR, exps=size * tokens * tokens,
        )

    shifted = move(hidden_states, NEXT_FRAME)
    other = move(hidden_states, CORE_SWAP)
    low, bits = call(low_kernel, [array(tokens // 2)], bits, hidden_states)
    *parts, bits = call(split_kernel, [array(tokens // 8)] * 4, bits, low, other)
    for step, sends in enumerate(rounds):
        come = [move(parts[which + 1 if step == 0 else 0], sent[0]) for which, sent in enumerate(sends)]
        if step == 0:
            query, bits = call(
                query_kernel, [array(tokens, inner)], bits, hidden_states, *norm, w_query,
                flops=2 * tokens * width * inner,
            )
        if step == 2:
            *held, rows, bits = prior(bits, 0, [shifted, hidden_states, *norm])
        if step == 3:
            *sums, bits = prior(bits, 1, [rows])
            held += sums
        outs = 2 if step == len(rounds) - 1 else 1
        *parts, bits = call(
            functools.partial(pick_kernel, step=step, count=1 + len(sends)),
            [array(tokens // 8 // outs)] * outs, bits, parts[0], *come,
        )

    first, second = parts
    first_come, second_come = move(first, exchange("x")), move(second, exchange("y"))
    *sums, bits = prior(bits, 2, [rows])
    held += sums
    early, first, second, bits = call(
        functools.partial(join_kernel, count=4, each=True),
        [array(tokens // 4), array(tokens // 8), array(tokens // 8)],
        bits, first, first_come, second, second_come,
    )
    first_come, second_come = move(first, exchange("y")), move(second, exchange("x"))
    early_other = move(early, CORE_SWAP)
    *held, bits = call(
        more_kernel, [jax.ShapeDtypeStruct(h.shape, h.dtype) for h in held],
        bits, query, *norm, w_key, w_value, early, early_other, *held,
        aliases={8 + i: i for i in range(len(held))}, flops=4 * tokens * width * inner,
    )
    late, bits = call(
        functools.partial(join_kernel, count=2, each=False), [array(tokens // 4)],
        bits, first_come, second_come,
    )
    late_other = move(late, CORE_SWAP)
    keys, values, bits = call(
        context_kernel, [array(tokens // 4, inner)] * 2, bits, late, *norm, w_key, w_value,
        flops=tokens * width * inner,
    )
    (out,) = call(
        last_kernel, [array(tokens)],
        bits, query, *norm, w_key, w_value, late_other, keys, values,
        hidden_states, w_out, out_bias.reshape(1, -1), *held,
        flops=4 * tokens * width * inner, scratch=[pltpu.VMEM((tokens, inner), jnp.bfloat16)],
        token=False,
    )
    return out


def solution(mesh):
    placed = (P(AXES, None), P(), P(), P(), P(), P(), P(), P())
    return jax.shard_map(
        body, mesh=mesh, in_specs=placed, out_specs=P(AXES, None), check_vma=False
    )
```

time: 65.3 us -> 58 us (0.89)
  the two profiles are of different devices: /device:TPU:177 before, /device:TPU:1 now
where the time goes in v6:
time: 58 us; the launch traced here: 57.7 us
  starting transfers between devices  29.6 us (51%)
  Pallas kernels  21.4 us (37%)
  waiting for transfers between devices  4.87 us (8%)
  local copies, waits for them, and re-layouts  1.4 us (2%)
    ppermute x18, starting transfers between devices, move(): return lax.ppermute(value, AXES, pairs)  29.6 us
    pallas_call x15, Pallas kernels, call(): pl.pallas_call(kernel, out_shape=outs, in_specs=[whole] * len(operands),...  21.4 us
    ppermute x18, waiting for transfers between devices, move(): return lax.ppermute(value, AXES, pairs)  4.87 us
    unnamed x18, local copies, waits for them, and re-layouts  1.39 us
  transfers between devices with their start and end apart: 18, of which 5 were waited for; matrix products, arithmetic and copies ran while one was open for 0% of the time, Pallas kernels for 25%

profile of v6, /device:TPU:1, one launch (start us, length us, event | category | flops | bytes accessed | tf_op | source)
XLA Modules:
  0.0 57.7 jit_solution(7027077119972287743)
XLA Ops:
  0.0 3.2 %collective-permute-start = (bf16[512,1280]{1,0:T(8,128)(2,1)}, bf16[512,1280]{1,0:T(8,128)(2,1)S(1)}, u32[]{:S(2)}, u32[]{:S(2)}) collective-permute-start(bf16[512,1280]{1,0:T(8,128)(2,1)} %hidden_ref.1), channel_id=1, source_target_pairs={{0,1},{1,0},{2,3},{3,2},{4,5},{5,4},{6,7},{7,6},{8,9},{9,8},{10,11... | collective-permute-start | bytes 3932168 | tf_op jit(solution)/shard_map/ppermute | solution.py:297
  3.2 0.0 collective-permute-start.7
  3.2 0.0 copy-start.2
  3.3 1.3 %copy-done.2 = bf16[512,1280]{1,0:T(8,128)(2,1)S(1)} copy-done((bf16[512,1280]{1,0:T(8,128)(2,1)S(1)}, bf16[512,1280]{1,0:T(8,128)(2,1)}, u32[]{:S(2)}) %copy-start.2) | copy-done | bytes 1310744
  4.6 0.0 copy-start.5
  4.6 0.0 copy-start.6
  4.7 0.0 copy-start.7
  4.7 0.0 copy-start.3
  4.7 1.4 %collective-permute-done.other_ref = bf16[512,1280]{1,0:T(8,128)(2,1)S(1)} collective-permute-done((bf16[512,1280]{1,0:T(8,128)(2,1)}, bf16[512,1280]{1,0:T(8,128)(2,1)S(1)}, u32[]{:S(2)}, u32[]{:S(2)}) %collective-permute-start) | collective-permute-done | bytes 1310752 | tf_op jit(solution)/shard_map/ppermute | solution.py:297
  6.1 0.2 shard_map.83
  6.3 2.8 %collective-permute-start.1 = (bf16[64,1280]{1,0:T(8,128)(2,1)S(1)}, bf16[64,1280]{1,0:T(8,128)(2,1)S(1)}, u32[]{:S(2)}, u32[]{:S(2)}) collective-permute-start(bf16[64,1280]{1,0:T(8,128)(2,1)S(1)} %get-tuple-element.54), channel_id=1, source_target_pairs={{0,32},{1,97}} | collective-permute-start | bytes 491528 | tf_op jit(solution)/shard_map/ppermute | solution.py:297
  9.1 1.3 %collective-permute-start.2 = (bf16[64,1280]{1,0:T(8,128)(2,1)S(1)}, bf16[64,1280]{1,0:T(8,128)(2,1)S(1)}, u32[]{:S(2)}, u32[]{:S(2)}) collective-permute-start(bf16[64,1280]{1,0:T(8,128)(2,1)S(1)} %get-tuple-element.55), channel_id=1, source_target_pairs={{0,2},{1,7}} | collective-permute-start | bytes 491528 | tf_op jit(solution)/shard_map/ppermute | solution.py:297
  10.4 2.5 %collective-permute-start.3 = (bf16[64,1280]{1,0:T(8,128)(2,1)S(1)}, bf16[64,1280]{1,0:T(8,128)(2,1)S(1)}, u32[]{:S(2)}, u32[]{:S(2)}) collective-permute-start(bf16[64,1280]{1,0:T(8,128)(2,1)S(1)} %get-tuple-element.56), channel_id=1, source_target_pairs={{0,34},{1,103}} | collective-permute-start | bytes 491528 | tf_op jit(solution)/shard_map/ppermute | solution.py:297
  12.9 0.0 copy-done.6
  12.9 0.0 copy-done.7
  12.9 0.0 copy-done.5
  12.9 0.0 copy-done.3
  12.9 0.0 copy-start
  13.0 0.0 copy-start.1
  13.0 1.8 %shard_map.84 = (bf16[512,640]{1,0:T(8,128)(2,1)S(1)}, s32[8,1280]{1,0:T(8,128)S(1)}) custom-call(s32[8,1280]{1,0:T(8,128)S(1)} %get-tuple-element.51.bits_ref, bf16[512,1280]{1,0:T(8,128)(2,1)S(1)} %copy-done.3, f32[1,1280]{1,0:T(1,128)S(1)} %reshape.9.gain_ref.refs_3_, f32[1,1280]{1,0:T(1,128)S(1)} %reshape.10.bias_ref.refs_4_, bf16[1280,640]{1,0:T(8,128)(2,1)S(1)} %copy-done.5), custom_call_target="tpu_custom_call" | custom-call | flops 838860800 | bytes 262144 | tf_op jit(solution)/shard_map/pallas_call | solution.py:274
  14.8 0.0 collective-permute-done.1.refs_1_
  14.8 0.0 collective-permute-done.2.refs_2_
  14.8 0.3 collective-permute-done.3.refs_3_
  15.1 0.1 shard_map.85
  15.2 1.3 %collective-permute-start.4 = (bf16[64,1280]{1,0:T(8,128)(2,1)S(1)}, bf16[64,1280]{1,0:T(8,128)(2,1)S(1)}, u32[]{:S(2)}, u32[]{:S(2)}) collective-permute-start(bf16[64,1280]{1,0:T(8,128)(2,1)S(1)} %get-tuple-element.58.refs_0_), channel_id=1, source_target_pairs={{0,96},{1,33},{2,98},{7,39},{32,64},{34,66},{97,65},{103,71}} | collective-permute-start | bytes 491528 | tf_op jit(solution)/shard_map/ppermute | solution.py:297
  16.5 1.3 %collective-permute-start.5 = (bf16[64,1280]{1,0:T(8,128)(2,1)S(1)}, bf16[64,1280]{1,0:T(8,128)(2,1)S(1)}, u32[]{:S(2)}, u32[]{:S(2)}) collective-permute-start(bf16[64,1280]{1,0:T(8,128)(2,1)S(1)} %get-tuple-element.58.refs_0_), channel_id=1, source_target_pairs={{0,24},{1,137},{2,26},{7,143},{32,56},{34,58},{97,233},{103,239}} | collective-permute-start | bytes 491528 | tf_op jit(solution)/shard_map/ppermute | solution.py:297
  17.8 1.6 %collective-permute-start.6 = (bf16[64,1280]{1,0:T(8,128)(2,1)S(1)}, bf16[64,1280]{1,0:T(8,128)(2,1)S(1)}, u32[]{:S(2)}, u32[]{:S(2)}) collective-permute-start(bf16[64,1280]{1,0:T(8,128)(2,1)S(1)} %get-tuple-element.58.refs_0_), channel_id=1, source_target_pairs={{0,120},{1,169},{2,122},{7,175},{32,88},{34,90},{97,201},{103,207}} | collective-permute-start | bytes 491528 | tf_op jit(solution)/shard_map/ppermute | solution.py:297
  19.4 0.0 collective-permute-done.4.refs_1_
  19.4 0.6 %collective-permute-done.5.refs_2_ = bf16[64,1280]{1,0:T(8,128)(2,1)S(1)} collective-permute-done((bf16[64,1280]{1,0:T(8,128)(2,1)S(1)}, bf16[64,1280]{1,0:T(8,128)(2,1)S(1)}, u32[]{:S(2)}, u32[]{:S(2)}) %collective-permute-start.5) | collective-permute-done | bytes 163872 | tf_op jit(solution)/shard_map/ppermute | solution.py:297
  20.1 1.8 %collective-permute-done.6.refs_3_ = bf16[64,1280]{1,0:T(8,128)(2,1)S(1)} collective-permute-done((bf16[64,1280]{1,0:T(8,128)(2,1)S(1)}, bf16[64,1280]{1,0:T(8,128)(2,1)S(1)}, u32[]{:S(2)}, u32[]{:S(2)}) %collective-permute-start.6) | collective-permute-done | bytes 163872 | tf_op jit(solution)/shard_map/ppermute | solution.py:297
  21.8 0.1 shard_map.86
  21.9 1.3 %collective-permute-start.10 = (bf16[64,1280]{1,0:T(8,128)(2,1)S(1)}, bf16[64,1280]{1,0:T(8,128)(2,1)S(1)}, u32[]{:S(2)}, u32[]{:S(2)}) collective-permute-start(bf16[64,1280]{1,0:T(8,128)(2,1)S(1)} %get-tuple-element.62.refs_0_), channel_id=1, source_target_pairs={{0,150},{1,19},{2,148},{7,21},{24,134},{26,132},{32,182},{33,51},{... | collective-permute-start | bytes 491528 | tf_op jit(solution)/shard_map/ppermute | solution.py:297
  23.2 1.3 %collective-permute-start.8 = (bf16[64,1280]{1,0:T(8,128)(2,1)S(1)}, bf16[64,1280]{1,0:T(8,128)(2,1)S(1)}, u32[]{:S(2)}, u32[]{:S(2)}) collective-permute-start(bf16[64,1280]{1,0:T(8,128)(2,1)S(1)} %get-tuple-element.62.refs_0_), channel_id=1, source_target_pairs={{0,6},{1,3},{2,4},{7,5},{24,30},{26,28},{32,38},{33,35},{34,36},{3... | collective-permute-start | bytes 491528 | tf_op jit(solution)/shard_map/ppermute | solution.py:297
  24.5 1.3 %collective-permute-start.9 = (bf16[64,1280]{1,0:T(8,128)(2,1)S(1)}, bf16[64,1280]{1,0:T(8,128)(2,1)S(1)}, u32[]{:S(2)}, u32[]{:S(2)}) collective-permute-start(bf16[64,1280]{1,0:T(8,128)(2,1)S(1)} %get-tuple-element.62.refs_0_), channel_id=1, source_target_pairs={{0,144},{1,17},{2,146},{7,23},{24,128},{26,130},{32,176},{33,49},{... | collective-permute-start | bytes 491528 | tf_op jit(solution)/shard_map/ppermute | solution.py:297
  25.9 0.0 collective-permute-done.7.refs_1_
  25.9 0.0 copy-done
  25.9 0.0 copy-done.1
  25.9 2.5 %shard_map.87 = (f32[512,256]{1,0:T(8,128)S(1)}, f32[512,256]{1,0:T(8,128)S(1)}, bf16[512,1280]{1,0:T(8,128)(2,1)S(1)}, s32[8,1280]{1,0:T(8,128)S(1)}) custom-call(s32[8,1280]{1,0:T(8,128)S(1)} %get-tuple-element.59.refs_0_, bf16[512,1280]{1,0:T(8,128)(2,1)S(1)} %collective-permute-done.7.refs_1_, bf16[512,1280]{1,0:T(8,128)(2,1)S(1)} %copy-done.3, ...), custom_call_target="tpu_custom_call" | custom-call | flops 268435456 | bytes 262144 | tf_op jit(solution)/shard_map/pallas_call | solution.py:274
  28.4 0.0 collective-permute-done.10.refs_3_
  28.4 0.0 collective-permute-done.8.refs_1_
  28.4 0.0 collective-permute-done.9.refs_2_
  28.4 0.1 shard_map.88
  28.5 1.3 %collective-permute-start.11 = (bf16[64,1280]{1,0:T(8,128)(2,1)S(1)}, bf16[64,1280]{1,0:T(8,128)(2,1)S(1)}, u32[]{:S(2)}, u32[]{:S(2)}) collective-permute-start(bf16[64,1280]{1,0:T(8,128)(2,1)S(1)} %get-tuple-element.66.refs_0_), channel_id=1, source_target_pairs={{0,8},{1,153},{2,10},{3,155},{4,12},{5,157},{6,14},{7,159},{17,9},... | collective-permute-start | bytes 491528 | tf_op jit(solution)/shard_map/ppermute | solution.py:297
  29.8 2.3 %shard_map.89 = (f32[512,512]{1,0:T(8,128)S(1)}, f32[512,512]{1,0:T(8,128)S(1)}, s32[8,1280]{1,0:T(8,128)S(1)}) custom-call(s32[8,1280]{1,0:T(8,128)S(1)} %get-tuple-element.63.refs_0_, bf16[512,1280]{1,0:T(8,128)(2,1)S(1)} %get-tuple-element.64.refs_1_, bf16[512,640]{1,0:T(8,128)(2,1)S(1)} %get-tuple-element.60.refs_5_.refs_2_.query_ref, ...), custom_call_target="tpu_custom_call" | custom-call | flops 536870912 | bytes 262144 | tf_op jit(solution)/shard_map/pallas_call | solution.py:274
  32.2 0.0 collective-permute-done.11.refs_1_
  32.2 2.5 %collective-permute-start.12 = (bf16[32,1280]{1,0:T(8,128)(2,1)S(1)}, bf16[32,1280]{1,0:T(8,128)(2,1)S(1)}, u32[]{:S(2)}, u32[]{:S(2)}) collective-permute-start(bf16[32,1280]{1,0:T(8,128)(2,1)S(1)} %get-tuple-element.69.refs_0_), channel_id=1, source_target_pairs={{0,32},{1,97},{2,34},{3,99},{4,36},{5,101},{6,38},{7,103},{8,40},{... | collective-permute-start | bytes 245768 | tf_op jit(solution)/shard_map/ppermute | solution.py:297
  34.8 3.1 %collective-permute-start.13 = (bf16[32,1280]{1,0:T(8,128)(2,1)S(1)}, bf16[32,1280]{1,0:T(8,128)(2,1)S(1)}, u32[]{:S(2)}, u32[]{:S(2)}) collective-permute-start(bf16[32,1280]{1,0:T(8,128)(2,1)S(1)} %get-tuple-element.70.refs_2_), channel_id=1, source_target_pairs={{0,2},{1,7},{2,0},{3,5},{4,6},{5,3},{6,4},{7,1},{8,10},{9,15},{10,... | collective-permute-start | bytes 245768 | tf_op jit(solution)/shard_map/ppermute | solution.py:297
  37.8 2.3 %shard_map.91 = (f32[512,512]{1,0:T(8,128)S(1)}, f32[512,512]{1,0:T(8,128)S(1)}, s32[8,1280]{1,0:T(8,128)S(1)}) custom-call(s32[8,1280]{1,0:T(8,128)S(1)} %get-tuple-element.67.refs_0_, bf16[512,1280]{1,0:T(8,128)(2,1)S(1)} %get-tuple-element.64.refs_1_, bf16[512,640]{1,0:T(8,128)(2,1)S(1)} %get-tuple-element.60.refs_5_.refs_2_.query_ref, ...), custom_call_target="tpu_custom_call" | custom-call | flops 536870912 | bytes 262144 | tf_op jit(solution)/shard_map/pallas_call | solution.py:274
  40.2 0.0 collective-permute-done.12.refs_1_
  40.2 0.0 collective-permute-done.13.refs_3_
  40.3 0.3 collective-permute-start.14
  40.5 2.2 %collective-permute-start.15 = (bf16[64,1280]{1,0:T(8,128)(2,1)S(1)}, bf16[64,1280]{1,0:T(8,128)(2,1)S(1)}, u32[]{:S(2)}, u32[]{:S(2)}) collective-permute-start(bf16[64,1280]{1,0:T(8,128)(2,1)S(1)} %get-tuple-element.80), channel_id=1, source_target_pairs={{0,2},{1,7},{2,0},{3,5},{4,6},{5,3},{6,4},{7,1},{8,10},{9,15},{10,... | collective-permute-start | bytes 491528 | tf_op jit(solution)/shard_map/ppermute | solution.py:297
  42.8 2.2 %collective-permute-start.16 = (bf16[64,1280]{1,0:T(8,128)(2,1)S(1)}, bf16[64,1280]{1,0:T(8,128)(2,1)S(1)}, u32[]{:S(2)}, u32[]{:S(2)}) collective-permute-start(bf16[64,1280]{1,0:T(8,128)(2,1)S(1)} %get-tuple-element.81), channel_id=1, source_target_pairs={{0,32},{1,97},{2,34},{3,99},{4,36},{5,101},{6,38},{7,103},{8,40},{... | collective-permute-start | bytes 491528 | tf_op jit(solution)/shard_map/ppermute | solution.py:297
  45.0 0.0 collective-permute-done.14.refs_1_
  45.0 4.3 %shard_map.93 = (f32[512,256]{1,0:T(8,128)S(1)}, f32[512,256]{1,0:T(8,128)S(1)}, f32[512,512]{1,0:T(8,128)S(1)}, f32[512,512]{1,0:T(8,128)S(1)}, f32[512,512]{1,...) custom-call(s32[8,1280]{1,0:T(8,128)S(1)} %get-tuple-element.71.bits, ...), custom_call_target="tpu_custom_call", output_to_operand_aliasing={{0}: (8, {}), {1}: (9, {}), {2}: (10, {}), {3}: (11, {}), {... | custom-call | flops 1677721600 | bytes 262144 | tf_op jit(solution)/shard_map/pallas_call | solution.py:274
  49.2 0.0 collective-permute-done.15.refs_0_
  49.2 0.0 collective-permute-done.16.refs_1_
  49.3 0.1 collective-permute-start.17
  49.4 0.0 copy-done.8
  49.4 0.0 copy-start.4
  49.4 0.9 %shard_map.95 = (bf16[128,640]{1,0:T(8,128)(2,1)S(1)}, bf16[128,640]{1,0:T(8,128)(2,1)S(1)}, s32[8,1280]{1,0:T(8,128)S(1)}) custom-call(s32[8,1280]{1,0:T(8,128)S(1)} %get-tuple-element.82.bits_ref, bf16[128,1280]{1,0:T(8,128)(2,1)S(1)} %get-tuple-element.83.rows_ref, f32[1,1280]{1,0:T(1,128)S(1)} %reshape.9.gain_ref.refs_3_, ...), custom_call_target="tpu_custom_call" | custom-call | flops 419430400 | bytes 262144 | tf_op jit(solution)/shard_map/pallas_call | solution.py:274
  50.3 0.7 %collective-permute-done.17.rows_ref = bf16[128,1280]{1,0:T(8,128)(2,1)S(1)} collective-permute-done((bf16[128,1280]{1,0:T(8,128)(2,1)S(1)}, bf16[128,1280]{1,0:T(8,128)(2,1)S(1)}, u32[]{:S(2)}, u32[]{:S(2)}) %collective-permute-start.17) | collective-permute-done | bytes 327712 | tf_op jit(solution)/shard_map/ppermute | solution.py:297
  51.0 0.0 copy-done.4
  51.0 6.7 %shard_map.96 = bf16[512,1280]{1,0:T(8,128)(2,1)} custom-call(s32[8,1280]{1,0:T(8,128)S(1)} %get-tuple-element.84.bits_ref, bf16[512,640]{1,0:T(8,128)(2,1)S(1)} %get-tuple-element.60.refs_5_.refs_2_.query_ref, f32[1,1280]{1,0:T(1,128)S(1)} %reshape.9.gain_ref.refs_3_, f32[1,1280]{1,0:T(1,128)S(1)} %reshape.10.bias_ref.refs_4_, ...), custom_call_target="tpu_custom_call" | custom-call | flops 1677721600 | bytes 262144 | tf_op jit(solution)/shard_map/pallas_call | solution.py:274
  (9 shorter events, 0.2 us)
Async XLA Ops:
  0.0 6.1 %collective-permute-start = (bf16[512,1280]{1,0:T(8,128)(2,1)}, bf16[512,1280]{1,0:T(8,128)(2,1)S(1)}, u32[]{:S(2)}, u32[]{:S(2)}) collective-permute-start(bf16[512,1280]{1,0:T(8,128)(2,1)} %hidden_ref.1), channel_id=1, source_target_pairs={{0,1},{1,0},{2,3},{3,2},{4,5},{5,4},{6,7},{7,6},{8,9},{9,8},{10,11... | collective-permute-start | bytes 3932168 | tf_op jit(solution)/shard_map/ppermute | solution.py:297
  3.2 22.6 %collective-permute-start.7 = (bf16[512,1280]{1,0:T(8,128)(2,1)}, bf16[512,1280]{1,0:T(8,128)(2,1)S(1)}, u32[]{:S(2)}, u32[]{:S(2)}) collective-permute-start(bf16[512,1280]{1,0:T(8,128)(2,1)} %hidden_ref.1), channel_id=1, source_target_pairs={{0,1},{1,2},{2,3},{3,4},{4,5},{5,6},{6,7},{7,8},{8,9},{9,10},{10,1... | collective-permute-start | bytes 3932168 | tf_op jit(solution)/shard_map/ppermute | solution.py:297
  3.2 1.3 %copy-start.2 = (bf16[512,1280]{1,0:T(8,128)(2,1)S(1)}, bf16[512,1280]{1,0:T(8,128)(2,1)}, u32[]{:S(2)}) copy-start(bf16[512,1280]{1,0:T(8,128)(2,1)} %hidden_ref.1) | copy-start | bytes 3932164
  4.6 8.3 %copy-start.5 = (bf16[1280,640]{1,0:T(8,128)(2,1)S(1)}, bf16[1280,640]{1,0:T(8,128)(2,1)}, u32[]{:S(2)}) copy-start(bf16[1280,640]{1,0:T(8,128)(2,1)} %weight_ref.1) | copy-start | bytes 4915204
  4.6 8.2 %copy-start.6 = (f32[1280]{0:T(1024)S(1)}, f32[1280]{0:T(1024)}, u32[]{:S(2)}) copy-start(f32[1280]{0:T(1024)} %param.10) | copy-start | bytes 15364
  4.7 8.2 %copy-start.7 = (f32[1280]{0:T(1024)S(1)}, f32[1280]{0:T(1024)}, u32[]{:S(2)}) copy-start(f32[1280]{0:T(1024)} %param.9) | copy-start | bytes 15364
  4.7 8.3 %copy-start.3 = (bf16[512,1280]{1,0:T(8,128)(2,1)S(1)}, bf16[512,1280]{1,0:T(8,128)(2,1)}, u32[]{:S(2)}) copy-start(bf16[512,1280]{1,0:T(8,128)(2,1)} %hidden_ref.1) | copy-start | bytes 3932164
  6.3 8.5 %collective-permute-start.1 = (bf16[64,1280]{1,0:T(8,128)(2,1)S(1)}, bf16[64,1280]{1,0:T(8,128)(2,1)S(1)}, u32[]{:S(2)}, u32[]{:S(2)}) collective-permute-start(bf16[64,1280]{1,0:T(8,128)(2,1)S(1)} %get-tuple-element.54), channel_id=1, source_target_pairs={{0,32},{1,97}} | collective-permute-start | bytes 491528 | tf_op jit(solution)/shard_map/ppermute | solution.py:297
  9.1 5.7 %collective-permute-start.2 = (bf16[64,1280]{1,0:T(8,128)(2,1)S(1)}, bf16[64,1280]{1,0:T(8,128)(2,1)S(1)}, u32[]{:S(2)}, u32[]{:S(2)}) collective-permute-start(bf16[64,1280]{1,0:T(8,128)(2,1)S(1)} %get-tuple-element.55), channel_id=1, source_target_pairs={{0,2},{1,7}} | collective-permute-start | bytes 491528 | tf_op jit(solution)/shard_map/ppermute | solution.py:297
  10.4 4.7 %collective-permute-start.3 = (bf16[64,1280]{1,0:T(8,128)(2,1)S(1)}, bf16[64,1280]{1,0:T(8,128)(2,1)S(1)}, u32[]{:S(2)}, u32[]{:S(2)}) collective-permute-start(bf16[64,1280]{1,0:T(8,128)(2,1)S(1)} %get-tuple-element.56), channel_id=1, source_target_pairs={{0,34},{1,103}} | collective-permute-start | bytes 491528 | tf_op jit(solution)/shard_map/ppermute | solution.py:297
  12.9 12.9 %copy-start = (bf16[1280,640]{1,0:T(8,128)(2,1)S(1)}, bf16[1280,640]{1,0:T(8,128)(2,1)}, u32[]{:S(2)}) copy-start(bf16[1280,640]{1,0:T(8,128)(2,1)} %key_ref.5) | copy-start | bytes 4915204
  13.0 12.9 %copy-start.1 = (bf16[1280,640]{1,0:T(8,128)(2,1)S(1)}, bf16[1280,640]{1,0:T(8,128)(2,1)}, u32[]{:S(2)}) copy-start(bf16[1280,640]{1,0:T(8,128)(2,1)} %value_ref.5) | copy-start | bytes 4915204
  15.2 4.2 %collective-permute-start.4 = (bf16[64,1280]{1,0:T(8,128)(2,1)S(1)}, bf16[64,1280]{1,0:T(8,128)(2,1)S(1)}, u32[]{:S(2)}, u32[]{:S(2)}) collective-permute-start(bf16[64,1280]{1,0:T(8,128)(2,1)S(1)} %get-tuple-element.58.refs_0_), channel_id=1, source_target_pairs={{0,96},{1,33},{2,98},{7,39},{32,64},{34,66},{97,65},{103,71}} | collective-permute-start | bytes 491528 | tf_op jit(solution)/shard_map/ppermute | solution.py:297
  16.5 3.5 %collective-permute-start.5 = (bf16[64,1280]{1,0:T(8,128)(2,1)S(1)}, bf16[64,1280]{1,0:T(8,128)(2,1)S(1)}, u32[]{:S(2)}, u32[]{:S(2)}) collective-permute-start(bf16[64,1280]{1,0:T(8,128)(2,1)S(1)} %get-tuple-element.58.refs_0_), channel_id=1, source_target_pairs={{0,24},{1,137},{2,26},{7,143},{32,56},{34,58},{97,233},{103,239}} | collective-permute-start | bytes 491528 | tf_op jit(solution)/shard_map/ppermute | solution.py:297
  17.8 4.0 %collective-permute-start.6 = (bf16[64,1280]{1,0:T(8,128)(2,1)S(1)}, bf16[64,1280]{1,0:T(8,128)(2,1)S(1)}, u32[]{:S(2)}, u32[]{:S(2)}) collective-permute-start(bf16[64,1280]{1,0:T(8,128)(2,1)S(1)} %get-tuple-element.58.refs_0_), channel_id=1, source_target_pairs={{0,120},{1,169},{2,122},{7,175},{32,88},{34,90},{97,201},{103,207}} | collective-permute-start | bytes 491528 | tf_op jit(solution)/shard_map/ppermute | solution.py:297
  21.9 6.5 %collective-permute-start.10 = (bf16[64,1280]{1,0:T(8,128)(2,1)S(1)}, bf16[64,1280]{1,0:T(8,128)(2,1)S(1)}, u32[]{:S(2)}, u32[]{:S(2)}) collective-permute-start(bf16[64,1280]{1,0:T(8,128)(2,1)S(1)} %get-tuple-element.62.refs_0_), channel_id=1, source_target_pairs={{0,150},{1,19},{2,148},{7,21},{24,134},{26,132},{32,182},{33,51},{... | collective-permute-start | bytes 491528 | tf_op jit(solution)/shard_map/ppermute | solution.py:297
  23.2 5.2 %collective-permute-start.8 = (bf16[64,1280]{1,0:T(8,128)(2,1)S(1)}, bf16[64,1280]{1,0:T(8,128)(2,1)S(1)}, u32[]{:S(2)}, u32[]{:S(2)}) collective-permute-start(bf16[64,1280]{1,0:T(8,128)(2,1)S(1)} %get-tuple-element.62.refs_0_), channel_id=1, source_target_pairs={{0,6},{1,3},{2,4},{7,5},{24,30},{26,28},{32,38},{33,35},{34,36},{3... | collective-permute-start | bytes 491528 | tf_op jit(solution)/shard_map/ppermute | solution.py:297
  24.5 3.9 %collective-permute-start.9 = (bf16[64,1280]{1,0:T(8,128)(2,1)S(1)}, bf16[64,1280]{1,0:T(8,128)(2,1)S(1)}, u32[]{:S(2)}, u32[]{:S(2)}) collective-permute-start(bf16[64,1280]{1,0:T(8,128)(2,1)S(1)} %get-tuple-element.62.refs_0_), channel_id=1, source_target_pairs={{0,144},{1,17},{2,146},{7,23},{24,128},{26,130},{32,176},{33,49},{... | collective-permute-start | bytes 491528 | tf_op jit(solution)/shard_map/ppermute | solution.py:297
  28.5 3.7 %collective-permute-start.11 = (bf16[64,1280]{1,0:T(8,128)(2,1)S(1)}, bf16[64,1280]{1,0:T(8,128)(2,1)S(1)}, u32[]{:S(2)}, u32[]{:S(2)}) collective-permute-start(bf16[64,1280]{1,0:T(8,128)(2,1)S(1)} %get-tuple-element.66.refs_0_), channel_id=1, source_target_pairs={{0,8},{1,153},{2,10},{3,155},{4,12},{5,157},{6,14},{7,159},{17,9},... | collective-permute-start | bytes 491528 | tf_op jit(solution)/shard_map/ppermute | solution.py:297
  32.2 7.9 %collective-permute-start.12 = (bf16[32,1280]{1,0:T(8,128)(2,1)S(1)}, bf16[32,1280]{1,0:T(8,128)(2,1)S(1)}, u32[]{:S(2)}, u32[]{:S(2)}) collective-permute-start(bf16[32,1280]{1,0:T(8,128)(2,1)S(1)} %get-tuple-element.69.refs_0_), channel_id=1, source_target_pairs={{0,32},{1,97},{2,34},{3,99},{4,36},{5,101},{6,38},{7,103},{8,40},{... | collective-permute-start | bytes 245768 | tf_op jit(solution)/shard_map/ppermute | solution.py:297
  34.8 5.4 %collective-permute-start.13 = (bf16[32,1280]{1,0:T(8,128)(2,1)S(1)}, bf16[32,1280]{1,0:T(8,128)(2,1)S(1)}, u32[]{:S(2)}, u32[]{:S(2)}) collective-permute-start(bf16[32,1280]{1,0:T(8,128)(2,1)S(1)} %get-tuple-element.70.refs_2_), channel_id=1, source_target_pairs={{0,2},{1,7},{2,0},{3,5},{4,6},{5,3},{6,4},{7,1},{8,10},{9,15},{10,... | collective-permute-start | bytes 245768 | tf_op jit(solution)/shard_map/ppermute | solution.py:297
  40.3 4.7 %collective-permute-start.14 = (bf16[128,1280]{1,0:T(8,128)(2,1)S(1)}, bf16[128,1280]{1,0:T(8,128)(2,1)S(1)}, u32[]{:S(2)}, u32[]{:S(2)}) collective-permute-start(bf16[128,1280]{1,0:T(8,128)(2,1)S(1)} %get-tuple-element.72.refs_0_), channel_id=1, source_target_pairs={{0,1},{1,0},{2,3},{3,2},{4,5},{5,4},{6,7},{7,6},{8,9},{9,8},{10,11... | collective-permute-start | bytes 983048 | tf_op jit(solution)/shard_map/ppermute | solution.py:297
  40.5 8.7 %collective-permute-start.15 = (bf16[64,1280]{1,0:T(8,128)(2,1)S(1)}, bf16[64,1280]{1,0:T(8,128)(2,1)S(1)}, u32[]{:S(2)}, u32[]{:S(2)}) collective-permute-start(bf16[64,1280]{1,0:T(8,128)(2,1)S(1)} %get-tuple-element.80), channel_id=1, source_target_pairs={{0,2},{1,7},{2,0},{3,5},{4,6},{5,3},{6,4},{7,1},{8,10},{9,15},{10,... | collective-permute-start | bytes 491528 | tf_op jit(solution)/shard_map/ppermute | solution.py:297
  42.8 6.5 %collective-permute-start.16 = (bf16[64,1280]{1,0:T(8,128)(2,1)S(1)}, bf16[64,1280]{1,0:T(8,128)(2,1)S(1)}, u32[]{:S(2)}, u32[]{:S(2)}) collective-permute-start(bf16[64,1280]{1,0:T(8,128)(2,1)S(1)} %get-tuple-element.81), channel_id=1, source_target_pairs={{0,32},{1,97},{2,34},{3,99},{4,36},{5,101},{6,38},{7,103},{8,40},{... | collective-permute-start | bytes 491528 | tf_op jit(solution)/shard_map/ppermute | solution.py:297
  45.0 4.4 %copy-start.8 = (f32[1280]{0:T(1024)S(1)}, f32[1280]{0:T(1024)}, u32[]{:S(2)}) copy-start(f32[1280]{0:T(1024)} %param.15) | copy-start | bytes 15364
  49.3 1.7 %collective-permute-start.17 = (bf16[128,1280]{1,0:T(8,128)(2,1)S(1)}, bf16[128,1280]{1,0:T(8,128)(2,1)S(1)}, u32[]{:S(2)}, u32[]{:S(2)}) collective-permute-start(bf16[128,1280]{1,0:T(8,128)(2,1)S(1)} %get-tuple-element.83.rows_ref), channel_id=1, source_target_pairs={{0,1},{1,0},{2,3},{3,2},{4,5},{5,4},{6,7},{7,6},{8,9},{9,8},{10,11... | collective-permute-start | bytes 983048 | tf_op jit(solution)/shard_map/ppermute | solution.py:297
  49.4 1.6 %copy-start.4 = (bf16[640,1280]{1,0:T(8,128)(2,1)S(1)}, bf16[640,1280]{1,0:T(8,128)(2,1)}, u32[]{:S(2)}) copy-start(bf16[640,1280]{1,0:T(8,128)(2,1)} %out_weight_ref.1) | copy-start | bytes 4915204

commit v7 on v6

--- a/solution.py
+++ b/solution.py
@@ -21,9 +21,9 @@
 FIRST, SECOND = ((0, 1),), ((0, 3), (1, 2))
 ROUNDS = (
     ({"x": FIRST}, {"y": FIRST}, {"x": FIRST, "y": FIRST}),
-    ({"x": SECOND}, {"z": ((0, 3),)}, {"x": SECOND, "z": ((0, 3),)}),
-    ({"y": SECOND}, {"z": ((0, 6), (3, 4))}, {"y": SECOND, "z": ((0, 6), (3, 4))}),
-    ({"z": ((0, 1), (3, 2), (4, 5), (6, 7))},),
+    ({"x": SECOND}, {"z": ((0, 1),)}, {"x": SECOND, "z": ((0, 1),)}),
+    ({"y": SECOND}, {"z": ((0, 6), (1, 3))}, {"y": SECOND, "z": ((0, 6), (1, 3))}),
+    ({"z": ((0, 7), (1, 2), (3, 4), (6, 5))},),
 )
 
 

time: 58 us -> 56.9 us (0.981)
  starting transfers between devices: 29.6 us -> 27.3 us
  waiting for transfers between devices: 4.87 us -> 6.06 us
    ppermute x18, starting transfers between devices: 29.6 us -> 27.3 us  [move(): return lax.ppermute(value, AXES, pairs)]
    ppermute x18, waiting for transfers between devices: 4.87 us -> 6.06 us  [move(): return lax.ppermute(value, AXES, pairs)]
  transfers between devices with their start and end apart: 18 -> 18, of which waited for: 5 -> 6; matrix products, arithmetic and copies ran while one was open for 0% -> 0% of each run, Pallas kernels for 25% -> 26%
where the time goes in v7:
time: 56.9 us; the launch traced here: 56.6 us
  starting transfers between devices  27.3 us (48%)
  Pallas kernels  21.4 us (38%)
  waiting for transfers between devices  6.06 us (11%)
  local copies, waits for them, and re-layouts  1.4 us (2%)
    ppermute x18, starting transfers between devices, move(): return lax.ppermute(value, AXES, pairs)  27.3 us
    pallas_call x15, Pallas kernels, call(): pl.pallas_call(kernel, out_shape=outs, in_specs=[whole] * len(operands),...  21.4 us
    ppermute x18, waiting for transfers between devices, move(): return lax.ppermute(value, AXES, pairs)  6.06 us
    unnamed x18, local copies, waits for them, and re-layouts  1.39 us
  transfers between devices with their start and end apart: 18, of which 6 were waited for; matrix products, arithmetic and copies ran while one was open for 0% of the time, Pallas kernels for 26%

profile of v7, /device:TPU:1, one launch (start us, length us, event | category | flops | bytes accessed | tf_op | source)
XLA Modules:
  0.0 56.6 jit_solution(11586960762576671049)
XLA Ops:
  0.0 3.2 %collective-permute-start = (bf16[512,1280]{1,0:T(8,128)(2,1)}, bf16[512,1280]{1,0:T(8,128)(2,1)S(1)}, u32[]{:S(2)}, u32[]{:S(2)}) collective-permute-start(bf16[512,1280]{1,0:T(8,128)(2,1)} %hidden_ref.1), channel_id=1, source_target_pairs={{0,1},{1,0},{2,3},{3,2},{4,5},{5,4},{6,7},{7,6},{8,9},{9,8},{10,11... | collective-permute-start | bytes 3932168 | tf_op jit(solution)/shard_map/ppermute | solution.py:297
  3.2 0.0 collective-permute-start.7
  3.2 0.0 copy-start.2
  3.3 1.3 %copy-done.2 = bf16[512,1280]{1,0:T(8,128)(2,1)S(1)} copy-done((bf16[512,1280]{1,0:T(8,128)(2,1)S(1)}, bf16[512,1280]{1,0:T(8,128)(2,1)}, u32[]{:S(2)}) %copy-start.2) | copy-done | bytes 1310744
  4.6 0.0 copy-start.5
  4.6 0.0 copy-start.6
  4.7 0.0 copy-start.7
  4.7 0.0 copy-start.3
  4.7 1.4 %collective-permute-done.other_ref = bf16[512,1280]{1,0:T(8,128)(2,1)S(1)} collective-permute-done((bf16[512,1280]{1,0:T(8,128)(2,1)}, bf16[512,1280]{1,0:T(8,128)(2,1)S(1)}, u32[]{:S(2)}, u32[]{:S(2)}) %collective-permute-start) | collective-permute-done | bytes 1310752 | tf_op jit(solution)/shard_map/ppermute | solution.py:297
  6.1 0.2 shard_map.83
  6.3 2.8 %collective-permute-start.1 = (bf16[64,1280]{1,0:T(8,128)(2,1)S(1)}, bf16[64,1280]{1,0:T(8,128)(2,1)S(1)}, u32[]{:S(2)}, u32[]{:S(2)}) collective-permute-start(bf16[64,1280]{1,0:T(8,128)(2,1)S(1)} %get-tuple-element.54), channel_id=1, source_target_pairs={{0,32},{1,97}} | collective-permute-start | bytes 491528 | tf_op jit(solution)/shard_map/ppermute | solution.py:297
  9.1 1.3 %collective-permute-start.2 = (bf16[64,1280]{1,0:T(8,128)(2,1)S(1)}, bf16[64,1280]{1,0:T(8,128)(2,1)S(1)}, u32[]{:S(2)}, u32[]{:S(2)}) collective-permute-start(bf16[64,1280]{1,0:T(8,128)(2,1)S(1)} %get-tuple-element.55), channel_id=1, source_target_pairs={{0,2},{1,7}} | collective-permute-start | bytes 491528 | tf_op jit(solution)/shard_map/ppermute | solution.py:297
  10.4 2.5 %collective-permute-start.3 = (bf16[64,1280]{1,0:T(8,128)(2,1)S(1)}, bf16[64,1280]{1,0:T(8,128)(2,1)S(1)}, u32[]{:S(2)}, u32[]{:S(2)}) collective-permute-start(bf16[64,1280]{1,0:T(8,128)(2,1)S(1)} %get-tuple-element.56), channel_id=1, source_target_pairs={{0,34},{1,103}} | collective-permute-start | bytes 491528 | tf_op jit(solution)/shard_map/ppermute | solution.py:297
  12.9 0.0 copy-done.6
  12.9 0.0 copy-done.7
  12.9 0.0 copy-done.5
  12.9 0.0 copy-done.3
  12.9 0.0 copy-start
  13.0 0.0 copy-start.1
  13.0 1.8 %shard_map.84 = (bf16[512,640]{1,0:T(8,128)(2,1)S(1)}, s32[8,1280]{1,0:T(8,128)S(1)}) custom-call(s32[8,1280]{1,0:T(8,128)S(1)} %get-tuple-element.51.bits_ref, bf16[512,1280]{1,0:T(8,128)(2,1)S(1)} %copy-done.3, f32[1,1280]{1,0:T(1,128)S(1)} %reshape.9.gain_ref.refs_3_, f32[1,1280]{1,0:T(1,128)S(1)} %reshape.10.bias_ref.refs_4_, bf16[1280,640]{1,0:T(8,128)(2,1)S(1)} %copy-done.5), custom_call_target="tpu_custom_call" | custom-call | flops 838860800 | bytes 262144 | tf_op jit(solution)/shard_map/pallas_call | solution.py:274
  14.8 0.0 collective-permute-done.1.refs_1_
  14.8 0.0 collective-permute-done.2.refs_2_
  14.8 0.3 collective-permute-done.3.refs_3_
  15.1 0.1 shard_map.85
  15.2 1.3 %collective-permute-start.4 = (bf16[64,1280]{1,0:T(8,128)(2,1)S(1)}, bf16[64,1280]{1,0:T(8,128)(2,1)S(1)}, u32[]{:S(2)}, u32[]{:S(2)}) collective-permute-start(bf16[64,1280]{1,0:T(8,128)(2,1)S(1)} %get-tuple-element.58.refs_0_), channel_id=1, source_target_pairs={{0,96},{1,33},{2,98},{7,39},{32,64},{34,66},{97,65},{103,71}} | collective-permute-start | bytes 491528 | tf_op jit(solution)/shard_map/ppermute | solution.py:297
  16.5 1.3 %collective-permute-start.5 = (bf16[64,1280]{1,0:T(8,128)(2,1)S(1)}, bf16[64,1280]{1,0:T(8,128)(2,1)S(1)}, u32[]{:S(2)}, u32[]{:S(2)}) collective-permute-start(bf16[64,1280]{1,0:T(8,128)(2,1)S(1)} %get-tuple-element.58.refs_0_), channel_id=1, source_target_pairs={{0,8},{1,153},{2,10},{7,159},{32,40},{34,42},{97,249},{103,255}} | collective-permute-start | bytes 491528 | tf_op jit(solution)/shard_map/ppermute | solution.py:297
  17.8 1.3 %collective-permute-start.6 = (bf16[64,1280]{1,0:T(8,128)(2,1)S(1)}, bf16[64,1280]{1,0:T(8,128)(2,1)S(1)}, u32[]{:S(2)}, u32[]{:S(2)}) collective-permute-start(bf16[64,1280]{1,0:T(8,128)(2,1)S(1)} %get-tuple-element.58.refs_0_), channel_id=1, source_target_pairs={{0,104},{1,185},{2,106},{7,191},{32,72},{34,74},{97,217},{103,223}} | collective-permute-start | bytes 491528 | tf_op jit(solution)/shard_map/ppermute | solution.py:297
  19.1 0.0 collective-permute-done.4.refs_1_
  19.2 0.9 %collective-permute-done.5.refs_2_ = bf16[64,1280]{1,0:T(8,128)(2,1)S(1)} collective-permute-done((bf16[64,1280]{1,0:T(8,128)(2,1)S(1)}, bf16[64,1280]{1,0:T(8,128)(2,1)S(1)}, u32[]{:S(2)}, u32[]{:S(2)}) %collective-permute-start.5) | collective-permute-done | bytes 163872 | tf_op jit(solution)/shard_map/ppermute | solution.py:297
  20.1 1.8 %collective-permute-done.6.refs_3_ = bf16[64,1280]{1,0:T(8,128)(2,1)S(1)} collective-permute-done((bf16[64,1280]{1,0:T(8,128)(2,1)S(1)}, bf16[64,1280]{1,0:T(8,128)(2,1)S(1)}, u32[]{:S(2)}, u32[]{:S(2)}) %collective-permute-start.6) | collective-permute-done | bytes 163872 | tf_op jit(solution)/shard_map/ppermute | solution.py:297
  21.8 0.1 shard_map.86
  21.9 1.3 %collective-permute-start.10 = (bf16[64,1280]{1,0:T(8,128)(2,1)S(1)}, bf16[64,1280]{1,0:T(8,128)(2,1)S(1)}, u32[]{:S(2)}, u32[]{:S(2)}) collective-permute-start(bf16[64,1280]{1,0:T(8,128)(2,1)S(1)} %get-tuple-element.62.refs_0_), channel_id=1, source_target_pairs={{0,150},{1,19},{2,148},{7,21},{8,30},{10,28},{32,182},{33,51},{34,... | collective-permute-start | bytes 491528 | tf_op jit(solution)/shard_map/ppermute | solution.py:297
  23.2 1.3 %collective-permute-start.8 = (bf16[64,1280]{1,0:T(8,128)(2,1)S(1)}, bf16[64,1280]{1,0:T(8,128)(2,1)S(1)}, u32[]{:S(2)}, u32[]{:S(2)}) collective-permute-start(bf16[64,1280]{1,0:T(8,128)(2,1)S(1)} %get-tuple-element.62.refs_0_), channel_id=1, source_target_pairs={{0,6},{1,3},{2,4},{7,5},{8,14},{10,12},{32,38},{33,35},{34,36},{39... | collective-permute-start | bytes 491528 | tf_op jit(solution)/shard_map/ppermute | solution.py:297
  24.5 1.3 %collective-permute-start.9 = (bf16[64,1280]{1,0:T(8,128)(2,1)S(1)}, bf16[64,1280]{1,0:T(8,128)(2,1)S(1)}, u32[]{:S(2)}, u32[]{:S(2)}) collective-permute-start(bf16[64,1280]{1,0:T(8,128)(2,1)S(1)} %get-tuple-element.62.refs_0_), channel_id=1, source_target_pairs={{0,144},{1,17},{2,146},{7,23},{8,24},{10,26},{32,176},{33,49},{34,... | collective-permute-start | bytes 491528 | tf_op jit(solution)/shard_map/ppermute | solution.py:297
  25.9 0.0 collective-permute-done.7.refs_1_
  25.9 0.0 copy-done
  25.9 0.0 copy-done.1
  25.9 2.5 %shard_map.87 = (f32[512,256]{1,0:T(8,128)S(1)}, f32[512,256]{1,0:T(8,128)S(1)}, bf16[512,1280]{1,0:T(8,128)(2,1)S(1)}, s32[8,1280]{1,0:T(8,128)S(1)}) custom-call(s32[8,1280]{1,0:T(8,128)S(1)} %get-tuple-element.59.refs_0_, bf16[512,1280]{1,0:T(8,128)(2,1)S(1)} %collective-permute-done.7.refs_1_, bf16[512,1280]{1,0:T(8,128)(2,1)S(1)} %copy-done.3, ...), custom_call_target="tpu_custom_call" | custom-call | flops 268435456 | bytes 262144 | tf_op jit(solution)/shard_map/pallas_call | solution.py:274
  28.4 0.0 collective-permute-done.10.refs_3_
  28.4 0.0 collective-permute-done.8.refs_1_
  28.4 0.0 collective-permute-done.9.refs_2_
  28.4 0.1 shard_map.88
  28.5 1.3 %collective-permute-start.11 = (bf16[64,1280]{1,0:T(8,128)(2,1)S(1)}, bf16[64,1280]{1,0:T(8,128)(2,1)S(1)}, u32[]{:S(2)}, u32[]{:S(2)}) collective-permute-start(bf16[64,1280]{1,0:T(8,128)(2,1)S(1)} %get-tuple-element.66.refs_0_), channel_id=1, source_target_pairs={{0,152},{1,9},{2,154},{3,11},{4,156},{5,13},{6,158},{7,15},{8,16},... | collective-permute-start | bytes 491528 | tf_op jit(solution)/shard_map/ppermute | solution.py:297
  29.8 2.3 %shard_map.89 = (f32[512,512]{1,0:T(8,128)S(1)}, f32[512,512]{1,0:T(8,128)S(1)}, s32[8,1280]{1,0:T(8,128)S(1)}) custom-call(s32[8,1280]{1,0:T(8,128)S(1)} %get-tuple-element.63.refs_0_, bf16[512,1280]{1,0:T(8,128)(2,1)S(1)} %get-tuple-element.64.refs_1_, bf16[512,640]{1,0:T(8,128)(2,1)S(1)} %get-tuple-element.60.refs_5_.refs_2_.query_ref, ...), custom_call_target="tpu_custom_call" | custom-call | flops 536870912 | bytes 262144 | tf_op jit(solution)/shard_map/pallas_call | solution.py:274
  32.2 0.0 collective-permute-done.11.refs_1_
  32.2 1.7 %collective-permute-start.12 = (bf16[32,1280]{1,0:T(8,128)(2,1)S(1)}, bf16[32,1280]{1,0:T(8,128)(2,1)S(1)}, u32[]{:S(2)}, u32[]{:S(2)}) collective-permute-start(bf16[32,1280]{1,0:T(8,128)(2,1)S(1)} %get-tuple-element.69.refs_0_), channel_id=1, source_target_pairs={{0,32},{1,97},{2,34},{3,99},{4,36},{5,101},{6,38},{7,103},{8,40},{... | collective-permute-start | bytes 245768 | tf_op jit(solution)/shard_map/ppermute | solution.py:297
  33.9 3.9 %collective-permute-start.13 = (bf16[32,1280]{1,0:T(8,128)(2,1)S(1)}, bf16[32,1280]{1,0:T(8,128)(2,1)S(1)}, u32[]{:S(2)}, u32[]{:S(2)}) collective-permute-start(bf16[32,1280]{1,0:T(8,128)(2,1)S(1)} %get-tuple-element.70.refs_2_), channel_id=1, source_target_pairs={{0,2},{1,7},{2,0},{3,5},{4,6},{5,3},{6,4},{7,1},{8,10},{9,15},{10,... | collective-permute-start | bytes 245768 | tf_op jit(solution)/shard_map/ppermute | solution.py:297
  37.8 2.3 %shard_map.91 = (f32[512,512]{1,0:T(8,128)S(1)}, f32[512,512]{1,0:T(8,128)S(1)}, s32[8,1280]{1,0:T(8,128)S(1)}) custom-call(s32[8,1280]{1,0:T(8,128)S(1)} %get-tuple-element.67.refs_0_, bf16[512,1280]{1,0:T(8,128)(2,1)S(1)} %get-tuple-element.64.refs_1_, bf16[512,640]{1,0:T(8,128)(2,1)S(1)} %get-tuple-element.60.refs_5_.refs_2_.query_ref, ...), custom_call_target="tpu_custom_call" | custom-call | flops 536870912 | bytes 262144 | tf_op jit(solution)/shard_map/pallas_call | solution.py:274
  40.2 0.0 collective-permute-done.12.refs_1_
  40.2 0.0 collective-permute-done.13.refs_3_
  40.3 0.3 collective-permute-start.14
  40.5 2.2 %collective-permute-start.15 = (bf16[64,1280]{1,0:T(8,128)(2,1)S(1)}, bf16[64,1280]{1,0:T(8,128)(2,1)S(1)}, u32[]{:S(2)}, u32[]{:S(2)}) collective-permute-start(bf16[64,1280]{1,0:T(8,128)(2,1)S(1)} %get-tuple-element.80), channel_id=1, source_target_pairs={{0,2},{1,7},{2,0},{3,5},{4,6},{5,3},{6,4},{7,1},{8,10},{9,15},{10,... | collective-permute-start | bytes 491528 | tf_op jit(solution)/shard_map/ppermute | solution.py:297
  42.8 0.2 collective-permute-start.16
  42.9 0.0 collective-permute-done.14.refs_1_
  42.9 4.3 %shard_map.93 = (f32[512,256]{1,0:T(8,128)S(1)}, f32[512,256]{1,0:T(8,128)S(1)}, f32[512,512]{1,0:T(8,128)S(1)}, f32[512,512]{1,0:T(8,128)S(1)}, f32[512,512]{1,...) custom-call(s32[8,1280]{1,0:T(8,128)S(1)} %get-tuple-element.71.bits, ...), custom_call_target="tpu_custom_call", output_to_operand_aliasing={{0}: (8, {}), {1}: (9, {}), {2}: (10, {}), {3}: (11, {}), {... | custom-call | flops 1677721600 | bytes 262144 | tf_op jit(solution)/shard_map/pallas_call | solution.py:274
  47.2 0.0 collective-permute-done.15.refs_0_
  47.2 0.9 %collective-permute-done.16.refs_1_ = bf16[64,1280]{1,0:T(8,128)(2,1)S(1)} collective-permute-done((bf16[64,1280]{1,0:T(8,128)(2,1)S(1)}, bf16[64,1280]{1,0:T(8,128)(2,1)S(1)}, u32[]{:S(2)}, u32[]{:S(2)}) %collective-permute-start.16) | collective-permute-done | bytes 163872 | tf_op jit(solution)/shard_map/ppermute | solution.py:297
  48.2 0.1 collective-permute-start.17
  48.3 0.0 copy-done.8
  48.3 0.0 copy-start.4
  48.3 0.9 %shard_map.95 = (bf16[128,640]{1,0:T(8,128)(2,1)S(1)}, bf16[128,640]{1,0:T(8,128)(2,1)S(1)}, s32[8,1280]{1,0:T(8,128)S(1)}) custom-call(s32[8,1280]{1,0:T(8,128)S(1)} %get-tuple-element.82.bits_ref, bf16[128,1280]{1,0:T(8,128)(2,1)S(1)} %get-tuple-element.83.rows_ref, f32[1,1280]{1,0:T(1,128)S(1)} %reshape.9.gain_ref.refs_3_, ...), custom_call_target="tpu_custom_call" | custom-call | flops 419430400 | bytes 262144 | tf_op jit(solution)/shard_map/pallas_call | solution.py:274
  49.2 0.7 %collective-permute-done.17.rows_ref = bf16[128,1280]{1,0:T(8,128)(2,1)S(1)} collective-permute-done((bf16[128,1280]{1,0:T(8,128)(2,1)S(1)}, bf16[128,1280]{1,0:T(8,128)(2,1)S(1)}, u32[]{:S(2)}, u32[]{:S(2)}) %collective-permute-start.17) | collective-permute-done | bytes 327712 | tf_op jit(solution)/shard_map/ppermute | solution.py:297
  49.9 0.0 copy-done.4
  49.9 6.7 %shard_map.96 = bf16[512,1280]{1,0:T(8,128)(2,1)} custom-call(s32[8,1280]{1,0:T(8,128)S(1)} %get-tuple-element.84.bits_ref, bf16[512,640]{1,0:T(8,128)(2,1)S(1)} %get-tuple-element.60.refs_5_.refs_2_.query_ref, f32[1,1280]{1,0:T(1,128)S(1)} %reshape.9.gain_ref.refs_3_, f32[1,1280]{1,0:T(1,128)S(1)} %reshape.10.bias_ref.refs_4_, ...), custom_call_target="tpu_custom_call" | custom-call | flops 1677721600 | bytes 262144 | tf_op jit(solution)/shard_map/pallas_call | solution.py:274
  (9 shorter events, 0.2 us)
Async XLA Ops:
  0.0 6.1 %collective-permute-start = (bf16[512,1280]{1,0:T(8,128)(2,1)}, bf16[512,1280]{1,0:T(8,128)(2,1)S(1)}, u32[]{:S(2)}, u32[]{:S(2)}) collective-permute-start(bf16[512,1280]{1,0:T(8,128)(2,1)} %hidden_ref.1), channel_id=1, source_target_pairs={{0,1},{1,0},{2,3},{3,2},{4,5},{5,4},{6,7},{7,6},{8,9},{9,8},{10,11... | collective-permute-start | bytes 3932168 | tf_op jit(solution)/shard_map/ppermute | solution.py:297
  3.2 22.6 %collective-permute-start.7 = (bf16[512,1280]{1,0:T(8,128)(2,1)}, bf16[512,1280]{1,0:T(8,128)(2,1)S(1)}, u32[]{:S(2)}, u32[]{:S(2)}) collective-permute-start(bf16[512,1280]{1,0:T(8,128)(2,1)} %hidden_ref.1), channel_id=1, source_target_pairs={{0,1},{1,2},{2,3},{3,4},{4,5},{5,6},{6,7},{7,8},{8,9},{9,10},{10,1... | collective-permute-start | bytes 3932168 | tf_op jit(solution)/shard_map/ppermute | solution.py:297
  3.2 1.3 %copy-start.2 = (bf16[512,1280]{1,0:T(8,128)(2,1)S(1)}, bf16[512,1280]{1,0:T(8,128)(2,1)}, u32[]{:S(2)}) copy-start(bf16[512,1280]{1,0:T(8,128)(2,1)} %hidden_ref.1) | copy-start | bytes 3932164
  4.6 8.3 %copy-start.5 = (bf16[1280,640]{1,0:T(8,128)(2,1)S(1)}, bf16[1280,640]{1,0:T(8,128)(2,1)}, u32[]{:S(2)}) copy-start(bf16[1280,640]{1,0:T(8,128)(2,1)} %weight_ref.1) | copy-start | bytes 4915204
  4.6 8.2 %copy-start.6 = (f32[1280]{0:T(1024)S(1)}, f32[1280]{0:T(1024)}, u32[]{:S(2)}) copy-start(f32[1280]{0:T(1024)} %param.10) | copy-start | bytes 15364
  4.7 8.2 %copy-start.7 = (f32[1280]{0:T(1024)S(1)}, f32[1280]{0:T(1024)}, u32[]{:S(2)}) copy-start(f32[1280]{0:T(1024)} %param.9) | copy-start | bytes 15364
  4.7 8.3 %copy-start.3 = (bf16[512,1280]{1,0:T(8,128)(2,1)S(1)}, bf16[512,1280]{1,0:T(8,128)(2,1)}, u32[]{:S(2)}) copy-start(bf16[512,1280]{1,0:T(8,128)(2,1)} %hidden_ref.1) | copy-start | bytes 3932164
  6.3 8.5 %collective-permute-start.1 = (bf16[64,1280]{1,0:T(8,128)(2,1)S(1)}, bf16[64,1280]{1,0:T(8,128)(2,1)S(1)}, u32[]{:S(2)}, u32[]{:S(2)}) collective-permute-start(bf16[64,1280]{1,0:T(8,128)(2,1)S(1)} %get-tuple-element.54), channel_id=1, source_target_pairs={{0,32},{1,97}} | collective-permute-start | bytes 491528 | tf_op jit(solution)/shard_map/ppermute | solution.py:297
  9.1 5.7 %collective-permute-start.2 = (bf16[64,1280]{1,0:T(8,128)(2,1)S(1)}, bf16[64,1280]{1,0:T(8,128)(2,1)S(1)}, u32[]{:S(2)}, u32[]{:S(2)}) collective-permute-start(bf16[64,1280]{1,0:T(8,128)(2,1)S(1)} %get-tuple-element.55), channel_id=1, source_target_pairs={{0,2},{1,7}} | collective-permute-start | bytes 491528 | tf_op jit(solution)/shard_map/ppermute | solution.py:297
  10.4 4.7 %collective-permute-start.3 = (bf16[64,1280]{1,0:T(8,128)(2,1)S(1)}, bf16[64,1280]{1,0:T(8,128)(2,1)S(1)}, u32[]{:S(2)}, u32[]{:S(2)}) collective-permute-start(bf16[64,1280]{1,0:T(8,128)(2,1)S(1)} %get-tuple-element.56), channel_id=1, source_target_pairs={{0,34},{1,103}} | collective-permute-start | bytes 491528 | tf_op jit(solution)/shard_map/ppermute | solution.py:297
  12.9 12.9 %copy-start = (bf16[1280,640]{1,0:T(8,128)(2,1)S(1)}, bf16[1280,640]{1,0:T(8,128)(2,1)}, u32[]{:S(2)}) copy-start(bf16[1280,640]{1,0:T(8,128)(2,1)} %key_ref.5) | copy-start | bytes 4915204
  13.0 12.9 %copy-start.1 = (bf16[1280,640]{1,0:T(8,128)(2,1)S(1)}, bf16[1280,640]{1,0:T(8,128)(2,1)}, u32[]{:S(2)}) copy-start(bf16[1280,640]{1,0:T(8,128)(2,1)} %value_ref.5) | copy-start | bytes 4915204
  15.2 3.9 %collective-permute-start.4 = (bf16[64,1280]{1,0:T(8,128)(2,1)S(1)}, bf16[64,1280]{1,0:T(8,128)(2,1)S(1)}, u32[]{:S(2)}, u32[]{:S(2)}) collective-permute-start(bf16[64,1280]{1,0:T(8,128)(2,1)S(1)} %get-tuple-element.58.refs_0_), channel_id=1, source_target_pairs={{0,96},{1,33},{2,98},{7,39},{32,64},{34,66},{97,65},{103,71}} | collective-permute-start | bytes 491528 | tf_op jit(solution)/shard_map/ppermute | solution.py:297
  16.5 3.5 %collective-permute-start.5 = (bf16[64,1280]{1,0:T(8,128)(2,1)S(1)}, bf16[64,1280]{1,0:T(8,128)(2,1)S(1)}, u32[]{:S(2)}, u32[]{:S(2)}) collective-permute-start(bf16[64,1280]{1,0:T(8,128)(2,1)S(1)} %get-tuple-element.58.refs_0_), channel_id=1, source_target_pairs={{0,8},{1,153},{2,10},{7,159},{32,40},{34,42},{97,249},{103,255}} | collective-permute-start | bytes 491528 | tf_op jit(solution)/shard_map/ppermute | solution.py:297
  17.8 4.0 %collective-permute-start.6 = (bf16[64,1280]{1,0:T(8,128)(2,1)S(1)}, bf16[64,1280]{1,0:T(8,128)(2,1)S(1)}, u32[]{:S(2)}, u32[]{:S(2)}) collective-permute-start(bf16[64,1280]{1,0:T(8,128)(2,1)S(1)} %get-tuple-element.58.refs_0_), channel_id=1, source_target_pairs={{0,104},{1,185},{2,106},{7,191},{32,72},{34,74},{97,217},{103,223}} | collective-permute-start | bytes 491528 | tf_op jit(solution)/shard_map/ppermute | solution.py:297
  21.9 6.5 %collective-permute-start.10 = (bf16[64,1280]{1,0:T(8,128)(2,1)S(1)}, bf16[64,1280]{1,0:T(8,128)(2,1)S(1)}, u32[]{:S(2)}, u32[]{:S(2)}) collective-permute-start(bf16[64,1280]{1,0:T(8,128)(2,1)S(1)} %get-tuple-element.62.refs_0_), channel_id=1, source_target_pairs={{0,150},{1,19},{2,148},{7,21},{8,30},{10,28},{32,182},{33,51},{34,... | collective-permute-start | bytes 491528 | tf_op jit(solution)/shard_map/ppermute | solution.py:297
  23.2 5.2 %collective-permute-start.8 = (bf16[64,1280]{1,0:T(8,128)(2,1)S(1)}, bf16[64,1280]{1,0:T(8,128)(2,1)S(1)}, u32[]{:S(2)}, u32[]{:S(2)}) collective-permute-start(bf16[64,1280]{1,0:T(8,128)(2,1)S(1)} %get-tuple-element.62.refs_0_), channel_id=1, source_target_pairs={{0,6},{1,3},{2,4},{7,5},{8,14},{10,12},{32,38},{33,35},{34,36},{39... | collective-permute-start | bytes 491528 | tf_op jit(solution)/shard_map/ppermute | solution.py:297
  24.5 3.9 %collective-permute-start.9 = (bf16[64,1280]{1,0:T(8,128)(2,1)S(1)}, bf16[64,1280]{1,0:T(8,128)(2,1)S(1)}, u32[]{:S(2)}, u32[]{:S(2)}) collective-permute-start(bf16[64,1280]{1,0:T(8,128)(2,1)S(1)} %get-tuple-element.62.refs_0_), channel_id=1, source_target_pairs={{0,144},{1,17},{2,146},{7,23},{8,24},{10,26},{32,176},{33,49},{34,... | collective-permute-start | bytes 491528 | tf_op jit(solution)/shard_map/ppermute | solution.py:297
  28.5 3.7 %collective-permute-start.11 = (bf16[64,1280]{1,0:T(8,128)(2,1)S(1)}, bf16[64,1280]{1,0:T(8,128)(2,1)S(1)}, u32[]{:S(2)}, u32[]{:S(2)}) collective-permute-start(bf16[64,1280]{1,0:T(8,128)(2,1)S(1)} %get-tuple-element.66.refs_0_), channel_id=1, source_target_pairs={{0,152},{1,9},{2,154},{3,11},{4,156},{5,13},{6,158},{7,15},{8,16},... | collective-permute-start | bytes 491528 | tf_op jit(solution)/shard_map/ppermute | solution.py:297
  32.2 7.9 %collective-permute-start.12 = (bf16[32,1280]{1,0:T(8,128)(2,1)S(1)}, bf16[32,1280]{1,0:T(8,128)(2,1)S(1)}, u32[]{:S(2)}, u32[]{:S(2)}) collective-permute-start(bf16[32,1280]{1,0:T(8,128)(2,1)S(1)} %get-tuple-element.69.refs_0_), channel_id=1, source_target_pairs={{0,32},{1,97},{2,34},{3,99},{4,36},{5,101},{6,38},{7,103},{8,40},{... | collective-permute-start | bytes 245768 | tf_op jit(solution)/shard_map/ppermute | solution.py:297
  33.9 6.3 %collective-permute-start.13 = (bf16[32,1280]{1,0:T(8,128)(2,1)S(1)}, bf16[32,1280]{1,0:T(8,128)(2,1)S(1)}, u32[]{:S(2)}, u32[]{:S(2)}) collective-permute-start(bf16[32,1280]{1,0:T(8,128)(2,1)S(1)} %get-tuple-element.70.refs_2_), channel_id=1, source_target_pairs={{0,2},{1,7},{2,0},{3,5},{4,6},{5,3},{6,4},{7,1},{8,10},{9,15},{10,... | collective-permute-start | bytes 245768 | tf_op jit(solution)/shard_map/ppermute | solution.py:297
  40.3 2.7 %collective-permute-start.14 = (bf16[128,1280]{1,0:T(8,128)(2,1)S(1)}, bf16[128,1280]{1,0:T(8,128)(2,1)S(1)}, u32[]{:S(2)}, u32[]{:S(2)}) collective-permute-start(bf16[128,1280]{1,0:T(8,128)(2,1)S(1)} %get-tuple-element.72.refs_0_), channel_id=1, source_target_pairs={{0,1},{1,0},{2,3},{3,2},{4,5},{5,4},{6,7},{7,6},{8,9},{9,8},{10,11... | collective-permute-start | bytes 983048 | tf_op jit(solution)/shard_map/ppermute | solution.py:297
  40.5 6.7 %collective-permute-start.15 = (bf16[64,1280]{1,0:T(8,128)(2,1)S(1)}, bf16[64,1280]{1,0:T(8,128)(2,1)S(1)}, u32[]{:S(2)}, u32[]{:S(2)}) collective-permute-start(bf16[64,1280]{1,0:T(8,128)(2,1)S(1)} %get-tuple-element.80), channel_id=1, source_target_pairs={{0,2},{1,7},{2,0},{3,5},{4,6},{5,3},{6,4},{7,1},{8,10},{9,15},{10,... | collective-permute-start | bytes 491528 | tf_op jit(solution)/shard_map/ppermute | solution.py:297
  42.8 5.4 %collective-permute-start.16 = (bf16[64,1280]{1,0:T(8,128)(2,1)S(1)}, bf16[64,1280]{1,0:T(8,128)(2,1)S(1)}, u32[]{:S(2)}, u32[]{:S(2)}) collective-permute-start(bf16[64,1280]{1,0:T(8,128)(2,1)S(1)} %get-tuple-element.81), channel_id=1, source_target_pairs={{0,32},{1,97},{2,34},{3,99},{4,36},{5,101},{6,38},{7,103},{8,40},{... | collective-permute-start | bytes 491528 | tf_op jit(solution)/shard_map/ppermute | solution.py:297
  42.9 5.3 %copy-start.8 = (f32[1280]{0:T(1024)S(1)}, f32[1280]{0:T(1024)}, u32[]{:S(2)}) copy-start(f32[1280]{0:T(1024)} %param.15) | copy-start | bytes 15364
  48.2 1.7 %collective-permute-start.17 = (bf16[128,1280]{1,0:T(8,128)(2,1)S(1)}, bf16[128,1280]{1,0:T(8,128)(2,1)S(1)}, u32[]{:S(2)}, u32[]{:S(2)}) collective-permute-start(bf16[128,1280]{1,0:T(8,128)(2,1)S(1)} %get-tuple-element.83.rows_ref), channel_id=1, source_target_pairs={{0,1},{1,0},{2,3},{3,2},{4,5},{5,4},{6,7},{7,6},{8,9},{9,8},{10,11... | collective-permute-start | bytes 983048 | tf_op jit(solution)/shard_map/ppermute | solution.py:297
  48.3 1.6 %copy-start.4 = (bf16[640,1280]{1,0:T(8,128)(2,1)S(1)}, bf16[640,1280]{1,0:T(8,128)(2,1)}, u32[]{:S(2)}) copy-start(bf16[640,1280]{1,0:T(8,128)(2,1)} %out_weight_ref.1) | copy-start | bytes 4915204

commit v8 on v7

--- a/solution.py
+++ b/solution.py
@@ -10,7 +10,7 @@
 HEADS = 10
 HEAD_DIM = 64
 PAIR = 2 * HEAD_DIM
-GROUPS = ((0,), (1, 2), (3, 4))
+GROUPS = ((0, 1), (2, 3), (4,))
 OUT_TILE = 256
 VMEM_BYTES = 16 << 20
 AXES = ("grp", "frame")

time: 56.9 us -> 57.5 us (1.011)
  transfers between devices with their start and end apart: 18 -> 18, of which waited for: 6 -> 7; matrix products, arithmetic and copies ran while one was open for 0% -> 0% of each run, Pallas kernels for 26% -> 25%
where the time goes in v8:
time: 57.5 us; the launch traced here: 57.2 us
  starting transfers between devices  27.8 us (48%)
  Pallas kernels  21.4 us (37%)
  waiting for transfers between devices  6.12 us (11%)
  local copies, waits for them, and re-layouts  1.4 us (2%)
    ppermute x18, starting transfers between devices, move(): return lax.ppermute(value, AXES, pairs)  27.8 us
    pallas_call x15, Pallas kernels, call(): pl.pallas_call(kernel, out_shape=outs, in_specs=[whole] * len(operands),...  21.4 us
    ppermute x18, waiting for transfers between devices, move(): return lax.ppermute(value, AXES, pairs)  6.12 us
    unnamed x18, local copies, waits for them, and re-layouts  1.39 us
  transfers between devices with their start and end apart: 18, of which 7 were waited for; matrix products, arithmetic and copies ran while one was open for 0% of the time, Pallas kernels for 25%

profile of v8, /device:TPU:1, one launch (start us, length us, event | category | flops | bytes accessed | tf_op | source)
XLA Modules:
  0.0 57.2 jit_solution(2596757791373773230)
XLA Ops:
  0.0 3.2 %collective-permute-start = (bf16[512,1280]{1,0:T(8,128)(2,1)}, bf16[512,1280]{1,0:T(8,128)(2,1)S(1)}, u32[]{:S(2)}, u32[]{:S(2)}) collective-permute-start(bf16[512,1280]{1,0:T(8,128)(2,1)} %hidden_ref.1), channel_id=1, source_target_pairs={{0,1},{1,0},{2,3},{3,2},{4,5},{5,4},{6,7},{7,6},{8,9},{9,8},{10,11... | collective-permute-start | bytes 3932168 | tf_op jit(solution)/shard_map/ppermute | solution.py:297
  3.2 0.0 collective-permute-start.7
  3.2 0.0 copy-start.2
  3.3 1.3 %copy-done.2 = bf16[512,1280]{1,0:T(8,128)(2,1)S(1)} copy-done((bf16[512,1280]{1,0:T(8,128)(2,1)S(1)}, bf16[512,1280]{1,0:T(8,128)(2,1)}, u32[]{:S(2)}) %copy-start.2) | copy-done | bytes 1310744
  4.6 0.0 copy-start.6
  4.7 0.0 copy-start.7
  4.7 0.0 copy-start.3
  4.7 1.4 %collective-permute-done.other_ref = bf16[512,1280]{1,0:T(8,128)(2,1)S(1)} collective-permute-done((bf16[512,1280]{1,0:T(8,128)(2,1)}, bf16[512,1280]{1,0:T(8,128)(2,1)S(1)}, u32[]{:S(2)}, u32[]{:S(2)}) %collective-permute-start) | collective-permute-done | bytes 1310752 | tf_op jit(solution)/shard_map/ppermute | solution.py:297
  6.1 0.2 shard_map.83
  6.3 2.8 %collective-permute-start.1 = (bf16[64,1280]{1,0:T(8,128)(2,1)S(1)}, bf16[64,1280]{1,0:T(8,128)(2,1)S(1)}, u32[]{:S(2)}, u32[]{:S(2)}) collective-permute-start(bf16[64,1280]{1,0:T(8,128)(2,1)S(1)} %get-tuple-element.54), channel_id=1, source_target_pairs={{0,32},{1,97}} | collective-permute-start | bytes 491528 | tf_op jit(solution)/shard_map/ppermute | solution.py:297
  9.1 1.3 %collective-permute-start.2 = (bf16[64,1280]{1,0:T(8,128)(2,1)S(1)}, bf16[64,1280]{1,0:T(8,128)(2,1)S(1)}, u32[]{:S(2)}, u32[]{:S(2)}) collective-permute-start(bf16[64,1280]{1,0:T(8,128)(2,1)S(1)} %get-tuple-element.55), channel_id=1, source_target_pairs={{0,2},{1,7}} | collective-permute-start | bytes 491528 | tf_op jit(solution)/shard_map/ppermute | solution.py:297
  10.4 2.5 %collective-permute-start.3 = (bf16[64,1280]{1,0:T(8,128)(2,1)S(1)}, bf16[64,1280]{1,0:T(8,128)(2,1)S(1)}, u32[]{:S(2)}, u32[]{:S(2)}) collective-permute-start(bf16[64,1280]{1,0:T(8,128)(2,1)S(1)} %get-tuple-element.56), channel_id=1, source_target_pairs={{0,34},{1,103}} | collective-permute-start | bytes 491528 | tf_op jit(solution)/shard_map/ppermute | solution.py:297
  12.9 0.0 copy-done.6
  12.9 0.0 copy-done.7
  12.9 0.0 copy-done.5
  12.9 0.0 copy-done.3
  12.9 0.0 copy-start
  13.0 0.0 copy-start.1
  13.0 1.8 %shard_map.84 = (bf16[512,640]{1,0:T(8,128)(2,1)S(1)}, s32[8,1280]{1,0:T(8,128)S(1)}) custom-call(s32[8,1280]{1,0:T(8,128)S(1)} %get-tuple-element.51.bits_ref, bf16[512,1280]{1,0:T(8,128)(2,1)S(1)} %copy-done.3, f32[1,1280]{1,0:T(1,128)S(1)} %reshape.9.gain_ref.refs_3_, f32[1,1280]{1,0:T(1,128)S(1)} %reshape.10.bias_ref.refs_4_, bf16[1280,640]{1,0:T(8,128)(2,1)S(1)} %copy-done.5), custom_call_target="tpu_custom_call" | custom-call | flops 838860800 | bytes 262144 | tf_op jit(solution)/shard_map/pallas_call | solution.py:274
  14.8 0.0 collective-permute-done.1.refs_1_
  14.8 0.0 collective-permute-done.2.refs_2_
  14.8 0.3 collective-permute-done.3.refs_3_
  15.1 0.1 shard_map.85
  15.2 1.3 %collective-permute-start.4 = (bf16[64,1280]{1,0:T(8,128)(2,1)S(1)}, bf16[64,1280]{1,0:T(8,128)(2,1)S(1)}, u32[]{:S(2)}, u32[]{:S(2)}) collective-permute-start(bf16[64,1280]{1,0:T(8,128)(2,1)S(1)} %get-tuple-element.58.refs_0_), channel_id=1, source_target_pairs={{0,96},{1,33},{2,98},{7,39},{32,64},{34,66},{97,65},{103,71}} | collective-permute-start | bytes 491528 | tf_op jit(solution)/shard_map/ppermute | solution.py:297
  16.5 1.3 %collective-permute-start.5 = (bf16[64,1280]{1,0:T(8,128)(2,1)S(1)}, bf16[64,1280]{1,0:T(8,128)(2,1)S(1)}, u32[]{:S(2)}, u32[]{:S(2)}) collective-permute-start(bf16[64,1280]{1,0:T(8,128)(2,1)S(1)} %get-tuple-element.58.refs_0_), channel_id=1, source_target_pairs={{0,8},{1,153},{2,10},{7,159},{32,40},{34,42},{97,249},{103,255}} | collective-permute-start | bytes 491528 | tf_op jit(solution)/shard_map/ppermute | solution.py:297
  17.8 1.3 %collective-permute-start.6 = (bf16[64,1280]{1,0:T(8,128)(2,1)S(1)}, bf16[64,1280]{1,0:T(8,128)(2,1)S(1)}, u32[]{:S(2)}, u32[]{:S(2)}) collective-permute-start(bf16[64,1280]{1,0:T(8,128)(2,1)S(1)} %get-tuple-element.58.refs_0_), channel_id=1, source_target_pairs={{0,104},{1,185},{2,106},{7,191},{32,72},{34,74},{97,217},{103,223}} | collective-permute-start | bytes 491528 | tf_op jit(solution)/shard_map/ppermute | solution.py:297
  19.1 0.0 collective-permute-done.4.refs_1_
  19.2 0.9 %collective-permute-done.5.refs_2_ = bf16[64,1280]{1,0:T(8,128)(2,1)S(1)} collective-permute-done((bf16[64,1280]{1,0:T(8,128)(2,1)S(1)}, bf16[64,1280]{1,0:T(8,128)(2,1)S(1)}, u32[]{:S(2)}, u32[]{:S(2)}) %collective-permute-start.5) | collective-permute-done | bytes 163872 | tf_op jit(solution)/shard_map/ppermute | solution.py:297
  20.1 1.8 %collective-permute-done.6.refs_3_ = bf16[64,1280]{1,0:T(8,128)(2,1)S(1)} collective-permute-done((bf16[64,1280]{1,0:T(8,128)(2,1)S(1)}, bf16[64,1280]{1,0:T(8,128)(2,1)S(1)}, u32[]{:S(2)}, u32[]{:S(2)}) %collective-permute-start.6) | collective-permute-done | bytes 163872 | tf_op jit(solution)/shard_map/ppermute | solution.py:297
  21.8 0.1 shard_map.86
  21.9 1.3 %collective-permute-start.10 = (bf16[64,1280]{1,0:T(8,128)(2,1)S(1)}, bf16[64,1280]{1,0:T(8,128)(2,1)S(1)}, u32[]{:S(2)}, u32[]{:S(2)}) collective-permute-start(bf16[64,1280]{1,0:T(8,128)(2,1)S(1)} %get-tuple-element.62.refs_0_), channel_id=1, source_target_pairs={{0,150},{1,19},{2,148},{7,21},{8,30},{10,28},{32,182},{33,51},{34,... | collective-permute-start | bytes 491528 | tf_op jit(solution)/shard_map/ppermute | solution.py:297
  23.2 1.3 %collective-permute-start.8 = (bf16[64,1280]{1,0:T(8,128)(2,1)S(1)}, bf16[64,1280]{1,0:T(8,128)(2,1)S(1)}, u32[]{:S(2)}, u32[]{:S(2)}) collective-permute-start(bf16[64,1280]{1,0:T(8,128)(2,1)S(1)} %get-tuple-element.62.refs_0_), channel_id=1, source_target_pairs={{0,6},{1,3},{2,4},{7,5},{8,14},{10,12},{32,38},{33,35},{34,36},{39... | collective-permute-start | bytes 491528 | tf_op jit(solution)/shard_map/ppermute | solution.py:297
  24.5 1.3 %collective-permute-start.9 = (bf16[64,1280]{1,0:T(8,128)(2,1)S(1)}, bf16[64,1280]{1,0:T(8,128)(2,1)S(1)}, u32[]{:S(2)}, u32[]{:S(2)}) collective-permute-start(bf16[64,1280]{1,0:T(8,128)(2,1)S(1)} %get-tuple-element.62.refs_0_), channel_id=1, source_target_pairs={{0,144},{1,17},{2,146},{7,23},{8,24},{10,26},{32,176},{33,49},{34,... | collective-permute-start | bytes 491528 | tf_op jit(solution)/shard_map/ppermute | solution.py:297
  25.9 0.0 collective-permute-done.7.refs_1_
  25.9 0.0 copy-done
  25.9 0.0 copy-done.1
  25.9 3.1 %shard_map.87 = (f32[512,512]{1,0:T(8,128)S(1)}, f32[512,512]{1,0:T(8,128)S(1)}, bf16[512,1280]{1,0:T(8,128)(2,1)S(1)}, s32[8,1280]{1,0:T(8,128)S(1)}) custom-call(s32[8,1280]{1,0:T(8,128)S(1)} %get-tuple-element.59.refs_0_, bf16[512,1280]{1,0:T(8,128)(2,1)S(1)} %collective-permute-done.7.refs_1_, bf16[512,1280]{1,0:T(8,128)(2,1)S(1)} %copy-done.3, ...), custom_call_target="tpu_custom_call" | custom-call | flops 536870912 | bytes 262144 | tf_op jit(solution)/shard_map/pallas_call | solution.py:274
  28.9 0.0 collective-permute-done.10.refs_3_
  29.0 0.0 collective-permute-done.8.refs_1_
  29.0 0.0 collective-permute-done.9.refs_2_
  29.0 0.1 shard_map.88
  29.1 1.3 %collective-permute-start.11 = (bf16[64,1280]{1,0:T(8,128)(2,1)S(1)}, bf16[64,1280]{1,0:T(8,128)(2,1)S(1)}, u32[]{:S(2)}, u32[]{:S(2)}) collective-permute-start(bf16[64,1280]{1,0:T(8,128)(2,1)S(1)} %get-tuple-element.66.refs_0_), channel_id=1, source_target_pairs={{0,152},{1,9},{2,154},{3,11},{4,156},{5,13},{6,158},{7,15},{8,16},... | collective-permute-start | bytes 491528 | tf_op jit(solution)/shard_map/ppermute | solution.py:297
  30.4 2.3 %shard_map.89 = (f32[512,512]{1,0:T(8,128)S(1)}, f32[512,512]{1,0:T(8,128)S(1)}, s32[8,1280]{1,0:T(8,128)S(1)}) custom-call(s32[8,1280]{1,0:T(8,128)S(1)} %get-tuple-element.63.refs_0_, bf16[512,1280]{1,0:T(8,128)(2,1)S(1)} %get-tuple-element.64.refs_1_, bf16[512,640]{1,0:T(8,128)(2,1)S(1)} %get-tuple-element.60.refs_5_.refs_2_.query_ref, ...), custom_call_target="tpu_custom_call" | custom-call | flops 536870912 | bytes 262144 | tf_op jit(solution)/shard_map/pallas_call | solution.py:274
  32.7 0.0 collective-permute-done.11.refs_1_
  32.8 1.7 %collective-permute-start.12 = (bf16[32,1280]{1,0:T(8,128)(2,1)S(1)}, bf16[32,1280]{1,0:T(8,128)(2,1)S(1)}, u32[]{:S(2)}, u32[]{:S(2)}) collective-permute-start(bf16[32,1280]{1,0:T(8,128)(2,1)S(1)} %get-tuple-element.69.refs_0_), channel_id=1, source_target_pairs={{0,32},{1,97},{2,34},{3,99},{4,36},{5,101},{6,38},{7,103},{8,40},{... | collective-permute-start | bytes 245768 | tf_op jit(solution)/shard_map/ppermute | solution.py:297
  34.5 3.9 %collective-permute-start.13 = (bf16[32,1280]{1,0:T(8,128)(2,1)S(1)}, bf16[32,1280]{1,0:T(8,128)(2,1)S(1)}, u32[]{:S(2)}, u32[]{:S(2)}) collective-permute-start(bf16[32,1280]{1,0:T(8,128)(2,1)S(1)} %get-tuple-element.70.refs_2_), channel_id=1, source_target_pairs={{0,2},{1,7},{2,0},{3,5},{4,6},{5,3},{6,4},{7,1},{8,10},{9,15},{10,... | collective-permute-start | bytes 245768 | tf_op jit(solution)/shard_map/ppermute | solution.py:297
  38.4 1.7 %shard_map.91 = (f32[512,256]{1,0:T(8,128)S(1)}, f32[512,256]{1,0:T(8,128)S(1)}, s32[8,1280]{1,0:T(8,128)S(1)}) custom-call(s32[8,1280]{1,0:T(8,128)S(1)} %get-tuple-element.67.refs_0_, bf16[512,1280]{1,0:T(8,128)(2,1)S(1)} %get-tuple-element.64.refs_1_, bf16[512,640]{1,0:T(8,128)(2,1)S(1)} %get-tuple-element.60.refs_5_.refs_2_.query_ref, ...), custom_call_target="tpu_custom_call" | custom-call | flops 268435456 | bytes 262144 | tf_op jit(solution)/shard_map/pallas_call | solution.py:274
  40.1 0.0 collective-permute-done.12.refs_1_
  40.2 0.1 collective-permute-done.13.refs_3_
  40.3 0.8 %collective-permute-start.14 = (bf16[128,1280]{1,0:T(8,128)(2,1)S(1)}, bf16[128,1280]{1,0:T(8,128)(2,1)S(1)}, u32[]{:S(2)}, u32[]{:S(2)}) collective-permute-start(bf16[128,1280]{1,0:T(8,128)(2,1)S(1)} %get-tuple-element.72.refs_0_), channel_id=1, source_target_pairs={{0,1},{1,0},{2,3},{3,2},{4,5},{5,4},{6,7},{7,6},{8,9},{9,8},{10,11... | collective-permute-start | bytes 983048 | tf_op jit(solution)/shard_map/ppermute | solution.py:297
  41.0 2.3 %collective-permute-start.15 = (bf16[64,1280]{1,0:T(8,128)(2,1)S(1)}, bf16[64,1280]{1,0:T(8,128)(2,1)S(1)}, u32[]{:S(2)}, u32[]{:S(2)}) collective-permute-start(bf16[64,1280]{1,0:T(8,128)(2,1)S(1)} %get-tuple-element.80), channel_id=1, source_target_pairs={{0,2},{1,7},{2,0},{3,5},{4,6},{5,3},{6,4},{7,1},{8,10},{9,15},{10,... | collective-permute-start | bytes 491528 | tf_op jit(solution)/shard_map/ppermute | solution.py:297
  43.3 0.2 collective-permute-start.16
  43.5 0.0 collective-permute-done.14.refs_1_
  43.5 0.0 copy-start.8
  43.5 4.3 %shard_map.93 = (f32[512,512]{1,0:T(8,128)S(1)}, f32[512,512]{1,0:T(8,128)S(1)}, f32[512,512]{1,0:T(8,128)S(1)}, f32[512,512]{1,0:T(8,128)S(1)}, f32[512,256]{1,...) custom-call(s32[8,1280]{1,0:T(8,128)S(1)} %get-tuple-element.71.bits, ...), custom_call_target="tpu_custom_call", output_to_operand_aliasing={{0}: (8, {}), {1}: (9, {}), {2}: (10, {}), {3}: (11, {}), {... | custom-call | flops 1677721600 | bytes 262144 | tf_op jit(solution)/shard_map/pallas_call | solution.py:274
  47.8 0.0 collective-permute-done.15.refs_0_
  47.8 0.9 %collective-permute-done.16.refs_1_ = bf16[64,1280]{1,0:T(8,128)(2,1)S(1)} collective-permute-done((bf16[64,1280]{1,0:T(8,128)(2,1)S(1)}, bf16[64,1280]{1,0:T(8,128)(2,1)S(1)}, u32[]{:S(2)}, u32[]{:S(2)}) %collective-permute-start.16) | collective-permute-done | bytes 163872 | tf_op jit(solution)/shard_map/ppermute | solution.py:297
  48.7 0.1 collective-permute-start.17
  48.8 0.0 copy-done.8
  48.9 0.0 copy-start.4
  48.9 0.9 %shard_map.95 = (bf16[128,640]{1,0:T(8,128)(2,1)S(1)}, bf16[128,640]{1,0:T(8,128)(2,1)S(1)}, s32[8,1280]{1,0:T(8,128)S(1)}) custom-call(s32[8,1280]{1,0:T(8,128)S(1)} %get-tuple-element.82.bits_ref, bf16[128,1280]{1,0:T(8,128)(2,1)S(1)} %get-tuple-element.83.rows_ref, f32[1,1280]{1,0:T(1,128)S(1)} %reshape.9.gain_ref.refs_3_, ...), custom_call_target="tpu_custom_call" | custom-call | flops 419430400 | bytes 262144 | tf_op jit(solution)/shard_map/pallas_call | solution.py:274
  49.8 0.7 %collective-permute-done.17.rows_ref = bf16[128,1280]{1,0:T(8,128)(2,1)S(1)} collective-permute-done((bf16[128,1280]{1,0:T(8,128)(2,1)S(1)}, bf16[128,1280]{1,0:T(8,128)(2,1)S(1)}, u32[]{:S(2)}, u32[]{:S(2)}) %collective-permute-start.17) | collective-permute-done | bytes 327712 | tf_op jit(solution)/shard_map/ppermute | solution.py:297
  50.4 0.0 copy-done.4
  50.4 6.7 %shard_map.96 = bf16[512,1280]{1,0:T(8,128)(2,1)} custom-call(s32[8,1280]{1,0:T(8,128)S(1)} %get-tuple-element.84.bits_ref, bf16[512,640]{1,0:T(8,128)(2,1)S(1)} %get-tuple-element.60.refs_5_.refs_2_.query_ref, f32[1,1280]{1,0:T(1,128)S(1)} %reshape.9.gain_ref.refs_3_, f32[1,1280]{1,0:T(1,128)S(1)} %reshape.10.bias_ref.refs_4_, ...), custom_call_target="tpu_custom_call" | custom-call | flops 1677721600 | bytes 262144 | tf_op jit(solution)/shard_map/pallas_call | solution.py:274
  (9 shorter events, 0.2 us)
Async XLA Ops:
  0.0 6.1 %collective-permute-start = (bf16[512,1280]{1,0:T(8,128)(2,1)}, bf16[512,1280]{1,0:T(8,128)(2,1)S(1)}, u32[]{:S(2)}, u32[]{:S(2)}) collective-permute-start(bf16[512,1280]{1,0:T(8,128)(2,1)} %hidden_ref.1), channel_id=1, source_target_pairs={{0,1},{1,0},{2,3},{3,2},{4,5},{5,4},{6,7},{7,6},{8,9},{9,8},{10,11... | collective-permute-start | bytes 3932168 | tf_op jit(solution)/shard_map/ppermute | solution.py:297
  3.2 22.6 %collective-permute-start.7 = (bf16[512,1280]{1,0:T(8,128)(2,1)}, bf16[512,1280]{1,0:T(8,128)(2,1)S(1)}, u32[]{:S(2)}, u32[]{:S(2)}) collective-permute-start(bf16[512,1280]{1,0:T(8,128)(2,1)} %hidden_ref.1), channel_id=1, source_target_pairs={{0,1},{1,2},{2,3},{3,4},{4,5},{5,6},{6,7},{7,8},{8,9},{9,10},{10,1... | collective-permute-start | bytes 3932168 | tf_op jit(solution)/shard_map/ppermute | solution.py:297
  3.2 1.3 %copy-start.2 = (bf16[512,1280]{1,0:T(8,128)(2,1)S(1)}, bf16[512,1280]{1,0:T(8,128)(2,1)}, u32[]{:S(2)}) copy-start(bf16[512,1280]{1,0:T(8,128)(2,1)} %hidden_ref.1) | copy-start | bytes 3932164
  4.6 8.3 %copy-start.5 = (bf16[1280,640]{1,0:T(8,128)(2,1)S(1)}, bf16[1280,640]{1,0:T(8,128)(2,1)}, u32[]{:S(2)}) copy-start(bf16[1280,640]{1,0:T(8,128)(2,1)} %weight_ref.1) | copy-start | bytes 4915204
  4.6 8.2 %copy-start.6 = (f32[1280]{0:T(1024)S(1)}, f32[1280]{0:T(1024)}, u32[]{:S(2)}) copy-start(f32[1280]{0:T(1024)} %param.10) | copy-start | bytes 15364
  4.7 8.2 %copy-start.7 = (f32[1280]{0:T(1024)S(1)}, f32[1280]{0:T(1024)}, u32[]{:S(2)}) copy-start(f32[1280]{0:T(1024)} %param.9) | copy-start | bytes 15364
  4.7 8.3 %copy-start.3 = (bf16[512,1280]{1,0:T(8,128)(2,1)S(1)}, bf16[512,1280]{1,0:T(8,128)(2,1)}, u32[]{:S(2)}) copy-start(bf16[512,1280]{1,0:T(8,128)(2,1)} %hidden_ref.1) | copy-start | bytes 3932164
  6.3 8.5 %collective-permute-start.1 = (bf16[64,1280]{1,0:T(8,128)(2,1)S(1)}, bf16[64,1280]{1,0:T(8,128)(2,1)S(1)}, u32[]{:S(2)}, u32[]{:S(2)}) collective-permute-start(bf16[64,1280]{1,0:T(8,128)(2,1)S(1)} %get-tuple-element.54), channel_id=1, source_target_pairs={{0,32},{1,97}} | collective-permute-start | bytes 491528 | tf_op jit(solution)/shard_map/ppermute | solution.py:297
  9.1 5.7 %collective-permute-start.2 = (bf16[64,1280]{1,0:T(8,128)(2,1)S(1)}, bf16[64,1280]{1,0:T(8,128)(2,1)S(1)}, u32[]{:S(2)}, u32[]{:S(2)}) collective-permute-start(bf16[64,1280]{1,0:T(8,128)(2,1)S(1)} %get-tuple-element.55), channel_id=1, source_target_pairs={{0,2},{1,7}} | collective-permute-start | bytes 491528 | tf_op jit(solution)/shard_map/ppermute | solution.py:297
  10.4 4.7 %collective-permute-start.3 = (bf16[64,1280]{1,0:T(8,128)(2,1)S(1)}, bf16[64,1280]{1,0:T(8,128)(2,1)S(1)}, u32[]{:S(2)}, u32[]{:S(2)}) collective-permute-start(bf16[64,1280]{1,0:T(8,128)(2,1)S(1)} %get-tuple-element.56), channel_id=1, source_target_pairs={{0,34},{1,103}} | collective-permute-start | bytes 491528 | tf_op jit(solution)/shard_map/ppermute | solution.py:297
  12.9 12.9 %copy-start = (bf16[1280,640]{1,0:T(8,128)(2,1)S(1)}, bf16[1280,640]{1,0:T(8,128)(2,1)}, u32[]{:S(2)}) copy-start(bf16[1280,640]{1,0:T(8,128)(2,1)} %key_ref.5) | copy-start | bytes 4915204
  13.0 12.9 %copy-start.1 = (bf16[1280,640]{1,0:T(8,128)(2,1)S(1)}, bf16[1280,640]{1,0:T(8,128)(2,1)}, u32[]{:S(2)}) copy-start(bf16[1280,640]{1,0:T(8,128)(2,1)} %value_ref.5) | copy-start | bytes 4915204
  15.2 3.9 %collective-permute-start.4 = (bf16[64,1280]{1,0:T(8,128)(2,1)S(1)}, bf16[64,1280]{1,0:T(8,128)(2,1)S(1)}, u32[]{:S(2)}, u32[]{:S(2)}) collective-permute-start(bf16[64,1280]{1,0:T(8,128)(2,1)S(1)} %get-tuple-element.58.refs_0_), channel_id=1, source_target_pairs={{0,96},{1,33},{2,98},{7,39},{32,64},{34,66},{97,65},{103,71}} | collective-permute-start | bytes 491528 | tf_op jit(solution)/shard_map/ppermute | solution.py:297
  16.5 3.5 %collective-permute-start.5 = (bf16[64,1280]{1,0:T(8,128)(2,1)S(1)}, bf16[64,1280]{1,0:T(8,128)(2,1)S(1)}, u32[]{:S(2)}, u32[]{:S(2)}) collective-permute-start(bf16[64,1280]{1,0:T(8,128)(2,1)S(1)} %get-tuple-element.58.refs_0_), channel_id=1, source_target_pairs={{0,8},{1,153},{2,10},{7,159},{32,40},{34,42},{97,249},{103,255}} | collective-permute-start | bytes 491528 | tf_op jit(solution)/shard_map/ppermute | solution.py:297
  17.8 4.0 %collective-permute-start.6 = (bf16[64,1280]{1,0:T(8,128)(2,1)S(1)}, bf16[64,1280]{1,0:T(8,128)(2,1)S(1)}, u32[]{:S(2)}, u32[]{:S(2)}) collective-permute-start(bf16[64,1280]{1,0:T(8,128)(2,1)S(1)} %get-tuple-element.58.refs_0_), channel_id=1, source_target_pairs={{0,104},{1,185},{2,106},{7,191},{32,72},{34,74},{97,217},{103,223}} | collective-permute-start | bytes 491528 | tf_op jit(solution)/shard_map/ppermute | solution.py:297
  21.9 7.0 %collective-permute-start.10 = (bf16[64,1280]{1,0:T(8,128)(2,1)S(1)}, bf16[64,1280]{1,0:T(8,128)(2,1)S(1)}, u32[]{:S(2)}, u32[]{:S(2)}) collective-permute-start(bf16[64,1280]{1,0:T(8,128)(2,1)S(1)} %get-tuple-element.62.refs_0_), channel_id=1, source_target_pairs={{0,150},{1,19},{2,148},{7,21},{8,30},{10,28},{32,182},{33,51},{34,... | collective-permute-start | bytes 491528 | tf_op jit(solution)/shard_map/ppermute | solution.py:297
  23.2 5.7 %collective-permute-start.8 = (bf16[64,1280]{1,0:T(8,128)(2,1)S(1)}, bf16[64,1280]{1,0:T(8,128)(2,1)S(1)}, u32[]{:S(2)}, u32[]{:S(2)}) collective-permute-start(bf16[64,1280]{1,0:T(8,128)(2,1)S(1)} %get-tuple-element.62.refs_0_), channel_id=1, source_target_pairs={{0,6},{1,3},{2,4},{7,5},{8,14},{10,12},{32,38},{33,35},{34,36},{39... | collective-permute-start | bytes 491528 | tf_op jit(solution)/shard_map/ppermute | solution.py:297
  24.5 4.4 %collective-permute-start.9 = (bf16[64,1280]{1,0:T(8,128)(2,1)S(1)}, bf16[64,1280]{1,0:T(8,128)(2,1)S(1)}, u32[]{:S(2)}, u32[]{:S(2)}) collective-permute-start(bf16[64,1280]{1,0:T(8,128)(2,1)S(1)} %get-tuple-element.62.refs_0_), channel_id=1, source_target_pairs={{0,144},{1,17},{2,146},{7,23},{8,24},{10,26},{32,176},{33,49},{34,... | collective-permute-start | bytes 491528 | tf_op jit(solution)/shard_map/ppermute | solution.py:297
  29.1 3.6 %collective-permute-start.11 = (bf16[64,1280]{1,0:T(8,128)(2,1)S(1)}, bf16[64,1280]{1,0:T(8,128)(2,1)S(1)}, u32[]{:S(2)}, u32[]{:S(2)}) collective-permute-start(bf16[64,1280]{1,0:T(8,128)(2,1)S(1)} %get-tuple-element.66.refs_0_), channel_id=1, source_target_pairs={{0,152},{1,9},{2,154},{3,11},{4,156},{5,13},{6,158},{7,15},{8,16},... | collective-permute-start | bytes 491528 | tf_op jit(solution)/shard_map/ppermute | solution.py:297
  32.8 7.4 %collective-permute-start.12 = (bf16[32,1280]{1,0:T(8,128)(2,1)S(1)}, bf16[32,1280]{1,0:T(8,128)(2,1)S(1)}, u32[]{:S(2)}, u32[]{:S(2)}) collective-permute-start(bf16[32,1280]{1,0:T(8,128)(2,1)S(1)} %get-tuple-element.69.refs_0_), channel_id=1, source_target_pairs={{0,32},{1,97},{2,34},{3,99},{4,36},{5,101},{6,38},{7,103},{8,40},{... | collective-permute-start | bytes 245768 | tf_op jit(solution)/shard_map/ppermute | solution.py:297
  34.5 5.8 %collective-permute-start.13 = (bf16[32,1280]{1,0:T(8,128)(2,1)S(1)}, bf16[32,1280]{1,0:T(8,128)(2,1)S(1)}, u32[]{:S(2)}, u32[]{:S(2)}) collective-permute-start(bf16[32,1280]{1,0:T(8,128)(2,1)S(1)} %get-tuple-element.70.refs_2_), channel_id=1, source_target_pairs={{0,2},{1,7},{2,0},{3,5},{4,6},{5,3},{6,4},{7,1},{8,10},{9,15},{10,... | collective-permute-start | bytes 245768 | tf_op jit(solution)/shard_map/ppermute | solution.py:297
  40.3 3.2 %collective-permute-start.14 = (bf16[128,1280]{1,0:T(8,128)(2,1)S(1)}, bf16[128,1280]{1,0:T(8,128)(2,1)S(1)}, u32[]{:S(2)}, u32[]{:S(2)}) collective-permute-start(bf16[128,1280]{1,0:T(8,128)(2,1)S(1)} %get-tuple-element.72.refs_0_), channel_id=1, source_target_pairs={{0,1},{1,0},{2,3},{3,2},{4,5},{5,4},{6,7},{7,6},{8,9},{9,8},{10,11... | collective-permute-start | bytes 983048 | tf_op jit(solution)/shard_map/ppermute | solution.py:297
  41.0 6.7 %collective-permute-start.15 = (bf16[64,1280]{1,0:T(8,128)(2,1)S(1)}, bf16[64,1280]{1,0:T(8,128)(2,1)S(1)}, u32[]{:S(2)}, u32[]{:S(2)}) collective-permute-start(bf16[64,1280]{1,0:T(8,128)(2,1)S(1)} %get-tuple-element.80), channel_id=1, source_target_pairs={{0,2},{1,7},{2,0},{3,5},{4,6},{5,3},{6,4},{7,1},{8,10},{9,15},{10,... | collective-permute-start | bytes 491528 | tf_op jit(solution)/shard_map/ppermute | solution.py:297
  43.3 5.4 %collective-permute-start.16 = (bf16[64,1280]{1,0:T(8,128)(2,1)S(1)}, bf16[64,1280]{1,0:T(8,128)(2,1)S(1)}, u32[]{:S(2)}, u32[]{:S(2)}) collective-permute-start(bf16[64,1280]{1,0:T(8,128)(2,1)S(1)} %get-tuple-element.81), channel_id=1, source_target_pairs={{0,32},{1,97},{2,34},{3,99},{4,36},{5,101},{6,38},{7,103},{8,40},{... | collective-permute-start | bytes 491528 | tf_op jit(solution)/shard_map/ppermute | solution.py:297
  43.5 5.3 %copy-start.8 = (f32[1280]{0:T(1024)S(1)}, f32[1280]{0:T(1024)}, u32[]{:S(2)}) copy-start(f32[1280]{0:T(1024)} %param.15) | copy-start | bytes 15364
  48.7 1.7 %collective-permute-start.17 = (bf16[128,1280]{1,0:T(8,128)(2,1)S(1)}, bf16[128,1280]{1,0:T(8,128)(2,1)S(1)}, u32[]{:S(2)}, u32[]{:S(2)}) collective-permute-start(bf16[128,1280]{1,0:T(8,128)(2,1)S(1)} %get-tuple-element.83.rows_ref), channel_id=1, source_target_pairs={{0,1},{1,0},{2,3},{3,2},{4,5},{5,4},{6,7},{7,6},{8,9},{9,8},{10,11... | collective-permute-start | bytes 983048 | tf_op jit(solution)/shard_map/ppermute | solution.py:297
  48.9 1.6 %copy-start.4 = (bf16[640,1280]{1,0:T(8,128)(2,1)S(1)}, bf16[640,1280]{1,0:T(8,128)(2,1)}, u32[]{:S(2)}) copy-start(bf16[640,1280]{1,0:T(8,128)(2,1)} %out_weight_ref.1) | copy-start | bytes 4915204

commit v9 on v7

--- a/solution.py
+++ b/solution.py
@@ -21,7 +21,7 @@
 FIRST, SECOND = ((0, 1),), ((0, 3), (1, 2))
 ROUNDS = (
     ({"x": FIRST}, {"y": FIRST}, {"x": FIRST, "y": FIRST}),
-    ({"x": SECOND}, {"z": ((0, 1),)}, {"x": SECOND, "z": ((0, 1),)}),
+    ({"x": SECOND, "z": ((0, 1),)}, {"x": SECOND}, {"z": ((0, 1),)}),
     ({"y": SECOND}, {"z": ((0, 6), (1, 3))}, {"y": SECOND, "z": ((0, 6), (1, 3))}),
     ({"z": ((0, 7), (1, 2), (3, 4), (6, 5))},),
 )

time: 56.9 us -> 56.6 us (level)
  waiting for transfers between devices: 6.06 us -> 4.69 us
  starting transfers between devices: 27.3 us -> 28.3 us
    ppermute x18, waiting for transfers between devices: 6.06 us -> 4.69 us  [move(): return lax.ppermute(value, AXES, pairs)]
    ppermute x18, starting transfers between devices: 27.3 us -> 28.3 us  [move(): return lax.ppermute(value, AXES, pairs)]
  transfers between devices with their start and end apart: 18 -> 18, of which waited for: 6 -> 5; matrix products, arithmetic and copies ran while one was open for 0% -> 0% of each run, Pallas kernels for 26% -> 26%
where the time goes in v9:
time: 56.6 us; the launch traced here: 56.3 us
  starting transfers between devices  28.3 us (50%)
  Pallas kernels  21.4 us (38%)
  waiting for transfers between devices  4.69 us (8%)
  local copies, waits for them, and re-layouts  1.4 us (2%)
    ppermute x18, starting transfers between devices, move(): return lax.ppermute(value, AXES, pairs)  28.3 us
    pallas_call x15, Pallas kernels, call(): pl.pallas_call(kernel, out_shape=outs, in_specs=[whole] * len(operands),...  21.4 us
    ppermute x18, waiting for transfers between devices, move(): return lax.ppermute(value, AXES, pairs)  4.69 us
    unnamed x18, local copies, waits for them, and re-layouts  1.39 us
  transfers between devices with their start and end apart: 18, of which 5 were waited for; matrix products, arithmetic and copies ran while one was open for 0% of the time, Pallas kernels for 26%

profile of v9, /device:TPU:1, one launch (start us, length us, event | category | flops | bytes accessed | tf_op | source)
XLA Modules:
  0.0 56.3 jit_solution(15135079217704810629)
XLA Ops:
  0.0 3.2 %collective-permute-start = (bf16[512,1280]{1,0:T(8,128)(2,1)}, bf16[512,1280]{1,0:T(8,128)(2,1)S(1)}, u32[]{:S(2)}, u32[]{:S(2)}) collective-permute-start(bf16[512,1280]{1,0:T(8,128)(2,1)} %hidden_ref.1), channel_id=1, source_target_pairs={{0,1},{1,0},{2,3},{3,2},{4,5},{5,4},{6,7},{7,6},{8,9},{9,8},{10,11... | collective-permute-start | bytes 3932168 | tf_op jit(solution)/shard_map/ppermute | solution.py:297
  3.2 0.0 collective-permute-start.7
  3.2 0.0 copy-start.2
  3.3 1.3 %copy-done.2 = bf16[512,1280]{1,0:T(8,128)(2,1)S(1)} copy-done((bf16[512,1280]{1,0:T(8,128)(2,1)S(1)}, bf16[512,1280]{1,0:T(8,128)(2,1)}, u32[]{:S(2)}) %copy-start.2) | copy-done | bytes 1310744
  4.6 0.0 copy-start.5
  4.6 0.0 copy-start.6
  4.7 0.0 copy-start.7
  4.7 0.0 copy-start.3
  4.7 1.4 %collective-permute-done.other_ref = bf16[512,1280]{1,0:T(8,128)(2,1)S(1)} collective-permute-done((bf16[512,1280]{1,0:T(8,128)(2,1)}, bf16[512,1280]{1,0:T(8,128)(2,1)S(1)}, u32[]{:S(2)}, u32[]{:S(2)}) %collective-permute-start) | collective-permute-done | bytes 1310752 | tf_op jit(solution)/shard_map/ppermute | solution.py:297
  6.1 0.2 shard_map.83
  6.3 2.8 %collective-permute-start.1 = (bf16[64,1280]{1,0:T(8,128)(2,1)S(1)}, bf16[64,1280]{1,0:T(8,128)(2,1)S(1)}, u32[]{:S(2)}, u32[]{:S(2)}) collective-permute-start(bf16[64,1280]{1,0:T(8,128)(2,1)S(1)} %get-tuple-element.54), channel_id=1, source_target_pairs={{0,32},{1,97}} | collective-permute-start | bytes 491528 | tf_op jit(solution)/shard_map/ppermute | solution.py:297
  9.1 1.3 %collective-permute-start.2 = (bf16[64,1280]{1,0:T(8,128)(2,1)S(1)}, bf16[64,1280]{1,0:T(8,128)(2,1)S(1)}, u32[]{:S(2)}, u32[]{:S(2)}) collective-permute-start(bf16[64,1280]{1,0:T(8,128)(2,1)S(1)} %get-tuple-element.55), channel_id=1, source_target_pairs={{0,2},{1,7}} | collective-permute-start | bytes 491528 | tf_op jit(solution)/shard_map/ppermute | solution.py:297
  10.4 2.5 %collective-permute-start.3 = (bf16[64,1280]{1,0:T(8,128)(2,1)S(1)}, bf16[64,1280]{1,0:T(8,128)(2,1)S(1)}, u32[]{:S(2)}, u32[]{:S(2)}) collective-permute-start(bf16[64,1280]{1,0:T(8,128)(2,1)S(1)} %get-tuple-element.56), channel_id=1, source_target_pairs={{0,34},{1,103}} | collective-permute-start | bytes 491528 | tf_op jit(solution)/shard_map/ppermute | solution.py:297
  12.9 0.0 copy-done.6
  12.9 0.0 copy-done.7
  12.9 0.0 copy-done.5
  12.9 0.0 copy-done.3
  12.9 0.0 copy-start
  13.0 0.0 copy-start.1
  13.0 1.8 %shard_map.84 = (bf16[512,640]{1,0:T(8,128)(2,1)S(1)}, s32[8,1280]{1,0:T(8,128)S(1)}) custom-call(s32[8,1280]{1,0:T(8,128)S(1)} %get-tuple-element.51.bits_ref, bf16[512,1280]{1,0:T(8,128)(2,1)S(1)} %copy-done.3, f32[1,1280]{1,0:T(1,128)S(1)} %reshape.9.gain_ref.refs_3_, f32[1,1280]{1,0:T(1,128)S(1)} %reshape.10.bias_ref.refs_4_, bf16[1280,640]{1,0:T(8,128)(2,1)S(1)} %copy-done.5), custom_call_target="tpu_custom_call" | custom-call | flops 838860800 | bytes 262144 | tf_op jit(solution)/shard_map/pallas_call | solution.py:274
  14.8 0.0 collective-permute-done.1.refs_1_
  14.8 0.0 collective-permute-done.2.refs_2_
  14.8 0.3 collective-permute-done.3.refs_3_
  15.1 0.1 shard_map.85
  15.2 1.9 %collective-permute-start.4 = (bf16[64,1280]{1,0:T(8,128)(2,1)S(1)}, bf16[64,1280]{1,0:T(8,128)(2,1)S(1)}, u32[]{:S(2)}, u32[]{:S(2)}) collective-permute-start(bf16[64,1280]{1,0:T(8,128)(2,1)S(1)} %get-tuple-element.58.refs_0_), channel_id=1, source_target_pairs={{0,104},{1,185},{2,106},{7,191},{32,72},{34,74},{97,217},{103,223}} | collective-permute-start | bytes 491528 | tf_op jit(solution)/shard_map/ppermute | solution.py:297
  17.2 1.3 %collective-permute-start.5 = (bf16[64,1280]{1,0:T(8,128)(2,1)S(1)}, bf16[64,1280]{1,0:T(8,128)(2,1)S(1)}, u32[]{:S(2)}, u32[]{:S(2)}) collective-permute-start(bf16[64,1280]{1,0:T(8,128)(2,1)S(1)} %get-tuple-element.58.refs_0_), channel_id=1, source_target_pairs={{0,96},{1,33},{2,98},{7,39},{32,64},{34,66},{97,65},{103,71}} | collective-permute-start | bytes 491528 | tf_op jit(solution)/shard_map/ppermute | solution.py:297
  18.5 1.3 %collective-permute-start.6 = (bf16[64,1280]{1,0:T(8,128)(2,1)S(1)}, bf16[64,1280]{1,0:T(8,128)(2,1)S(1)}, u32[]{:S(2)}, u32[]{:S(2)}) collective-permute-start(bf16[64,1280]{1,0:T(8,128)(2,1)S(1)} %get-tuple-element.58.refs_0_), channel_id=1, source_target_pairs={{0,8},{1,153},{2,10},{7,159},{32,40},{34,42},{97,249},{103,255}} | collective-permute-start | bytes 491528 | tf_op jit(solution)/shard_map/ppermute | solution.py:297
  19.8 0.0 collective-permute-done.4.refs_1_
  19.8 0.9 %collective-permute-done.5.refs_2_ = bf16[64,1280]{1,0:T(8,128)(2,1)S(1)} collective-permute-done((bf16[64,1280]{1,0:T(8,128)(2,1)S(1)}, bf16[64,1280]{1,0:T(8,128)(2,1)S(1)}, u32[]{:S(2)}, u32[]{:S(2)}) %collective-permute-start.5) | collective-permute-done | bytes 163872 | tf_op jit(solution)/shard_map/ppermute | solution.py:297
  20.7 1.3 %collective-permute-done.6.refs_3_ = bf16[64,1280]{1,0:T(8,128)(2,1)S(1)} collective-permute-done((bf16[64,1280]{1,0:T(8,128)(2,1)S(1)}, bf16[64,1280]{1,0:T(8,128)(2,1)S(1)}, u32[]{:S(2)}, u32[]{:S(2)}) %collective-permute-start.6) | collective-permute-done | bytes 163872 | tf_op jit(solution)/shard_map/ppermute | solution.py:297
  22.0 0.1 shard_map.86
  22.1 1.3 %collective-permute-start.10 = (bf16[64,1280]{1,0:T(8,128)(2,1)S(1)}, bf16[64,1280]{1,0:T(8,128)(2,1)S(1)}, u32[]{:S(2)}, u32[]{:S(2)}) collective-permute-start(bf16[64,1280]{1,0:T(8,128)(2,1)S(1)} %get-tuple-element.62.refs_0_), channel_id=1, source_target_pairs={{0,150},{1,19},{2,148},{7,21},{8,30},{10,28},{32,182},{33,51},{34,... | collective-permute-start | bytes 491528 | tf_op jit(solution)/shard_map/ppermute | solution.py:297
  23.4 1.3 %collective-permute-start.8 = (bf16[64,1280]{1,0:T(8,128)(2,1)S(1)}, bf16[64,1280]{1,0:T(8,128)(2,1)S(1)}, u32[]{:S(2)}, u32[]{:S(2)}) collective-permute-start(bf16[64,1280]{1,0:T(8,128)(2,1)S(1)} %get-tuple-element.62.refs_0_), channel_id=1, source_target_pairs={{0,6},{1,3},{2,4},{7,5},{8,14},{10,12},{32,38},{33,35},{34,36},{39... | collective-permute-start | bytes 491528 | tf_op jit(solution)/shard_map/ppermute | solution.py:297
  24.7 1.3 %collective-permute-start.9 = (bf16[64,1280]{1,0:T(8,128)(2,1)S(1)}, bf16[64,1280]{1,0:T(8,128)(2,1)S(1)}, u32[]{:S(2)}, u32[]{:S(2)}) collective-permute-start(bf16[64,1280]{1,0:T(8,128)(2,1)S(1)} %get-tuple-element.62.refs_0_), channel_id=1, source_target_pairs={{0,144},{1,17},{2,146},{7,23},{8,24},{10,26},{32,176},{33,49},{34,... | collective-permute-start | bytes 491528 | tf_op jit(solution)/shard_map/ppermute | solution.py:297
  26.0 0.0 collective-permute-done.7.refs_1_
  26.1 0.0 copy-done
  26.1 0.0 copy-done.1
  26.1 2.5 %shard_map.87 = (f32[512,256]{1,0:T(8,128)S(1)}, f32[512,256]{1,0:T(8,128)S(1)}, bf16[512,1280]{1,0:T(8,128)(2,1)S(1)}, s32[8,1280]{1,0:T(8,128)S(1)}) custom-call(s32[8,1280]{1,0:T(8,128)S(1)} %get-tuple-element.59.refs_0_, bf16[512,1280]{1,0:T(8,128)(2,1)S(1)} %collective-permute-done.7.refs_1_, bf16[512,1280]{1,0:T(8,128)(2,1)S(1)} %copy-done.3, ...), custom_call_target="tpu_custom_call" | custom-call | flops 268435456 | bytes 262144 | tf_op jit(solution)/shard_map/pallas_call | solution.py:274
  28.6 0.0 collective-permute-done.10.refs_3_
  28.6 0.0 collective-permute-done.8.refs_1_
  28.6 0.0 collective-permute-done.9.refs_2_
  28.6 0.1 shard_map.88
  28.7 1.3 %collective-permute-start.11 = (bf16[64,1280]{1,0:T(8,128)(2,1)S(1)}, bf16[64,1280]{1,0:T(8,128)(2,1)S(1)}, u32[]{:S(2)}, u32[]{:S(2)}) collective-permute-start(bf16[64,1280]{1,0:T(8,128)(2,1)S(1)} %get-tuple-element.66.refs_0_), channel_id=1, source_target_pairs={{0,152},{1,9},{2,154},{3,11},{4,156},{5,13},{6,158},{7,15},{8,16},... | collective-permute-start | bytes 491528 | tf_op jit(solution)/shard_map/ppermute | solution.py:297
  30.0 2.3 %shard_map.89 = (f32[512,512]{1,0:T(8,128)S(1)}, f32[512,512]{1,0:T(8,128)S(1)}, s32[8,1280]{1,0:T(8,128)S(1)}) custom-call(s32[8,1280]{1,0:T(8,128)S(1)} %get-tuple-element.63.refs_0_, bf16[512,1280]{1,0:T(8,128)(2,1)S(1)} %get-tuple-element.64.refs_1_, bf16[512,640]{1,0:T(8,128)(2,1)S(1)} %get-tuple-element.60.refs_5_.refs_2_.query_ref, ...), custom_call_target="tpu_custom_call" | custom-call | flops 536870912 | bytes 262144 | tf_op jit(solution)/shard_map/pallas_call | solution.py:274
  32.4 0.0 collective-permute-done.11.refs_1_
  32.4 1.9 %collective-permute-start.12 = (bf16[32,1280]{1,0:T(8,128)(2,1)S(1)}, bf16[32,1280]{1,0:T(8,128)(2,1)S(1)}, u32[]{:S(2)}, u32[]{:S(2)}) collective-permute-start(bf16[32,1280]{1,0:T(8,128)(2,1)S(1)} %get-tuple-element.69.refs_0_), channel_id=1, source_target_pairs={{0,32},{1,97},{2,34},{3,99},{4,36},{5,101},{6,38},{7,103},{8,40},{... | collective-permute-start | bytes 245768 | tf_op jit(solution)/shard_map/ppermute | solution.py:297
  34.3 3.1 %collective-permute-start.13 = (bf16[32,1280]{1,0:T(8,128)(2,1)S(1)}, bf16[32,1280]{1,0:T(8,128)(2,1)S(1)}, u32[]{:S(2)}, u32[]{:S(2)}) collective-permute-start(bf16[32,1280]{1,0:T(8,128)(2,1)S(1)} %get-tuple-element.70.refs_2_), channel_id=1, source_target_pairs={{0,2},{1,7},{2,0},{3,5},{4,6},{5,3},{6,4},{7,1},{8,10},{9,15},{10,... | collective-permute-start | bytes 245768 | tf_op jit(solution)/shard_map/ppermute | solution.py:297
  37.5 2.3 %shard_map.91 = (f32[512,512]{1,0:T(8,128)S(1)}, f32[512,512]{1,0:T(8,128)S(1)}, s32[8,1280]{1,0:T(8,128)S(1)}) custom-call(s32[8,1280]{1,0:T(8,128)S(1)} %get-tuple-element.67.refs_0_, bf16[512,1280]{1,0:T(8,128)(2,1)S(1)} %get-tuple-element.64.refs_1_, bf16[512,640]{1,0:T(8,128)(2,1)S(1)} %get-tuple-element.60.refs_5_.refs_2_.query_ref, ...), custom_call_target="tpu_custom_call" | custom-call | flops 536870912 | bytes 262144 | tf_op jit(solution)/shard_map/pallas_call | solution.py:274
  39.8 0.0 collective-permute-done.12.refs_1_
  39.8 0.0 collective-permute-done.13.refs_3_
  39.9 0.6 %collective-permute-start.14 = (bf16[128,1280]{1,0:T(8,128)(2,1)S(1)}, bf16[128,1280]{1,0:T(8,128)(2,1)S(1)}, u32[]{:S(2)}, u32[]{:S(2)}) collective-permute-start(bf16[128,1280]{1,0:T(8,128)(2,1)S(1)} %get-tuple-element.72.refs_0_), channel_id=1, source_target_pairs={{0,1},{1,0},{2,3},{3,2},{4,5},{5,4},{6,7},{7,6},{8,9},{9,8},{10,11... | collective-permute-start | bytes 983048 | tf_op jit(solution)/shard_map/ppermute | solution.py:297
  40.5 1.9 %collective-permute-start.15 = (bf16[64,1280]{1,0:T(8,128)(2,1)S(1)}, bf16[64,1280]{1,0:T(8,128)(2,1)S(1)}, u32[]{:S(2)}, u32[]{:S(2)}) collective-permute-start(bf16[64,1280]{1,0:T(8,128)(2,1)S(1)} %get-tuple-element.80), channel_id=1, source_target_pairs={{0,2},{1,7},{2,0},{3,5},{4,6},{5,3},{6,4},{7,1},{8,10},{9,15},{10,... | collective-permute-start | bytes 491528 | tf_op jit(solution)/shard_map/ppermute | solution.py:297
  42.4 1.1 %collective-permute-start.16 = (bf16[64,1280]{1,0:T(8,128)(2,1)S(1)}, bf16[64,1280]{1,0:T(8,128)(2,1)S(1)}, u32[]{:S(2)}, u32[]{:S(2)}) collective-permute-start(bf16[64,1280]{1,0:T(8,128)(2,1)S(1)} %get-tuple-element.81), channel_id=1, source_target_pairs={{0,32},{1,97},{2,34},{3,99},{4,36},{5,101},{6,38},{7,103},{8,40},{... | collective-permute-start | bytes 491528 | tf_op jit(solution)/shard_map/ppermute | solution.py:297
  43.5 0.0 collective-permute-done.14.refs_1_
  43.5 4.3 %shard_map.93 = (f32[512,256]{1,0:T(8,128)S(1)}, f32[512,256]{1,0:T(8,128)S(1)}, f32[512,512]{1,0:T(8,128)S(1)}, f32[512,512]{1,0:T(8,128)S(1)}, f32[512,512]{1,...) custom-call(s32[8,1280]{1,0:T(8,128)S(1)} %get-tuple-element.71.bits, ...), custom_call_target="tpu_custom_call", output_to_operand_aliasing={{0}: (8, {}), {1}: (9, {}), {2}: (10, {}), {3}: (11, {}), {... | custom-call | flops 1677721600 | bytes 262144 | tf_op jit(solution)/shard_map/pallas_call | solution.py:274
  47.8 0.0 collective-permute-done.15.refs_0_
  47.8 0.0 collective-permute-done.16.refs_1_
  47.9 0.1 collective-permute-start.17
  48.0 0.0 copy-done.8
  48.0 0.0 copy-start.4
  48.0 0.9 %shard_map.95 = (bf16[128,640]{1,0:T(8,128)(2,1)S(1)}, bf16[128,640]{1,0:T(8,128)(2,1)S(1)}, s32[8,1280]{1,0:T(8,128)S(1)}) custom-call(s32[8,1280]{1,0:T(8,128)S(1)} %get-tuple-element.82.bits_ref, bf16[128,1280]{1,0:T(8,128)(2,1)S(1)} %get-tuple-element.83.rows_ref, f32[1,1280]{1,0:T(1,128)S(1)} %reshape.9.gain_ref.refs_3_, ...), custom_call_target="tpu_custom_call" | custom-call | flops 419430400 | bytes 262144 | tf_op jit(solution)/shard_map/pallas_call | solution.py:274
  48.9 0.7 %collective-permute-done.17.rows_ref = bf16[128,1280]{1,0:T(8,128)(2,1)S(1)} collective-permute-done((bf16[128,1280]{1,0:T(8,128)(2,1)S(1)}, bf16[128,1280]{1,0:T(8,128)(2,1)S(1)}, u32[]{:S(2)}, u32[]{:S(2)}) %collective-permute-start.17) | collective-permute-done | bytes 327712 | tf_op jit(solution)/shard_map/ppermute | solution.py:297
  49.6 0.0 copy-done.4
  49.6 6.7 %shard_map.96 = bf16[512,1280]{1,0:T(8,128)(2,1)} custom-call(s32[8,1280]{1,0:T(8,128)S(1)} %get-tuple-element.84.bits_ref, bf16[512,640]{1,0:T(8,128)(2,1)S(1)} %get-tuple-element.60.refs_5_.refs_2_.query_ref, f32[1,1280]{1,0:T(1,128)S(1)} %reshape.9.gain_ref.refs_3_, f32[1,1280]{1,0:T(1,128)S(1)} %reshape.10.bias_ref.refs_4_, ...), custom_call_target="tpu_custom_call" | custom-call | flops 1677721600 | bytes 262144 | tf_op jit(solution)/shard_map/pallas_call | solution.py:274
  (9 shorter events, 0.2 us)
Async XLA Ops:
  0.0 6.1 %collective-permute-start = (bf16[512,1280]{1,0:T(8,128)(2,1)}, bf16[512,1280]{1,0:T(8,128)(2,1)S(1)}, u32[]{:S(2)}, u32[]{:S(2)}) collective-permute-start(bf16[512,1280]{1,0:T(8,128)(2,1)} %hidden_ref.1), channel_id=1, source_target_pairs={{0,1},{1,0},{2,3},{3,2},{4,5},{5,4},{6,7},{7,6},{8,9},{9,8},{10,11... | collective-permute-start | bytes 3932168 | tf_op jit(solution)/shard_map/ppermute | solution.py:297
  3.2 22.8 %collective-permute-start.7 = (bf16[512,1280]{1,0:T(8,128)(2,1)}, bf16[512,1280]{1,0:T(8,128)(2,1)S(1)}, u32[]{:S(2)}, u32[]{:S(2)}) collective-permute-start(bf16[512,1280]{1,0:T(8,128)(2,1)} %hidden_ref.1), channel_id=1, source_target_pairs={{0,1},{1,2},{2,3},{3,4},{4,5},{5,6},{6,7},{7,8},{8,9},{9,10},{10,1... | collective-permute-start | bytes 3932168 | tf_op jit(solution)/shard_map/ppermute | solution.py:297
  3.2 1.3 %copy-start.2 = (bf16[512,1280]{1,0:T(8,128)(2,1)S(1)}, bf16[512,1280]{1,0:T(8,128)(2,1)}, u32[]{:S(2)}) copy-start(bf16[512,1280]{1,0:T(8,128)(2,1)} %hidden_ref.1) | copy-start | bytes 3932164
  4.6 8.3 %copy-start.5 = (bf16[1280,640]{1,0:T(8,128)(2,1)S(1)}, bf16[1280,640]{1,0:T(8,128)(2,1)}, u32[]{:S(2)}) copy-start(bf16[1280,640]{1,0:T(8,128)(2,1)} %weight_ref.1) | copy-start | bytes 4915204
  4.6 8.2 %copy-start.6 = (f32[1280]{0:T(1024)S(1)}, f32[1280]{0:T(1024)}, u32[]{:S(2)}) copy-start(f32[1280]{0:T(1024)} %param.10) | copy-start | bytes 15364
  4.7 8.2 %copy-start.7 = (f32[1280]{0:T(1024)S(1)}, f32[1280]{0:T(1024)}, u32[]{:S(2)}) copy-start(f32[1280]{0:T(1024)} %param.9) | copy-start | bytes 15364
  4.7 8.3 %copy-start.3 = (bf16[512,1280]{1,0:T(8,128)(2,1)S(1)}, bf16[512,1280]{1,0:T(8,128)(2,1)}, u32[]{:S(2)}) copy-start(bf16[512,1280]{1,0:T(8,128)(2,1)} %hidden_ref.1) | copy-start | bytes 3932164
  6.3 8.5 %collective-permute-start.1 = (bf16[64,1280]{1,0:T(8,128)(2,1)S(1)}, bf16[64,1280]{1,0:T(8,128)(2,1)S(1)}, u32[]{:S(2)}, u32[]{:S(2)}) collective-permute-start(bf16[64,1280]{1,0:T(8,128)(2,1)S(1)} %get-tuple-element.54), channel_id=1, source_target_pairs={{0,32},{1,97}} | collective-permute-start | bytes 491528 | tf_op jit(solution)/shard_map/ppermute | solution.py:297
  9.1 5.7 %collective-permute-start.2 = (bf16[64,1280]{1,0:T(8,128)(2,1)S(1)}, bf16[64,1280]{1,0:T(8,128)(2,1)S(1)}, u32[]{:S(2)}, u32[]{:S(2)}) collective-permute-start(bf16[64,1280]{1,0:T(8,128)(2,1)S(1)} %get-tuple-element.55), channel_id=1, source_target_pairs={{0,2},{1,7}} | collective-permute-start | bytes 491528 | tf_op jit(solution)/shard_map/ppermute | solution.py:297
  10.4 4.7 %collective-permute-start.3 = (bf16[64,1280]{1,0:T(8,128)(2,1)S(1)}, bf16[64,1280]{1,0:T(8,128)(2,1)S(1)}, u32[]{:S(2)}, u32[]{:S(2)}) collective-permute-start(bf16[64,1280]{1,0:T(8,128)(2,1)S(1)} %get-tuple-element.56), channel_id=1, source_target_pairs={{0,34},{1,103}} | collective-permute-start | bytes 491528 | tf_op jit(solution)/shard_map/ppermute | solution.py:297
  12.9 13.1 %copy-start = (bf16[1280,640]{1,0:T(8,128)(2,1)S(1)}, bf16[1280,640]{1,0:T(8,128)(2,1)}, u32[]{:S(2)}) copy-start(bf16[1280,640]{1,0:T(8,128)(2,1)} %key_ref.5) | copy-start | bytes 4915204
  13.0 13.1 %copy-start.1 = (bf16[1280,640]{1,0:T(8,128)(2,1)S(1)}, bf16[1280,640]{1,0:T(8,128)(2,1)}, u32[]{:S(2)}) copy-start(bf16[1280,640]{1,0:T(8,128)(2,1)} %value_ref.5) | copy-start | bytes 4915204
  15.2 4.6 %collective-permute-start.4 = (bf16[64,1280]{1,0:T(8,128)(2,1)S(1)}, bf16[64,1280]{1,0:T(8,128)(2,1)S(1)}, u32[]{:S(2)}, u32[]{:S(2)}) collective-permute-start(bf16[64,1280]{1,0:T(8,128)(2,1)S(1)} %get-tuple-element.58.refs_0_), channel_id=1, source_target_pairs={{0,104},{1,185},{2,106},{7,191},{32,72},{34,74},{97,217},{103,223}} | collective-permute-start | bytes 491528 | tf_op jit(solution)/shard_map/ppermute | solution.py:297
  17.2 3.5 %collective-permute-start.5 = (bf16[64,1280]{1,0:T(8,128)(2,1)S(1)}, bf16[64,1280]{1,0:T(8,128)(2,1)S(1)}, u32[]{:S(2)}, u32[]{:S(2)}) collective-permute-start(bf16[64,1280]{1,0:T(8,128)(2,1)S(1)} %get-tuple-element.58.refs_0_), channel_id=1, source_target_pairs={{0,96},{1,33},{2,98},{7,39},{32,64},{34,66},{97,65},{103,71}} | collective-permute-start | bytes 491528 | tf_op jit(solution)/shard_map/ppermute | solution.py:297
  18.5 3.5 %collective-permute-start.6 = (bf16[64,1280]{1,0:T(8,128)(2,1)S(1)}, bf16[64,1280]{1,0:T(8,128)(2,1)S(1)}, u32[]{:S(2)}, u32[]{:S(2)}) collective-permute-start(bf16[64,1280]{1,0:T(8,128)(2,1)S(1)} %get-tuple-element.58.refs_0_), channel_id=1, source_target_pairs={{0,8},{1,153},{2,10},{7,159},{32,40},{34,42},{97,249},{103,255}} | collective-permute-start | bytes 491528 | tf_op jit(solution)/shard_map/ppermute | solution.py:297
  22.1 6.5 %collective-permute-start.10 = (bf16[64,1280]{1,0:T(8,128)(2,1)S(1)}, bf16[64,1280]{1,0:T(8,128)(2,1)S(1)}, u32[]{:S(2)}, u32[]{:S(2)}) collective-permute-start(bf16[64,1280]{1,0:T(8,128)(2,1)S(1)} %get-tuple-element.62.refs_0_), channel_id=1, source_target_pairs={{0,150},{1,19},{2,148},{7,21},{8,30},{10,28},{32,182},{33,51},{34,... | collective-permute-start | bytes 491528 | tf_op jit(solution)/shard_map/ppermute | solution.py:297
  23.4 5.2 %collective-permute-start.8 = (bf16[64,1280]{1,0:T(8,128)(2,1)S(1)}, bf16[64,1280]{1,0:T(8,128)(2,1)S(1)}, u32[]{:S(2)}, u32[]{:S(2)}) collective-permute-start(bf16[64,1280]{1,0:T(8,128)(2,1)S(1)} %get-tuple-element.62.refs_0_), channel_id=1, source_target_pairs={{0,6},{1,3},{2,4},{7,5},{8,14},{10,12},{32,38},{33,35},{34,36},{39... | collective-permute-start | bytes 491528 | tf_op jit(solution)/shard_map/ppermute | solution.py:297
  24.7 3.9 %collective-permute-start.9 = (bf16[64,1280]{1,0:T(8,128)(2,1)S(1)}, bf16[64,1280]{1,0:T(8,128)(2,1)S(1)}, u32[]{:S(2)}, u32[]{:S(2)}) collective-permute-start(bf16[64,1280]{1,0:T(8,128)(2,1)S(1)} %get-tuple-element.62.refs_0_), channel_id=1, source_target_pairs={{0,144},{1,17},{2,146},{7,23},{8,24},{10,26},{32,176},{33,49},{34,... | collective-permute-start | bytes 491528 | tf_op jit(solution)/shard_map/ppermute | solution.py:297
  28.7 3.7 %collective-permute-start.11 = (bf16[64,1280]{1,0:T(8,128)(2,1)S(1)}, bf16[64,1280]{1,0:T(8,128)(2,1)S(1)}, u32[]{:S(2)}, u32[]{:S(2)}) collective-permute-start(bf16[64,1280]{1,0:T(8,128)(2,1)S(1)} %get-tuple-element.66.refs_0_), channel_id=1, source_target_pairs={{0,152},{1,9},{2,154},{3,11},{4,156},{5,13},{6,158},{7,15},{8,16},... | collective-permute-start | bytes 491528 | tf_op jit(solution)/shard_map/ppermute | solution.py:297
  32.4 7.4 %collective-permute-start.12 = (bf16[32,1280]{1,0:T(8,128)(2,1)S(1)}, bf16[32,1280]{1,0:T(8,128)(2,1)S(1)}, u32[]{:S(2)}, u32[]{:S(2)}) collective-permute-start(bf16[32,1280]{1,0:T(8,128)(2,1)S(1)} %get-tuple-element.69.refs_0_), channel_id=1, source_target_pairs={{0,32},{1,97},{2,34},{3,99},{4,36},{5,101},{6,38},{7,103},{8,40},{... | collective-permute-start | bytes 245768 | tf_op jit(solution)/shard_map/ppermute | solution.py:297
  34.3 5.5 %collective-permute-start.13 = (bf16[32,1280]{1,0:T(8,128)(2,1)S(1)}, bf16[32,1280]{1,0:T(8,128)(2,1)S(1)}, u32[]{:S(2)}, u32[]{:S(2)}) collective-permute-start(bf16[32,1280]{1,0:T(8,128)(2,1)S(1)} %get-tuple-element.70.refs_2_), channel_id=1, source_target_pairs={{0,2},{1,7},{2,0},{3,5},{4,6},{5,3},{6,4},{7,1},{8,10},{9,15},{10,... | collective-permute-start | bytes 245768 | tf_op jit(solution)/shard_map/ppermute | solution.py:297
  39.9 3.6 %collective-permute-start.14 = (bf16[128,1280]{1,0:T(8,128)(2,1)S(1)}, bf16[128,1280]{1,0:T(8,128)(2,1)S(1)}, u32[]{:S(2)}, u32[]{:S(2)}) collective-permute-start(bf16[128,1280]{1,0:T(8,128)(2,1)S(1)} %get-tuple-element.72.refs_0_), channel_id=1, source_target_pairs={{0,1},{1,0},{2,3},{3,2},{4,5},{5,4},{6,7},{7,6},{8,9},{9,8},{10,11... | collective-permute-start | bytes 983048 | tf_op jit(solution)/shard_map/ppermute | solution.py:297
  40.5 7.3 %collective-permute-start.15 = (bf16[64,1280]{1,0:T(8,128)(2,1)S(1)}, bf16[64,1280]{1,0:T(8,128)(2,1)S(1)}, u32[]{:S(2)}, u32[]{:S(2)}) collective-permute-start(bf16[64,1280]{1,0:T(8,128)(2,1)S(1)} %get-tuple-element.80), channel_id=1, source_target_pairs={{0,2},{1,7},{2,0},{3,5},{4,6},{5,3},{6,4},{7,1},{8,10},{9,15},{10,... | collective-permute-start | bytes 491528 | tf_op jit(solution)/shard_map/ppermute | solution.py:297
  42.4 5.4 %collective-permute-start.16 = (bf16[64,1280]{1,0:T(8,128)(2,1)S(1)}, bf16[64,1280]{1,0:T(8,128)(2,1)S(1)}, u32[]{:S(2)}, u32[]{:S(2)}) collective-permute-start(bf16[64,1280]{1,0:T(8,128)(2,1)S(1)} %get-tuple-element.81), channel_id=1, source_target_pairs={{0,32},{1,97},{2,34},{3,99},{4,36},{5,101},{6,38},{7,103},{8,40},{... | collective-permute-start | bytes 491528 | tf_op jit(solution)/shard_map/ppermute | solution.py:297
  43.5 4.4 %copy-start.8 = (f32[1280]{0:T(1024)S(1)}, f32[1280]{0:T(1024)}, u32[]{:S(2)}) copy-start(f32[1280]{0:T(1024)} %param.15) | copy-start | bytes 15364
  47.9 1.7 %collective-permute-start.17 = (bf16[128,1280]{1,0:T(8,128)(2,1)S(1)}, bf16[128,1280]{1,0:T(8,128)(2,1)S(1)}, u32[]{:S(2)}, u32[]{:S(2)}) collective-permute-start(bf16[128,1280]{1,0:T(8,128)(2,1)S(1)} %get-tuple-element.83.rows_ref), channel_id=1, source_target_pairs={{0,1},{1,0},{2,3},{3,2},{4,5},{5,4},{6,7},{7,6},{8,9},{9,8},{10,11... | collective-permute-start | bytes 983048 | tf_op jit(solution)/shard_map/ppermute | solution.py:297
  48.0 1.6 %copy-start.4 = (bf16[640,1280]{1,0:T(8,128)(2,1)S(1)}, bf16[640,1280]{1,0:T(8,128)(2,1)}, u32[]{:S(2)}) copy-start(bf16[640,1280]{1,0:T(8,128)(2,1)} %out_weight_ref.1) | copy-start | bytes 4915204
